TPU v7x, 32 devices: a whole 2x2x4 slice. The times are simulated.
32 devices in a mesh: seq: 8 (over z, y), fsdp: 4 (over x, core).
Axes of the slice: x: 2, y: 2, z: 4, core: 2. Of those that a mesh axis runs over, the one named last changes fastest.
Arguments:
- queries: bfloat16 [2048, 4096], P('seq', 'fsdp'), may hold values from -6 to 6
- keys: bfloat16 [2048, 4096], P('seq', 'fsdp'), may hold values from -6 to 6
- values: bfloat16 [2048, 4096], P('seq', 'fsdp'), may hold values from -6 to 6
- filters: float32 [2048, 4096], P('seq', 'fsdp'), as said below
- skip_weight: float32 [4096], P('fsdp'), may hold values from -4 to 4
- out_weight: bfloat16 [4096, 4096], P('fsdp'), may hold values from -0.125 to 0.125
Outputs:
- mixed_out: bfloat16 [2048, 4096], P('seq', 'fsdp')
Inputs may be any that keep to these rules, and one draw needn't show every extreme that they name: `filters`: real filter values of the 4096 channels at 2048 lags.
All inputs are finite; a program needn't handle non-finite values.
Results may differ from a plain program's by a relative error of at most 0.0049.
Values may be sent and summed in bfloat16 or wider, within the bound.
No kernel may reach another device: no remote copies, remote signals or barrier semaphores. Data moves between devices by JAX's collectives and lax.ppermute only.
A program may use at most 128 MiB of HBM per device.

v0:
```python
import functools

import numpy as np

import jax
import jax.numpy as jnp
from jax import lax
from jax.experimental import pallas as pl
from jax.experimental.pallas import tpu as pltpu
from jax.sharding import PartitionSpec as P

BF16 = jnp.bfloat16
F32 = jnp.float32
CONV_VMEM = 24 * 2**20
PROJECT_VMEM = 24 * 2**20
SMALL_VMEM = 12 * 2**20


def split_bf16(table):
    high = table.astype(BF16)
    low = (table - high.astype(np.float64)).astype(BF16)
    return np.concatenate([high, low], axis=0)


def make_tables(rows):
    order = np.concatenate([np.arange(0, rows, 2), np.arange(1, rows, 2)])
    times = np.arange(rows)
    angle = np.pi * (((2 * order[:, None] + 1) * times[None, :]) % (4 * rows)) / (2 * rows)
    forward = np.concatenate([np.cos(angle), -np.sin(angle)], axis=0)
    backward = forward.T / rows
    return split_bf16(forward), split_bf16(backward)


def peer_of(slot):
    return lax.bitwise_xor(lax.axis_index("seq"), slot)


def peer_block(slot, size):
    return pl.ds(pl.multiple_of(peer_of(slot) * size, size), size)


def pre_kernel(n_peers, keys_hbm, values_hbm, filters_hbm, fwd_hbm, bwd_hbm, *refs):
    out_refs = refs[:n_peers]
    fwd_ref, bwd_ref, keys, values, filters, sem = refs[n_peers:]
    chans = keys.shape[1] // n_peers
    copies = [
        pltpu.make_async_copy(src, dst, sem.at[i])
        for i, (src, dst) in enumerate(
            (
                (keys_hbm, keys),
                (values_hbm, values),
                (filters_hbm, filters),
                (fwd_hbm, fwd_ref),
                (bwd_hbm, bwd_ref),
            )
        )
    ]
    for copy in copies:
        copy.start()
    for copy in copies[:3]:
        copy.wait()
    for slot, out_ref in zip(slots_of(n_peers, False), out_refs):
        at = peer_block(slot, chans)
        product = keys[:, at].astype(F32) * values[:, at].astype(F32)
        out_ref[:, :chans] = product.astype(BF16)
        out_ref[:, chans:] = filters[:, at].astype(BF16)
    for copy in copies[3:]:
        copy.wait()


def pre(keys, values, filters, fwd, bwd, n_peers):
    rows, width = keys.shape
    chans = width // n_peers
    args = [
        pltpu.with_memory_space_constraint(a, pltpu.HBM) for a in (keys, values, filters, fwd, bwd)
    ]
    *blocks, fwd, bwd = pl.pallas_call(
        functools.partial(pre_kernel, n_peers),
        in_specs=[pl.BlockSpec(memory_space=pltpu.HBM)] * 5,
        out_specs=[pl.BlockSpec(memory_space=pltpu.VMEM)] * (n_peers + 2),
        out_shape=[jax.ShapeDtypeStruct((rows, 2 * chans), BF16)] * n_peers
        + [jax.ShapeDtypeStruct(t.shape, BF16) for t in (fwd, bwd)],
        scratch_shapes=[
            pltpu.VMEM((rows, width), BF16),
            pltpu.VMEM((rows, width), BF16),
            pltpu.VMEM((rows, width), F32),
            pltpu.SemaphoreType.DMA((5,)),
        ],
        compiler_params=pltpu.CompilerParams(vmem_limit_bytes=SMALL_VMEM),
        cost_estimate=pl.CostEstimate(
            flops=rows * width, bytes_accessed=12 * rows * width, transcendentals=0
        ),
    )(*args)
    return blocks, fwd, bwd


def slots_of(n_peers, back):
    half = n_peers // 2
    near, far = list(range(1, half)), list(range(half, n_peers))
    if back:
        return [0, near[0], far[0], near[1], far[1]] + near[2:] + far[2:]
    return [0, far[0], near[0], far[1], near[1]] + near[2:] + far[2:]


def exchange(blocks, n_peers, back):
    return [
        lax.ppermute(block, "seq", [(i, i ^ slot) for i in range(n_peers)]) if slot else block
        for slot, block in zip(slots_of(n_peers, back), blocks)
    ]


def conv_kernel(fwd_ref, bwd_ref, *refs):
    *refs, spec, turned = refs
    n_blocks = spec.shape[0]
    in_refs, out_refs = refs[:n_blocks], refs[n_blocks:]
    rows, chans = in_refs[0].shape[0], in_refs[0].shape[1] // 2
    step = 8

    for slot, in_ref in zip(slots_of(n_blocks, False), in_refs):
        j = peer_of(slot)
        block = in_ref[...]
        high = jnp.dot(fwd_ref[: 2 * rows], block, preferred_element_type=F32)
        low = jnp.dot(fwd_ref[2 * rows :], block, preferred_element_type=F32)
        spec[j] = high + low

    def mix(row, sign):
        re, im = pl.ds(row, step), pl.ds(row + rows, step)
        x_re = [spec[j, re, :chans] for j in range(n_blocks)]
        x_im = [spec[j, im, :chans] for j in range(n_blocks)]
        out_re, out_im = [None] * n_blocks, [None] * n_blocks
        last_re = last_im = None
        for d in range(n_blocks):
            f_re, f_im = spec[d, re, chans:], spec[d, im, chans:]
            g_re, g_im = f_re, f_im
            if d > 0:
                g_re, g_im = f_re - sign * last_im, f_im + sign * last_re
            last_re, last_im = f_re, f_im
            for i in range(d, n_blocks):
                a_re, a_im = x_re[i - d], x_im[i - d]
                t_re = g_re * a_re - g_im * a_im
                t_im = g_re * a_im + g_im * a_re
                out_re[i] = t_re if d == 0 else out_re[i] + t_re
                out_im[i] = t_im if d == 0 else out_im[i] + t_im
        for i in range(n_blocks):
            for where, value in ((re, out_re[i]), (im, out_im[i])):
                high = value.astype(BF16).astype(F32)
                turned[i, where, :chans] = high
                turned[i, where, chans:] = value - high

    half = rows // 2

    @pl.loop(0, half // step)
    def _(t):
        row = pl.multiple_of(t * step, step)
        mix(row, 1.0)

    @pl.loop(half // step, rows // step)
    def _(t):
        row = pl.multiple_of(t * step, step)
        mix(row, -1.0)

    for slot, out_ref in zip(slots_of(n_blocks, True), out_refs):
        i = peer_of(slot)
        both = jnp.dot(bwd_ref[...], turned[i].astype(BF16), preferred_element_type=F32)
        value = both[:rows, :chans] + both[:rows, chans:] + both[rows:, :chans]
        out_ref[...] = value.astype(BF16)


def conv_fast(received, fwd, bwd):
    n_blocks = len(received)
    rows, chans = received[0].shape[0], received[0].shape[1] // 2
    whole = pl.BlockSpec(memory_space=pltpu.VMEM)
    return pl.pallas_call(
        conv_kernel,
        in_specs=[whole] * (2 + n_blocks),
        out_specs=[whole] * n_blocks,
        out_shape=[jax.ShapeDtypeStruct((rows, chans), BF16)] * n_blocks,
        scratch_shapes=[
            pltpu.VMEM((n_blocks, 2 * rows, 2 * chans), F32),
            pltpu.VMEM((n_blocks, 2 * rows, 2 * chans), F32),
        ],
        compiler_params=pltpu.CompilerParams(vmem_limit_bytes=CONV_VMEM),
        cost_estimate=pl.CostEstimate(
            flops=16 * n_blocks * rows * rows * chans * 2, bytes_accessed=4 * 2**20, transcendentals=0
        ),
    )(fwd, bwd, *received)


def conv_plain(received, fwd, bwd):
    n_blocks, rows, chans = received.shape[0], received.shape[1], received.shape[2] // 2
    exact = lax.Precision.HIGHEST
    fwd32 = fwd[: 2 * rows].astype(F32) + fwd[2 * rows :].astype(F32)
    bwd32 = bwd[:rows].astype(F32) + bwd[rows:].astype(F32)
    sign = jnp.where(jnp.arange(rows) < rows // 2, 1.0, -1.0).astype(F32)[:, None]

    def spectrum(blocks):
        spec = jnp.einsum("kt,jtc->jkc", fwd32, blocks.astype(F32), precision=exact)
        return spec[:, :rows], spec[:, rows:]

    x_re, x_im = spectrum(received[:, :, :chans])
    f_re, f_im = spectrum(received[:, :, chans:])
    g_re = f_re.at[1:].add(-sign * f_im[:-1])
    g_im = f_im.at[1:].add(sign * f_re[:-1])

    def one(d, total):
        t_re, t_im = total
        later = (jnp.arange(n_blocks) >= d)[:, None, None]
        a_re = jnp.where(later, jnp.roll(x_re, d, axis=0), 0.0)
        a_im = jnp.where(later, jnp.roll(x_im, d, axis=0), 0.0)
        return (
            t_re + g_re[d] * a_re - g_im[d] * a_im,
            t_im + g_re[d] * a_im + g_im[d] * a_re,
        )

    zero = jnp.zeros_like(x_re)
    y_re, y_im = lax.fori_loop(0, n_blocks, one, (zero, zero))
    both = jnp.concatenate([y_re, y_im], axis=1)
    return jnp.einsum("tk,jkc->jtc", bwd32, both, precision=exact).astype(BF16)


def gate_kernel(queries_ref, keys_ref, values_ref, skip_ref, *refs):
    *conv_refs, out_ref = refs
    chans = conv_refs[0].shape[1]
    for slot, conv_ref in zip(slots_of(len(conv_refs), True), conv_refs):
        at = peer_block(slot, chans)
        product = keys_ref[:, at].astype(F32) * values_ref[:, at].astype(F32)
        mixed = conv_ref[...].astype(F32) + skip_ref[:, at] * product
        out_ref[:, at] = (queries_ref[:, at].astype(F32) * mixed).astype(BF16)


def gate(queries, keys, values, skip, conv):
    rows, width = queries.shape
    whole = pl.BlockSpec(memory_space=pltpu.VMEM)
    return pl.pallas_call(
        gate_kernel,
        in_specs=[whole] * (4 + len(conv)),
        out_specs=whole,
        out_shape=jax.ShapeDtypeStruct((rows, width), BF16),
        compiler_params=pltpu.CompilerParams(vmem_limit_bytes=SMALL_VMEM),
        cost_estimate=pl.CostEstimate(
            flops=4 * rows * width, bytes_accessed=10 * rows * width, transcendentals=0
        ),
    )(queries, keys, values, skip, *conv)


def side_columns(across, out_width):
    place = lax.axis_index("fsdp")
    core, side = lax.rem(place, 2), lax.div(place, 2)
    side = jnp.where(across, 1 - side, side)
    return pl.multiple_of((2 * side + core) * out_width, out_width)


def project_kernel(across, first, mine_ref, theirs_ref, own_w_ref, their_w_ref, out_ref):
    width = out_ref.shape[1]
    start = side_columns(across, own_w_ref.shape[1] // 4) + first
    at = pl.ds(pl.multiple_of(start, width), width)
    total = jnp.dot(mine_ref[...], own_w_ref[:, at], preferred_element_type=F32)
    total += jnp.dot(theirs_ref[...], their_w_ref[:, at], preferred_element_type=F32)
    out_ref[...] = total.astype(out_ref.dtype)


def project(mine, theirs, own_weight, their_weight, across, first, width, dtype):
    rows, depth = mine.shape
    return pl.pallas_call(
        functools.partial(project_kernel, across, first),
        in_specs=[pl.BlockSpec(memory_space=pltpu.VMEM)] * 4,
        out_specs=pl.BlockSpec(memory_space=pltpu.VMEM),
        out_shape=jax.ShapeDtypeStruct((rows, width), dtype),
        compiler_params=pltpu.CompilerParams(vmem_limit_bytes=PROJECT_VMEM),
        cost_estimate=pl.CostEstimate(
            flops=4 * rows * depth * width, bytes_accessed=4 * depth * width, transcendentals=0
        ),
    )(mine, theirs, own_weight, their_weight)


def finish_kernel(own_ref, *refs):
    *arrived_refs, out_ref = refs
    width = out_ref.shape[1] // len(arrived_refs)
    for c, arrived_ref in enumerate(arrived_refs):
        at = slice(c * width, (c + 1) * width)
        out_ref[:, at] = (own_ref[:, at] + arrived_ref[...].astype(F32)).astype(out_ref.dtype)


def finish(own, arrived):
    rows, width = own.shape
    whole = pl.BlockSpec(memory_space=pltpu.VMEM)
    return pl.pallas_call(
        finish_kernel,
        in_specs=[whole] * (1 + len(arrived)),
        out_specs=whole,
        out_shape=jax.ShapeDtypeStruct((rows, width), BF16),
        compiler_params=pltpu.CompilerParams(vmem_limit_bytes=SMALL_VMEM),
        cost_estimate=pl.CostEstimate(
            flops=rows * width, bytes_accessed=8 * rows * width, transcendentals=0
        ),
    )(own, *arrived)


def body(pieces, tables, queries, keys, values, filters, skip_weight, out_weight):
    rows, width = keys.shape
    n_peers = lax.axis_size("seq")
    chans = width // n_peers
    fwd, bwd = (jnp.asarray(t) for t in tables)
    skip = skip_weight[None, :]
    in_chip = [(0, 1), (1, 0), (2, 3), (3, 2)]
    across = [(0, 2), (2, 0), (1, 3), (3, 1)]

    if chans % 128 == 0 and n_peers in (8, 16):
        blocks, fwd, bwd = pre(keys, values, filters, fwd, bwd, n_peers)
        received = exchange(blocks, n_peers, False)
        out_weight, received = lax.optimization_barrier((out_weight, received))
        their_weight = lax.ppermute(out_weight, "fsdp", in_chip)
        back = exchange(conv_fast(received, fwd, bwd), n_peers, True)
        gated = gate(queries, keys, values, skip, back)
    else:
        their_weight = lax.ppermute(out_weight, "fsdp", in_chip)
        product = keys.astype(F32) * values.astype(F32)
        parts = [a.astype(BF16).reshape(rows, n_peers, chans) for a in (product, filters)]
        sent = jnp.concatenate(parts, axis=2).transpose(1, 0, 2)
        received = lax.all_to_all(sent, "seq", split_axis=0, concat_axis=0, tiled=True)
        conv = conv_plain(received, fwd, bwd)
        back = lax.all_to_all(conv, "seq", split_axis=0, concat_axis=0, tiled=True)
        mixed = back.transpose(1, 0, 2).reshape(rows, width).astype(F32) + skip * product
        gated = (queries.astype(F32) * mixed).astype(BF16)

    theirs = lax.ppermute(gated, "fsdp", in_chip)
    out_width = out_weight.shape[1] // 4
    piece = out_width // pieces
    arrived = []
    for c in range(pieces):
        remote = project(gated, theirs, out_weight, their_weight, True, c * piece, piece, BF16)
        arrived.append(lax.ppermute(remote, "fsdp", across))
    own = project(gated, theirs, out_weight, their_weight, False, 0, out_width, F32)
    return finish(own, arrived)


def solution(mesh):
    in_specs = (
        P("seq", "fsdp"),
        P("seq", "fsdp"),
        P("seq", "fsdp"),
        P("seq", "fsdp"),
        P("fsdp"),
        P("fsdp", None),
    )
    out_specs = P("seq", "fsdp")

    def run(queries, keys, values, filters, skip_weight, out_weight):
        rows = keys.shape[0] // mesh.shape["seq"]
        fn = functools.partial(body, 2, make_tables(rows))
        return jax.shard_map(fn, mesh=mesh, in_specs=in_specs, out_specs=out_specs, check_vma=False)(
            queries, keys, values, filters, skip_weight, out_weight
        )

    return run
```

profile of v0, /device:TPU:0, one launch (start us, length us, event | category | flops | bytes accessed | tf_op | source)
XLA Modules:
  0.0 69.5 jit_solution(6236276909175688886)
XLA Ops:
  0.0 2.2 %shard_map.82 = (bf16[256,256]{1,0:T(8,128)(2,1)S(1)}, bf16[256,256]{1,0:T(8,128)(2,1)S(1)}, bf16[256,256]{1,0:T(8,128)(2,1)S(1)}, bf16[256,256]{1,0:T(8,128)(2,...) custom-call(bf16[256,1024]{1,0:T(8,128)(2,1)} %keys_ref.1, ...), custom_call_target="tpu_custom_call" | custom-call | flops 262144 | bytes 3145728 | tf_op jit(solution)/shard_map/pallas_call | solution.py:77
  2.2 4.1 %collective-permute-start = (bf16[256,256]{1,0:T(8,128)(2,1)S(1)}, bf16[256,256]{1,0:T(8,128)(2,1)S(1)}, u32[]{:S(2)}, u32[]{:S(2)}) collective-permute-start(bf16[256,256]{1,0:T(8,128)(2,1)S(1)} %get-tuple-element.35), channel_id=1, source_target_pairs={{0,16},{4,20},{8,24},{12,28},{16,0},{20,4},{24,8},{28,12},{1,17},{... | collective-permute-start | bytes 393224 | tf_op jit(solution)/shard_map/ppermute | solution.py:107
  6.3 1.5 %collective-permute-start.1 = (bf16[256,256]{1,0:T(8,128)(2,1)S(1)}, bf16[256,256]{1,0:T(8,128)(2,1)S(1)}, u32[]{:S(2)}, u32[]{:S(2)}) collective-permute-start(bf16[256,256]{1,0:T(8,128)(2,1)S(1)} %get-tuple-element.36), channel_id=1, source_target_pairs={{0,4},{4,0},{8,12},{12,8},{16,20},{20,16},{24,28},{28,24},{1,5},{5... | collective-permute-start | bytes 393224 | tf_op jit(solution)/shard_map/ppermute | solution.py:107
  7.8 1.8 %collective-permute-start.3 = (bf16[256,256]{1,0:T(8,128)(2,1)S(1)}, bf16[256,256]{1,0:T(8,128)(2,1)S(1)}, u32[]{:S(2)}, u32[]{:S(2)}) collective-permute-start(bf16[256,256]{1,0:T(8,128)(2,1)S(1)} %get-tuple-element.38), channel_id=1, source_target_pairs={{0,8},{4,12},{8,0},{12,4},{16,24},{20,28},{24,16},{28,20},{1,9},{5... | collective-permute-start | bytes 393224 | tf_op jit(solution)/shard_map/ppermute | solution.py:107
  9.7 1.4 %collective-permute-start.4 = (bf16[256,256]{1,0:T(8,128)(2,1)S(1)}, bf16[256,256]{1,0:T(8,128)(2,1)S(1)}, u32[]{:S(2)}, u32[]{:S(2)}) collective-permute-start(bf16[256,256]{1,0:T(8,128)(2,1)S(1)} %get-tuple-element.39), channel_id=1, source_target_pairs={{0,12},{4,8},{8,4},{12,0},{16,28},{20,24},{24,20},{28,16},{1,13},{... | collective-permute-start | bytes 393224 | tf_op jit(solution)/shard_map/ppermute | solution.py:107
  11.1 5.2 %collective-permute-done.refs_1_ = bf16[256,256]{1,0:T(8,128)(2,1)S(1)} collective-permute-done((bf16[256,256]{1,0:T(8,128)(2,1)S(1)}, bf16[256,256]{1,0:T(8,128)(2,1)S(1)}, u32[]{:S(2)}, u32[]{:S(2)}) %collective-permute-start) | collective-permute-done | bytes 131104 | tf_op jit(solution)/shard_map/ppermute | solution.py:107
  16.2 2.9 %collective-permute-start.5 = (bf16[256,256]{1,0:T(8,128)(2,1)S(1)}, bf16[256,256]{1,0:T(8,128)(2,1)S(1)}, u32[]{:S(2)}, u32[]{:S(2)}) collective-permute-start(bf16[256,256]{1,0:T(8,128)(2,1)S(1)} %get-tuple-element.40), channel_id=1, source_target_pairs={{0,24},{4,28},{8,16},{12,20},{16,8},{20,12},{24,0},{28,4},{1,25},{... | collective-permute-start | bytes 393224 | tf_op jit(solution)/shard_map/ppermute | solution.py:107
  19.1 2.2 %collective-permute-start.6 = (bf16[256,256]{1,0:T(8,128)(2,1)S(1)}, bf16[256,256]{1,0:T(8,128)(2,1)S(1)}, u32[]{:S(2)}, u32[]{:S(2)}) collective-permute-start(bf16[256,256]{1,0:T(8,128)(2,1)S(1)} %get-tuple-element.41), channel_id=1, source_target_pairs={{0,28},{4,24},{8,20},{12,16},{16,12},{20,8},{24,4},{28,0},{1,29},{... | collective-permute-start | bytes 393224 | tf_op jit(solution)/shard_map/ppermute | solution.py:107
  21.4 1.7 %collective-permute-done.5.refs_6_ = bf16[256,256]{1,0:T(8,128)(2,1)S(1)} collective-permute-done((bf16[256,256]{1,0:T(8,128)(2,1)S(1)}, bf16[256,256]{1,0:T(8,128)(2,1)S(1)}, u32[]{:S(2)}, u32[]{:S(2)}) %collective-permute-start.5) | collective-permute-done | bytes 131104 | tf_op jit(solution)/shard_map/ppermute | solution.py:107
  23.0 4.1 %collective-permute-done.6.refs_7_ = bf16[256,256]{1,0:T(8,128)(2,1)S(1)} collective-permute-done((bf16[256,256]{1,0:T(8,128)(2,1)S(1)}, bf16[256,256]{1,0:T(8,128)(2,1)S(1)}, u32[]{:S(2)}, u32[]{:S(2)}) %collective-permute-start.6) | collective-permute-done | bytes 131104 | tf_op jit(solution)/shard_map/ppermute | solution.py:107
  27.1 4.4 %shard_map.83 = (bf16[256,128]{1,0:T(8,128)(2,1)S(1)}, bf16[256,128]{1,0:T(8,128)(2,1)S(1)}, bf16[256,128]{1,0:T(8,128)(2,1)S(1)}, bf16[256,128]{1,0:T(8,128)(2,...) custom-call(bf16[1024,256]{1,0:T(8,128)(2,1)S(1)} %get-tuple-element, ...), custom_call_target="tpu_custom_call" | custom-call | flops 2147483648 | bytes 4194304 | tf_op jit(solution)/shard_map/pallas_call | solution.py:173
  31.6 1.4 %collective-permute-start.7 = (bf16[256,128]{1,0:T(8,128)(2,1)S(1)}, bf16[256,128]{1,0:T(8,128)(2,1)S(1)}, u32[]{:S(2)}, u32[]{:S(2)}) collective-permute-start(bf16[256,128]{1,0:T(8,128)(2,1)S(1)} %get-tuple-element.51), channel_id=1, source_target_pairs={{0,4},{4,0},{8,12},{12,8},{16,20},{20,16},{24,28},{28,24},{1,5},{5... | collective-permute-start | bytes 196616 | tf_op jit(solution)/shard_map/ppermute | solution.py:107
  33.0 5.2 %collective-permute-start.8 = (bf16[256,128]{1,0:T(8,128)(2,1)S(1)}, bf16[256,128]{1,0:T(8,128)(2,1)S(1)}, u32[]{:S(2)}, u32[]{:S(2)}) collective-permute-start(bf16[256,128]{1,0:T(8,128)(2,1)S(1)} %get-tuple-element.52), channel_id=1, source_target_pairs={{0,16},{4,20},{8,24},{12,28},{16,0},{20,4},{24,8},{28,12},{1,17},{... | collective-permute-start | bytes 196616 | tf_op jit(solution)/shard_map/ppermute | solution.py:107
  38.1 1.8 %collective-permute-start.10 = (bf16[256,128]{1,0:T(8,128)(2,1)S(1)}, bf16[256,128]{1,0:T(8,128)(2,1)S(1)}, u32[]{:S(2)}, u32[]{:S(2)}) collective-permute-start(bf16[256,128]{1,0:T(8,128)(2,1)S(1)} %get-tuple-element.54), channel_id=1, source_target_pairs={{0,20},{4,16},{8,28},{12,24},{16,4},{20,0},{24,12},{28,8},{1,21},{... | collective-permute-start | bytes 196616 | tf_op jit(solution)/shard_map/ppermute | solution.py:107
  39.9 1.2 %collective-permute-start.11 = (bf16[256,128]{1,0:T(8,128)(2,1)S(1)}, bf16[256,128]{1,0:T(8,128)(2,1)S(1)}, u32[]{:S(2)}, u32[]{:S(2)}) collective-permute-start(bf16[256,128]{1,0:T(8,128)(2,1)S(1)} %get-tuple-element.55), channel_id=1, source_target_pairs={{0,12},{4,8},{8,4},{12,0},{16,28},{20,24},{24,20},{28,16},{1,13},{... | collective-permute-start | bytes 196616 | tf_op jit(solution)/shard_map/ppermute | solution.py:107
  41.1 1.0 %collective-permute-done.8.refs_2_ = bf16[256,128]{1,0:T(8,128)(2,1)S(1)} collective-permute-done((bf16[256,128]{1,0:T(8,128)(2,1)S(1)}, bf16[256,128]{1,0:T(8,128)(2,1)S(1)}, u32[]{:S(2)}, u32[]{:S(2)}) %collective-permute-start.8) | collective-permute-done | bytes 65568 | tf_op jit(solution)/shard_map/ppermute | solution.py:107
  42.1 1.5 %collective-permute-start.12 = (bf16[256,128]{1,0:T(8,128)(2,1)S(1)}, bf16[256,128]{1,0:T(8,128)(2,1)S(1)}, u32[]{:S(2)}, u32[]{:S(2)}) collective-permute-start(bf16[256,128]{1,0:T(8,128)(2,1)S(1)} %get-tuple-element.56), channel_id=1, source_target_pairs={{0,24},{4,28},{8,16},{12,20},{16,8},{20,12},{24,0},{28,4},{1,25},{... | collective-permute-start | bytes 196616 | tf_op jit(solution)/shard_map/ppermute | solution.py:107
  43.6 0.9 %collective-permute-done.9.refs_3_ = bf16[256,128]{1,0:T(8,128)(2,1)S(1)} collective-permute-done((bf16[256,128]{1,0:T(8,128)(2,1)S(1)}, bf16[256,128]{1,0:T(8,128)(2,1)S(1)}, u32[]{:S(2)}, u32[]{:S(2)}) %collective-permute-start.9) | collective-permute-done | bytes 65568 | tf_op jit(solution)/shard_map/ppermute | solution.py:107
  44.5 2.5 %collective-permute-start.13 = (bf16[256,128]{1,0:T(8,128)(2,1)S(1)}, bf16[256,128]{1,0:T(8,128)(2,1)S(1)}, u32[]{:S(2)}, u32[]{:S(2)}) collective-permute-start(bf16[256,128]{1,0:T(8,128)(2,1)S(1)} %get-tuple-element.57), channel_id=1, source_target_pairs={{0,28},{4,24},{8,20},{12,16},{16,12},{20,8},{24,4},{28,0},{1,29},{... | collective-permute-start | bytes 196616 | tf_op jit(solution)/shard_map/ppermute | solution.py:107
  46.9 0.1 collective-permute-done.11.refs_5_
  47.0 1.2 %collective-permute-done.12.refs_6_ = bf16[256,128]{1,0:T(8,128)(2,1)S(1)} collective-permute-done((bf16[256,128]{1,0:T(8,128)(2,1)S(1)}, bf16[256,128]{1,0:T(8,128)(2,1)S(1)}, u32[]{:S(2)}, u32[]{:S(2)}) %collective-permute-start.12) | collective-permute-done | bytes 65568 | tf_op jit(solution)/shard_map/ppermute | solution.py:107
  48.2 3.3 %collective-permute-done.13.refs_7_ = bf16[256,128]{1,0:T(8,128)(2,1)S(1)} collective-permute-done((bf16[256,128]{1,0:T(8,128)(2,1)S(1)}, bf16[256,128]{1,0:T(8,128)(2,1)S(1)}, u32[]{:S(2)}, u32[]{:S(2)}) %collective-permute-start.13) | collective-permute-done | bytes 65568 | tf_op jit(solution)/shard_map/ppermute | solution.py:107
  51.5 0.4 shard_map.84.mine_ref
  52.0 1.9 %collective-permute-done.14.theirs_ref = bf16[256,1024]{1,0:T(8,128)(2,1)S(1)} collective-permute-done((bf16[256,1024]{1,0:T(8,128)(2,1)S(1)}, bf16[256,1024]{1,0:T(8,128)(2,1)S(1)}, u32[]{:S(2)}, u32[]{:S(2)}) %collective-permute-start.14) | collective-permute-done | bytes 524320 | tf_op jit(solution)/shard_map/ppermute | solution.py:326
  53.9 0.7 %shard_map.86 = bf16[256,512]{1,0:T(8,128)(2,1)S(1)} custom-call(bf16[256,1024]{1,0:T(8,128)(2,1)S(1)} %shard_map.84.mine_ref, bf16[256,1024]{1,0:T(8,128)(2,1)S(1)} %collective-permute-done.14.theirs_ref, bf16[1024,4096]{1,0:T(8,128)(2,1)S(1)} %copy-done, bf16[1024,4096]{1,0:T(8,128)(2,1)S(1)} %collective-permute-done.15.their_w_ref), custom_call_target="tpu_custom_call" | custom-call | flops 536870912 | bytes 2097152 | tf_op jit(solution)/shard_map/pallas_call | solution.py:264
  54.6 1.6 %collective-permute-start.16 = (bf16[256,512]{1,0:T(8,128)(2,1)S(1)}, bf16[256,512]{1,0:T(8,128)(2,1)S(1)}, u32[]{:S(2)}, u32[]{:S(2)}) collective-permute-start(bf16[256,512]{1,0:T(8,128)(2,1)S(1)} %shard_map.86), channel_id=1, source_target_pairs={{0,2},{2,0},{1,3},{3,1},{4,6},{6,4},{5,7},{7,5},{8,10},{10,8},{9,1... | collective-permute-start | bytes 786440 | tf_op jit(solution)/shard_map/ppermute | solution.py:332
  56.2 0.7 %shard_map.87 = bf16[256,512]{1,0:T(8,128)(2,1)S(1)} custom-call(bf16[256,1024]{1,0:T(8,128)(2,1)S(1)} %shard_map.84.mine_ref, bf16[256,1024]{1,0:T(8,128)(2,1)S(1)} %collective-permute-done.14.theirs_ref, bf16[1024,4096]{1,0:T(8,128)(2,1)S(1)} %copy-done, bf16[1024,4096]{1,0:T(8,128)(2,1)S(1)} %collective-permute-done.15.their_w_ref), custom_call_target="tpu_custom_call" | custom-call | flops 536870912 | bytes 2097152 | tf_op jit(solution)/shard_map/pallas_call | solution.py:264
  56.9 0.6 collective-permute-start.17
  57.5 1.2 %shard_map.85.own_ref = f32[256,1024]{1,0:T(8,128)S(1)} custom-call(bf16[256,1024]{1,0:T(8,128)(2,1)S(1)} %shard_map.84.mine_ref, bf16[256,1024]{1,0:T(8,128)(2,1)S(1)} %collective-permute-done.14.theirs_ref, bf16[1024,4096]{1,0:T(8,128)(2,1)S(1)} %copy-done, bf16[1024,4096]{1,0:T(8,128)(2,1)S(1)} %collective-permute-done.15.their_w_ref), custom_call_target="tpu_custom_call" | custom-call | flops 1073741824 | bytes 4194304 | tf_op jit(solution)/shard_map/pallas_call | solution.py:264
  58.7 5.1 %collective-permute-done.16.refs_0_ = bf16[256,512]{1,0:T(8,128)(2,1)S(1)} collective-permute-done((bf16[256,512]{1,0:T(8,128)(2,1)S(1)}, bf16[256,512]{1,0:T(8,128)(2,1)S(1)}, u32[]{:S(2)}, u32[]{:S(2)}) %collective-permute-start.16) | collective-permute-done | bytes 262176 | tf_op jit(solution)/shard_map/ppermute | solution.py:332
  63.8 4.8 %collective-permute-done.17.refs_1_ = bf16[256,512]{1,0:T(8,128)(2,1)S(1)} collective-permute-done((bf16[256,512]{1,0:T(8,128)(2,1)S(1)}, bf16[256,512]{1,0:T(8,128)(2,1)S(1)}, u32[]{:S(2)}, u32[]{:S(2)}) %collective-permute-start.17) | collective-permute-done | bytes 262176 | tf_op jit(solution)/shard_map/ppermute | solution.py:332
  68.6 0.9 %shard_map.88 = bf16[256,1024]{1,0:T(8,128)(2,1)} custom-call(f32[256,1024]{1,0:T(8,128)S(1)} %shard_map.85.own_ref, bf16[256,512]{1,0:T(8,128)(2,1)S(1)} %collective-permute-done.16.refs_0_, bf16[256,512]{1,0:T(8,128)(2,1)S(1)} %collective-permute-done.17.refs_1_), custom_call_target="tpu_custom_call" | custom-call | flops 262144 | bytes 2097152 | tf_op jit(solution)/shard_map/pallas_call | solution.py:287
  (21 shorter events, 0.1 us)
Async XLA Ops:
  0.0 51.4 %copy-start.2 = (bf16[256,1024]{1,0:T(8,128)(2,1)S(1)}, bf16[256,1024]{1,0:T(8,128)(2,1)}, u32[]{:S(2)}) copy-start(bf16[256,1024]{1,0:T(8,128)(2,1)} %values_ref.1) | copy-start | bytes 1572868
  0.0 51.4 %copy-start.1 = (bf16[256,1024]{1,0:T(8,128)(2,1)S(1)}, bf16[256,1024]{1,0:T(8,128)(2,1)}, u32[]{:S(2)}) copy-start(bf16[256,1024]{1,0:T(8,128)(2,1)} %keys_ref.1) | copy-start | bytes 1572868
  0.0 53.9 %copy-start = (bf16[1024,4096]{1,0:T(8,128)(2,1)S(1)}, bf16[1024,4096]{1,0:T(8,128)(2,1)}, u32[]{:S(2)}) copy-start(bf16[1024,4096]{1,0:T(8,128)(2,1)} %own_w_ref.2) | copy-start | bytes 25165828
  0.0 51.4 %copy-start.4 = (f32[1024]{0:T(1024)S(1)}, f32[1024]{0:T(1024)}, u32[]{:S(2)}) copy-start(f32[1024]{0:T(1024)} %param.12) | copy-start | bytes 12292
  0.0 51.4 %copy-start.3 = (bf16[256,1024]{1,0:T(8,128)(2,1)S(1)}, bf16[256,1024]{1,0:T(8,128)(2,1)}, u32[]{:S(2)}) copy-start(bf16[256,1024]{1,0:T(8,128)(2,1)} %queries_ref.1) | copy-start | bytes 1572868
  2.2 14.1 %collective-permute-start = (bf16[256,256]{1,0:T(8,128)(2,1)S(1)}, bf16[256,256]{1,0:T(8,128)(2,1)S(1)}, u32[]{:S(2)}, u32[]{:S(2)}) collective-permute-start(bf16[256,256]{1,0:T(8,128)(2,1)S(1)} %get-tuple-element.35), channel_id=1, source_target_pairs={{0,16},{4,20},{8,24},{12,28},{16,0},{20,4},{24,8},{28,12},{1,17},{... | collective-permute-start | bytes 393224 | tf_op jit(solution)/shard_map/ppermute | solution.py:107
  6.3 12.9 %collective-permute-start.1 = (bf16[256,256]{1,0:T(8,128)(2,1)S(1)}, bf16[256,256]{1,0:T(8,128)(2,1)S(1)}, u32[]{:S(2)}, u32[]{:S(2)}) collective-permute-start(bf16[256,256]{1,0:T(8,128)(2,1)S(1)} %get-tuple-element.36), channel_id=1, source_target_pairs={{0,4},{4,0},{8,12},{12,8},{16,20},{20,16},{24,28},{28,24},{1,5},{5... | collective-permute-start | bytes 393224 | tf_op jit(solution)/shard_map/ppermute | solution.py:107
  7.8 13.6 %collective-permute-start.2 = (bf16[256,256]{1,0:T(8,128)(2,1)S(1)}, bf16[256,256]{1,0:T(8,128)(2,1)S(1)}, u32[]{:S(2)}, u32[]{:S(2)}) collective-permute-start(bf16[256,256]{1,0:T(8,128)(2,1)S(1)} %get-tuple-element.37), channel_id=1, source_target_pairs={{0,20},{4,16},{8,28},{12,24},{16,4},{20,0},{24,12},{28,8},{1,21},{... | collective-permute-start | bytes 393224 | tf_op jit(solution)/shard_map/ppermute | solution.py:107
  7.8 13.5 %collective-permute-start.3 = (bf16[256,256]{1,0:T(8,128)(2,1)S(1)}, bf16[256,256]{1,0:T(8,128)(2,1)S(1)}, u32[]{:S(2)}, u32[]{:S(2)}) collective-permute-start(bf16[256,256]{1,0:T(8,128)(2,1)S(1)} %get-tuple-element.38), channel_id=1, source_target_pairs={{0,8},{4,12},{8,0},{12,4},{16,24},{20,28},{24,16},{28,20},{1,9},{5... | collective-permute-start | bytes 393224 | tf_op jit(solution)/shard_map/ppermute | solution.py:107
  9.7 11.7 %collective-permute-start.4 = (bf16[256,256]{1,0:T(8,128)(2,1)S(1)}, bf16[256,256]{1,0:T(8,128)(2,1)S(1)}, u32[]{:S(2)}, u32[]{:S(2)}) collective-permute-start(bf16[256,256]{1,0:T(8,128)(2,1)S(1)} %get-tuple-element.39), channel_id=1, source_target_pairs={{0,12},{4,8},{8,4},{12,0},{16,28},{20,24},{24,20},{28,16},{1,13},{... | collective-permute-start | bytes 393224 | tf_op jit(solution)/shard_map/ppermute | solution.py:107
  16.2 6.8 %collective-permute-start.5 = (bf16[256,256]{1,0:T(8,128)(2,1)S(1)}, bf16[256,256]{1,0:T(8,128)(2,1)S(1)}, u32[]{:S(2)}, u32[]{:S(2)}) collective-permute-start(bf16[256,256]{1,0:T(8,128)(2,1)S(1)} %get-tuple-element.40), channel_id=1, source_target_pairs={{0,24},{4,28},{8,16},{12,20},{16,8},{20,12},{24,0},{28,4},{1,25},{... | collective-permute-start | bytes 393224 | tf_op jit(solution)/shard_map/ppermute | solution.py:107
  19.1 8.0 %collective-permute-start.6 = (bf16[256,256]{1,0:T(8,128)(2,1)S(1)}, bf16[256,256]{1,0:T(8,128)(2,1)S(1)}, u32[]{:S(2)}, u32[]{:S(2)}) collective-permute-start(bf16[256,256]{1,0:T(8,128)(2,1)S(1)} %get-tuple-element.41), channel_id=1, source_target_pairs={{0,28},{4,24},{8,20},{12,16},{16,12},{20,8},{24,4},{28,0},{1,29},{... | collective-permute-start | bytes 393224 | tf_op jit(solution)/shard_map/ppermute | solution.py:107
  27.1 26.8 %collective-permute-start.15 = (bf16[1024,4096]{1,0:T(8,128)(2,1)}, bf16[1024,4096]{1,0:T(8,128)(2,1)S(1)}, u32[]{:S(2)}, u32[]{:S(2)}) collective-permute-start(bf16[1024,4096]{1,0:T(8,128)(2,1)} %own_w_ref.2), channel_id=1, source_target_pairs={{0,1},{1,0},{2,3},{3,2},{4,5},{5,4},{6,7},{7,6},{8,9},{9,8},{10,11... | collective-permute-start | bytes 25165832 | tf_op jit(solution)/shard_map/ppermute | solution.py:312
  31.6 8.4 %collective-permute-start.7 = (bf16[256,128]{1,0:T(8,128)(2,1)S(1)}, bf16[256,128]{1,0:T(8,128)(2,1)S(1)}, u32[]{:S(2)}, u32[]{:S(2)}) collective-permute-start(bf16[256,128]{1,0:T(8,128)(2,1)S(1)} %get-tuple-element.51), channel_id=1, source_target_pairs={{0,4},{4,0},{8,12},{12,8},{16,20},{20,16},{24,28},{28,24},{1,5},{5... | collective-permute-start | bytes 196616 | tf_op jit(solution)/shard_map/ppermute | solution.py:107
  33.0 9.1 %collective-permute-start.8 = (bf16[256,128]{1,0:T(8,128)(2,1)S(1)}, bf16[256,128]{1,0:T(8,128)(2,1)S(1)}, u32[]{:S(2)}, u32[]{:S(2)}) collective-permute-start(bf16[256,128]{1,0:T(8,128)(2,1)S(1)} %get-tuple-element.52), channel_id=1, source_target_pairs={{0,16},{4,20},{8,24},{12,28},{16,0},{20,4},{24,8},{28,12},{1,17},{... | collective-permute-start | bytes 196616 | tf_op jit(solution)/shard_map/ppermute | solution.py:107
  38.1 6.3 %collective-permute-start.9 = (bf16[256,128]{1,0:T(8,128)(2,1)S(1)}, bf16[256,128]{1,0:T(8,128)(2,1)S(1)}, u32[]{:S(2)}, u32[]{:S(2)}) collective-permute-start(bf16[256,128]{1,0:T(8,128)(2,1)S(1)} %get-tuple-element.53), channel_id=1, source_target_pairs={{0,8},{4,12},{8,0},{12,4},{16,24},{20,28},{24,16},{28,20},{1,9},{5... | collective-permute-start | bytes 196616 | tf_op jit(solution)/shard_map/ppermute | solution.py:107
  38.1 8.8 %collective-permute-start.10 = (bf16[256,128]{1,0:T(8,128)(2,1)S(1)}, bf16[256,128]{1,0:T(8,128)(2,1)S(1)}, u32[]{:S(2)}, u32[]{:S(2)}) collective-permute-start(bf16[256,128]{1,0:T(8,128)(2,1)S(1)} %get-tuple-element.54), channel_id=1, source_target_pairs={{0,20},{4,16},{8,28},{12,24},{16,4},{20,0},{24,12},{28,8},{1,21},{... | collective-permute-start | bytes 196616 | tf_op jit(solution)/shard_map/ppermute | solution.py:107
  39.9 7.1 %collective-permute-start.11 = (bf16[256,128]{1,0:T(8,128)(2,1)S(1)}, bf16[256,128]{1,0:T(8,128)(2,1)S(1)}, u32[]{:S(2)}, u32[]{:S(2)}) collective-permute-start(bf16[256,128]{1,0:T(8,128)(2,1)S(1)} %get-tuple-element.55), channel_id=1, source_target_pairs={{0,12},{4,8},{8,4},{12,0},{16,28},{20,24},{24,20},{28,16},{1,13},{... | collective-permute-start | bytes 196616 | tf_op jit(solution)/shard_map/ppermute | solution.py:107
  42.1 6.1 %collective-permute-start.12 = (bf16[256,128]{1,0:T(8,128)(2,1)S(1)}, bf16[256,128]{1,0:T(8,128)(2,1)S(1)}, u32[]{:S(2)}, u32[]{:S(2)}) collective-permute-start(bf16[256,128]{1,0:T(8,128)(2,1)S(1)} %get-tuple-element.56), channel_id=1, source_target_pairs={{0,24},{4,28},{8,16},{12,20},{16,8},{20,12},{24,0},{28,4},{1,25},{... | collective-permute-start | bytes 196616 | tf_op jit(solution)/shard_map/ppermute | solution.py:107
  44.5 7.0 %collective-permute-start.13 = (bf16[256,128]{1,0:T(8,128)(2,1)S(1)}, bf16[256,128]{1,0:T(8,128)(2,1)S(1)}, u32[]{:S(2)}, u32[]{:S(2)}) collective-permute-start(bf16[256,128]{1,0:T(8,128)(2,1)S(1)} %get-tuple-element.57), channel_id=1, source_target_pairs={{0,28},{4,24},{8,20},{12,16},{16,12},{20,8},{24,4},{28,0},{1,29},{... | collective-permute-start | bytes 196616 | tf_op jit(solution)/shard_map/ppermute | solution.py:107
  51.9 2.0 %collective-permute-start.14 = (bf16[256,1024]{1,0:T(8,128)(2,1)S(1)}, bf16[256,1024]{1,0:T(8,128)(2,1)S(1)}, u32[]{:S(2)}, u32[]{:S(2)}) collective-permute-start(bf16[256,1024]{1,0:T(8,128)(2,1)S(1)} %shard_map.84.mine_ref), channel_id=1, source_target_pairs={{0,1},{1,0},{2,3},{3,2},{4,5},{5,4},{6,7},{7,6},{8,9},{9,8},{10,11... | collective-permute-start | bytes 1572872 | tf_op jit(solution)/shard_map/ppermute | solution.py:326
  54.6 9.2 %collective-permute-start.16 = (bf16[256,512]{1,0:T(8,128)(2,1)S(1)}, bf16[256,512]{1,0:T(8,128)(2,1)S(1)}, u32[]{:S(2)}, u32[]{:S(2)}) collective-permute-start(bf16[256,512]{1,0:T(8,128)(2,1)S(1)} %shard_map.86), channel_id=1, source_target_pairs={{0,2},{2,0},{1,3},{3,1},{4,6},{6,4},{5,7},{7,5},{8,10},{10,8},{9,1... | collective-permute-start | bytes 786440 | tf_op jit(solution)/shard_map/ppermute | solution.py:332
  56.9 11.7 %collective-permute-start.17 = (bf16[256,512]{1,0:T(8,128)(2,1)S(1)}, bf16[256,512]{1,0:T(8,128)(2,1)S(1)}, u32[]{:S(2)}, u32[]{:S(2)}) collective-permute-start(bf16[256,512]{1,0:T(8,128)(2,1)S(1)} %shard_map.87), channel_id=1, source_target_pairs={{0,2},{2,0},{1,3},{3,1},{4,6},{6,4},{5,7},{7,5},{8,10},{10,8},{9,1... | collective-permute-start | bytes 786440 | tf_op jit(solution)/shard_map/ppermute | solution.py:332
where the time goes:
time: 69.7 us; the launch traced here: 69.5 us
  starting transfers between devices  29.7 us (43%)
  waiting for transfers between devices  29.1 us (42%)
  Pallas kernels  10.6 us (15%)
    ppermute x14, starting transfers between devices, exchange(): lax.ppermute(block, 'seq', [(i, i ^ slot) for i in range(n_peers)])  27.5 us
    ppermute x14, waiting for transfers between devices, exchange(): lax.ppermute(block, 'seq', [(i, i ^ slot) for i in range(n_peers)])  17.3 us
    ppermute x2, waiting for transfers between devices, body(): arrived.append(lax.ppermute(remote, 'fsdp', across))  9.9 us
    pallas_call x1, Pallas kernels, conv_fast(): pl.pallas_call(conv_kernel, in_specs=[whole] * (2 + n_blocks), out_specs=...  4.45 us
    pallas_call x3, Pallas kernels, project(): pl.pallas_call(functools.partial(project_kernel, across, first), in_specs...  2.67 us
    ppermute x2, starting transfers between devices, body(): arrived.append(lax.ppermute(remote, 'fsdp', across))  2.16 us
    pallas_call x1, Pallas kernels, pre(): pl.pallas_call(functools.partial(pre_kernel, n_peers), in_specs=[pl.Block...  2.15 us
    ppermute x1, waiting for transfers between devices, body(): theirs = lax.ppermute(gated, 'fsdp', in_chip)  1.9 us
  transfers between devices with their start and end apart: 18, of which 11 were waited for; matrix products, arithmetic and copies ran while one was open for 0% of the time, Pallas kernels for 10%

commit v1 on v0

--- a/solution.py
+++ b/solution.py
@@ -18,8 +18,7 @@
 
 def split_bf16(table):
     high = table.astype(BF16)
-    low = (table - high.astype(np.float64)).astype(BF16)
-    return np.concatenate([high, low], axis=0)
+    return high, (table - high.astype(np.float64)).astype(BF16)
 
 
 def make_tables(rows):
@@ -27,8 +26,12 @@
     times = np.arange(rows)
     angle = np.pi * (((2 * order[:, None] + 1) * times[None, :]) % (4 * rows)) / (2 * rows)
     forward = np.concatenate([np.cos(angle), -np.sin(angle)], axis=0)
-    backward = forward.T / rows
-    return split_bf16(forward), split_bf16(backward)
+    high, low = split_bf16(forward)
+    back_high, back_low = split_bf16(forward.T / rows)
+    return (
+        np.concatenate([high, low], axis=1),
+        np.concatenate([back_high, back_low, back_high], axis=1),
+    )
 
 
 def peer_of(slot):
@@ -39,67 +42,62 @@
     return pl.ds(pl.multiple_of(peer_of(slot) * size, size), size)
 
 
-def pre_kernel(n_peers, keys_hbm, values_hbm, filters_hbm, fwd_hbm, bwd_hbm, *refs):
+def pre_kernel(n_peers, keys_hbm, values_hbm, filters_hbm, *refs):
     out_refs = refs[:n_peers]
-    fwd_ref, bwd_ref, keys, values, filters, sem = refs[n_peers:]
-    chans = keys.shape[1] // n_peers
-    copies = [
-        pltpu.make_async_copy(src, dst, sem.at[i])
-        for i, (src, dst) in enumerate(
-            (
-                (keys_hbm, keys),
-                (values_hbm, values),
-                (filters_hbm, filters),
-                (fwd_hbm, fwd_ref),
-                (bwd_hbm, bwd_ref),
-            )
-        )
-    ]
-    for copy in copies:
-        copy.start()
-    for copy in copies[:3]:
-        copy.wait()
-    for slot, out_ref in zip(slots_of(n_peers, False), out_refs):
-        at = peer_block(slot, chans)
-        product = keys[:, at].astype(F32) * values[:, at].astype(F32)
-        out_ref[:, :chans] = product.astype(BF16)
-        out_ref[:, chans:] = filters[:, at].astype(BF16)
-    for copy in copies[3:]:
-        copy.wait()
-
-
-def pre(keys, values, filters, fwd, bwd, n_peers):
+    keys, values, filters, sem = refs[n_peers:]
     rows, width = keys.shape
     chans = width // n_peers
-    args = [
-        pltpu.with_memory_space_constraint(a, pltpu.HBM) for a in (keys, values, filters, fwd, bwd)
+    steps = sem.shape[0]
+    parts = [pl.ds(c * rows // steps, rows // steps) for c in range(steps)]
+    pairs = ((keys_hbm, keys), (values_hbm, values), (filters_hbm, filters))
+    copies = [
+        [
+            pltpu.make_async_copy(src.at[part], dst.at[part], sem.at[c, i])
+            for i, (src, dst) in enumerate(pairs)
+        ]
+        for c, part in enumerate(parts)
     ]
-    *blocks, fwd, bwd = pl.pallas_call(
+    for group in copies:
+        for copy in group:
+            copy.start()
+    for part, group in zip(parts, copies):
+        for copy in group:
+            copy.wait()
+        for slot, out_ref in zip(slots_of(n_peers, False), out_refs):
+            at = peer_block(slot, chans)
+            product = keys[part, at].astype(F32) * values[part, at].astype(F32)
+            out_ref[part, :chans] = product.astype(BF16)
+            out_ref[part, chans:] = filters[part, at].astype(BF16)
+
+
+def pre(keys, values, filters, n_peers):
+    rows, width = keys.shape
+    chans = width // n_peers
+    args = [pltpu.with_memory_space_constraint(a, pltpu.HBM) for a in (keys, values, filters)]
+    return pl.pallas_call(
         functools.partial(pre_kernel, n_peers),
-        in_specs=[pl.BlockSpec(memory_space=pltpu.HBM)] * 5,
-        out_specs=[pl.BlockSpec(memory_space=pltpu.VMEM)] * (n_peers + 2),
-        out_shape=[jax.ShapeDtypeStruct((rows, 2 * chans), BF16)] * n_peers
-        + [jax.ShapeDtypeStruct(t.shape, BF16) for t in (fwd, bwd)],
+        in_specs=[pl.BlockSpec(memory_space=pltpu.HBM)] * 3,
+        out_specs=[pl.BlockSpec(memory_space=pltpu.VMEM)] * n_peers,
+        out_shape=[jax.ShapeDtypeStruct((rows, 2 * chans), BF16)] * n_peers,
         scratch_shapes=[
             pltpu.VMEM((rows, width), BF16),
             pltpu.VMEM((rows, width), BF16),
             pltpu.VMEM((rows, width), F32),
-            pltpu.SemaphoreType.DMA((5,)),
+            pltpu.SemaphoreType.DMA((2, 3)),
         ],
         compiler_params=pltpu.CompilerParams(vmem_limit_bytes=SMALL_VMEM),
         cost_estimate=pl.CostEstimate(
             flops=rows * width, bytes_accessed=12 * rows * width, transcendentals=0
         ),
     )(*args)
-    return blocks, fwd, bwd
 
 
 def slots_of(n_peers, back):
     half = n_peers // 2
     near, far = list(range(1, half)), list(range(half, n_peers))
     if back:
-        return [0, near[0], far[0], near[1], far[1]] + near[2:] + far[2:]
-    return [0, far[0], near[0], far[1], near[1]] + near[2:] + far[2:]
+        return [0, near[0]] + far[:3] + [near[1]] + far[3:] + near[2:]
+    return [0, near[0], far[0], near[1], far[1]] + near[2:] + far[2:]
 
 
 def exchange(blocks, n_peers, back):
@@ -109,88 +107,134 @@
     ]
 
 
-def conv_kernel(fwd_ref, bwd_ref, *refs):
-    *refs, spec, turned = refs
-    n_blocks = spec.shape[0]
-    in_refs, out_refs = refs[:n_blocks], refs[n_blocks:]
+def block_spectrum(table, block):
+    return jnp.dot(table, jnp.concatenate([block, block], axis=0), preferred_element_type=F32)
+
+
+def spectra_kernel(n_peers, fwd_hbm, bwd_hbm, *refs):
+    *in_refs, fwd_ref, bwd_ref, spec_ref, sem = refs
+    copies = [
+        pltpu.make_async_copy(fwd_hbm, fwd_ref, sem.at[0]),
+        pltpu.make_async_copy(bwd_hbm, bwd_ref, sem.at[1]),
+    ]
+    for copy in copies:
+        copy.start()
+    for copy in copies:
+        copy.wait()
+    for slot, in_ref in zip(slots_of(n_peers, False), in_refs):
+        spec_ref[peer_of(slot)] = block_spectrum(fwd_ref[...], in_ref[...])
+
+
+def spectra(received, fwd, bwd, n_peers):
+    rows, width = received[0].shape
+    whole = pl.BlockSpec(memory_space=pltpu.VMEM)
+    args = [pltpu.with_memory_space_constraint(a, pltpu.HBM) for a in (fwd, bwd)]
+    return pl.pallas_call(
+        functools.partial(spectra_kernel, n_peers),
+        in_specs=[pl.BlockSpec(memory_space=pltpu.HBM)] * 2 + [whole] * len(received),
+        out_specs=[whole] * 3,
+        out_shape=[
+            jax.ShapeDtypeStruct(fwd.shape, BF16),
+            jax.ShapeDtypeStruct(bwd.shape, BF16),
+            jax.ShapeDtypeStruct((n_peers, 2 * rows, width), F32),
+        ],
+        scratch_shapes=[pltpu.SemaphoreType.DMA((2,))],
+        compiler_params=pltpu.CompilerParams(vmem_limit_bytes=CONV_VMEM),
+        cost_estimate=pl.CostEstimate(
+            flops=8 * len(received) * rows * rows * width, bytes_accessed=4 * 2**20, transcendentals=0
+        ),
+    )(*args, *received)
+
+
+def conv_kernel(fwd_ref, bwd_ref, early_ref, *refs):
+    *refs, late, held, turned = refs
+    n_blocks, step = early_ref.shape[0], held.shape[2]
+    in_refs, out_refs = refs[:-n_blocks], refs[-n_blocks:]
     rows, chans = in_refs[0].shape[0], in_refs[0].shape[1] // 2
-    step = 8
-
-    for slot, in_ref in zip(slots_of(n_blocks, False), in_refs):
-        j = peer_of(slot)
-        block = in_ref[...]
-        high = jnp.dot(fwd_ref[: 2 * rows], block, preferred_element_type=F32)
-        low = jnp.dot(fwd_ref[2 * rows :], block, preferred_element_type=F32)
-        spec[j] = high + low
+    late_slots = slots_of(n_blocks, False)[-2:]
+    for slot, in_ref in zip(late_slots, in_refs):
+        late[lax.bitwise_and(peer_of(slot), 1)] = block_spectrum(fwd_ref[...], in_ref[...])
+    late_pair = lax.div(peer_of(late_slots[0]), 2)
+
+    def spectrum(j, at, lanes):
+        return jnp.where(late_pair == j // 2, late[j % 2, at, lanes], early_ref[j, at, lanes])
 
     def mix(row, sign):
         re, im = pl.ds(row, step), pl.ds(row + rows, step)
-        x_re = [spec[j, re, :chans] for j in range(n_blocks)]
-        x_im = [spec[j, im, :chans] for j in range(n_blocks)]
-        out_re, out_im = [None] * n_blocks, [None] * n_blocks
+        x_at, f_at = slice(0, chans), slice(chans, 2 * chans)
+        gains = []
         last_re = last_im = None
-        for d in range(n_blocks):
-            f_re, f_im = spec[d, re, chans:], spec[d, im, chans:]
-            g_re, g_im = f_re, f_im
-            if d > 0:
-                g_re, g_im = f_re - sign * last_im, f_im + sign * last_re
+        for j in range(n_blocks):
+            held[j, 0] = spectrum(j, re, x_at)
+            held[j, 1] = spectrum(j, im, x_at)
+            f_re, f_im = spectrum(j, re, f_at), spectrum(j, im, f_at)
+            if j == 0:
+                gains.append((f_re, f_im))
+            else:
+                gains.append((f_re - sign * last_im, f_im + sign * last_re))
             last_re, last_im = f_re, f_im
-            for i in range(d, n_blocks):
-                a_re, a_im = x_re[i - d], x_im[i - d]
-                t_re = g_re * a_re - g_im * a_im
-                t_im = g_re * a_im + g_im * a_re
-                out_re[i] = t_re if d == 0 else out_re[i] + t_re
-                out_im[i] = t_im if d == 0 else out_im[i] + t_im
         for i in range(n_blocks):
-            for where, value in ((re, out_re[i]), (im, out_im[i])):
-                high = value.astype(BF16).astype(F32)
-                turned[i, where, :chans] = high
-                turned[i, where, chans:] = value - high
+            out_re = out_im = None
+            for d in range(i + 1):
+                (g_re, g_im), x_re, x_im = gains[d], held[i - d, 0], held[i - d, 1]
+                t_re = g_re * x_re - g_im * x_im
+                t_im = g_re * x_im + g_im * x_re
+                out_re = t_re if d == 0 else out_re + t_re
+                out_im = t_im if d == 0 else out_im + t_im
+            lanes = slice(i % 2 * chans, (i % 2 + 1) * chans)
+            for first, value in ((row, out_re), (row + rows, out_im)):
+                high = value.astype(BF16)
+                low = (value - high.astype(F32)).astype(BF16)
+                for part, piece in enumerate((high, high, low)):
+                    turned[i // 2, pl.ds(first + 2 * part * rows, step), lanes] = piece
 
     half = rows // 2
 
     @pl.loop(0, half // step)
     def _(t):
-        row = pl.multiple_of(t * step, step)
-        mix(row, 1.0)
+        mix(pl.multiple_of(t * step, step), 1.0)
 
     @pl.loop(half // step, rows // step)
     def _(t):
-        row = pl.multiple_of(t * step, step)
-        mix(row, -1.0)
-
-    for slot, out_ref in zip(slots_of(n_blocks, True), out_refs):
-        i = peer_of(slot)
-        both = jnp.dot(bwd_ref[...], turned[i].astype(BF16), preferred_element_type=F32)
-        value = both[:rows, :chans] + both[:rows, chans:] + both[rows:, :chans]
-        out_ref[...] = value.astype(BF16)
-
-
-def conv_fast(received, fwd, bwd):
-    n_blocks = len(received)
-    rows, chans = received[0].shape[0], received[0].shape[1] // 2
+        mix(pl.multiple_of(t * step, step), -1.0)
+
+    odd = lax.bitwise_and(lax.axis_index("seq"), 1) == 1
+    by_slot = dict(zip(slots_of(n_blocks, True), out_refs))
+    for slot in range(0, n_blocks, 2):
+        pair = lax.div(peer_of(slot), 2)
+        both = jnp.dot(bwd_ref[...], turned[pair], preferred_element_type=F32)
+        left, right = both[:, :chans], both[:, chans:]
+        by_slot[slot][...] = jnp.where(odd, right, left).astype(BF16)
+        by_slot[slot + 1][...] = jnp.where(odd, left, right).astype(BF16)
+
+
+def conv_fast(early, late, fwd, bwd):
+    n_blocks = early.shape[0]
+    rows, chans = late[0].shape[0], late[0].shape[1] // 2
+    step = 16
     whole = pl.BlockSpec(memory_space=pltpu.VMEM)
     return pl.pallas_call(
         conv_kernel,
-        in_specs=[whole] * (2 + n_blocks),
+        in_specs=[whole] * 5,
         out_specs=[whole] * n_blocks,
         out_shape=[jax.ShapeDtypeStruct((rows, chans), BF16)] * n_blocks,
         scratch_shapes=[
-            pltpu.VMEM((n_blocks, 2 * rows, 2 * chans), F32),
-            pltpu.VMEM((n_blocks, 2 * rows, 2 * chans), F32),
+            pltpu.VMEM((2, 2 * rows, 2 * chans), F32),
+            pltpu.VMEM((n_blocks, 2, step, chans), F32),
+            pltpu.VMEM((n_blocks // 2, 6 * rows, 2 * chans), BF16),
         ],
         compiler_params=pltpu.CompilerParams(vmem_limit_bytes=CONV_VMEM),
         cost_estimate=pl.CostEstimate(
-            flops=16 * n_blocks * rows * rows * chans * 2, bytes_accessed=4 * 2**20, transcendentals=0
-        ),
-    )(fwd, bwd, *received)
+            flops=16 * n_blocks * rows * rows * chans, bytes_accessed=4 * 2**20, transcendentals=0
+        ),
+    )(fwd, bwd, early, *late)
 
 
 def conv_plain(received, fwd, bwd):
     n_blocks, rows, chans = received.shape[0], received.shape[1], received.shape[2] // 2
     exact = lax.Precision.HIGHEST
-    fwd32 = fwd[: 2 * rows].astype(F32) + fwd[2 * rows :].astype(F32)
-    bwd32 = bwd[:rows].astype(F32) + bwd[rows:].astype(F32)
+    fwd32 = fwd[:, :rows].astype(F32) + fwd[:, rows:].astype(F32)
+    bwd32 = bwd[:, : 2 * rows].astype(F32) + bwd[:, 2 * rows : 4 * rows].astype(F32)
     sign = jnp.where(jnp.arange(rows) < rows // 2, 1.0, -1.0).astype(F32)[:, None]
 
     def spectrum(blocks):
@@ -305,15 +349,16 @@
     in_chip = [(0, 1), (1, 0), (2, 3), (3, 2)]
     across = [(0, 2), (2, 0), (1, 3), (3, 1)]
 
-    if chans % 128 == 0 and n_peers in (8, 16):
-        blocks, fwd, bwd = pre(keys, values, filters, fwd, bwd, n_peers)
+    their_weight = lax.ppermute(out_weight, "fsdp", in_chip)
+
+    if chans % 128 == 0 and n_peers == 8:
+        blocks = pre(keys, values, filters, n_peers)
         received = exchange(blocks, n_peers, False)
-        out_weight, received = lax.optimization_barrier((out_weight, received))
-        their_weight = lax.ppermute(out_weight, "fsdp", in_chip)
-        back = exchange(conv_fast(received, fwd, bwd), n_peers, True)
+        fwd, bwd, early = spectra(received[:-2], fwd, bwd, n_peers)
+        their_weight, early = lax.optimization_barrier((their_weight, early))
+        back = exchange(conv_fast(early, received[-2:], fwd, bwd), n_peers, True)
         gated = gate(queries, keys, values, skip, back)
     else:
-        their_weight = lax.ppermute(out_weight, "fsdp", in_chip)
         product = keys.astype(F32) * values.astype(F32)
         parts = [a.astype(BF16).reshape(rows, n_peers, chans) for a in (product, filters)]
         sent = jnp.concatenate(parts, axis=2).transpose(1, 0, 2)

time: 69.7 us -> 68.7 us (0.986)
  waiting for transfers between devices: 29.1 us -> 27.6 us
  Pallas kernels: 10.6 us -> 11.8 us
    ppermute x14, waiting for transfers between devices: 17.3 us -> 15.8 us  [exchange(): lax.ppermute(block, 'seq', [(i, i ^ slot) for i in range(n_peers)])]
    pallas_call x1 -> x2, Pallas kernels: 4.45 us -> 5.87 us  [the longest x1 3.46 us: conv_fast(): pl.pallas_call(conv_kernel, in_specs=[whole] * 5, out_specs=[whole] * n_b...]
    ppermute x14, starting transfers between devices: 27.5 us -> 26.3 us  [exchange(): lax.ppermute(block, 'seq', [(i, i ^ slot) for i in range(n_peers)])]
  transfers between devices with their start and end apart: 18 -> 18, of which waited for: 11 -> 11; matrix products, arithmetic and copies ran while one was open for 0% -> 0% of each run, Pallas kernels for 10% -> 9%
where the time goes in v1:
time: 68.7 us; the launch traced here: 68.5 us
  starting transfers between devices  29.1 us (42%)
  waiting for transfers between devices  27.6 us (40%)
  Pallas kernels  11.8 us (17%)
    ppermute x14, starting transfers between devices, exchange(): lax.ppermute(block, 'seq', [(i, i ^ slot) for i in range(n_peers)])  26.3 us
    ppermute x14, waiting for transfers between devices, exchange(): lax.ppermute(block, 'seq', [(i, i ^ slot) for i in range(n_peers)])  15.8 us
    ppermute x2, waiting for transfers between devices, body(): arrived.append(lax.ppermute(remote, 'fsdp', across))  9.91 us
    pallas_call x1, Pallas kernels, conv_fast(): pl.pallas_call(conv_kernel, in_specs=[whole] * 5, out_specs=[whole] * n_b...  3.46 us
    pallas_call x3, Pallas kernels, project(): pl.pallas_call(functools.partial(project_kernel, across, first), in_specs...  2.66 us
    pallas_call x1, Pallas kernels, spectra(): pl.pallas_call(functools.partial(spectra_kernel, n_peers), in_specs=[pl.B...  2.4 us
    ppermute x2, starting transfers between devices, body(): arrived.append(lax.ppermute(remote, 'fsdp', across))  2.16 us
    pallas_call x1, Pallas kernels, pre(): pl.pallas_call(functools.partial(pre_kernel, n_peers), in_specs=[pl.Block...  1.92 us
  transfers between devices with their start and end apart: 18, of which 11 were waited for; matrix products, arithmetic and copies ran while one was open for 0% of the time, Pallas kernels for 9%

profile of v1, /device:TPU:0, one launch (start us, length us, event | category | flops | bytes accessed | tf_op | source)
XLA Modules:
  0.0 68.5 jit_solution(7039053527493658821)
XLA Ops:
  0.0 0.5 collective-permute-start.5
  0.5 1.9 %shard_map.82 = (bf16[256,256]{1,0:T(8,128)(2,1)S(1)}, bf16[256,256]{1,0:T(8,128)(2,1)S(1)}, bf16[256,256]{1,0:T(8,128)(2,1)S(1)}, bf16[256,256]{1,0:T(8,128)(2,...) custom-call(bf16[256,1024]{1,0:T(8,128)(2,1)} %keys_ref.1, ...), custom_call_target="tpu_custom_call" | custom-call | flops 262144 | bytes 3145728 | tf_op jit(solution)/shard_map/pallas_call | solution.py:77
  2.5 2.6 %collective-permute-start = (bf16[256,256]{1,0:T(8,128)(2,1)S(1)}, bf16[256,256]{1,0:T(8,128)(2,1)S(1)}, u32[]{:S(2)}, u32[]{:S(2)}) collective-permute-start(bf16[256,256]{1,0:T(8,128)(2,1)S(1)} %get-tuple-element.27), channel_id=1, source_target_pairs={{0,4},{4,0},{8,12},{12,8},{16,20},{20,16},{24,28},{28,24},{1,5},{5... | collective-permute-start | bytes 393224 | tf_op jit(solution)/shard_map/ppermute | solution.py:105
  5.1 2.6 %collective-permute-start.1 = (bf16[256,256]{1,0:T(8,128)(2,1)S(1)}, bf16[256,256]{1,0:T(8,128)(2,1)S(1)}, u32[]{:S(2)}, u32[]{:S(2)}) collective-permute-start(bf16[256,256]{1,0:T(8,128)(2,1)S(1)} %get-tuple-element.28), channel_id=1, source_target_pairs={{0,16},{4,20},{8,24},{12,28},{16,0},{20,4},{24,8},{28,12},{1,17},{... | collective-permute-start | bytes 393224 | tf_op jit(solution)/shard_map/ppermute | solution.py:105
  7.7 1.6 %collective-permute-start.2 = (bf16[256,256]{1,0:T(8,128)(2,1)S(1)}, bf16[256,256]{1,0:T(8,128)(2,1)S(1)}, u32[]{:S(2)}, u32[]{:S(2)}) collective-permute-start(bf16[256,256]{1,0:T(8,128)(2,1)S(1)} %get-tuple-element.29), channel_id=1, source_target_pairs={{0,8},{4,12},{8,0},{12,4},{16,24},{20,28},{24,16},{28,20},{1,9},{5... | collective-permute-start | bytes 393224 | tf_op jit(solution)/shard_map/ppermute | solution.py:105
  9.5 2.3 %collective-permute-start.4 = (bf16[256,256]{1,0:T(8,128)(2,1)S(1)}, bf16[256,256]{1,0:T(8,128)(2,1)S(1)}, u32[]{:S(2)}, u32[]{:S(2)}) collective-permute-start(bf16[256,256]{1,0:T(8,128)(2,1)S(1)} %get-tuple-element.31), channel_id=1, source_target_pairs={{0,12},{4,8},{8,4},{12,0},{16,28},{20,24},{24,20},{28,16},{1,13},{... | collective-permute-start | bytes 393224 | tf_op jit(solution)/shard_map/ppermute | solution.py:105
  11.8 4.1 %collective-permute-done.1.refs_2_ = bf16[256,256]{1,0:T(8,128)(2,1)S(1)} collective-permute-done((bf16[256,256]{1,0:T(8,128)(2,1)S(1)}, bf16[256,256]{1,0:T(8,128)(2,1)S(1)}, u32[]{:S(2)}, u32[]{:S(2)}) %collective-permute-start.1) | collective-permute-done | bytes 131104 | tf_op jit(solution)/shard_map/ppermute | solution.py:105
  15.9 2.8 %collective-permute-start.6 = (bf16[256,256]{1,0:T(8,128)(2,1)S(1)}, bf16[256,256]{1,0:T(8,128)(2,1)S(1)}, u32[]{:S(2)}, u32[]{:S(2)}) collective-permute-start(bf16[256,256]{1,0:T(8,128)(2,1)S(1)} %get-tuple-element.36), channel_id=1, source_target_pairs={{0,24},{4,28},{8,16},{12,20},{16,8},{20,12},{24,0},{28,4},{1,25},{... | collective-permute-start | bytes 393224 | tf_op jit(solution)/shard_map/ppermute | solution.py:105
  19.0 1.4 %collective-permute-done.3.refs_4_ = bf16[256,256]{1,0:T(8,128)(2,1)S(1)} collective-permute-done((bf16[256,256]{1,0:T(8,128)(2,1)S(1)}, bf16[256,256]{1,0:T(8,128)(2,1)S(1)}, u32[]{:S(2)}, u32[]{:S(2)}) %collective-permute-start.3) | collective-permute-done | bytes 131104 | tf_op jit(solution)/shard_map/ppermute | solution.py:105
  20.4 2.4 %shard_map.83 = (bf16[512,512]{1,0:T(8,128)(2,1)S(1)}, bf16[256,1536]{1,0:T(8,128)(2,1)S(1)}, f32[8,512,256]{2,1,0:T(8,128)S(1)}) custom-call(bf16[512,512]{1,0:T(8,128)(2,1)} %constant.4.clone.fwd_hbm, bf16[256,1536]{1,0:T(8,128)(2,1)} %constant.5.clone.bwd_hbm, bf16[256,256]{1,0:T(8,128)(2,1)S(1)} %get-tuple-element.26.refs_0_, ...), custom_call_target="tpu_custom_call" | custom-call | flops 805306368 | bytes 4194304 | tf_op jit(solution)/shard_map/pallas_call | solution.py:132
  22.8 2.5 %collective-permute-done.6.refs_0_ = bf16[256,256]{1,0:T(8,128)(2,1)S(1)} collective-permute-done((bf16[256,256]{1,0:T(8,128)(2,1)S(1)}, bf16[256,256]{1,0:T(8,128)(2,1)S(1)}, u32[]{:S(2)}, u32[]{:S(2)}) %collective-permute-start.6) | collective-permute-done | bytes 131104 | tf_op jit(solution)/shard_map/ppermute | solution.py:105
  25.3 1.9 %collective-permute-done.7.refs_1_ = bf16[256,256]{1,0:T(8,128)(2,1)S(1)} collective-permute-done((bf16[256,256]{1,0:T(8,128)(2,1)S(1)}, bf16[256,256]{1,0:T(8,128)(2,1)S(1)}, u32[]{:S(2)}, u32[]{:S(2)}) %collective-permute-start.7) | collective-permute-done | bytes 131104 | tf_op jit(solution)/shard_map/ppermute | solution.py:105
  27.2 3.5 %shard_map.84 = (bf16[256,128]{1,0:T(8,128)(2,1)S(1)}, bf16[256,128]{1,0:T(8,128)(2,1)S(1)}, bf16[256,128]{1,0:T(8,128)(2,1)S(1)}, bf16[256,128]{1,0:T(8,128)(2,...) custom-call(bf16[512,512]{1,0:T(8,128)(2,1)S(1)} %get-tuple-element., ...), custom_call_target="tpu_custom_call" | custom-call | flops 1073741824 | bytes 4194304 | tf_op jit(solution)/shard_map/pallas_call | solution.py:216
  30.6 1.6 %collective-permute-start.8 = (bf16[256,128]{1,0:T(8,128)(2,1)S(1)}, bf16[256,128]{1,0:T(8,128)(2,1)S(1)}, u32[]{:S(2)}, u32[]{:S(2)}) collective-permute-start(bf16[256,128]{1,0:T(8,128)(2,1)S(1)} %get-tuple-element.39), channel_id=1, source_target_pairs={{0,4},{4,0},{8,12},{12,8},{16,20},{20,16},{24,28},{28,24},{1,5},{5... | collective-permute-start | bytes 196616 | tf_op jit(solution)/shard_map/ppermute | solution.py:105
  32.2 6.5 %collective-permute-start.9 = (bf16[256,128]{1,0:T(8,128)(2,1)S(1)}, bf16[256,128]{1,0:T(8,128)(2,1)S(1)}, u32[]{:S(2)}, u32[]{:S(2)}) collective-permute-start(bf16[256,128]{1,0:T(8,128)(2,1)S(1)} %get-tuple-element.40), channel_id=1, source_target_pairs={{0,16},{4,20},{8,24},{12,28},{16,0},{20,4},{24,8},{28,12},{1,17},{... | collective-permute-start | bytes 196616 | tf_op jit(solution)/shard_map/ppermute | solution.py:105
  39.1 3.0 %collective-permute-start.12 = (bf16[256,128]{1,0:T(8,128)(2,1)S(1)}, bf16[256,128]{1,0:T(8,128)(2,1)S(1)}, u32[]{:S(2)}, u32[]{:S(2)}) collective-permute-start(bf16[256,128]{1,0:T(8,128)(2,1)S(1)} %get-tuple-element.43), channel_id=1, source_target_pairs={{0,8},{4,12},{8,0},{12,4},{16,24},{20,28},{24,16},{28,20},{1,9},{5... | collective-permute-start | bytes 196616 | tf_op jit(solution)/shard_map/ppermute | solution.py:105
  42.1 1.9 %collective-permute-start.13 = (bf16[256,128]{1,0:T(8,128)(2,1)S(1)}, bf16[256,128]{1,0:T(8,128)(2,1)S(1)}, u32[]{:S(2)}, u32[]{:S(2)}) collective-permute-start(bf16[256,128]{1,0:T(8,128)(2,1)S(1)} %get-tuple-element.44), channel_id=1, source_target_pairs={{0,28},{4,24},{8,20},{12,16},{16,12},{20,8},{24,4},{28,0},{1,29},{... | collective-permute-start | bytes 196616 | tf_op jit(solution)/shard_map/ppermute | solution.py:105
  44.0 0.6 collective-permute-start.14
  44.5 2.8 %collective-permute-done.10.refs_3_ = bf16[256,128]{1,0:T(8,128)(2,1)S(1)} collective-permute-done((bf16[256,128]{1,0:T(8,128)(2,1)S(1)}, bf16[256,128]{1,0:T(8,128)(2,1)S(1)}, u32[]{:S(2)}, u32[]{:S(2)}) %collective-permute-start.10) | collective-permute-done | bytes 65568 | tf_op jit(solution)/shard_map/ppermute | solution.py:105
  47.3 0.5 collective-permute-done.12.refs_5_
  47.8 1.4 %collective-permute-done.13.refs_6_ = bf16[256,128]{1,0:T(8,128)(2,1)S(1)} collective-permute-done((bf16[256,128]{1,0:T(8,128)(2,1)S(1)}, bf16[256,128]{1,0:T(8,128)(2,1)S(1)}, u32[]{:S(2)}, u32[]{:S(2)}) %collective-permute-start.13) | collective-permute-done | bytes 65568 | tf_op jit(solution)/shard_map/ppermute | solution.py:105
  49.2 1.3 %collective-permute-done.14.refs_7_ = bf16[256,128]{1,0:T(8,128)(2,1)S(1)} collective-permute-done((bf16[256,128]{1,0:T(8,128)(2,1)S(1)}, bf16[256,128]{1,0:T(8,128)(2,1)S(1)}, u32[]{:S(2)}, u32[]{:S(2)}) %collective-permute-start.14) | collective-permute-done | bytes 65568 | tf_op jit(solution)/shard_map/ppermute | solution.py:105
  50.5 0.4 shard_map.85.mine_ref
  51.0 1.9 %collective-permute-done.15.theirs_ref = bf16[256,1024]{1,0:T(8,128)(2,1)S(1)} collective-permute-done((bf16[256,1024]{1,0:T(8,128)(2,1)S(1)}, bf16[256,1024]{1,0:T(8,128)(2,1)S(1)}, u32[]{:S(2)}, u32[]{:S(2)}) %collective-permute-start.15) | collective-permute-done | bytes 524320 | tf_op jit(solution)/shard_map/ppermute | solution.py:371
  52.9 0.7 %shard_map.87 = bf16[256,512]{1,0:T(8,128)(2,1)S(1)} custom-call(bf16[256,1024]{1,0:T(8,128)(2,1)S(1)} %shard_map.85.mine_ref, bf16[256,1024]{1,0:T(8,128)(2,1)S(1)} %collective-permute-done.15.theirs_ref, bf16[1024,4096]{1,0:T(8,128)(2,1)S(1)} %copy-done, bf16[1024,4096]{1,0:T(8,128)(2,1)S(1)} %collective-permute-done.5.their_w_ref), custom_call_target="tpu_custom_call" | custom-call | flops 536870912 | bytes 2097152 | tf_op jit(solution)/shard_map/pallas_call | solution.py:308
  53.6 1.6 %collective-permute-start.16 = (bf16[256,512]{1,0:T(8,128)(2,1)S(1)}, bf16[256,512]{1,0:T(8,128)(2,1)S(1)}, u32[]{:S(2)}, u32[]{:S(2)}) collective-permute-start(bf16[256,512]{1,0:T(8,128)(2,1)S(1)} %shard_map.87), channel_id=1, source_target_pairs={{0,2},{2,0},{1,3},{3,1},{4,6},{6,4},{5,7},{7,5},{8,10},{10,8},{9,1... | collective-permute-start | bytes 786440 | tf_op jit(solution)/shard_map/ppermute | solution.py:377
  55.2 0.7 %shard_map.88 = bf16[256,512]{1,0:T(8,128)(2,1)S(1)} custom-call(bf16[256,1024]{1,0:T(8,128)(2,1)S(1)} %shard_map.85.mine_ref, bf16[256,1024]{1,0:T(8,128)(2,1)S(1)} %collective-permute-done.15.theirs_ref, bf16[1024,4096]{1,0:T(8,128)(2,1)S(1)} %copy-done, bf16[1024,4096]{1,0:T(8,128)(2,1)S(1)} %collective-permute-done.5.their_w_ref), custom_call_target="tpu_custom_call" | custom-call | flops 536870912 | bytes 2097152 | tf_op jit(solution)/shard_map/pallas_call | solution.py:308
  55.9 0.6 collective-permute-start.17
  56.5 1.2 %shard_map.86.own_ref = f32[256,1024]{1,0:T(8,128)S(1)} custom-call(bf16[256,1024]{1,0:T(8,128)(2,1)S(1)} %shard_map.85.mine_ref, bf16[256,1024]{1,0:T(8,128)(2,1)S(1)} %collective-permute-done.15.theirs_ref, bf16[1024,4096]{1,0:T(8,128)(2,1)S(1)} %copy-done, bf16[1024,4096]{1,0:T(8,128)(2,1)S(1)} %collective-permute-done.5.their_w_ref), custom_call_target="tpu_custom_call" | custom-call | flops 1073741824 | bytes 4194304 | tf_op jit(solution)/shard_map/pallas_call | solution.py:308
  57.8 5.1 %collective-permute-done.16.refs_0_ = bf16[256,512]{1,0:T(8,128)(2,1)S(1)} collective-permute-done((bf16[256,512]{1,0:T(8,128)(2,1)S(1)}, bf16[256,512]{1,0:T(8,128)(2,1)S(1)}, u32[]{:S(2)}, u32[]{:S(2)}) %collective-permute-start.16) | collective-permute-done | bytes 262176 | tf_op jit(solution)/shard_map/ppermute | solution.py:377
  62.8 4.8 %collective-permute-done.17.refs_1_ = bf16[256,512]{1,0:T(8,128)(2,1)S(1)} collective-permute-done((bf16[256,512]{1,0:T(8,128)(2,1)S(1)}, bf16[256,512]{1,0:T(8,128)(2,1)S(1)}, u32[]{:S(2)}, u32[]{:S(2)}) %collective-permute-start.17) | collective-permute-done | bytes 262176 | tf_op jit(solution)/shard_map/ppermute | solution.py:377
  67.7 0.9 %shard_map.89 = bf16[256,1024]{1,0:T(8,128)(2,1)} custom-call(f32[256,1024]{1,0:T(8,128)S(1)} %shard_map.86.own_ref, bf16[256,512]{1,0:T(8,128)(2,1)S(1)} %collective-permute-done.16.refs_0_, bf16[256,512]{1,0:T(8,128)(2,1)S(1)} %collective-permute-done.17.refs_1_), custom_call_target="tpu_custom_call" | custom-call | flops 262144 | bytes 2097152 | tf_op jit(solution)/shard_map/pallas_call | solution.py:331
  (22 shorter events, 1.1 us)
Async XLA Ops:
  0.0 52.9 %copy-start = (bf16[1024,4096]{1,0:T(8,128)(2,1)S(1)}, bf16[1024,4096]{1,0:T(8,128)(2,1)}, u32[]{:S(2)}) copy-start(bf16[1024,4096]{1,0:T(8,128)(2,1)} %own_w_ref.5) | copy-start | bytes 25165828
  0.0 50.5 %copy-start.2 = (bf16[256,1024]{1,0:T(8,128)(2,1)S(1)}, bf16[256,1024]{1,0:T(8,128)(2,1)}, u32[]{:S(2)}) copy-start(bf16[256,1024]{1,0:T(8,128)(2,1)} %values_ref.1) | copy-start | bytes 1572868
  0.0 50.5 %copy-start.1 = (bf16[256,1024]{1,0:T(8,128)(2,1)S(1)}, bf16[256,1024]{1,0:T(8,128)(2,1)}, u32[]{:S(2)}) copy-start(bf16[256,1024]{1,0:T(8,128)(2,1)} %keys_ref.1) | copy-start | bytes 1572868
  0.0 50.5 %copy-start.4 = (f32[1024]{0:T(1024)S(1)}, f32[1024]{0:T(1024)}, u32[]{:S(2)}) copy-start(f32[1024]{0:T(1024)} %param.12) | copy-start | bytes 12292
  0.0 50.5 %copy-start.3 = (bf16[256,1024]{1,0:T(8,128)(2,1)S(1)}, bf16[256,1024]{1,0:T(8,128)(2,1)}, u32[]{:S(2)}) copy-start(bf16[256,1024]{1,0:T(8,128)(2,1)} %queries_ref.1) | copy-start | bytes 1572868
  0.0 22.8 %collective-permute-start.5 = (bf16[1024,4096]{1,0:T(8,128)(2,1)}, bf16[1024,4096]{1,0:T(8,128)(2,1)S(1)}, u32[]{:S(2)}, u32[]{:S(2)}) collective-permute-start(bf16[1024,4096]{1,0:T(8,128)(2,1)} %own_w_ref.5), channel_id=1, source_target_pairs={{0,1},{1,0},{2,3},{3,2},{4,5},{5,4},{6,7},{7,6},{8,9},{9,8},{10,11... | collective-permute-start | bytes 25165832 | tf_op jit(solution)/shard_map/ppermute | solution.py:352
  2.5 7.0 %collective-permute-start = (bf16[256,256]{1,0:T(8,128)(2,1)S(1)}, bf16[256,256]{1,0:T(8,128)(2,1)S(1)}, u32[]{:S(2)}, u32[]{:S(2)}) collective-permute-start(bf16[256,256]{1,0:T(8,128)(2,1)S(1)} %get-tuple-element.27), channel_id=1, source_target_pairs={{0,4},{4,0},{8,12},{12,8},{16,20},{20,16},{24,28},{28,24},{1,5},{5... | collective-permute-start | bytes 393224 | tf_op jit(solution)/shard_map/ppermute | solution.py:105
  5.1 10.9 %collective-permute-start.1 = (bf16[256,256]{1,0:T(8,128)(2,1)S(1)}, bf16[256,256]{1,0:T(8,128)(2,1)S(1)}, u32[]{:S(2)}, u32[]{:S(2)}) collective-permute-start(bf16[256,256]{1,0:T(8,128)(2,1)S(1)} %get-tuple-element.28), channel_id=1, source_target_pairs={{0,16},{4,20},{8,24},{12,28},{16,0},{20,4},{24,8},{28,12},{1,17},{... | collective-permute-start | bytes 393224 | tf_op jit(solution)/shard_map/ppermute | solution.py:105
  7.7 11.1 %collective-permute-start.2 = (bf16[256,256]{1,0:T(8,128)(2,1)S(1)}, bf16[256,256]{1,0:T(8,128)(2,1)S(1)}, u32[]{:S(2)}, u32[]{:S(2)}) collective-permute-start(bf16[256,256]{1,0:T(8,128)(2,1)S(1)} %get-tuple-element.29), channel_id=1, source_target_pairs={{0,8},{4,12},{8,0},{12,4},{16,24},{20,28},{24,16},{28,20},{1,9},{5... | collective-permute-start | bytes 393224 | tf_op jit(solution)/shard_map/ppermute | solution.py:105
  9.2 11.1 %collective-permute-start.3 = (bf16[256,256]{1,0:T(8,128)(2,1)S(1)}, bf16[256,256]{1,0:T(8,128)(2,1)S(1)}, u32[]{:S(2)}, u32[]{:S(2)}) collective-permute-start(bf16[256,256]{1,0:T(8,128)(2,1)S(1)} %get-tuple-element.30), channel_id=1, source_target_pairs={{0,20},{4,16},{8,28},{12,24},{16,4},{20,0},{24,12},{28,8},{1,21},{... | collective-permute-start | bytes 393224 | tf_op jit(solution)/shard_map/ppermute | solution.py:105
  9.5 10.9 %collective-permute-start.4 = (bf16[256,256]{1,0:T(8,128)(2,1)S(1)}, bf16[256,256]{1,0:T(8,128)(2,1)S(1)}, u32[]{:S(2)}, u32[]{:S(2)}) collective-permute-start(bf16[256,256]{1,0:T(8,128)(2,1)S(1)} %get-tuple-element.31), channel_id=1, source_target_pairs={{0,12},{4,8},{8,4},{12,0},{16,28},{20,24},{24,20},{28,16},{1,13},{... | collective-permute-start | bytes 393224 | tf_op jit(solution)/shard_map/ppermute | solution.py:105
  15.9 9.4 %collective-permute-start.6 = (bf16[256,256]{1,0:T(8,128)(2,1)S(1)}, bf16[256,256]{1,0:T(8,128)(2,1)S(1)}, u32[]{:S(2)}, u32[]{:S(2)}) collective-permute-start(bf16[256,256]{1,0:T(8,128)(2,1)S(1)} %get-tuple-element.36), channel_id=1, source_target_pairs={{0,24},{4,28},{8,16},{12,20},{16,8},{20,12},{24,0},{28,4},{1,25},{... | collective-permute-start | bytes 393224 | tf_op jit(solution)/shard_map/ppermute | solution.py:105
  18.7 8.4 %collective-permute-start.7 = (bf16[256,256]{1,0:T(8,128)(2,1)S(1)}, bf16[256,256]{1,0:T(8,128)(2,1)S(1)}, u32[]{:S(2)}, u32[]{:S(2)}) collective-permute-start(bf16[256,256]{1,0:T(8,128)(2,1)S(1)} %get-tuple-element.37), channel_id=1, source_target_pairs={{0,28},{4,24},{8,20},{12,16},{16,12},{20,8},{24,4},{28,0},{1,29},{... | collective-permute-start | bytes 393224 | tf_op jit(solution)/shard_map/ppermute | solution.py:105
  30.6 11.5 %collective-permute-start.8 = (bf16[256,128]{1,0:T(8,128)(2,1)S(1)}, bf16[256,128]{1,0:T(8,128)(2,1)S(1)}, u32[]{:S(2)}, u32[]{:S(2)}) collective-permute-start(bf16[256,128]{1,0:T(8,128)(2,1)S(1)} %get-tuple-element.39), channel_id=1, source_target_pairs={{0,4},{4,0},{8,12},{12,8},{16,20},{20,16},{24,28},{28,24},{1,5},{5... | collective-permute-start | bytes 196616 | tf_op jit(solution)/shard_map/ppermute | solution.py:105
  32.2 11.8 %collective-permute-start.9 = (bf16[256,128]{1,0:T(8,128)(2,1)S(1)}, bf16[256,128]{1,0:T(8,128)(2,1)S(1)}, u32[]{:S(2)}, u32[]{:S(2)}) collective-permute-start(bf16[256,128]{1,0:T(8,128)(2,1)S(1)} %get-tuple-element.40), channel_id=1, source_target_pairs={{0,16},{4,20},{8,24},{12,28},{16,0},{20,4},{24,8},{28,12},{1,17},{... | collective-permute-start | bytes 196616 | tf_op jit(solution)/shard_map/ppermute | solution.py:105
  38.7 8.6 %collective-permute-start.10 = (bf16[256,128]{1,0:T(8,128)(2,1)S(1)}, bf16[256,128]{1,0:T(8,128)(2,1)S(1)}, u32[]{:S(2)}, u32[]{:S(2)}) collective-permute-start(bf16[256,128]{1,0:T(8,128)(2,1)S(1)} %get-tuple-element.41), channel_id=1, source_target_pairs={{0,20},{4,16},{8,28},{12,24},{16,4},{20,0},{24,12},{28,8},{1,21},{... | collective-permute-start | bytes 196616 | tf_op jit(solution)/shard_map/ppermute | solution.py:105
  38.7 8.6 %collective-permute-start.11 = (bf16[256,128]{1,0:T(8,128)(2,1)S(1)}, bf16[256,128]{1,0:T(8,128)(2,1)S(1)}, u32[]{:S(2)}, u32[]{:S(2)}) collective-permute-start(bf16[256,128]{1,0:T(8,128)(2,1)S(1)} %get-tuple-element.42), channel_id=1, source_target_pairs={{0,24},{4,28},{8,16},{12,20},{16,8},{20,12},{24,0},{28,4},{1,25},{... | collective-permute-start | bytes 196616 | tf_op jit(solution)/shard_map/ppermute | solution.py:105
  39.1 8.7 %collective-permute-start.12 = (bf16[256,128]{1,0:T(8,128)(2,1)S(1)}, bf16[256,128]{1,0:T(8,128)(2,1)S(1)}, u32[]{:S(2)}, u32[]{:S(2)}) collective-permute-start(bf16[256,128]{1,0:T(8,128)(2,1)S(1)} %get-tuple-element.43), channel_id=1, source_target_pairs={{0,8},{4,12},{8,0},{12,4},{16,24},{20,28},{24,16},{28,20},{1,9},{5... | collective-permute-start | bytes 196616 | tf_op jit(solution)/shard_map/ppermute | solution.py:105
  42.1 7.1 %collective-permute-start.13 = (bf16[256,128]{1,0:T(8,128)(2,1)S(1)}, bf16[256,128]{1,0:T(8,128)(2,1)S(1)}, u32[]{:S(2)}, u32[]{:S(2)}) collective-permute-start(bf16[256,128]{1,0:T(8,128)(2,1)S(1)} %get-tuple-element.44), channel_id=1, source_target_pairs={{0,28},{4,24},{8,20},{12,16},{16,12},{20,8},{24,4},{28,0},{1,29},{... | collective-permute-start | bytes 196616 | tf_op jit(solution)/shard_map/ppermute | solution.py:105
  44.0 6.5 %collective-permute-start.14 = (bf16[256,128]{1,0:T(8,128)(2,1)S(1)}, bf16[256,128]{1,0:T(8,128)(2,1)S(1)}, u32[]{:S(2)}, u32[]{:S(2)}) collective-permute-start(bf16[256,128]{1,0:T(8,128)(2,1)S(1)} %get-tuple-element.45), channel_id=1, source_target_pairs={{0,12},{4,8},{8,4},{12,0},{16,28},{20,24},{24,20},{28,16},{1,13},{... | collective-permute-start | bytes 196616 | tf_op jit(solution)/shard_map/ppermute | solution.py:105
  50.9 2.0 %collective-permute-start.15 = (bf16[256,1024]{1,0:T(8,128)(2,1)S(1)}, bf16[256,1024]{1,0:T(8,128)(2,1)S(1)}, u32[]{:S(2)}, u32[]{:S(2)}) collective-permute-start(bf16[256,1024]{1,0:T(8,128)(2,1)S(1)} %shard_map.85.mine_ref), channel_id=1, source_target_pairs={{0,1},{1,0},{2,3},{3,2},{4,5},{5,4},{6,7},{7,6},{8,9},{9,8},{10,11... | collective-permute-start | bytes 1572872 | tf_op jit(solution)/shard_map/ppermute | solution.py:371
  53.6 9.2 %collective-permute-start.16 = (bf16[256,512]{1,0:T(8,128)(2,1)S(1)}, bf16[256,512]{1,0:T(8,128)(2,1)S(1)}, u32[]{:S(2)}, u32[]{:S(2)}) collective-permute-start(bf16[256,512]{1,0:T(8,128)(2,1)S(1)} %shard_map.87), channel_id=1, source_target_pairs={{0,2},{2,0},{1,3},{3,1},{4,6},{6,4},{5,7},{7,5},{8,10},{10,8},{9,1... | collective-permute-start | bytes 786440 | tf_op jit(solution)/shard_map/ppermute | solution.py:377
  55.9 11.8 %collective-permute-start.17 = (bf16[256,512]{1,0:T(8,128)(2,1)S(1)}, bf16[256,512]{1,0:T(8,128)(2,1)S(1)}, u32[]{:S(2)}, u32[]{:S(2)}) collective-permute-start(bf16[256,512]{1,0:T(8,128)(2,1)S(1)} %shard_map.88), channel_id=1, source_target_pairs={{0,2},{2,0},{1,3},{3,1},{4,6},{6,4},{5,7},{7,5},{8,10},{10,8},{9,1... | collective-permute-start | bytes 786440 | tf_op jit(solution)/shard_map/ppermute | solution.py:377

commit v2 on v1

--- a/solution.py
+++ b/solution.py
@@ -287,57 +287,93 @@
     )(queries, keys, values, skip, *conv)
 
 
-def side_columns(across, out_width):
+def weight_block(weight_ref, other, across, piece, pieces):
+    width = weight_ref.shape[1] // 4 // pieces
     place = lax.axis_index("fsdp")
     core, side = lax.rem(place, 2), lax.div(place, 2)
-    side = jnp.where(across, 1 - side, side)
-    return pl.multiple_of((2 * side + core) * out_width, out_width)
-
-
-def project_kernel(across, first, mine_ref, theirs_ref, own_w_ref, their_w_ref, out_ref):
-    width = out_ref.shape[1]
-    start = side_columns(across, own_w_ref.shape[1] // 4) + first
-    at = pl.ds(pl.multiple_of(start, width), width)
-    total = jnp.dot(mine_ref[...], own_w_ref[:, at], preferred_element_type=F32)
-    total += jnp.dot(theirs_ref[...], their_w_ref[:, at], preferred_element_type=F32)
+    block = 2 * (1 - side if across else side) + (1 - core if other else core)
+    return weight_ref[:, pl.ds(pl.multiple_of((block * pieces + piece) * width, width), width)]
+
+
+def project_kernel(blocks, gated_ref, weight_ref, *out_refs):
+    for block, out_ref in zip(blocks, out_refs):
+        columns = weight_block(weight_ref, *block)
+        total = jnp.dot(gated_ref[...], columns, preferred_element_type=F32)
+        out_ref[...] = total.astype(out_ref.dtype)
+
+
+def project(gated, weight, blocks, dtypes):
+    rows, depth = gated.shape
+    widths = [weight.shape[1] // 4 // pieces for *_, pieces in blocks]
+    whole = pl.BlockSpec(memory_space=pltpu.VMEM)
+    return pl.pallas_call(
+        functools.partial(project_kernel, blocks),
+        in_specs=[whole] * 2,
+        out_specs=[whole] * len(blocks),
+        out_shape=[jax.ShapeDtypeStruct((rows, w), t) for w, t in zip(widths, dtypes)],
+        compiler_params=pltpu.CompilerParams(vmem_limit_bytes=PROJECT_VMEM),
+        cost_estimate=pl.CostEstimate(
+            flops=2 * rows * depth * sum(widths), bytes_accessed=2 * depth * sum(widths), transcendentals=0
+        ),
+    )(gated, weight)
+
+
+def add_kernel(own_ref, arrived_ref, out_ref):
+    total = own_ref[...] + arrived_ref[...].astype(F32)
     out_ref[...] = total.astype(out_ref.dtype)
 
 
-def project(mine, theirs, own_weight, their_weight, across, first, width, dtype):
-    rows, depth = mine.shape
-    return pl.pallas_call(
-        functools.partial(project_kernel, across, first),
-        in_specs=[pl.BlockSpec(memory_space=pltpu.VMEM)] * 4,
+def add(own, arrived):
+    whole = pl.BlockSpec(memory_space=pltpu.VMEM)
+    return pl.pallas_call(
+        add_kernel,
+        in_specs=[whole] * 2,
+        out_specs=whole,
+        out_shape=jax.ShapeDtypeStruct(arrived.shape, BF16),
+        compiler_params=pltpu.CompilerParams(vmem_limit_bytes=SMALL_VMEM),
+        cost_estimate=pl.CostEstimate(
+            flops=arrived.size, bytes_accessed=8 * arrived.size, transcendentals=0
+        ),
+    )(own, arrived)
+
+
+def mark_kernel(*refs):
+    refs[-1][...] = jnp.zeros_like(refs[-1])
+
+
+def mark(arrays):
+    return pl.pallas_call(
+        mark_kernel,
+        in_specs=[pl.BlockSpec(memory_space=pl.ANY)] * len(arrays),
         out_specs=pl.BlockSpec(memory_space=pltpu.VMEM),
-        out_shape=jax.ShapeDtypeStruct((rows, width), dtype),
-        compiler_params=pltpu.CompilerParams(vmem_limit_bytes=PROJECT_VMEM),
-        cost_estimate=pl.CostEstimate(
-            flops=4 * rows * depth * width, bytes_accessed=4 * depth * width, transcendentals=0
-        ),
-    )(mine, theirs, own_weight, their_weight)
-
-
-def finish_kernel(own_ref, *refs):
-    *arrived_refs, out_ref = refs
+        out_shape=jax.ShapeDtypeStruct((8, 128), F32),
+        compiler_params=pltpu.CompilerParams(vmem_limit_bytes=SMALL_VMEM),
+        cost_estimate=pl.CostEstimate(flops=2 * 10**10, bytes_accessed=2**20, transcendentals=0),
+    )(*arrays)
+
+
+def finish_kernel(own_ref, near_ref, *refs):
+    *arrived_refs, _, out_ref = refs
     width = out_ref.shape[1] // len(arrived_refs)
     for c, arrived_ref in enumerate(arrived_refs):
         at = slice(c * width, (c + 1) * width)
-        out_ref[:, at] = (own_ref[:, at] + arrived_ref[...].astype(F32)).astype(out_ref.dtype)
-
-
-def finish(own, arrived):
+        total = own_ref[:, at] + near_ref[:, at].astype(F32) + arrived_ref[...].astype(F32)
+        out_ref[:, at] = total.astype(out_ref.dtype)
+
+
+def finish(own, near, arrived):
     rows, width = own.shape
     whole = pl.BlockSpec(memory_space=pltpu.VMEM)
     return pl.pallas_call(
         finish_kernel,
-        in_specs=[whole] * (1 + len(arrived)),
+        in_specs=[whole] * (2 + len(arrived)) + [pl.BlockSpec(memory_space=pl.ANY)],
         out_specs=whole,
         out_shape=jax.ShapeDtypeStruct((rows, width), BF16),
         compiler_params=pltpu.CompilerParams(vmem_limit_bytes=SMALL_VMEM),
         cost_estimate=pl.CostEstimate(
             flops=rows * width, bytes_accessed=8 * rows * width, transcendentals=0
         ),
-    )(own, *arrived)
+    )(own, near, *arrived, mark(arrived))
 
 
 def body(pieces, tables, queries, keys, values, filters, skip_weight, out_weight):
@@ -349,13 +385,10 @@
     in_chip = [(0, 1), (1, 0), (2, 3), (3, 2)]
     across = [(0, 2), (2, 0), (1, 3), (3, 1)]
 
-    their_weight = lax.ppermute(out_weight, "fsdp", in_chip)
-
     if chans % 128 == 0 and n_peers == 8:
         blocks = pre(keys, values, filters, n_peers)
         received = exchange(blocks, n_peers, False)
         fwd, bwd, early = spectra(received[:-2], fwd, bwd, n_peers)
-        their_weight, early = lax.optimization_barrier((their_weight, early))
         back = exchange(conv_fast(early, received[-2:], fwd, bwd), n_peers, True)
         gated = gate(queries, keys, values, skip, back)
     else:
@@ -368,15 +401,17 @@
         mixed = back.transpose(1, 0, 2).reshape(rows, width).astype(F32) + skip * product
         gated = (queries.astype(F32) * mixed).astype(BF16)
 
-    theirs = lax.ppermute(gated, "fsdp", in_chip)
-    out_width = out_weight.shape[1] // 4
-    piece = out_width // pieces
-    arrived = []
+    theirs = []
     for c in range(pieces):
-        remote = project(gated, theirs, out_weight, their_weight, True, c * piece, piece, BF16)
-        arrived.append(lax.ppermute(remote, "fsdp", across))
-    own = project(gated, theirs, out_weight, their_weight, False, 0, out_width, F32)
-    return finish(own, arrived)
+        (sent,) = project(gated, out_weight, [(True, True, c, pieces)], [BF16])
+        theirs.append(lax.ppermute(sent, "fsdp", in_chip))
+    blocks = [(False, True, c, pieces) for c in range(pieces)]
+    ours = project(gated, out_weight, blocks, [F32] * pieces)
+    arrived = [lax.ppermute(add(*pair), "fsdp", across) for pair in zip(ours, theirs)]
+    blocks = [(True, False, 0, 1), (False, False, 0, 1)]
+    sent, own = project(gated, out_weight, blocks, [BF16, F32])
+    near = lax.ppermute(sent, "fsdp", in_chip)
+    return finish(own, near, arrived)
 
 
 def solution(mesh):

time: 68.7 us -> 67.7 us (0.985)
  waiting for transfers between devices: 27.6 us -> 23 us
  starting transfers between devices: 29.1 us -> 32.2 us
    ppermute x14, waiting for transfers between devices: 15.8 us -> 12.6 us  [exchange(): lax.ppermute(block, 'seq', [(i, i ^ slot) for i in range(n_peers)])]
    ppermute x14, starting transfers between devices: 26.3 us -> 29.4 us  [exchange(): lax.ppermute(block, 'seq', [(i, i ^ slot) for i in range(n_peers)])]
    ppermute x4 -> x5, waiting for transfers between devices: 11.8 us -> 10.4 us  [the longest x2 10.4 us: body(): lax.ppermute(add(*pair), 'fsdp', across)]
    pallas_call x4 -> x8, Pallas kernels: 3.54 us -> 3.92 us  [the longest x4 2.85 us: project(): pl.pallas_call(functools.partial(project_kernel, blocks), in_specs=[whole...]
    ppermute x4 -> x5, starting transfers between devices: 2.77 us -> 2.85 us  [the longest x2 2.16 us: body(): lax.ppermute(add(*pair), 'fsdp', across)]
  transfers between devices with their start and end apart: 18 -> 19, of which waited for: 11 -> 10; matrix products, arithmetic and copies ran while one was open for 0% -> 0% of each run, Pallas kernels for 9% -> 7%
where the time goes in v2:
time: 67.7 us; the launch traced here: 67.6 us
  starting transfers between devices  32.2 us (48%)
  waiting for transfers between devices  23 us (34%)
  Pallas kernels  12.2 us (18%)
    ppermute x14, starting transfers between devices, exchange(): lax.ppermute(block, 'seq', [(i, i ^ slot) for i in range(n_peers)])  29.4 us
    ppermute x14, waiting for transfers between devices, exchange(): lax.ppermute(block, 'seq', [(i, i ^ slot) for i in range(n_peers)])  12.6 us
    ppermute x2, waiting for transfers between devices, body(): lax.ppermute(add(*pair), 'fsdp', across)  10.4 us
    pallas_call x1, Pallas kernels, conv_fast(): pl.pallas_call(conv_kernel, in_specs=[whole] * 5, out_specs=[whole] * n_b...  3.46 us
    pallas_call x4, Pallas kernels, project(): pl.pallas_call(functools.partial(project_kernel, blocks), in_specs=[whole...  2.85 us
    pallas_call x1, Pallas kernels, spectra(): pl.pallas_call(functools.partial(spectra_kernel, n_peers), in_specs=[pl.B...  2.4 us
    ppermute x2, starting transfers between devices, body(): lax.ppermute(add(*pair), 'fsdp', across)  2.16 us
    pallas_call x1, Pallas kernels, pre(): pl.pallas_call(functools.partial(pre_kernel, n_peers), in_specs=[pl.Block...  1.92 us
  transfers between devices with their start and end apart: 19, of which 10 were waited for; matrix products, arithmetic and copies ran while one was open for 0% of the time, Pallas kernels for 7%

profile of v2, /device:TPU:0, one launch (start us, length us, event | category | flops | bytes accessed | tf_op | source)
XLA Modules:
  0.0 67.6 jit_solution(14207734925313699530)
XLA Ops:
  0.0 1.9 %shard_map.82 = (bf16[256,256]{1,0:T(8,128)(2,1)S(1)}, bf16[256,256]{1,0:T(8,128)(2,1)S(1)}, bf16[256,256]{1,0:T(8,128)(2,1)S(1)}, bf16[256,256]{1,0:T(8,128)(2,...) custom-call(bf16[256,1024]{1,0:T(8,128)(2,1)} %keys_ref.1, ...), custom_call_target="tpu_custom_call" | custom-call | flops 262144 | bytes 3145728 | tf_op jit(solution)/shard_map/pallas_call | solution.py:77
  1.9 3.0 %collective-permute-start = (bf16[256,256]{1,0:T(8,128)(2,1)S(1)}, bf16[256,256]{1,0:T(8,128)(2,1)S(1)}, u32[]{:S(2)}, u32[]{:S(2)}) collective-permute-start(bf16[256,256]{1,0:T(8,128)(2,1)S(1)} %get-tuple-element.29), channel_id=1, source_target_pairs={{0,4},{4,0},{8,12},{12,8},{16,20},{20,16},{24,28},{28,24},{1,5},{5... | collective-permute-start | bytes 393224 | tf_op jit(solution)/shard_map/ppermute | solution.py:105
  5.0 2.6 %collective-permute-start.1 = (bf16[256,256]{1,0:T(8,128)(2,1)S(1)}, bf16[256,256]{1,0:T(8,128)(2,1)S(1)}, u32[]{:S(2)}, u32[]{:S(2)}) collective-permute-start(bf16[256,256]{1,0:T(8,128)(2,1)S(1)} %get-tuple-element.30), channel_id=1, source_target_pairs={{0,16},{4,20},{8,24},{12,28},{16,0},{20,4},{24,8},{28,12},{1,17},{... | collective-permute-start | bytes 393224 | tf_op jit(solution)/shard_map/ppermute | solution.py:105
  7.6 1.6 %collective-permute-start.2 = (bf16[256,256]{1,0:T(8,128)(2,1)S(1)}, bf16[256,256]{1,0:T(8,128)(2,1)S(1)}, u32[]{:S(2)}, u32[]{:S(2)}) collective-permute-start(bf16[256,256]{1,0:T(8,128)(2,1)S(1)} %get-tuple-element.31), channel_id=1, source_target_pairs={{0,8},{4,12},{8,0},{12,4},{16,24},{20,28},{24,16},{28,20},{1,9},{5... | collective-permute-start | bytes 393224 | tf_op jit(solution)/shard_map/ppermute | solution.py:105
  9.4 1.4 %collective-permute-start.4 = (bf16[256,256]{1,0:T(8,128)(2,1)S(1)}, bf16[256,256]{1,0:T(8,128)(2,1)S(1)}, u32[]{:S(2)}, u32[]{:S(2)}) collective-permute-start(bf16[256,256]{1,0:T(8,128)(2,1)S(1)} %get-tuple-element.33), channel_id=1, source_target_pairs={{0,12},{4,8},{8,4},{12,0},{16,28},{20,24},{24,20},{28,16},{1,13},{... | collective-permute-start | bytes 393224 | tf_op jit(solution)/shard_map/ppermute | solution.py:105
  10.8 3.6 %collective-permute-start.5 = (bf16[256,256]{1,0:T(8,128)(2,1)S(1)}, bf16[256,256]{1,0:T(8,128)(2,1)S(1)}, u32[]{:S(2)}, u32[]{:S(2)}) collective-permute-start(bf16[256,256]{1,0:T(8,128)(2,1)S(1)} %get-tuple-element.37), channel_id=1, source_target_pairs={{0,24},{4,28},{8,16},{12,20},{16,8},{20,12},{24,0},{28,4},{1,25},{... | collective-permute-start | bytes 393224 | tf_op jit(solution)/shard_map/ppermute | solution.py:105
  14.5 1.9 %collective-permute-done.1.refs_2_ = bf16[256,256]{1,0:T(8,128)(2,1)S(1)} collective-permute-done((bf16[256,256]{1,0:T(8,128)(2,1)S(1)}, bf16[256,256]{1,0:T(8,128)(2,1)S(1)}, u32[]{:S(2)}, u32[]{:S(2)}) %collective-permute-start.1) | collective-permute-done | bytes 131104 | tf_op jit(solution)/shard_map/ppermute | solution.py:105
  16.3 2.4 %collective-permute-start.6 = (bf16[256,256]{1,0:T(8,128)(2,1)S(1)}, bf16[256,256]{1,0:T(8,128)(2,1)S(1)}, u32[]{:S(2)}, u32[]{:S(2)}) collective-permute-start(bf16[256,256]{1,0:T(8,128)(2,1)S(1)} %get-tuple-element.38), channel_id=1, source_target_pairs={{0,28},{4,24},{8,20},{12,16},{16,12},{20,8},{24,4},{28,0},{1,29},{... | collective-permute-start | bytes 393224 | tf_op jit(solution)/shard_map/ppermute | solution.py:105
  18.7 1.9 %collective-permute-done.3.refs_4_ = bf16[256,256]{1,0:T(8,128)(2,1)S(1)} collective-permute-done((bf16[256,256]{1,0:T(8,128)(2,1)S(1)}, bf16[256,256]{1,0:T(8,128)(2,1)S(1)}, u32[]{:S(2)}, u32[]{:S(2)}) %collective-permute-start.3) | collective-permute-done | bytes 131104 | tf_op jit(solution)/shard_map/ppermute | solution.py:105
  20.6 2.4 %shard_map.83 = (bf16[512,512]{1,0:T(8,128)(2,1)S(1)}, bf16[256,1536]{1,0:T(8,128)(2,1)S(1)}, f32[8,512,256]{2,1,0:T(8,128)S(1)}) custom-call(bf16[512,512]{1,0:T(8,128)(2,1)} %constant.4.clone.fwd_hbm, bf16[256,1536]{1,0:T(8,128)(2,1)} %constant.5.clone.bwd_hbm, bf16[256,256]{1,0:T(8,128)(2,1)S(1)} %get-tuple-element.28.refs_0_, ...), custom_call_target="tpu_custom_call" | custom-call | flops 805306368 | bytes 4194304 | tf_op jit(solution)/shard_map/pallas_call | solution.py:132
  23.0 1.5 %collective-permute-done.5.refs_0_ = bf16[256,256]{1,0:T(8,128)(2,1)S(1)} collective-permute-done((bf16[256,256]{1,0:T(8,128)(2,1)S(1)}, bf16[256,256]{1,0:T(8,128)(2,1)S(1)}, u32[]{:S(2)}, u32[]{:S(2)}) %collective-permute-start.5) | collective-permute-done | bytes 131104 | tf_op jit(solution)/shard_map/ppermute | solution.py:105
  24.5 1.4 %collective-permute-done.6.refs_1_ = bf16[256,256]{1,0:T(8,128)(2,1)S(1)} collective-permute-done((bf16[256,256]{1,0:T(8,128)(2,1)S(1)}, bf16[256,256]{1,0:T(8,128)(2,1)S(1)}, u32[]{:S(2)}, u32[]{:S(2)}) %collective-permute-start.6) | collective-permute-done | bytes 131104 | tf_op jit(solution)/shard_map/ppermute | solution.py:105
  26.0 3.5 %shard_map.84 = (bf16[256,128]{1,0:T(8,128)(2,1)S(1)}, bf16[256,128]{1,0:T(8,128)(2,1)S(1)}, bf16[256,128]{1,0:T(8,128)(2,1)S(1)}, bf16[256,128]{1,0:T(8,128)(2,...) custom-call(bf16[512,512]{1,0:T(8,128)(2,1)S(1)} %get-tuple-element., ...), custom_call_target="tpu_custom_call" | custom-call | flops 1073741824 | bytes 4194304 | tf_op jit(solution)/shard_map/pallas_call | solution.py:216
  29.4 4.1 %collective-permute-start.7 = (bf16[256,128]{1,0:T(8,128)(2,1)S(1)}, bf16[256,128]{1,0:T(8,128)(2,1)S(1)}, u32[]{:S(2)}, u32[]{:S(2)}) collective-permute-start(bf16[256,128]{1,0:T(8,128)(2,1)S(1)} %get-tuple-element.40), channel_id=1, source_target_pairs={{0,4},{4,0},{8,12},{12,8},{16,20},{20,16},{24,28},{28,24},{1,5},{5... | collective-permute-start | bytes 196616 | tf_op jit(solution)/shard_map/ppermute | solution.py:105
  33.5 4.6 %collective-permute-start.8 = (bf16[256,128]{1,0:T(8,128)(2,1)S(1)}, bf16[256,128]{1,0:T(8,128)(2,1)S(1)}, u32[]{:S(2)}, u32[]{:S(2)}) collective-permute-start(bf16[256,128]{1,0:T(8,128)(2,1)S(1)} %get-tuple-element.41), channel_id=1, source_target_pairs={{0,16},{4,20},{8,24},{12,28},{16,0},{20,4},{24,8},{28,12},{1,17},{... | collective-permute-start | bytes 196616 | tf_op jit(solution)/shard_map/ppermute | solution.py:105
  38.1 0.7 %collective-permute-start.10 = (bf16[256,128]{1,0:T(8,128)(2,1)S(1)}, bf16[256,128]{1,0:T(8,128)(2,1)S(1)}, u32[]{:S(2)}, u32[]{:S(2)}) collective-permute-start(bf16[256,128]{1,0:T(8,128)(2,1)S(1)} %get-tuple-element.43), channel_id=1, source_target_pairs={{0,24},{4,28},{8,16},{12,20},{16,8},{20,12},{24,0},{28,4},{1,25},{... | collective-permute-start | bytes 196616 | tf_op jit(solution)/shard_map/ppermute | solution.py:105
  38.8 2.7 %collective-permute-start.11 = (bf16[256,128]{1,0:T(8,128)(2,1)S(1)}, bf16[256,128]{1,0:T(8,128)(2,1)S(1)}, u32[]{:S(2)}, u32[]{:S(2)}) collective-permute-start(bf16[256,128]{1,0:T(8,128)(2,1)S(1)} %get-tuple-element.44), channel_id=1, source_target_pairs={{0,8},{4,12},{8,0},{12,4},{16,24},{20,28},{24,16},{28,20},{1,9},{5... | collective-permute-start | bytes 196616 | tf_op jit(solution)/shard_map/ppermute | solution.py:105
  41.5 1.9 %collective-permute-start.12 = (bf16[256,128]{1,0:T(8,128)(2,1)S(1)}, bf16[256,128]{1,0:T(8,128)(2,1)S(1)}, u32[]{:S(2)}, u32[]{:S(2)}) collective-permute-start(bf16[256,128]{1,0:T(8,128)(2,1)S(1)} %get-tuple-element.45), channel_id=1, source_target_pairs={{0,28},{4,24},{8,20},{12,16},{16,12},{20,8},{24,4},{28,0},{1,29},{... | collective-permute-start | bytes 196616 | tf_op jit(solution)/shard_map/ppermute | solution.py:105
  43.4 0.6 collective-permute-start.13
  44.0 2.7 %collective-permute-done.9.refs_3_ = bf16[256,128]{1,0:T(8,128)(2,1)S(1)} collective-permute-done((bf16[256,128]{1,0:T(8,128)(2,1)S(1)}, bf16[256,128]{1,0:T(8,128)(2,1)S(1)}, u32[]{:S(2)}, u32[]{:S(2)}) %collective-permute-start.9) | collective-permute-done | bytes 65568 | tf_op jit(solution)/shard_map/ppermute | solution.py:105
  46.7 0.5 collective-permute-done.11.refs_5_
  47.2 1.4 %collective-permute-done.12.refs_6_ = bf16[256,128]{1,0:T(8,128)(2,1)S(1)} collective-permute-done((bf16[256,128]{1,0:T(8,128)(2,1)S(1)}, bf16[256,128]{1,0:T(8,128)(2,1)S(1)}, u32[]{:S(2)}, u32[]{:S(2)}) %collective-permute-start.12) | collective-permute-done | bytes 65568 | tf_op jit(solution)/shard_map/ppermute | solution.py:105
  48.6 1.3 %collective-permute-done.13.refs_7_ = bf16[256,128]{1,0:T(8,128)(2,1)S(1)} collective-permute-done((bf16[256,128]{1,0:T(8,128)(2,1)S(1)}, bf16[256,128]{1,0:T(8,128)(2,1)S(1)}, u32[]{:S(2)}, u32[]{:S(2)}) %collective-permute-start.13) | collective-permute-done | bytes 65568 | tf_op jit(solution)/shard_map/ppermute | solution.py:105
  50.3 0.5 shard_map.90
  51.3 0.6 collective-permute-start.15
  51.9 0.7 %shard_map.87 = (f32[256,512]{1,0:T(8,128)S(1)}, f32[256,512]{1,0:T(8,128)S(1)}) custom-call(bf16[256,1024]{1,0:T(8,128)(2,1)S(1)} %shard_map.85.gated_ref, bf16[1024,4096]{1,0:T(8,128)(2,1)S(1)} %copy-done), custom_call_target="tpu_custom_call" | custom-call | flops 536870912 | bytes 2097152 | tf_op jit(solution)/shard_map/pallas_call | solution.py:309
  52.7 1.6 %collective-permute-start.18 = (bf16[256,512]{1,0:T(8,128)(2,1)S(1)}, bf16[256,512]{1,0:T(8,128)(2,1)S(1)}, u32[]{:S(2)}, u32[]{:S(2)}) collective-permute-start(bf16[256,512]{1,0:T(8,128)(2,1)S(1)} %shard_map.91), channel_id=1, source_target_pairs={{0,2},{2,0},{1,3},{3,1},{4,6},{6,4},{5,7},{7,5},{8,10},{10,8},{9,1... | collective-permute-start | bytes 786440 | tf_op jit(solution)/shard_map/ppermute | solution.py:410
  54.3 0.6 collective-permute-start.16
  54.9 1.2 %shard_map.86 = (bf16[256,1024]{1,0:T(8,128)(2,1)S(1)}, f32[256,1024]{1,0:T(8,128)S(1)}) custom-call(bf16[256,1024]{1,0:T(8,128)(2,1)S(1)} %shard_map.85.gated_ref, bf16[1024,4096]{1,0:T(8,128)(2,1)S(1)} %copy-done), custom_call_target="tpu_custom_call" | custom-call | flops 1073741824 | bytes 4194304 | tf_op jit(solution)/shard_map/pallas_call | solution.py:309
  56.2 5.7 %collective-permute-done.18.refs_1_ = bf16[256,512]{1,0:T(8,128)(2,1)S(1)} collective-permute-done((bf16[256,512]{1,0:T(8,128)(2,1)S(1)}, bf16[256,512]{1,0:T(8,128)(2,1)S(1)}, u32[]{:S(2)}, u32[]{:S(2)}) %collective-permute-start.18) | collective-permute-done | bytes 262176 | tf_op jit(solution)/shard_map/ppermute | solution.py:410
  61.9 4.7 %collective-permute-done.16.refs_0_ = bf16[256,512]{1,0:T(8,128)(2,1)S(1)} collective-permute-done((bf16[256,512]{1,0:T(8,128)(2,1)S(1)}, bf16[256,512]{1,0:T(8,128)(2,1)S(1)}, u32[]{:S(2)}, u32[]{:S(2)}) %collective-permute-start.16) | collective-permute-done | bytes 262176 | tf_op jit(solution)/shard_map/ppermute | solution.py:410
  66.6 1.0 %shard_map.93 = bf16[256,1024]{1,0:T(8,128)(2,1)} custom-call(f32[256,1024]{1,0:T(8,128)S(1)} %get-tuple-element.47.own_ref, bf16[256,1024]{1,0:T(8,128)(2,1)S(1)} %collective-permute-done.14.near_ref, bf16[256,512]{1,0:T(8,128)(2,1)S(1)} %collective-permute-done.16.refs_0_, bf16[256,512]{1,0:T(8,128)(2,1)S(1)} %collective-permute-done.18.refs_1_, ...), custom_call_target="tpu_custom_call" | custom-call | flops 262144 | bytes 2097152 | tf_op jit(solution)/shard_map/pallas_call | solution.py:367
  (28 shorter events, 1.5 us)
Async XLA Ops:
  0.0 49.9 %copy-start.2 = (bf16[256,1024]{1,0:T(8,128)(2,1)S(1)}, bf16[256,1024]{1,0:T(8,128)(2,1)}, u32[]{:S(2)}) copy-start(bf16[256,1024]{1,0:T(8,128)(2,1)} %values_ref.1) | copy-start | bytes 1572868
  0.0 49.9 %copy-start.1 = (bf16[256,1024]{1,0:T(8,128)(2,1)S(1)}, bf16[256,1024]{1,0:T(8,128)(2,1)}, u32[]{:S(2)}) copy-start(bf16[256,1024]{1,0:T(8,128)(2,1)} %keys_ref.1) | copy-start | bytes 1572868
  0.0 49.9 %copy-start.4 = (f32[1024]{0:T(1024)S(1)}, f32[1024]{0:T(1024)}, u32[]{:S(2)}) copy-start(f32[1024]{0:T(1024)} %param.12) | copy-start | bytes 12292
  0.0 49.9 %copy-start.3 = (bf16[256,1024]{1,0:T(8,128)(2,1)S(1)}, bf16[256,1024]{1,0:T(8,128)(2,1)}, u32[]{:S(2)}) copy-start(bf16[256,1024]{1,0:T(8,128)(2,1)} %queries_ref.1) | copy-start | bytes 1572868
  0.0 50.3 %copy-start = (bf16[1024,4096]{1,0:T(8,128)(2,1)S(1)}, bf16[1024,4096]{1,0:T(8,128)(2,1)}, u32[]{:S(2)}) copy-start(bf16[1024,4096]{1,0:T(8,128)(2,1)} %weight_ref.7) | copy-start | bytes 25165828
  1.9 8.9 %collective-permute-start = (bf16[256,256]{1,0:T(8,128)(2,1)S(1)}, bf16[256,256]{1,0:T(8,128)(2,1)S(1)}, u32[]{:S(2)}, u32[]{:S(2)}) collective-permute-start(bf16[256,256]{1,0:T(8,128)(2,1)S(1)} %get-tuple-element.29), channel_id=1, source_target_pairs={{0,4},{4,0},{8,12},{12,8},{16,20},{20,16},{24,28},{28,24},{1,5},{5... | collective-permute-start | bytes 393224 | tf_op jit(solution)/shard_map/ppermute | solution.py:105
  5.0 11.3 %collective-permute-start.1 = (bf16[256,256]{1,0:T(8,128)(2,1)S(1)}, bf16[256,256]{1,0:T(8,128)(2,1)S(1)}, u32[]{:S(2)}, u32[]{:S(2)}) collective-permute-start(bf16[256,256]{1,0:T(8,128)(2,1)S(1)} %get-tuple-element.30), channel_id=1, source_target_pairs={{0,16},{4,20},{8,24},{12,28},{16,0},{20,4},{24,8},{28,12},{1,17},{... | collective-permute-start | bytes 393224 | tf_op jit(solution)/shard_map/ppermute | solution.py:105
  7.6 11.1 %collective-permute-start.2 = (bf16[256,256]{1,0:T(8,128)(2,1)S(1)}, bf16[256,256]{1,0:T(8,128)(2,1)S(1)}, u32[]{:S(2)}, u32[]{:S(2)}) collective-permute-start(bf16[256,256]{1,0:T(8,128)(2,1)S(1)} %get-tuple-element.31), channel_id=1, source_target_pairs={{0,8},{4,12},{8,0},{12,4},{16,24},{20,28},{24,16},{28,20},{1,9},{5... | collective-permute-start | bytes 393224 | tf_op jit(solution)/shard_map/ppermute | solution.py:105
  9.2 11.5 %collective-permute-start.3 = (bf16[256,256]{1,0:T(8,128)(2,1)S(1)}, bf16[256,256]{1,0:T(8,128)(2,1)S(1)}, u32[]{:S(2)}, u32[]{:S(2)}) collective-permute-start(bf16[256,256]{1,0:T(8,128)(2,1)S(1)} %get-tuple-element.32), channel_id=1, source_target_pairs={{0,20},{4,16},{8,28},{12,24},{16,4},{20,0},{24,12},{28,8},{1,21},{... | collective-permute-start | bytes 393224 | tf_op jit(solution)/shard_map/ppermute | solution.py:105
  9.4 11.2 %collective-permute-start.4 = (bf16[256,256]{1,0:T(8,128)(2,1)S(1)}, bf16[256,256]{1,0:T(8,128)(2,1)S(1)}, u32[]{:S(2)}, u32[]{:S(2)}) collective-permute-start(bf16[256,256]{1,0:T(8,128)(2,1)S(1)} %get-tuple-element.33), channel_id=1, source_target_pairs={{0,12},{4,8},{8,4},{12,0},{16,28},{20,24},{24,20},{28,16},{1,13},{... | collective-permute-start | bytes 393224 | tf_op jit(solution)/shard_map/ppermute | solution.py:105
  10.8 13.7 %collective-permute-start.5 = (bf16[256,256]{1,0:T(8,128)(2,1)S(1)}, bf16[256,256]{1,0:T(8,128)(2,1)S(1)}, u32[]{:S(2)}, u32[]{:S(2)}) collective-permute-start(bf16[256,256]{1,0:T(8,128)(2,1)S(1)} %get-tuple-element.37), channel_id=1, source_target_pairs={{0,24},{4,28},{8,16},{12,20},{16,8},{20,12},{24,0},{28,4},{1,25},{... | collective-permute-start | bytes 393224 | tf_op jit(solution)/shard_map/ppermute | solution.py:105
  16.3 9.6 %collective-permute-start.6 = (bf16[256,256]{1,0:T(8,128)(2,1)S(1)}, bf16[256,256]{1,0:T(8,128)(2,1)S(1)}, u32[]{:S(2)}, u32[]{:S(2)}) collective-permute-start(bf16[256,256]{1,0:T(8,128)(2,1)S(1)} %get-tuple-element.38), channel_id=1, source_target_pairs={{0,28},{4,24},{8,20},{12,16},{16,12},{20,8},{24,4},{28,0},{1,29},{... | collective-permute-start | bytes 393224 | tf_op jit(solution)/shard_map/ppermute | solution.py:105
  29.4 12.1 %collective-permute-start.7 = (bf16[256,128]{1,0:T(8,128)(2,1)S(1)}, bf16[256,128]{1,0:T(8,128)(2,1)S(1)}, u32[]{:S(2)}, u32[]{:S(2)}) collective-permute-start(bf16[256,128]{1,0:T(8,128)(2,1)S(1)} %get-tuple-element.40), channel_id=1, source_target_pairs={{0,4},{4,0},{8,12},{12,8},{16,20},{20,16},{24,28},{28,24},{1,5},{5... | collective-permute-start | bytes 196616 | tf_op jit(solution)/shard_map/ppermute | solution.py:105
  33.5 9.9 %collective-permute-start.8 = (bf16[256,128]{1,0:T(8,128)(2,1)S(1)}, bf16[256,128]{1,0:T(8,128)(2,1)S(1)}, u32[]{:S(2)}, u32[]{:S(2)}) collective-permute-start(bf16[256,128]{1,0:T(8,128)(2,1)S(1)} %get-tuple-element.41), channel_id=1, source_target_pairs={{0,16},{4,20},{8,24},{12,28},{16,0},{20,4},{24,8},{28,12},{1,17},{... | collective-permute-start | bytes 196616 | tf_op jit(solution)/shard_map/ppermute | solution.py:105
  38.1 8.6 %collective-permute-start.9 = (bf16[256,128]{1,0:T(8,128)(2,1)S(1)}, bf16[256,128]{1,0:T(8,128)(2,1)S(1)}, u32[]{:S(2)}, u32[]{:S(2)}) collective-permute-start(bf16[256,128]{1,0:T(8,128)(2,1)S(1)} %get-tuple-element.42), channel_id=1, source_target_pairs={{0,20},{4,16},{8,28},{12,24},{16,4},{20,0},{24,12},{28,8},{1,21},{... | collective-permute-start | bytes 196616 | tf_op jit(solution)/shard_map/ppermute | solution.py:105
  38.1 8.6 %collective-permute-start.10 = (bf16[256,128]{1,0:T(8,128)(2,1)S(1)}, bf16[256,128]{1,0:T(8,128)(2,1)S(1)}, u32[]{:S(2)}, u32[]{:S(2)}) collective-permute-start(bf16[256,128]{1,0:T(8,128)(2,1)S(1)} %get-tuple-element.43), channel_id=1, source_target_pairs={{0,24},{4,28},{8,16},{12,20},{16,8},{20,12},{24,0},{28,4},{1,25},{... | collective-permute-start | bytes 196616 | tf_op jit(solution)/shard_map/ppermute | solution.py:105
  38.8 8.4 %collective-permute-start.11 = (bf16[256,128]{1,0:T(8,128)(2,1)S(1)}, bf16[256,128]{1,0:T(8,128)(2,1)S(1)}, u32[]{:S(2)}, u32[]{:S(2)}) collective-permute-start(bf16[256,128]{1,0:T(8,128)(2,1)S(1)} %get-tuple-element.44), channel_id=1, source_target_pairs={{0,8},{4,12},{8,0},{12,4},{16,24},{20,28},{24,16},{28,20},{1,9},{5... | collective-permute-start | bytes 196616 | tf_op jit(solution)/shard_map/ppermute | solution.py:105
  41.5 7.1 %collective-permute-start.12 = (bf16[256,128]{1,0:T(8,128)(2,1)S(1)}, bf16[256,128]{1,0:T(8,128)(2,1)S(1)}, u32[]{:S(2)}, u32[]{:S(2)}) collective-permute-start(bf16[256,128]{1,0:T(8,128)(2,1)S(1)} %get-tuple-element.45), channel_id=1, source_target_pairs={{0,28},{4,24},{8,20},{12,16},{16,12},{20,8},{24,4},{28,0},{1,29},{... | collective-permute-start | bytes 196616 | tf_op jit(solution)/shard_map/ppermute | solution.py:105
  43.4 6.5 %collective-permute-start.13 = (bf16[256,128]{1,0:T(8,128)(2,1)S(1)}, bf16[256,128]{1,0:T(8,128)(2,1)S(1)}, u32[]{:S(2)}, u32[]{:S(2)}) collective-permute-start(bf16[256,128]{1,0:T(8,128)(2,1)S(1)} %get-tuple-element.46), channel_id=1, source_target_pairs={{0,12},{4,8},{8,4},{12,0},{16,28},{20,24},{24,20},{28,16},{1,13},{... | collective-permute-start | bytes 196616 | tf_op jit(solution)/shard_map/ppermute | solution.py:105
  50.8 1.8 %collective-permute-start.17 = (bf16[256,512]{1,0:T(8,128)(2,1)S(1)}, bf16[256,512]{1,0:T(8,128)(2,1)S(1)}, u32[]{:S(2)}, u32[]{:S(2)}) collective-permute-start(bf16[256,512]{1,0:T(8,128)(2,1)S(1)} %shard_map.90), channel_id=1, source_target_pairs={{0,1},{1,0},{2,3},{3,2},{4,5},{5,4},{6,7},{7,6},{8,9},{9,8},{10,11... | collective-permute-start | bytes 786440 | tf_op jit(solution)/shard_map/ppermute | solution.py:407
  51.3 2.9 %collective-permute-start.15 = (bf16[256,512]{1,0:T(8,128)(2,1)S(1)}, bf16[256,512]{1,0:T(8,128)(2,1)S(1)}, u32[]{:S(2)}, u32[]{:S(2)}) collective-permute-start(bf16[256,512]{1,0:T(8,128)(2,1)S(1)} %shard_map.88), channel_id=1, source_target_pairs={{0,1},{1,0},{2,3},{3,2},{4,5},{5,4},{6,7},{7,6},{8,9},{9,8},{10,11... | collective-permute-start | bytes 786440 | tf_op jit(solution)/shard_map/ppermute | solution.py:407
  52.7 9.2 %collective-permute-start.18 = (bf16[256,512]{1,0:T(8,128)(2,1)S(1)}, bf16[256,512]{1,0:T(8,128)(2,1)S(1)}, u32[]{:S(2)}, u32[]{:S(2)}) collective-permute-start(bf16[256,512]{1,0:T(8,128)(2,1)S(1)} %shard_map.91), channel_id=1, source_target_pairs={{0,2},{2,0},{1,3},{3,1},{4,6},{6,4},{5,7},{7,5},{8,10},{10,8},{9,1... | collective-permute-start | bytes 786440 | tf_op jit(solution)/shard_map/ppermute | solution.py:410
  54.3 12.3 %collective-permute-start.16 = (bf16[256,512]{1,0:T(8,128)(2,1)S(1)}, bf16[256,512]{1,0:T(8,128)(2,1)S(1)}, u32[]{:S(2)}, u32[]{:S(2)}) collective-permute-start(bf16[256,512]{1,0:T(8,128)(2,1)S(1)} %shard_map.89), channel_id=1, source_target_pairs={{0,2},{2,0},{1,3},{3,1},{4,6},{6,4},{5,7},{7,5},{8,10},{10,8},{9,1... | collective-permute-start | bytes 786440 | tf_op jit(solution)/shard_map/ppermute | solution.py:410
  56.1 10.5 %collective-permute-start.14 = (bf16[256,1024]{1,0:T(8,128)(2,1)S(1)}, bf16[256,1024]{1,0:T(8,128)(2,1)S(1)}, u32[]{:S(2)}, u32[]{:S(2)}) collective-permute-start(bf16[256,1024]{1,0:T(8,128)(2,1)S(1)} %get-tuple-element.48), channel_id=1, source_target_pairs={{0,1},{1,0},{2,3},{3,2},{4,5},{5,4},{6,7},{7,6},{8,9},{9,8},{10,11... | collective-permute-start | bytes 1572872 | tf_op jit(solution)/shard_map/ppermute | solution.py:413

commit v3 on v2

--- a/solution.py
+++ b/solution.py
@@ -42,52 +42,48 @@
     return pl.ds(pl.multiple_of(peer_of(slot) * size, size), size)
 
 
-def pre_kernel(n_peers, keys_hbm, values_hbm, filters_hbm, *refs):
-    out_refs = refs[:n_peers]
-    keys, values, filters, sem = refs[n_peers:]
-    rows, width = keys.shape
-    chans = width // n_peers
-    steps = sem.shape[0]
-    parts = [pl.ds(c * rows // steps, rows // steps) for c in range(steps)]
+def pre_kernel(slots, keys_hbm, values_hbm, filters_hbm, *refs):
+    out_refs, (keys, values, filters, sem) = refs[: len(slots)], refs[len(slots) :]
+    chans = keys.shape[2]
     pairs = ((keys_hbm, keys), (values_hbm, values), (filters_hbm, filters))
     copies = [
         [
-            pltpu.make_async_copy(src.at[part], dst.at[part], sem.at[c, i])
+            pltpu.make_async_copy(src.at[:, peer_block(slot, chans)], dst.at[s], sem.at[s, i])
             for i, (src, dst) in enumerate(pairs)
         ]
-        for c, part in enumerate(parts)
+        for s, slot in enumerate(slots)
     ]
     for group in copies:
         for copy in group:
             copy.start()
-    for part, group in zip(parts, copies):
+    for s, (group, out_ref) in enumerate(zip(copies, out_refs)):
         for copy in group:
             copy.wait()
-        for slot, out_ref in zip(slots_of(n_peers, False), out_refs):
-            at = peer_block(slot, chans)
-            product = keys[part, at].astype(F32) * values[part, at].astype(F32)
-            out_ref[part, :chans] = product.astype(BF16)
-            out_ref[part, chans:] = filters[part, at].astype(BF16)
-
-
-def pre(keys, values, filters, n_peers):
+        product = keys[s].astype(F32) * values[s].astype(F32)
+        out_ref[:, :chans] = product.astype(BF16)
+        out_ref[:, chans:] = filters[s].astype(BF16)
+
+
+def pre(keys, values, filters, slots, n_peers):
     rows, width = keys.shape
     chans = width // n_peers
     args = [pltpu.with_memory_space_constraint(a, pltpu.HBM) for a in (keys, values, filters)]
     return pl.pallas_call(
-        functools.partial(pre_kernel, n_peers),
+        functools.partial(pre_kernel, slots),
         in_specs=[pl.BlockSpec(memory_space=pltpu.HBM)] * 3,
-        out_specs=[pl.BlockSpec(memory_space=pltpu.VMEM)] * n_peers,
-        out_shape=[jax.ShapeDtypeStruct((rows, 2 * chans), BF16)] * n_peers,
+        out_specs=[pl.BlockSpec(memory_space=pltpu.VMEM)] * len(slots),
+        out_shape=[jax.ShapeDtypeStruct((rows, 2 * chans), BF16)] * len(slots),
         scratch_shapes=[
-            pltpu.VMEM((rows, width), BF16),
-            pltpu.VMEM((rows, width), BF16),
-            pltpu.VMEM((rows, width), F32),
-            pltpu.SemaphoreType.DMA((2, 3)),
+            pltpu.VMEM((len(slots), rows, chans), BF16),
+            pltpu.VMEM((len(slots), rows, chans), BF16),
+            pltpu.VMEM((len(slots), rows, chans), F32),
+            pltpu.SemaphoreType.DMA((len(slots), 3)),
         ],
         compiler_params=pltpu.CompilerParams(vmem_limit_bytes=SMALL_VMEM),
         cost_estimate=pl.CostEstimate(
-            flops=rows * width, bytes_accessed=12 * rows * width, transcendentals=0
+            flops=rows * chans * len(slots),
+            bytes_accessed=12 * rows * chans * len(slots),
+            transcendentals=0,
         ),
     )(*args)
 
@@ -97,7 +93,7 @@
     near, far = list(range(1, half)), list(range(half, n_peers))
     if back:
         return [0, near[0]] + far[:3] + [near[1]] + far[3:] + near[2:]
-    return [0, near[0], far[0], near[1], far[1]] + near[2:] + far[2:]
+    return [0] + far[:2] + near + far[2:]
 
 
 def exchange(blocks, n_peers, back):
@@ -386,8 +382,11 @@
     across = [(0, 2), (2, 0), (1, 3), (3, 1)]
 
     if chans % 128 == 0 and n_peers == 8:
-        blocks = pre(keys, values, filters, n_peers)
-        received = exchange(blocks, n_peers, False)
+        slots = slots_of(n_peers, False)
+        first, rest = slots[1:3], slots[:1] + slots[3:]
+        mine = pre(keys, values, filters, first, n_peers)
+        own, *others = pre(keys, values, filters, rest, n_peers)
+        received = exchange([own, *mine, *others], n_peers, False)
         fwd, bwd, early = spectra(received[:-2], fwd, bwd, n_peers)
         back = exchange(conv_fast(early, received[-2:], fwd, bwd), n_peers, True)
         gated = gate(queries, keys, values, skip, back)

time: 67.7 us -> 67.3 us (level)
  starting transfers between devices: 32.2 us -> 29.3 us
  waiting for transfers between devices: 23 us -> 24.4 us
  Pallas kernels: 12.2 us -> 13.2 us
    ppermute x14, starting transfers between devices: 29.4 us -> 26.4 us  [exchange(): lax.ppermute(block, 'seq', [(i, i ^ slot) for i in range(n_peers)])]
    ppermute x14, waiting for transfers between devices: 12.6 us -> 14 us  [exchange(): lax.ppermute(block, 'seq', [(i, i ^ slot) for i in range(n_peers)])]
    pallas_call x1 -> x2, Pallas kernels: 1.92 us -> 3.01 us  [pre(): pl.pallas_call(functools.partial(pre_kernel, slots), in_specs=[pl.BlockSp...]
  transfers between devices with their start and end apart: 19 -> 19, of which waited for: 10 -> 8; matrix products, arithmetic and copies ran while one was open for 0% -> 0% of each run, Pallas kernels for 7% -> 10%
where the time goes in v3:
time: 67.3 us; the launch traced here: 67.1 us
  starting transfers between devices  29.3 us (44%)
  waiting for transfers between devices  24.4 us (36%)
  Pallas kernels  13.2 us (20%)
    ppermute x14, starting transfers between devices, exchange(): lax.ppermute(block, 'seq', [(i, i ^ slot) for i in range(n_peers)])  26.4 us
    ppermute x14, waiting for transfers between devices, exchange(): lax.ppermute(block, 'seq', [(i, i ^ slot) for i in range(n_peers)])  14 us
    ppermute x2, waiting for transfers between devices, body(): lax.ppermute(add(*pair), 'fsdp', across)  10.4 us
    pallas_call x1, Pallas kernels, conv_fast(): pl.pallas_call(conv_kernel, in_specs=[whole] * 5, out_specs=[whole] * n_b...  3.47 us
    pallas_call x2, Pallas kernels, pre(): pl.pallas_call(functools.partial(pre_kernel, slots), in_specs=[pl.BlockSp...  3.01 us
    pallas_call x4, Pallas kernels, project(): pl.pallas_call(functools.partial(project_kernel, blocks), in_specs=[whole...  2.85 us
    pallas_call x1, Pallas kernels, spectra(): pl.pallas_call(functools.partial(spectra_kernel, n_peers), in_specs=[pl.B...  2.4 us
    ppermute x2, starting transfers between devices, body(): lax.ppermute(add(*pair), 'fsdp', across)  2.16 us
  transfers between devices with their start and end apart: 19, of which 8 were waited for; matrix products, arithmetic and copies ran while one was open for 0% of the time, Pallas kernels for 10%

profile of v3, /device:TPU:0, one launch (start us, length us, event | category | flops | bytes accessed | tf_op | source)
XLA Modules:
  0.0 67.1 jit_solution(17747514663898211337)
XLA Ops:
  0.0 1.3 %shard_map.83 = (bf16[256,256]{1,0:T(8,128)(2,1)S(1)}, bf16[256,256]{1,0:T(8,128)(2,1)S(1)}) custom-call(bf16[256,1024]{1,0:T(8,128)(2,1)} %keys_ref.1, bf16[256,1024]{1,0:T(8,128)(2,1)} %values_ref.1, f32[256,1024]{1,0:T(8,128)} %filters_hbm.3), custom_call_target="tpu_custom_call" | custom-call | flops 65536 | bytes 786432 | tf_op jit(solution)/shard_map/pallas_call | solution.py:71
  1.4 4.1 %collective-permute-start = (bf16[256,256]{1,0:T(8,128)(2,1)S(1)}, bf16[256,256]{1,0:T(8,128)(2,1)S(1)}, u32[]{:S(2)}, u32[]{:S(2)}) collective-permute-start(bf16[256,256]{1,0:T(8,128)(2,1)S(1)} %get-tuple-element.29), channel_id=1, source_target_pairs={{0,16},{4,20},{8,24},{12,28},{16,0},{20,4},{24,8},{28,12},{1,17},{... | collective-permute-start | bytes 393224 | tf_op jit(solution)/shard_map/ppermute | solution.py:101
  5.5 1.3 %collective-permute-start.1 = (bf16[256,256]{1,0:T(8,128)(2,1)S(1)}, bf16[256,256]{1,0:T(8,128)(2,1)S(1)}, u32[]{:S(2)}, u32[]{:S(2)}) collective-permute-start(bf16[256,256]{1,0:T(8,128)(2,1)S(1)} %get-tuple-element.30), channel_id=1, source_target_pairs={{0,20},{4,16},{8,28},{12,24},{16,4},{20,0},{24,12},{28,8},{1,21},{... | collective-permute-start | bytes 393224 | tf_op jit(solution)/shard_map/ppermute | solution.py:101
  6.8 1.7 %shard_map.82 = (bf16[256,256]{1,0:T(8,128)(2,1)S(1)}, bf16[256,256]{1,0:T(8,128)(2,1)S(1)}, bf16[256,256]{1,0:T(8,128)(2,1)S(1)}, bf16[256,256]{1,0:T(8,128)(2,...) custom-call(bf16[256,1024]{1,0:T(8,128)(2,1)} %keys_ref.1, bf16[256,1024]{1,0:T(8,128)(2,1)} %values_ref.1, ...), custom_call_target="tpu_custom_call" | custom-call | flops 196608 | bytes 2359296 | tf_op jit(solution)/shard_map/pallas_call | solution.py:71
  8.5 0.3 collective-permute-start.2
  8.8 1.8 %collective-permute-start.3 = (bf16[256,256]{1,0:T(8,128)(2,1)S(1)}, bf16[256,256]{1,0:T(8,128)(2,1)S(1)}, u32[]{:S(2)}, u32[]{:S(2)}) collective-permute-start(bf16[256,256]{1,0:T(8,128)(2,1)S(1)} %get-tuple-element.32), channel_id=1, source_target_pairs={{0,8},{4,12},{8,0},{12,4},{16,24},{20,28},{24,16},{28,20},{1,9},{5... | collective-permute-start | bytes 393224 | tf_op jit(solution)/shard_map/ppermute | solution.py:101
  10.6 1.4 %collective-permute-start.4 = (bf16[256,256]{1,0:T(8,128)(2,1)S(1)}, bf16[256,256]{1,0:T(8,128)(2,1)S(1)}, u32[]{:S(2)}, u32[]{:S(2)}) collective-permute-start(bf16[256,256]{1,0:T(8,128)(2,1)S(1)} %get-tuple-element.33), channel_id=1, source_target_pairs={{0,12},{4,8},{8,4},{12,0},{16,28},{20,24},{24,20},{28,16},{1,13},{... | collective-permute-start | bytes 393224 | tf_op jit(solution)/shard_map/ppermute | solution.py:101
  12.0 3.4 %collective-permute-done.refs_1_ = bf16[256,256]{1,0:T(8,128)(2,1)S(1)} collective-permute-done((bf16[256,256]{1,0:T(8,128)(2,1)S(1)}, bf16[256,256]{1,0:T(8,128)(2,1)S(1)}, u32[]{:S(2)}, u32[]{:S(2)}) %collective-permute-start) | collective-permute-done | bytes 131104 | tf_op jit(solution)/shard_map/ppermute | solution.py:101
  15.4 2.9 %collective-permute-start.5 = (bf16[256,256]{1,0:T(8,128)(2,1)S(1)}, bf16[256,256]{1,0:T(8,128)(2,1)S(1)}, u32[]{:S(2)}, u32[]{:S(2)}) collective-permute-start(bf16[256,256]{1,0:T(8,128)(2,1)S(1)} %get-tuple-element.37), channel_id=1, source_target_pairs={{0,24},{4,28},{8,16},{12,20},{16,8},{20,12},{24,0},{28,4},{1,25},{... | collective-permute-start | bytes 393224 | tf_op jit(solution)/shard_map/ppermute | solution.py:101
  18.5 3.5 %collective-permute-start.6 = (bf16[256,256]{1,0:T(8,128)(2,1)S(1)}, bf16[256,256]{1,0:T(8,128)(2,1)S(1)}, u32[]{:S(2)}, u32[]{:S(2)}) collective-permute-start(bf16[256,256]{1,0:T(8,128)(2,1)S(1)} %get-tuple-element.38), channel_id=1, source_target_pairs={{0,28},{4,24},{8,20},{12,16},{16,12},{20,8},{24,4},{28,0},{1,29},{... | collective-permute-start | bytes 393224 | tf_op jit(solution)/shard_map/ppermute | solution.py:101
  22.0 5.3 %collective-permute-done.4.refs_5_ = bf16[256,256]{1,0:T(8,128)(2,1)S(1)} collective-permute-done((bf16[256,256]{1,0:T(8,128)(2,1)S(1)}, bf16[256,256]{1,0:T(8,128)(2,1)S(1)}, u32[]{:S(2)}, u32[]{:S(2)}) %collective-permute-start.4) | collective-permute-done | bytes 131104 | tf_op jit(solution)/shard_map/ppermute | solution.py:101
  27.3 2.4 %shard_map.84 = (bf16[512,512]{1,0:T(8,128)(2,1)S(1)}, bf16[256,1536]{1,0:T(8,128)(2,1)S(1)}, f32[8,512,256]{2,1,0:T(8,128)S(1)}) custom-call(bf16[512,512]{1,0:T(8,128)(2,1)} %constant.4.clone.fwd_hbm, bf16[256,1536]{1,0:T(8,128)(2,1)} %constant.5.clone.bwd_hbm, bf16[256,256]{1,0:T(8,128)(2,1)S(1)} %get-tuple-element.28.refs_0_, ...), custom_call_target="tpu_custom_call" | custom-call | flops 805306368 | bytes 4194304 | tf_op jit(solution)/shard_map/pallas_call | solution.py:128
  29.8 3.5 %shard_map.85 = (bf16[256,128]{1,0:T(8,128)(2,1)S(1)}, bf16[256,128]{1,0:T(8,128)(2,1)S(1)}, bf16[256,128]{1,0:T(8,128)(2,1)S(1)}, bf16[256,128]{1,0:T(8,128)(2,...) custom-call(bf16[512,512]{1,0:T(8,128)(2,1)S(1)} %get-tuple-element., ...), custom_call_target="tpu_custom_call" | custom-call | flops 1073741824 | bytes 4194304 | tf_op jit(solution)/shard_map/pallas_call | solution.py:212
  33.2 0.4 collective-permute-start.7
  33.7 2.9 %collective-permute-start.8 = (bf16[256,128]{1,0:T(8,128)(2,1)S(1)}, bf16[256,128]{1,0:T(8,128)(2,1)S(1)}, u32[]{:S(2)}, u32[]{:S(2)}) collective-permute-start(bf16[256,128]{1,0:T(8,128)(2,1)S(1)} %get-tuple-element.41), channel_id=1, source_target_pairs={{0,16},{4,20},{8,24},{12,28},{16,0},{20,4},{24,8},{28,12},{1,17},{... | collective-permute-start | bytes 196616 | tf_op jit(solution)/shard_map/ppermute | solution.py:101
  36.6 1.1 %collective-permute-start.9 = (bf16[256,128]{1,0:T(8,128)(2,1)S(1)}, bf16[256,128]{1,0:T(8,128)(2,1)S(1)}, u32[]{:S(2)}, u32[]{:S(2)}) collective-permute-start(bf16[256,128]{1,0:T(8,128)(2,1)S(1)} %get-tuple-element.42), channel_id=1, source_target_pairs={{0,20},{4,16},{8,28},{12,24},{16,4},{20,0},{24,12},{28,8},{1,21},{... | collective-permute-start | bytes 196616 | tf_op jit(solution)/shard_map/ppermute | solution.py:101
  37.7 4.6 %collective-permute-start.10 = (bf16[256,128]{1,0:T(8,128)(2,1)S(1)}, bf16[256,128]{1,0:T(8,128)(2,1)S(1)}, u32[]{:S(2)}, u32[]{:S(2)}) collective-permute-start(bf16[256,128]{1,0:T(8,128)(2,1)S(1)} %get-tuple-element.43), channel_id=1, source_target_pairs={{0,24},{4,28},{8,16},{12,20},{16,8},{20,12},{24,0},{28,4},{1,25},{... | collective-permute-start | bytes 196616 | tf_op jit(solution)/shard_map/ppermute | solution.py:101
  42.3 0.6 collective-permute-start.12
  42.9 1.5 %collective-permute-start.13 = (bf16[256,128]{1,0:T(8,128)(2,1)S(1)}, bf16[256,128]{1,0:T(8,128)(2,1)S(1)}, u32[]{:S(2)}, u32[]{:S(2)}) collective-permute-start(bf16[256,128]{1,0:T(8,128)(2,1)S(1)} %get-tuple-element.46), channel_id=1, source_target_pairs={{0,12},{4,8},{8,4},{12,0},{16,28},{20,24},{24,20},{28,16},{1,13},{... | collective-permute-start | bytes 196616 | tf_op jit(solution)/shard_map/ppermute | solution.py:101
  44.4 2.4 %collective-permute-done.9.refs_3_ = bf16[256,128]{1,0:T(8,128)(2,1)S(1)} collective-permute-done((bf16[256,128]{1,0:T(8,128)(2,1)S(1)}, bf16[256,128]{1,0:T(8,128)(2,1)S(1)}, u32[]{:S(2)}, u32[]{:S(2)}) %collective-permute-start.9) | collective-permute-done | bytes 65568 | tf_op jit(solution)/shard_map/ppermute | solution.py:101
  47.0 2.4 %collective-permute-done.12.refs_6_ = bf16[256,128]{1,0:T(8,128)(2,1)S(1)} collective-permute-done((bf16[256,128]{1,0:T(8,128)(2,1)S(1)}, bf16[256,128]{1,0:T(8,128)(2,1)S(1)}, u32[]{:S(2)}, u32[]{:S(2)}) %collective-permute-start.12) | collective-permute-done | bytes 65568 | tf_op jit(solution)/shard_map/ppermute | solution.py:101
  49.4 0.4 shard_map.86.gated_ref
  49.9 0.5 shard_map.91
  50.4 0.4 shard_map.89
  50.9 0.6 collective-permute-start.15
  51.4 0.7 %shard_map.88 = (f32[256,512]{1,0:T(8,128)S(1)}, f32[256,512]{1,0:T(8,128)S(1)}) custom-call(bf16[256,1024]{1,0:T(8,128)(2,1)S(1)} %shard_map.86.gated_ref, bf16[1024,4096]{1,0:T(8,128)(2,1)S(1)} %bitcast.2), custom_call_target="tpu_custom_call" | custom-call | flops 536870912 | bytes 2097152 | tf_op jit(solution)/shard_map/pallas_call | solution.py:305
  52.2 1.6 %collective-permute-start.18 = (bf16[256,512]{1,0:T(8,128)(2,1)S(1)}, bf16[256,512]{1,0:T(8,128)(2,1)S(1)}, u32[]{:S(2)}, u32[]{:S(2)}) collective-permute-start(bf16[256,512]{1,0:T(8,128)(2,1)S(1)} %shard_map.92), channel_id=1, source_target_pairs={{0,2},{2,0},{1,3},{3,1},{4,6},{6,4},{5,7},{7,5},{8,10},{10,8},{9,1... | collective-permute-start | bytes 786440 | tf_op jit(solution)/shard_map/ppermute | solution.py:409
  53.8 0.6 collective-permute-start.16
  54.4 1.2 %shard_map.87 = (bf16[256,1024]{1,0:T(8,128)(2,1)S(1)}, f32[256,1024]{1,0:T(8,128)S(1)}) custom-call(bf16[256,1024]{1,0:T(8,128)(2,1)S(1)} %shard_map.86.gated_ref, bf16[1024,4096]{1,0:T(8,128)(2,1)S(1)} %bitcast.2), custom_call_target="tpu_custom_call" | custom-call | flops 1073741824 | bytes 4194304 | tf_op jit(solution)/shard_map/pallas_call | solution.py:305
  55.7 5.7 %collective-permute-done.18.refs_1_ = bf16[256,512]{1,0:T(8,128)(2,1)S(1)} collective-permute-done((bf16[256,512]{1,0:T(8,128)(2,1)S(1)}, bf16[256,512]{1,0:T(8,128)(2,1)S(1)}, u32[]{:S(2)}, u32[]{:S(2)}) %collective-permute-start.18) | collective-permute-done | bytes 262176 | tf_op jit(solution)/shard_map/ppermute | solution.py:409
  61.4 4.7 %collective-permute-done.16.refs_0_ = bf16[256,512]{1,0:T(8,128)(2,1)S(1)} collective-permute-done((bf16[256,512]{1,0:T(8,128)(2,1)S(1)}, bf16[256,512]{1,0:T(8,128)(2,1)S(1)}, u32[]{:S(2)}, u32[]{:S(2)}) %collective-permute-start.16) | collective-permute-done | bytes 262176 | tf_op jit(solution)/shard_map/ppermute | solution.py:409
  66.1 1.0 %shard_map.94 = bf16[256,1024]{1,0:T(8,128)(2,1)} custom-call(f32[256,1024]{1,0:T(8,128)S(1)} %get-tuple-element.47.own_ref, bf16[256,1024]{1,0:T(8,128)(2,1)S(1)} %collective-permute-done.14.near_ref, bf16[256,512]{1,0:T(8,128)(2,1)S(1)} %collective-permute-done.16.refs_0_, bf16[256,512]{1,0:T(8,128)(2,1)S(1)} %collective-permute-done.18.refs_1_, ...), custom_call_target="tpu_custom_call" | custom-call | flops 262144 | bytes 2097152 | tf_op jit(solution)/shard_map/pallas_call | solution.py:363
  (32 shorter events, 0.8 us)
Async XLA Ops:
  0.0 49.4 %copy-start.1 = (bf16[256,1024]{1,0:T(8,128)(2,1)S(1)}, bf16[256,1024]{1,0:T(8,128)(2,1)}, u32[]{:S(2)}) copy-start(bf16[256,1024]{1,0:T(8,128)(2,1)} %values_ref.1) | copy-start | bytes 1572868
  0.0 49.4 %copy-start = (bf16[256,1024]{1,0:T(8,128)(2,1)S(1)}, bf16[256,1024]{1,0:T(8,128)(2,1)}, u32[]{:S(2)}) copy-start(bf16[256,1024]{1,0:T(8,128)(2,1)} %keys_ref.1) | copy-start | bytes 1572868
  0.0 49.4 %copy-start.3 = (f32[1024]{0:T(1024)S(1)}, f32[1024]{0:T(1024)}, u32[]{:S(2)}) copy-start(f32[1024]{0:T(1024)} %param.12) | copy-start | bytes 12292
  0.0 49.4 %copy-start.2 = (bf16[256,1024]{1,0:T(8,128)(2,1)S(1)}, bf16[256,1024]{1,0:T(8,128)(2,1)}, u32[]{:S(2)}) copy-start(bf16[256,1024]{1,0:T(8,128)(2,1)} %queries_ref.1) | copy-start | bytes 1572868
  0.0 49.8 %slice-start = ((s8[8388608]{0:T(1024)(128)(4,1)}), s8[4194304]{0:T(1024)(128)(4,1)S(1)}, s32[]{:S(2)}) async-start(s8[8388608]{0:T(1024)(128)(4,1)} %bitcast.1), calls=%async_computation | async-start | bytes 8388608
  1.4 14.1 %collective-permute-start = (bf16[256,256]{1,0:T(8,128)(2,1)S(1)}, bf16[256,256]{1,0:T(8,128)(2,1)S(1)}, u32[]{:S(2)}, u32[]{:S(2)}) collective-permute-start(bf16[256,256]{1,0:T(8,128)(2,1)S(1)} %get-tuple-element.29), channel_id=1, source_target_pairs={{0,16},{4,20},{8,24},{12,28},{16,0},{20,4},{24,8},{28,12},{1,17},{... | collective-permute-start | bytes 393224 | tf_op jit(solution)/shard_map/ppermute | solution.py:101
  5.5 13.0 %collective-permute-start.1 = (bf16[256,256]{1,0:T(8,128)(2,1)S(1)}, bf16[256,256]{1,0:T(8,128)(2,1)S(1)}, u32[]{:S(2)}, u32[]{:S(2)}) collective-permute-start(bf16[256,256]{1,0:T(8,128)(2,1)S(1)} %get-tuple-element.30), channel_id=1, source_target_pairs={{0,20},{4,16},{8,28},{12,24},{16,4},{20,0},{24,12},{28,8},{1,21},{... | collective-permute-start | bytes 393224 | tf_op jit(solution)/shard_map/ppermute | solution.py:101
  8.5 13.5 %collective-permute-start.2 = (bf16[256,256]{1,0:T(8,128)(2,1)S(1)}, bf16[256,256]{1,0:T(8,128)(2,1)S(1)}, u32[]{:S(2)}, u32[]{:S(2)}) collective-permute-start(bf16[256,256]{1,0:T(8,128)(2,1)S(1)} %get-tuple-element.31), channel_id=1, source_target_pairs={{0,4},{4,0},{8,12},{12,8},{16,20},{20,16},{24,28},{28,24},{1,5},{5... | collective-permute-start | bytes 393224 | tf_op jit(solution)/shard_map/ppermute | solution.py:101
  8.8 13.2 %collective-permute-start.3 = (bf16[256,256]{1,0:T(8,128)(2,1)S(1)}, bf16[256,256]{1,0:T(8,128)(2,1)S(1)}, u32[]{:S(2)}, u32[]{:S(2)}) collective-permute-start(bf16[256,256]{1,0:T(8,128)(2,1)S(1)} %get-tuple-element.32), channel_id=1, source_target_pairs={{0,8},{4,12},{8,0},{12,4},{16,24},{20,28},{24,16},{28,20},{1,9},{5... | collective-permute-start | bytes 393224 | tf_op jit(solution)/shard_map/ppermute | solution.py:101
  10.6 16.7 %collective-permute-start.4 = (bf16[256,256]{1,0:T(8,128)(2,1)S(1)}, bf16[256,256]{1,0:T(8,128)(2,1)S(1)}, u32[]{:S(2)}, u32[]{:S(2)}) collective-permute-start(bf16[256,256]{1,0:T(8,128)(2,1)S(1)} %get-tuple-element.33), channel_id=1, source_target_pairs={{0,12},{4,8},{8,4},{12,0},{16,28},{20,24},{24,20},{28,16},{1,13},{... | collective-permute-start | bytes 393224 | tf_op jit(solution)/shard_map/ppermute | solution.py:101
  15.4 14.3 %collective-permute-start.5 = (bf16[256,256]{1,0:T(8,128)(2,1)S(1)}, bf16[256,256]{1,0:T(8,128)(2,1)S(1)}, u32[]{:S(2)}, u32[]{:S(2)}) collective-permute-start(bf16[256,256]{1,0:T(8,128)(2,1)S(1)} %get-tuple-element.37), channel_id=1, source_target_pairs={{0,24},{4,28},{8,16},{12,20},{16,8},{20,12},{24,0},{28,4},{1,25},{... | collective-permute-start | bytes 393224 | tf_op jit(solution)/shard_map/ppermute | solution.py:101
  18.5 11.2 %collective-permute-start.6 = (bf16[256,256]{1,0:T(8,128)(2,1)S(1)}, bf16[256,256]{1,0:T(8,128)(2,1)S(1)}, u32[]{:S(2)}, u32[]{:S(2)}) collective-permute-start(bf16[256,256]{1,0:T(8,128)(2,1)S(1)} %get-tuple-element.38), channel_id=1, source_target_pairs={{0,28},{4,24},{8,20},{12,16},{16,12},{20,8},{24,4},{28,0},{1,29},{... | collective-permute-start | bytes 393224 | tf_op jit(solution)/shard_map/ppermute | solution.py:101
  29.8 20.1 %slice-start.1 = ((s8[8388608]{0:T(1024)(128)(4,1)}), s8[4194304]{0:T(1024)(128)(4,1)S(1)}, s32[]{:S(2)}) async-start(s8[8388608]{0:T(1024)(128)(4,1)} %bitcast.1), calls=%async_computation.1 | async-start | bytes 8388608
  33.2 9.1 %collective-permute-start.7 = (bf16[256,128]{1,0:T(8,128)(2,1)S(1)}, bf16[256,128]{1,0:T(8,128)(2,1)S(1)}, u32[]{:S(2)}, u32[]{:S(2)}) collective-permute-start(bf16[256,128]{1,0:T(8,128)(2,1)S(1)} %get-tuple-element.40), channel_id=1, source_target_pairs={{0,4},{4,0},{8,12},{12,8},{16,20},{20,16},{24,28},{28,24},{1,5},{5... | collective-permute-start | bytes 196616 | tf_op jit(solution)/shard_map/ppermute | solution.py:101
  33.7 9.2 %collective-permute-start.8 = (bf16[256,128]{1,0:T(8,128)(2,1)S(1)}, bf16[256,128]{1,0:T(8,128)(2,1)S(1)}, u32[]{:S(2)}, u32[]{:S(2)}) collective-permute-start(bf16[256,128]{1,0:T(8,128)(2,1)S(1)} %get-tuple-element.41), channel_id=1, source_target_pairs={{0,16},{4,20},{8,24},{12,28},{16,0},{20,4},{24,8},{28,12},{1,17},{... | collective-permute-start | bytes 196616 | tf_op jit(solution)/shard_map/ppermute | solution.py:101
  36.6 10.1 %collective-permute-start.9 = (bf16[256,128]{1,0:T(8,128)(2,1)S(1)}, bf16[256,128]{1,0:T(8,128)(2,1)S(1)}, u32[]{:S(2)}, u32[]{:S(2)}) collective-permute-start(bf16[256,128]{1,0:T(8,128)(2,1)S(1)} %get-tuple-element.42), channel_id=1, source_target_pairs={{0,20},{4,16},{8,28},{12,24},{16,4},{20,0},{24,12},{28,8},{1,21},{... | collective-permute-start | bytes 196616 | tf_op jit(solution)/shard_map/ppermute | solution.py:101
  37.7 9.0 %collective-permute-start.10 = (bf16[256,128]{1,0:T(8,128)(2,1)S(1)}, bf16[256,128]{1,0:T(8,128)(2,1)S(1)}, u32[]{:S(2)}, u32[]{:S(2)}) collective-permute-start(bf16[256,128]{1,0:T(8,128)(2,1)S(1)} %get-tuple-element.43), channel_id=1, source_target_pairs={{0,24},{4,28},{8,16},{12,20},{16,8},{20,12},{24,0},{28,4},{1,25},{... | collective-permute-start | bytes 196616 | tf_op jit(solution)/shard_map/ppermute | solution.py:101
  42.3 4.7 %collective-permute-start.11 = (bf16[256,128]{1,0:T(8,128)(2,1)S(1)}, bf16[256,128]{1,0:T(8,128)(2,1)S(1)}, u32[]{:S(2)}, u32[]{:S(2)}) collective-permute-start(bf16[256,128]{1,0:T(8,128)(2,1)S(1)} %get-tuple-element.44), channel_id=1, source_target_pairs={{0,8},{4,12},{8,0},{12,4},{16,24},{20,28},{24,16},{28,20},{1,9},{5... | collective-permute-start | bytes 196616 | tf_op jit(solution)/shard_map/ppermute | solution.py:101
  42.3 7.1 %collective-permute-start.12 = (bf16[256,128]{1,0:T(8,128)(2,1)S(1)}, bf16[256,128]{1,0:T(8,128)(2,1)S(1)}, u32[]{:S(2)}, u32[]{:S(2)}) collective-permute-start(bf16[256,128]{1,0:T(8,128)(2,1)S(1)} %get-tuple-element.45), channel_id=1, source_target_pairs={{0,28},{4,24},{8,20},{12,16},{16,12},{20,8},{24,4},{28,0},{1,29},{... | collective-permute-start | bytes 196616 | tf_op jit(solution)/shard_map/ppermute | solution.py:101
  42.9 6.5 %collective-permute-start.13 = (bf16[256,128]{1,0:T(8,128)(2,1)S(1)}, bf16[256,128]{1,0:T(8,128)(2,1)S(1)}, u32[]{:S(2)}, u32[]{:S(2)}) collective-permute-start(bf16[256,128]{1,0:T(8,128)(2,1)S(1)} %get-tuple-element.46), channel_id=1, source_target_pairs={{0,12},{4,8},{8,4},{12,0},{16,28},{20,24},{24,20},{28,16},{1,13},{... | collective-permute-start | bytes 196616 | tf_op jit(solution)/shard_map/ppermute | solution.py:101
  50.3 1.8 %collective-permute-start.17 = (bf16[256,512]{1,0:T(8,128)(2,1)S(1)}, bf16[256,512]{1,0:T(8,128)(2,1)S(1)}, u32[]{:S(2)}, u32[]{:S(2)}) collective-permute-start(bf16[256,512]{1,0:T(8,128)(2,1)S(1)} %shard_map.91), channel_id=1, source_target_pairs={{0,1},{1,0},{2,3},{3,2},{4,5},{5,4},{6,7},{7,6},{8,9},{9,8},{10,11... | collective-permute-start | bytes 786440 | tf_op jit(solution)/shard_map/ppermute | solution.py:406
  50.9 2.9 %collective-permute-start.15 = (bf16[256,512]{1,0:T(8,128)(2,1)S(1)}, bf16[256,512]{1,0:T(8,128)(2,1)S(1)}, u32[]{:S(2)}, u32[]{:S(2)}) collective-permute-start(bf16[256,512]{1,0:T(8,128)(2,1)S(1)} %shard_map.89), channel_id=1, source_target_pairs={{0,1},{1,0},{2,3},{3,2},{4,5},{5,4},{6,7},{7,6},{8,9},{9,8},{10,11... | collective-permute-start | bytes 786440 | tf_op jit(solution)/shard_map/ppermute | solution.py:406
  52.2 9.2 %collective-permute-start.18 = (bf16[256,512]{1,0:T(8,128)(2,1)S(1)}, bf16[256,512]{1,0:T(8,128)(2,1)S(1)}, u32[]{:S(2)}, u32[]{:S(2)}) collective-permute-start(bf16[256,512]{1,0:T(8,128)(2,1)S(1)} %shard_map.92), channel_id=1, source_target_pairs={{0,2},{2,0},{1,3},{3,1},{4,6},{6,4},{5,7},{7,5},{8,10},{10,8},{9,1... | collective-permute-start | bytes 786440 | tf_op jit(solution)/shard_map/ppermute | solution.py:409
  53.8 12.3 %collective-permute-start.16 = (bf16[256,512]{1,0:T(8,128)(2,1)S(1)}, bf16[256,512]{1,0:T(8,128)(2,1)S(1)}, u32[]{:S(2)}, u32[]{:S(2)}) collective-permute-start(bf16[256,512]{1,0:T(8,128)(2,1)S(1)} %shard_map.90), channel_id=1, source_target_pairs={{0,2},{2,0},{1,3},{3,1},{4,6},{6,4},{5,7},{7,5},{8,10},{10,8},{9,1... | collective-permute-start | bytes 786440 | tf_op jit(solution)/shard_map/ppermute | solution.py:409
  55.7 10.5 %collective-permute-start.14 = (bf16[256,1024]{1,0:T(8,128)(2,1)S(1)}, bf16[256,1024]{1,0:T(8,128)(2,1)S(1)}, u32[]{:S(2)}, u32[]{:S(2)}) collective-permute-start(bf16[256,1024]{1,0:T(8,128)(2,1)S(1)} %get-tuple-element.48), channel_id=1, source_target_pairs={{0,1},{1,0},{2,3},{3,2},{4,5},{5,4},{6,7},{7,6},{8,9},{9,8},{10,11... | collective-permute-start | bytes 1572872 | tf_op jit(solution)/shard_map/ppermute | solution.py:412

commit v4 on v2

--- a/solution.py
+++ b/solution.py
@@ -14,6 +14,7 @@
 CONV_VMEM = 24 * 2**20
 PROJECT_VMEM = 24 * 2**20
 SMALL_VMEM = 12 * 2**20
+STEP = 16
 
 
 def split_bf16(table):
@@ -111,18 +112,58 @@
     return jnp.dot(table, jnp.concatenate([block, block], axis=0), preferred_element_type=F32)
 
 
+def times(a, b):
+    return a[0] * b[0] - a[1] * b[1], a[0] * b[1] + a[1] * b[0]
+
+
+def plus(a, b):
+    return b if a is None else (a[0] + b[0], a[1] + b[1])
+
+
+def late_place(n_blocks):
+    return lax.div(peer_of(slots_of(n_blocks, False)[-1]), 2)
+
+
+def load(ref, at, row, step, rows, lanes):
+    return tuple(ref[(*at, pl.ds(row + part * rows, step), lanes)] for part in range(2))
+
+
+def mix_early(pair, step, spec_ref, part_ref):
+    n_blocks, rows, chans = spec_ref.shape[0], spec_ref.shape[1] // 2, spec_ref.shape[2] // 2
+    early = [j for j in range(n_blocks) if j // 2 != pair]
+
+    @pl.loop(0, rows // step)
+    def _(t):
+        row = pl.multiple_of(t * step, step)
+        signal = {j: load(spec_ref, (j,), row, step, rows, slice(0, chans)) for j in early}
+        filt = {j: load(spec_ref, (j,), row, step, rows, slice(chans, 2 * chans)) for j in early}
+        for i in range(n_blocks):
+            total = None
+            for d in early:
+                if i - d in early:
+                    total = plus(total, times(filt[d], signal[i - d]))
+            if total is None:
+                total = (jnp.zeros((step, chans), F32),) * 2
+            for part in range(2):
+                part_ref[i, pl.ds(row + part * rows, step)] = total[part]
+
+
 def spectra_kernel(n_peers, fwd_hbm, bwd_hbm, *refs):
-    *in_refs, fwd_ref, bwd_ref, spec_ref, sem = refs
+    *in_refs, fwd_ref, bwd_ref, spec_ref, part_ref, sem = refs
     copies = [
         pltpu.make_async_copy(fwd_hbm, fwd_ref, sem.at[0]),
         pltpu.make_async_copy(bwd_hbm, bwd_ref, sem.at[1]),
     ]
     for copy in copies:
         copy.start()
-    for copy in copies:
-        copy.wait()
+    copies[0].wait()
     for slot, in_ref in zip(slots_of(n_peers, False), in_refs):
         spec_ref[peer_of(slot)] = block_spectrum(fwd_ref[...], in_ref[...])
+    for pair in range(n_peers // 2):
+        pl.when(late_place(n_peers) == pair)(
+            functools.partial(mix_early, pair, STEP, spec_ref, part_ref)
+        )
+    copies[1].wait()
 
 
 def spectra(received, fwd, bwd, n_peers):
@@ -132,11 +173,12 @@
     return pl.pallas_call(
         functools.partial(spectra_kernel, n_peers),
         in_specs=[pl.BlockSpec(memory_space=pltpu.HBM)] * 2 + [whole] * len(received),
-        out_specs=[whole] * 3,
+        out_specs=[whole] * 4,
         out_shape=[
             jax.ShapeDtypeStruct(fwd.shape, BF16),
             jax.ShapeDtypeStruct(bwd.shape, BF16),
             jax.ShapeDtypeStruct((n_peers, 2 * rows, width), F32),
+            jax.ShapeDtypeStruct((n_peers, 2 * rows, width // 2), F32),
         ],
         scratch_shapes=[pltpu.SemaphoreType.DMA((2,))],
         compiler_params=pltpu.CompilerParams(vmem_limit_bytes=CONV_VMEM),
@@ -146,57 +188,61 @@
     )(*args, *received)
 
 
-def conv_kernel(fwd_ref, bwd_ref, early_ref, *refs):
-    *refs, late, held, turned = refs
-    n_blocks, step = early_ref.shape[0], held.shape[2]
+def mix_late(pair, step, first, last, sign, spec_ref, part_ref, late_ref, turned):
+    n_blocks, rows, chans = spec_ref.shape[0], spec_ref.shape[1] // 2, spec_ref.shape[2] // 2
+    early = [j for j in range(n_blocks) if j // 2 != pair]
+    x_at, f_at = slice(0, chans), slice(chans, 2 * chans)
+
+    @pl.loop(first // step, last // step)
+    def _(t):
+        row = pl.multiple_of(t * step, step)
+        late = [2 * pair, 2 * pair + 1]
+        signal = {j: load(late_ref, (j % 2,), row, step, rows, x_at) for j in late}
+        filt = {j: load(late_ref, (j % 2,), row, step, rows, f_at) for j in late}
+        total = [load(part_ref, (i,), row, step, rows, slice(0, chans)) for i in range(n_blocks)]
+        for b in early:
+            if b + late[0] >= n_blocks:
+                continue
+            x_b = load(spec_ref, (b,), row, step, rows, x_at)
+            f_b = load(spec_ref, (b,), row, step, rows, f_at)
+            for j in late:
+                if b + j < n_blocks:
+                    total[b + j] = plus(total[b + j], times(filt[j], x_b))
+                    total[b + j] = plus(total[b + j], times(f_b, signal[j]))
+        for j in late:
+            for d in late:
+                if j + d < n_blocks:
+                    total[j + d] = plus(total[j + d], times(filt[d], signal[j]))
+        for i in range(n_blocks):
+            value = total[i]
+            if i > 0:
+                turn_re, turn_im = total[i - 1]
+                if sign > 0:
+                    value = value[0] - turn_im, value[1] + turn_re
+                else:
+                    value = value[0] + turn_im, value[1] - turn_re
+            lanes = slice(i % 2 * chans, (i % 2 + 1) * chans)
+            for part in range(2):
+                high = value[part].astype(BF16)
+                low = (value[part] - high.astype(F32)).astype(BF16)
+                for c, piece in enumerate((high, high, low)):
+                    turned[i // 2, pl.ds(row + (2 * c + part) * rows, step), lanes] = piece
+
+
+def conv_kernel(fwd_ref, bwd_ref, spec_ref, part_ref, *refs):
+    *refs, late_ref, turned = refs
+    n_blocks = spec_ref.shape[0]
     in_refs, out_refs = refs[:-n_blocks], refs[-n_blocks:]
     rows, chans = in_refs[0].shape[0], in_refs[0].shape[1] // 2
-    late_slots = slots_of(n_blocks, False)[-2:]
-    for slot, in_ref in zip(late_slots, in_refs):
-        late[lax.bitwise_and(peer_of(slot), 1)] = block_spectrum(fwd_ref[...], in_ref[...])
-    late_pair = lax.div(peer_of(late_slots[0]), 2)
-
-    def spectrum(j, at, lanes):
-        return jnp.where(late_pair == j // 2, late[j % 2, at, lanes], early_ref[j, at, lanes])
-
-    def mix(row, sign):
-        re, im = pl.ds(row, step), pl.ds(row + rows, step)
-        x_at, f_at = slice(0, chans), slice(chans, 2 * chans)
-        gains = []
-        last_re = last_im = None
-        for j in range(n_blocks):
-            held[j, 0] = spectrum(j, re, x_at)
-            held[j, 1] = spectrum(j, im, x_at)
-            f_re, f_im = spectrum(j, re, f_at), spectrum(j, im, f_at)
-            if j == 0:
-                gains.append((f_re, f_im))
-            else:
-                gains.append((f_re - sign * last_im, f_im + sign * last_re))
-            last_re, last_im = f_re, f_im
-        for i in range(n_blocks):
-            out_re = out_im = None
-            for d in range(i + 1):
-                (g_re, g_im), x_re, x_im = gains[d], held[i - d, 0], held[i - d, 1]
-                t_re = g_re * x_re - g_im * x_im
-                t_im = g_re * x_im + g_im * x_re
-                out_re = t_re if d == 0 else out_re + t_re
-                out_im = t_im if d == 0 else out_im + t_im
-            lanes = slice(i % 2 * chans, (i % 2 + 1) * chans)
-            for first, value in ((row, out_re), (row + rows, out_im)):
-                high = value.astype(BF16)
-                low = (value - high.astype(F32)).astype(BF16)
-                for part, piece in enumerate((high, high, low)):
-                    turned[i // 2, pl.ds(first + 2 * part * rows, step), lanes] = piece
-
-    half = rows // 2
-
-    @pl.loop(0, half // step)
-    def _(t):
-        mix(pl.multiple_of(t * step, step), 1.0)
-
-    @pl.loop(half // step, rows // step)
-    def _(t):
-        mix(pl.multiple_of(t * step, step), -1.0)
+    for slot, in_ref in zip(slots_of(n_blocks, False)[-2:], in_refs):
+        late_ref[lax.bitwise_and(peer_of(slot), 1)] = block_spectrum(fwd_ref[...], in_ref[...])
+
+    def mix(pair):
+        for first, last, sign in ((0, rows // 2, 1), (rows // 2, rows, -1)):
+            mix_late(pair, STEP, first, last, sign, spec_ref, part_ref, late_ref, turned)
+
+    for pair in range(n_blocks // 2):
+        pl.when(late_place(n_blocks) == pair)(functools.partial(mix, pair))
 
     odd = lax.bitwise_and(lax.axis_index("seq"), 1) == 1
     by_slot = dict(zip(slots_of(n_blocks, True), out_refs))
@@ -208,26 +254,24 @@
         by_slot[slot + 1][...] = jnp.where(odd, left, right).astype(BF16)
 
 
-def conv_fast(early, late, fwd, bwd):
+def conv_fast(early, part, late, fwd, bwd):
     n_blocks = early.shape[0]
     rows, chans = late[0].shape[0], late[0].shape[1] // 2
-    step = 16
     whole = pl.BlockSpec(memory_space=pltpu.VMEM)
     return pl.pallas_call(
         conv_kernel,
-        in_specs=[whole] * 5,
+        in_specs=[whole] * 6,
         out_specs=[whole] * n_blocks,
         out_shape=[jax.ShapeDtypeStruct((rows, chans), BF16)] * n_blocks,
         scratch_shapes=[
             pltpu.VMEM((2, 2 * rows, 2 * chans), F32),
-            pltpu.VMEM((n_blocks, 2, step, chans), F32),
             pltpu.VMEM((n_blocks // 2, 6 * rows, 2 * chans), BF16),
         ],
         compiler_params=pltpu.CompilerParams(vmem_limit_bytes=CONV_VMEM),
         cost_estimate=pl.CostEstimate(
             flops=16 * n_blocks * rows * rows * chans, bytes_accessed=4 * 2**20, transcendentals=0
         ),
-    )(fwd, bwd, early, *late)
+    )(fwd, bwd, early, part, *late)
 
 
 def conv_plain(received, fwd, bwd):
@@ -262,42 +306,134 @@
     return jnp.einsum("tk,jkc->jtc", bwd32, both, precision=exact).astype(BF16)
 
 
-def gate_kernel(queries_ref, keys_ref, values_ref, skip_ref, *refs):
-    *conv_refs, out_ref = refs
-    chans = conv_refs[0].shape[1]
-    for slot, conv_ref in zip(slots_of(len(conv_refs), True), conv_refs):
-        at = peer_block(slot, chans)
-        product = keys_ref[:, at].astype(F32) * values_ref[:, at].astype(F32)
-        mixed = conv_ref[...].astype(F32) + skip_ref[:, at] * product
-        out_ref[:, at] = (queries_ref[:, at].astype(F32) * mixed).astype(BF16)
-
-
-def gate(queries, keys, values, skip, conv):
-    rows, width = queries.shape
-    whole = pl.BlockSpec(memory_space=pltpu.VMEM)
-    return pl.pallas_call(
-        gate_kernel,
-        in_specs=[whole] * (4 + len(conv)),
-        out_specs=whole,
-        out_shape=jax.ShapeDtypeStruct((rows, width), BF16),
-        compiler_params=pltpu.CompilerParams(vmem_limit_bytes=SMALL_VMEM),
-        cost_estimate=pl.CostEstimate(
-            flops=4 * rows * width, bytes_accessed=10 * rows * width, transcendentals=0
-        ),
-    )(queries, keys, values, skip, *conv)
-
-
-def weight_block(weight_ref, other, across, piece, pieces):
-    width = weight_ref.shape[1] // 4 // pieces
+def columns_of(other, across, piece, pieces, width):
+    count = width // 4 // pieces
     place = lax.axis_index("fsdp")
     core, side = lax.rem(place, 2), lax.div(place, 2)
     block = 2 * (1 - side if across else side) + (1 - core if other else core)
-    return weight_ref[:, pl.ds(pl.multiple_of((block * pieces + piece) * width, width), width)]
+    return pl.ds(pl.multiple_of((block * pieces + piece) * count, count), count)
+
+
+def gate_slot(slot, queries_ref, keys_ref, values_ref, skip_ref, conv_ref):
+    at = peer_block(slot, conv_ref.shape[1])
+    product = keys_ref[:, at].astype(F32) * values_ref[:, at].astype(F32)
+    mixed = conv_ref[...].astype(F32) + skip_ref[:, at] * product
+    return (queries_ref[:, at].astype(F32) * mixed).astype(BF16)
+
+
+def gate_early_kernel(n_peers, queries_ref, keys_ref, values_ref, skip_ref, weight_ref, *refs):
+    conv_refs, (gated_ref, *part_refs) = refs[:-3], refs[-3:]
+    chans = conv_refs[0].shape[1]
+    slots = slots_of(n_peers, True)
+    for slot, conv_ref in zip(slots, conv_refs):
+        gated = gate_slot(slot, queries_ref, keys_ref, values_ref, skip_ref, conv_ref)
+        gated_ref[:, peer_block(slot, chans)] = gated
+    for slot in slots[len(conv_refs) :]:
+        gated_ref[:, peer_block(slot, chans)] = jnp.zeros((gated_ref.shape[0], chans), BF16)
+    for other, part_ref in zip((True, False), part_refs):
+        columns = weight_ref[:, columns_of(other, True, 0, 1, weight_ref.shape[1])]
+        part_ref[...] = jnp.dot(gated_ref[...], columns, preferred_element_type=F32)
+
+
+def gate_early(queries, keys, values, skip, weight, conv, n_peers):
+    rows, width = queries.shape
+    out_width = weight.shape[1] // 4
+    whole = pl.BlockSpec(memory_space=pltpu.VMEM)
+    return pl.pallas_call(
+        functools.partial(gate_early_kernel, n_peers),
+        in_specs=[whole] * (5 + len(conv)),
+        out_specs=[whole] * 3,
+        out_shape=[jax.ShapeDtypeStruct((rows, width), BF16)]
+        + [jax.ShapeDtypeStruct((rows, out_width), F32)] * 2,
+        compiler_params=pltpu.CompilerParams(vmem_limit_bytes=PROJECT_VMEM),
+        cost_estimate=pl.CostEstimate(
+            flops=4 * rows * width * out_width, bytes_accessed=10 * rows * width, transcendentals=0
+        ),
+    )(queries, keys, values, skip, weight, *conv)
+
+
+def late_product(late, late_slots, block, weight_ref, part_ref):
+    chans = late.shape[1] // len(late_slots)
+    at = columns_of(*block, weight_ref.shape[1])
+    _, _, piece, pieces = block
+    count = part_ref.shape[1] // pieces
+    columns = jnp.concatenate([weight_ref[peer_block(s, chans), at] for s in late_slots], axis=0)
+    part = part_ref[:, piece * count : (piece + 1) * count]
+    return part + jnp.dot(late, columns, preferred_element_type=F32)
+
+
+def gate_late_kernel(late_slots, block, queries_ref, keys_ref, values_ref, skip_ref, weight_ref, part_ref, *refs):
+    *conv_refs, late_ref, sent_ref = refs
+    chans = conv_refs[0].shape[1]
+    for c, (slot, conv_ref) in enumerate(zip(late_slots, conv_refs)):
+        gated = gate_slot(slot, queries_ref, keys_ref, values_ref, skip_ref, conv_ref)
+        late_ref[:, c * chans : (c + 1) * chans] = gated
+    total = late_product(late_ref[...], late_slots, block, weight_ref, part_ref)
+    sent_ref[...] = total.astype(BF16)
+
+
+def gate_late(queries, keys, values, skip, weight, part, conv, late_slots, block):
+    rows, chans = conv[0].shape
+    whole = pl.BlockSpec(memory_space=pltpu.VMEM)
+    return pl.pallas_call(
+        functools.partial(gate_late_kernel, late_slots, block),
+        in_specs=[whole] * (6 + len(conv)),
+        out_specs=[whole] * 2,
+        out_shape=[
+            jax.ShapeDtypeStruct((rows, chans * len(conv)), BF16),
+            jax.ShapeDtypeStruct((rows, weight.shape[1] // 4 // block[-1]), BF16),
+        ],
+        compiler_params=pltpu.CompilerParams(vmem_limit_bytes=PROJECT_VMEM),
+        cost_estimate=pl.CostEstimate(
+            flops=rows * chans * weight.shape[1], bytes_accessed=2**20, transcendentals=0
+        ),
+    )(queries, keys, values, skip, weight, part, *conv)
+
+
+def late_project_kernel(late_slots, blocks, weight_ref, late_ref, part_ref, *out_refs):
+    for block, out_ref in zip(blocks, out_refs):
+        total = late_product(late_ref[...], late_slots, block, weight_ref, part_ref)
+        out_ref[...] = total.astype(out_ref.dtype)
+
+
+def late_project(weight, late, part, late_slots, blocks, dtype):
+    rows, depth = late.shape
+    widths = [weight.shape[1] // 4 // pieces for *_, pieces in blocks]
+    whole = pl.BlockSpec(memory_space=pltpu.VMEM)
+    return pl.pallas_call(
+        functools.partial(late_project_kernel, late_slots, blocks),
+        in_specs=[whole] * 3,
+        out_specs=[whole] * len(blocks),
+        out_shape=[jax.ShapeDtypeStruct((rows, w), dtype) for w in widths],
+        compiler_params=pltpu.CompilerParams(vmem_limit_bytes=PROJECT_VMEM),
+        cost_estimate=pl.CostEstimate(
+            flops=2 * rows * depth * sum(widths), bytes_accessed=2**20, transcendentals=0
+        ),
+    )(weight, late, part)
+
+
+def assemble_kernel(late_slots, gated_ref, late_ref, out_ref):
+    chans = late_ref.shape[1] // len(late_slots)
+    out_ref[...] = gated_ref[...]
+    for c, slot in enumerate(late_slots):
+        out_ref[:, peer_block(slot, chans)] = late_ref[:, c * chans : (c + 1) * chans]
+
+
+def assemble(gated, late, late_slots):
+    whole = pl.BlockSpec(memory_space=pltpu.VMEM)
+    return pl.pallas_call(
+        functools.partial(assemble_kernel, late_slots),
+        in_specs=[whole] * 2,
+        out_specs=whole,
+        out_shape=jax.ShapeDtypeStruct(gated.shape, BF16),
+        compiler_params=pltpu.CompilerParams(vmem_limit_bytes=SMALL_VMEM),
+        cost_estimate=pl.CostEstimate(flops=1000, bytes_accessed=2**20, transcendentals=0),
+    )(gated, late)
 
 
 def project_kernel(blocks, gated_ref, weight_ref, *out_refs):
     for block, out_ref in zip(blocks, out_refs):
-        columns = weight_block(weight_ref, *block)
+        columns = weight_ref[:, columns_of(*block, weight_ref.shape[1])]
         total = jnp.dot(gated_ref[...], columns, preferred_element_type=F32)
         out_ref[...] = total.astype(out_ref.dtype)
 
@@ -353,22 +489,32 @@
 
 
 def finish_kernel(own_ref, near_ref, *refs):
-    *arrived_refs, _, out_ref = refs
+    *arrived_refs, _, out_ref, stage, sem = refs
     width = out_ref.shape[1] // len(arrived_refs)
-    for c, arrived_ref in enumerate(arrived_refs):
-        at = slice(c * width, (c + 1) * width)
-        total = own_ref[:, at] + near_ref[:, at].astype(F32) + arrived_ref[...].astype(F32)
-        out_ref[:, at] = total.astype(out_ref.dtype)
+    steps = sem.shape[0]
+    rows = out_ref.shape[0] // steps
+    copies = []
+    for step in range(steps):
+        part = pl.ds(step * rows, rows)
+        for c, arrived_ref in enumerate(arrived_refs):
+            at = slice(c * width, (c + 1) * width)
+            total = own_ref[part, at] + near_ref[part, at].astype(F32)
+            stage[part, at] = (total + arrived_ref[part].astype(F32)).astype(stage.dtype)
+        copies.append(pltpu.make_async_copy(stage.at[part], out_ref.at[part], sem.at[step]))
+        copies[-1].start()
+    for copy in copies:
+        copy.wait()
 
 
 def finish(own, near, arrived):
     rows, width = own.shape
-    whole = pl.BlockSpec(memory_space=pltpu.VMEM)
+    whole, anywhere = pl.BlockSpec(memory_space=pltpu.VMEM), pl.BlockSpec(memory_space=pl.ANY)
     return pl.pallas_call(
         finish_kernel,
-        in_specs=[whole] * (2 + len(arrived)) + [pl.BlockSpec(memory_space=pl.ANY)],
-        out_specs=whole,
+        in_specs=[whole] * (2 + len(arrived)) + [anywhere],
+        out_specs=anywhere,
         out_shape=jax.ShapeDtypeStruct((rows, width), BF16),
+        scratch_shapes=[pltpu.VMEM((rows, width), BF16), pltpu.SemaphoreType.DMA((4,))],
         compiler_params=pltpu.CompilerParams(vmem_limit_bytes=SMALL_VMEM),
         cost_estimate=pl.CostEstimate(
             flops=rows * width, bytes_accessed=8 * rows * width, transcendentals=0
@@ -385,12 +531,27 @@
     in_chip = [(0, 1), (1, 0), (2, 3), (3, 2)]
     across = [(0, 2), (2, 0), (1, 3), (3, 1)]
 
+    sends = [(True, True, c, pieces) for c in range(pieces)]
+    keeps = [(False, True, c, pieces) for c in range(pieces)]
+
     if chans % 128 == 0 and n_peers == 8:
         blocks = pre(keys, values, filters, n_peers)
         received = exchange(blocks, n_peers, False)
-        fwd, bwd, early = spectra(received[:-2], fwd, bwd, n_peers)
-        back = exchange(conv_fast(early, received[-2:], fwd, bwd), n_peers, True)
-        gated = gate(queries, keys, values, skip, back)
+        fwd, bwd, early, part = spectra(received[:-2], fwd, bwd, n_peers)
+        back = exchange(conv_fast(early, part, received[-2:], fwd, bwd), n_peers, True)
+        slots = slots_of(n_peers, True)[-2:]
+        gated, send_part, own_part = gate_early(
+            queries, keys, values, skip, out_weight, back[:-2], n_peers
+        )
+        late, last = gate_late(
+            queries, keys, values, skip, out_weight, send_part, back[-2:], slots, sends[-1]
+        )
+        sent = [
+            *(late_project(out_weight, late, send_part, slots, [s], BF16)[0] for s in sends[:-1]),
+            last,
+        ]
+        ours = late_project(out_weight, late, own_part, slots, keeps, F32)
+        gated = assemble(gated, late, slots)
     else:
         product = keys.astype(F32) * values.astype(F32)
         parts = [a.astype(BF16).reshape(rows, n_peers, chans) for a in (product, filters)]
@@ -400,13 +561,10 @@
         back = lax.all_to_all(conv, "seq", split_axis=0, concat_axis=0, tiled=True)
         mixed = back.transpose(1, 0, 2).reshape(rows, width).astype(F32) + skip * product
         gated = (queries.astype(F32) * mixed).astype(BF16)
-
-    theirs = []
-    for c in range(pieces):
-        (sent,) = project(gated, out_weight, [(True, True, c, pieces)], [BF16])
-        theirs.append(lax.ppermute(sent, "fsdp", in_chip))
-    blocks = [(False, True, c, pieces) for c in range(pieces)]
-    ours = project(gated, out_weight, blocks, [F32] * pieces)
+        sent = project(gated, out_weight, sends, [BF16] * pieces)
+        ours = project(gated, out_weight, keeps, [F32] * pieces)
+
+    theirs = [lax.ppermute(piece, "fsdp", in_chip) for piece in sent]
     arrived = [lax.ppermute(add(*pair), "fsdp", across) for pair in zip(ours, theirs)]
     blocks = [(True, False, 0, 1), (False, False, 0, 1)]
     sent, own = project(gated, out_weight, blocks, [BF16, F32])

time: 67.7 us -> 65.4 us (0.966)
  waiting for transfers between devices: 23 us -> 20 us
    ppermute x14, waiting for transfers between devices: 12.6 us -> 9.24 us  [exchange(): lax.ppermute(block, 'seq', [(i, i ^ slot) for i in range(n_peers)])]
    pallas_call x4 -> x1, Pallas kernels: 2.85 us -> 1.29 us  [project(): pl.pallas_call(functools.partial(project_kernel, blocks), in_specs=[whole...]
    pallas_call x1, Pallas kernels: 2.4 us -> 3.37 us  [spectra(): pl.pallas_call(functools.partial(spectra_kernel, n_peers), in_specs=[pl.B...]
    pallas_call x3 -> x7, Pallas kernels: 4.88 us -> 5.77 us  [the longest x1 2.26 us: conv_fast(): pl.pallas_call(conv_kernel, in_specs=[whole] * 6, out_specs=[whole] * n_b...]
  transfers between devices with their start and end apart: 19 -> 19, of which waited for: 10 -> 10; matrix products, arithmetic and copies ran while one was open for 0% -> 0% of each run, Pallas kernels for 7% -> 11%
where the time goes in v4:
time: 65.4 us; the launch traced here: 65.2 us
  starting transfers between devices  32.7 us (50%)
  waiting for transfers between devices  20 us (31%)
  Pallas kernels  12.3 us (19%)
    ppermute x14, starting transfers between devices, exchange(): lax.ppermute(block, 'seq', [(i, i ^ slot) for i in range(n_peers)])  29.9 us
    ppermute x2, waiting for transfers between devices, body(): lax.ppermute(add(*pair), 'fsdp', across)  10.4 us
    ppermute x14, waiting for transfers between devices, exchange(): lax.ppermute(block, 'seq', [(i, i ^ slot) for i in range(n_peers)])  9.24 us
    pallas_call x1, Pallas kernels, spectra(): pl.pallas_call(functools.partial(spectra_kernel, n_peers), in_specs=[pl.B...  3.37 us
    pallas_call x1, Pallas kernels, conv_fast(): pl.pallas_call(conv_kernel, in_specs=[whole] * 6, out_specs=[whole] * n_b...  2.26 us
    ppermute x2, starting transfers between devices, body(): lax.ppermute(add(*pair), 'fsdp', across)  2.16 us
    pallas_call x1, Pallas kernels, pre(): pl.pallas_call(functools.partial(pre_kernel, n_peers), in_specs=[pl.Block...  1.77 us
    pallas_call x1, Pallas kernels, gate_early(): pl.pallas_call(functools.partial(gate_early_kernel, n_peers), in_specs=[w...  1.73 us
  transfers between devices with their start and end apart: 19, of which 10 were waited for; matrix products, arithmetic and copies ran while one was open for 0% of the time, Pallas kernels for 11%

profile of v4, /device:TPU:0, one launch (start us, length us, event | category | flops | bytes accessed | tf_op | source)
XLA Modules:
  0.0 65.2 jit_solution(10472431700520531558)
XLA Ops:
  0.0 1.8 %shard_map.82 = (bf16[256,256]{1,0:T(8,128)(2,1)S(1)}, bf16[256,256]{1,0:T(8,128)(2,1)S(1)}, bf16[256,256]{1,0:T(8,128)(2,1)S(1)}, bf16[256,256]{1,0:T(8,128)(2,...) custom-call(bf16[256,1024]{1,0:T(8,128)(2,1)} %keys_ref.3, ...), custom_call_target="tpu_custom_call" | custom-call | flops 262144 | bytes 3145728 | tf_op jit(solution)/shard_map/pallas_call | solution.py:78
  1.8 3.0 %collective-permute-start = (bf16[256,256]{1,0:T(8,128)(2,1)S(1)}, bf16[256,256]{1,0:T(8,128)(2,1)S(1)}, u32[]{:S(2)}, u32[]{:S(2)}) collective-permute-start(bf16[256,256]{1,0:T(8,128)(2,1)S(1)} %get-tuple-element.35), channel_id=1, source_target_pairs={{0,4},{4,0},{8,12},{12,8},{16,20},{20,16},{24,28},{28,24},{1,5},{5... | collective-permute-start | bytes 393224 | tf_op jit(solution)/shard_map/ppermute | solution.py:106
  4.8 2.6 %collective-permute-start.1 = (bf16[256,256]{1,0:T(8,128)(2,1)S(1)}, bf16[256,256]{1,0:T(8,128)(2,1)S(1)}, u32[]{:S(2)}, u32[]{:S(2)}) collective-permute-start(bf16[256,256]{1,0:T(8,128)(2,1)S(1)} %get-tuple-element.36), channel_id=1, source_target_pairs={{0,16},{4,20},{8,24},{12,28},{16,0},{20,4},{24,8},{28,12},{1,17},{... | collective-permute-start | bytes 393224 | tf_op jit(solution)/shard_map/ppermute | solution.py:106
  7.4 1.6 %collective-permute-start.2 = (bf16[256,256]{1,0:T(8,128)(2,1)S(1)}, bf16[256,256]{1,0:T(8,128)(2,1)S(1)}, u32[]{:S(2)}, u32[]{:S(2)}) collective-permute-start(bf16[256,256]{1,0:T(8,128)(2,1)S(1)} %get-tuple-element.37), channel_id=1, source_target_pairs={{0,8},{4,12},{8,0},{12,4},{16,24},{20,28},{24,16},{28,20},{1,9},{5... | collective-permute-start | bytes 393224 | tf_op jit(solution)/shard_map/ppermute | solution.py:106
  9.3 1.4 %collective-permute-start.4 = (bf16[256,256]{1,0:T(8,128)(2,1)S(1)}, bf16[256,256]{1,0:T(8,128)(2,1)S(1)}, u32[]{:S(2)}, u32[]{:S(2)}) collective-permute-start(bf16[256,256]{1,0:T(8,128)(2,1)S(1)} %get-tuple-element.39), channel_id=1, source_target_pairs={{0,12},{4,8},{8,4},{12,0},{16,28},{20,24},{24,20},{28,16},{1,13},{... | collective-permute-start | bytes 393224 | tf_op jit(solution)/shard_map/ppermute | solution.py:106
  10.7 3.6 %collective-permute-start.5 = (bf16[256,256]{1,0:T(8,128)(2,1)S(1)}, bf16[256,256]{1,0:T(8,128)(2,1)S(1)}, u32[]{:S(2)}, u32[]{:S(2)}) collective-permute-start(bf16[256,256]{1,0:T(8,128)(2,1)S(1)} %get-tuple-element.44), channel_id=1, source_target_pairs={{0,24},{4,28},{8,16},{12,20},{16,8},{20,12},{24,0},{28,4},{1,25},{... | collective-permute-start | bytes 393224 | tf_op jit(solution)/shard_map/ppermute | solution.py:106
  14.3 1.9 %collective-permute-done.1.refs_2_ = bf16[256,256]{1,0:T(8,128)(2,1)S(1)} collective-permute-done((bf16[256,256]{1,0:T(8,128)(2,1)S(1)}, bf16[256,256]{1,0:T(8,128)(2,1)S(1)}, u32[]{:S(2)}, u32[]{:S(2)}) %collective-permute-start.1) | collective-permute-done | bytes 131104 | tf_op jit(solution)/shard_map/ppermute | solution.py:106
  16.1 2.4 %collective-permute-start.6 = (bf16[256,256]{1,0:T(8,128)(2,1)S(1)}, bf16[256,256]{1,0:T(8,128)(2,1)S(1)}, u32[]{:S(2)}, u32[]{:S(2)}) collective-permute-start(bf16[256,256]{1,0:T(8,128)(2,1)S(1)} %get-tuple-element.45), channel_id=1, source_target_pairs={{0,28},{4,24},{8,20},{12,16},{16,12},{20,8},{24,4},{28,0},{1,29},{... | collective-permute-start | bytes 393224 | tf_op jit(solution)/shard_map/ppermute | solution.py:106
  18.5 1.9 %collective-permute-done.3.refs_4_ = bf16[256,256]{1,0:T(8,128)(2,1)S(1)} collective-permute-done((bf16[256,256]{1,0:T(8,128)(2,1)S(1)}, bf16[256,256]{1,0:T(8,128)(2,1)S(1)}, u32[]{:S(2)}, u32[]{:S(2)}) %collective-permute-start.3) | collective-permute-done | bytes 131104 | tf_op jit(solution)/shard_map/ppermute | solution.py:106
  20.4 3.4 %shard_map.83 = (bf16[512,512]{1,0:T(8,128)(2,1)S(1)}, bf16[256,1536]{1,0:T(8,128)(2,1)S(1)}, f32[8,512,256]{2,1,0:T(8,128)S(1)}, f32[8,512,128]{2,1,0:T(8,128)S(1)}) custom-call(bf16[512,512]{1,0:T(8,128)(2,1)} %constant.4.clone.fwd_hbm, bf16[256,1536]{1,0:T(8,128)(2,1)} %constant.5.clone.bwd_hbm, bf16[256,256]{1,0:T(8,128)(2,1)S(1)} %get-tuple-element.34.refs_0_, ...), custom_call_target="tpu_custom_call" | custom-call | flops 805306368 | bytes 4194304 | tf_op jit(solution)/shard_map/pallas_call | solution.py:173
  23.9 0.5 collective-permute-done.5.refs_0_
  24.4 1.4 %collective-permute-done.6.refs_1_ = bf16[256,256]{1,0:T(8,128)(2,1)S(1)} collective-permute-done((bf16[256,256]{1,0:T(8,128)(2,1)S(1)}, bf16[256,256]{1,0:T(8,128)(2,1)S(1)}, u32[]{:S(2)}, u32[]{:S(2)}) %collective-permute-start.6) | collective-permute-done | bytes 131104 | tf_op jit(solution)/shard_map/ppermute | solution.py:106
  25.8 2.3 %shard_map.84 = (bf16[256,128]{1,0:T(8,128)(2,1)S(1)}, bf16[256,128]{1,0:T(8,128)(2,1)S(1)}, bf16[256,128]{1,0:T(8,128)(2,1)S(1)}, bf16[256,128]{1,0:T(8,128)(2,...) custom-call(bf16[512,512]{1,0:T(8,128)(2,1)S(1)} %get-tuple-element., ...), custom_call_target="tpu_custom_call" | custom-call | flops 1073741824 | bytes 4194304 | tf_op jit(solution)/shard_map/pallas_call | solution.py:261
  28.0 5.1 %collective-permute-start.7 = (bf16[256,128]{1,0:T(8,128)(2,1)S(1)}, bf16[256,128]{1,0:T(8,128)(2,1)S(1)}, u32[]{:S(2)}, u32[]{:S(2)}) collective-permute-start(bf16[256,128]{1,0:T(8,128)(2,1)S(1)} %get-tuple-element.47), channel_id=1, source_target_pairs={{0,4},{4,0},{8,12},{12,8},{16,20},{20,16},{24,28},{28,24},{1,5},{5... | collective-permute-start | bytes 196616 | tf_op jit(solution)/shard_map/ppermute | solution.py:106
  33.1 4.1 %collective-permute-start.8 = (bf16[256,128]{1,0:T(8,128)(2,1)S(1)}, bf16[256,128]{1,0:T(8,128)(2,1)S(1)}, u32[]{:S(2)}, u32[]{:S(2)}) collective-permute-start(bf16[256,128]{1,0:T(8,128)(2,1)S(1)} %get-tuple-element.48), channel_id=1, source_target_pairs={{0,16},{4,20},{8,24},{12,28},{16,0},{20,4},{24,8},{28,12},{1,17},{... | collective-permute-start | bytes 196616 | tf_op jit(solution)/shard_map/ppermute | solution.py:106
  37.2 1.4 %collective-permute-start.10 = (bf16[256,128]{1,0:T(8,128)(2,1)S(1)}, bf16[256,128]{1,0:T(8,128)(2,1)S(1)}, u32[]{:S(2)}, u32[]{:S(2)}) collective-permute-start(bf16[256,128]{1,0:T(8,128)(2,1)S(1)} %get-tuple-element.50), channel_id=1, source_target_pairs={{0,24},{4,28},{8,16},{12,20},{16,8},{20,12},{24,0},{28,4},{1,25},{... | collective-permute-start | bytes 196616 | tf_op jit(solution)/shard_map/ppermute | solution.py:106
  38.6 2.0 %collective-permute-start.11 = (bf16[256,128]{1,0:T(8,128)(2,1)S(1)}, bf16[256,128]{1,0:T(8,128)(2,1)S(1)}, u32[]{:S(2)}, u32[]{:S(2)}) collective-permute-start(bf16[256,128]{1,0:T(8,128)(2,1)S(1)} %get-tuple-element.51), channel_id=1, source_target_pairs={{0,8},{4,12},{8,0},{12,4},{16,24},{20,28},{24,16},{28,20},{1,9},{5... | collective-permute-start | bytes 196616 | tf_op jit(solution)/shard_map/ppermute | solution.py:106
  40.6 1.9 %collective-permute-start.12 = (bf16[256,128]{1,0:T(8,128)(2,1)S(1)}, bf16[256,128]{1,0:T(8,128)(2,1)S(1)}, u32[]{:S(2)}, u32[]{:S(2)}) collective-permute-start(bf16[256,128]{1,0:T(8,128)(2,1)S(1)} %get-tuple-element.54), channel_id=1, source_target_pairs={{0,28},{4,24},{8,20},{12,16},{16,12},{20,8},{24,4},{28,0},{1,29},{... | collective-permute-start | bytes 196616 | tf_op jit(solution)/shard_map/ppermute | solution.py:106
  42.5 0.6 collective-permute-start.13
  43.1 2.6 %collective-permute-done.9.refs_3_ = bf16[256,128]{1,0:T(8,128)(2,1)S(1)} collective-permute-done((bf16[256,128]{1,0:T(8,128)(2,1)S(1)}, bf16[256,128]{1,0:T(8,128)(2,1)S(1)}, u32[]{:S(2)}, u32[]{:S(2)}) %collective-permute-start.9) | collective-permute-done | bytes 65568 | tf_op jit(solution)/shard_map/ppermute | solution.py:106
  45.7 0.6 collective-permute-done.11.refs_5_
  46.3 1.7 %shard_map.85 = (bf16[256,1024]{1,0:T(8,128)(2,1)S(1)}, f32[256,1024]{1,0:T(8,128)S(1)}, f32[256,1024]{1,0:T(8,128)S(1)}) custom-call(bf16[256,1024]{1,0:T(8,128)(2,1)S(1)} %copy-done.3, bf16[256,1024]{1,0:T(8,128)(2,1)S(1)} %copy-done.1, bf16[256,1024]{1,0:T(8,128)(2,1)S(1)} %copy-done.2, f32[1,1024]{1,0:T(1,128)S(1)} %bitcast.1, ...), custom_call_target="tpu_custom_call" | custom-call | flops 1073741824 | bytes 2621440 | tf_op jit(solution)/shard_map/pallas_call | solution.py:342
  48.4 0.3 shard_map.86
  49.0 0.5 collective-permute-start.15
  49.5 0.3 shard_map.89
  49.8 0.4 collective-permute-done.17.arrived_ref
  50.3 1.5 %collective-permute-start.18 = (bf16[256,512]{1,0:T(8,128)(2,1)S(1)}, bf16[256,512]{1,0:T(8,128)(2,1)S(1)}, u32[]{:S(2)}, u32[]{:S(2)}) collective-permute-start(bf16[256,512]{1,0:T(8,128)(2,1)S(1)} %shard_map.92), channel_id=1, source_target_pairs={{0,2},{2,0},{1,3},{3,1},{4,6},{6,4},{5,7},{7,5},{8,10},{10,8},{9,1... | collective-permute-start | bytes 786440 | tf_op jit(solution)/shard_map/ppermute | solution.py:568
  51.9 0.6 collective-permute-start.16
  52.6 1.3 %shard_map.88 = (bf16[256,1024]{1,0:T(8,128)(2,1)S(1)}, f32[256,1024]{1,0:T(8,128)S(1)}) custom-call(bf16[256,1024]{1,0:T(8,128)(2,1)S(1)} %shard_map.87.gated_ref, bf16[1024,4096]{1,0:T(8,128)(2,1)S(1)} %copy-done), custom_call_target="tpu_custom_call" | custom-call | flops 1073741824 | bytes 4194304 | tf_op jit(solution)/shard_map/pallas_call | solution.py:445
  54.0 5.5 %collective-permute-done.18.refs_1_ = bf16[256,512]{1,0:T(8,128)(2,1)S(1)} collective-permute-done((bf16[256,512]{1,0:T(8,128)(2,1)S(1)}, bf16[256,512]{1,0:T(8,128)(2,1)S(1)}, u32[]{:S(2)}, u32[]{:S(2)}) %collective-permute-start.18) | collective-permute-done | bytes 262176 | tf_op jit(solution)/shard_map/ppermute | solution.py:568
  59.5 4.8 %collective-permute-done.16.refs_0_ = bf16[256,512]{1,0:T(8,128)(2,1)S(1)} collective-permute-done((bf16[256,512]{1,0:T(8,128)(2,1)S(1)}, bf16[256,512]{1,0:T(8,128)(2,1)S(1)}, u32[]{:S(2)}, u32[]{:S(2)}) %collective-permute-start.16) | collective-permute-done | bytes 262176 | tf_op jit(solution)/shard_map/ppermute | solution.py:568
  64.3 0.9 %shard_map.94 = bf16[256,1024]{1,0:T(8,128)(2,1)} custom-call(f32[256,1024]{1,0:T(8,128)S(1)} %get-tuple-element.57.own_ref, bf16[256,1024]{1,0:T(8,128)(2,1)S(1)} %collective-permute-done.14.near_ref, bf16[256,512]{1,0:T(8,128)(2,1)S(1)} %collective-permute-done.16.refs_0_, bf16[256,512]{1,0:T(8,128)(2,1)S(1)} %collective-permute-done.18.refs_1_, ...), custom_call_target="tpu_custom_call" | custom-call | flops 262144 | bytes 2097152 | tf_op jit(solution)/shard_map/pallas_call | solution.py:512
  (29 shorter events, 1.2 us)
Async XLA Ops:
  1.8 8.9 %collective-permute-start = (bf16[256,256]{1,0:T(8,128)(2,1)S(1)}, bf16[256,256]{1,0:T(8,128)(2,1)S(1)}, u32[]{:S(2)}, u32[]{:S(2)}) collective-permute-start(bf16[256,256]{1,0:T(8,128)(2,1)S(1)} %get-tuple-element.35), channel_id=1, source_target_pairs={{0,4},{4,0},{8,12},{12,8},{16,20},{20,16},{24,28},{28,24},{1,5},{5... | collective-permute-start | bytes 393224 | tf_op jit(solution)/shard_map/ppermute | solution.py:106
  4.8 11.3 %collective-permute-start.1 = (bf16[256,256]{1,0:T(8,128)(2,1)S(1)}, bf16[256,256]{1,0:T(8,128)(2,1)S(1)}, u32[]{:S(2)}, u32[]{:S(2)}) collective-permute-start(bf16[256,256]{1,0:T(8,128)(2,1)S(1)} %get-tuple-element.36), channel_id=1, source_target_pairs={{0,16},{4,20},{8,24},{12,28},{16,0},{20,4},{24,8},{28,12},{1,17},{... | collective-permute-start | bytes 393224 | tf_op jit(solution)/shard_map/ppermute | solution.py:106
  7.4 11.1 %collective-permute-start.2 = (bf16[256,256]{1,0:T(8,128)(2,1)S(1)}, bf16[256,256]{1,0:T(8,128)(2,1)S(1)}, u32[]{:S(2)}, u32[]{:S(2)}) collective-permute-start(bf16[256,256]{1,0:T(8,128)(2,1)S(1)} %get-tuple-element.37), channel_id=1, source_target_pairs={{0,8},{4,12},{8,0},{12,4},{16,24},{20,28},{24,16},{28,20},{1,9},{5... | collective-permute-start | bytes 393224 | tf_op jit(solution)/shard_map/ppermute | solution.py:106
  9.0 11.5 %collective-permute-start.3 = (bf16[256,256]{1,0:T(8,128)(2,1)S(1)}, bf16[256,256]{1,0:T(8,128)(2,1)S(1)}, u32[]{:S(2)}, u32[]{:S(2)}) collective-permute-start(bf16[256,256]{1,0:T(8,128)(2,1)S(1)} %get-tuple-element.38), channel_id=1, source_target_pairs={{0,20},{4,16},{8,28},{12,24},{16,4},{20,0},{24,12},{28,8},{1,21},{... | collective-permute-start | bytes 393224 | tf_op jit(solution)/shard_map/ppermute | solution.py:106
  9.3 11.2 %collective-permute-start.4 = (bf16[256,256]{1,0:T(8,128)(2,1)S(1)}, bf16[256,256]{1,0:T(8,128)(2,1)S(1)}, u32[]{:S(2)}, u32[]{:S(2)}) collective-permute-start(bf16[256,256]{1,0:T(8,128)(2,1)S(1)} %get-tuple-element.39), channel_id=1, source_target_pairs={{0,12},{4,8},{8,4},{12,0},{16,28},{20,24},{24,20},{28,16},{1,13},{... | collective-permute-start | bytes 393224 | tf_op jit(solution)/shard_map/ppermute | solution.py:106
  10.7 13.7 %collective-permute-start.5 = (bf16[256,256]{1,0:T(8,128)(2,1)S(1)}, bf16[256,256]{1,0:T(8,128)(2,1)S(1)}, u32[]{:S(2)}, u32[]{:S(2)}) collective-permute-start(bf16[256,256]{1,0:T(8,128)(2,1)S(1)} %get-tuple-element.44), channel_id=1, source_target_pairs={{0,24},{4,28},{8,16},{12,20},{16,8},{20,12},{24,0},{28,4},{1,25},{... | collective-permute-start | bytes 393224 | tf_op jit(solution)/shard_map/ppermute | solution.py:106
  16.1 9.6 %collective-permute-start.6 = (bf16[256,256]{1,0:T(8,128)(2,1)S(1)}, bf16[256,256]{1,0:T(8,128)(2,1)S(1)}, u32[]{:S(2)}, u32[]{:S(2)}) collective-permute-start(bf16[256,256]{1,0:T(8,128)(2,1)S(1)} %get-tuple-element.45), channel_id=1, source_target_pairs={{0,28},{4,24},{8,20},{12,16},{16,12},{20,8},{24,4},{28,0},{1,29},{... | collective-permute-start | bytes 393224 | tf_op jit(solution)/shard_map/ppermute | solution.py:106
  20.4 25.9 %copy-start = (bf16[1024,4096]{1,0:T(8,128)(2,1)S(1)}, bf16[1024,4096]{1,0:T(8,128)(2,1)}, u32[]{:S(2)}) copy-start(bf16[1024,4096]{1,0:T(8,128)(2,1)} %weight_ref.9) | copy-start | bytes 25165828
  23.8 22.5 %copy-start.1 = (bf16[256,1024]{1,0:T(8,128)(2,1)S(1)}, bf16[256,1024]{1,0:T(8,128)(2,1)}, u32[]{:S(2)}) copy-start(bf16[256,1024]{1,0:T(8,128)(2,1)} %keys_ref.3) | copy-start | bytes 1572868
  23.8 22.5 %copy-start.2 = (bf16[256,1024]{1,0:T(8,128)(2,1)S(1)}, bf16[256,1024]{1,0:T(8,128)(2,1)}, u32[]{:S(2)}) copy-start(bf16[256,1024]{1,0:T(8,128)(2,1)} %values_ref.3) | copy-start | bytes 1572868
  23.8 22.5 %copy-start.3 = (bf16[256,1024]{1,0:T(8,128)(2,1)S(1)}, bf16[256,1024]{1,0:T(8,128)(2,1)}, u32[]{:S(2)}) copy-start(bf16[256,1024]{1,0:T(8,128)(2,1)} %queries_ref.3) | copy-start | bytes 1572868
  23.9 22.5 %copy-start.4 = (f32[1024]{0:T(1024)S(1)}, f32[1024]{0:T(1024)}, u32[]{:S(2)}) copy-start(f32[1024]{0:T(1024)} %param.12) | copy-start | bytes 12292
  28.0 12.6 %collective-permute-start.7 = (bf16[256,128]{1,0:T(8,128)(2,1)S(1)}, bf16[256,128]{1,0:T(8,128)(2,1)S(1)}, u32[]{:S(2)}, u32[]{:S(2)}) collective-permute-start(bf16[256,128]{1,0:T(8,128)(2,1)S(1)} %get-tuple-element.47), channel_id=1, source_target_pairs={{0,4},{4,0},{8,12},{12,8},{16,20},{20,16},{24,28},{28,24},{1,5},{5... | collective-permute-start | bytes 196616 | tf_op jit(solution)/shard_map/ppermute | solution.py:106
  33.1 9.4 %collective-permute-start.8 = (bf16[256,128]{1,0:T(8,128)(2,1)S(1)}, bf16[256,128]{1,0:T(8,128)(2,1)S(1)}, u32[]{:S(2)}, u32[]{:S(2)}) collective-permute-start(bf16[256,128]{1,0:T(8,128)(2,1)S(1)} %get-tuple-element.48), channel_id=1, source_target_pairs={{0,16},{4,20},{8,24},{12,28},{16,0},{20,4},{24,8},{28,12},{1,17},{... | collective-permute-start | bytes 196616 | tf_op jit(solution)/shard_map/ppermute | solution.py:106
  37.2 8.5 %collective-permute-start.9 = (bf16[256,128]{1,0:T(8,128)(2,1)S(1)}, bf16[256,128]{1,0:T(8,128)(2,1)S(1)}, u32[]{:S(2)}, u32[]{:S(2)}) collective-permute-start(bf16[256,128]{1,0:T(8,128)(2,1)S(1)} %get-tuple-element.49), channel_id=1, source_target_pairs={{0,20},{4,16},{8,28},{12,24},{16,4},{20,0},{24,12},{28,8},{1,21},{... | collective-permute-start | bytes 196616 | tf_op jit(solution)/shard_map/ppermute | solution.py:106
  37.2 8.5 %collective-permute-start.10 = (bf16[256,128]{1,0:T(8,128)(2,1)S(1)}, bf16[256,128]{1,0:T(8,128)(2,1)S(1)}, u32[]{:S(2)}, u32[]{:S(2)}) collective-permute-start(bf16[256,128]{1,0:T(8,128)(2,1)S(1)} %get-tuple-element.50), channel_id=1, source_target_pairs={{0,24},{4,28},{8,16},{12,20},{16,8},{20,12},{24,0},{28,4},{1,25},{... | collective-permute-start | bytes 196616 | tf_op jit(solution)/shard_map/ppermute | solution.py:106
  38.6 7.7 %collective-permute-start.11 = (bf16[256,128]{1,0:T(8,128)(2,1)S(1)}, bf16[256,128]{1,0:T(8,128)(2,1)S(1)}, u32[]{:S(2)}, u32[]{:S(2)}) collective-permute-start(bf16[256,128]{1,0:T(8,128)(2,1)S(1)} %get-tuple-element.51), channel_id=1, source_target_pairs={{0,8},{4,12},{8,0},{12,4},{16,24},{20,28},{24,16},{28,20},{1,9},{5... | collective-permute-start | bytes 196616 | tf_op jit(solution)/shard_map/ppermute | solution.py:106
  40.6 7.4 %collective-permute-start.12 = (bf16[256,128]{1,0:T(8,128)(2,1)S(1)}, bf16[256,128]{1,0:T(8,128)(2,1)S(1)}, u32[]{:S(2)}, u32[]{:S(2)}) collective-permute-start(bf16[256,128]{1,0:T(8,128)(2,1)S(1)} %get-tuple-element.54), channel_id=1, source_target_pairs={{0,28},{4,24},{8,20},{12,16},{16,12},{20,8},{24,4},{28,0},{1,29},{... | collective-permute-start | bytes 196616 | tf_op jit(solution)/shard_map/ppermute | solution.py:106
  42.5 5.9 %collective-permute-start.13 = (bf16[256,128]{1,0:T(8,128)(2,1)S(1)}, bf16[256,128]{1,0:T(8,128)(2,1)S(1)}, u32[]{:S(2)}, u32[]{:S(2)}) collective-permute-start(bf16[256,128]{1,0:T(8,128)(2,1)S(1)} %get-tuple-element.55), channel_id=1, source_target_pairs={{0,12},{4,8},{8,4},{12,0},{16,28},{20,24},{24,20},{28,16},{1,13},{... | collective-permute-start | bytes 196616 | tf_op jit(solution)/shard_map/ppermute | solution.py:106
  48.7 1.6 %collective-permute-start.17 = (bf16[256,512]{1,0:T(8,128)(2,1)S(1)}, bf16[256,512]{1,0:T(8,128)(2,1)S(1)}, u32[]{:S(2)}, u32[]{:S(2)}) collective-permute-start(bf16[256,512]{1,0:T(8,128)(2,1)S(1)} %get-tuple-element.62), channel_id=1, source_target_pairs={{0,1},{1,0},{2,3},{3,2},{4,5},{5,4},{6,7},{7,6},{8,9},{9,8},{10,11... | collective-permute-start | bytes 786440 | tf_op jit(solution)/shard_map/ppermute | solution.py:567
  49.0 2.9 %collective-permute-start.15 = (bf16[256,512]{1,0:T(8,128)(2,1)S(1)}, bf16[256,512]{1,0:T(8,128)(2,1)S(1)}, u32[]{:S(2)}, u32[]{:S(2)}) collective-permute-start(bf16[256,512]{1,0:T(8,128)(2,1)S(1)} %shard_map.90), channel_id=1, source_target_pairs={{0,1},{1,0},{2,3},{3,2},{4,5},{5,4},{6,7},{7,6},{8,9},{9,8},{10,11... | collective-permute-start | bytes 786440 | tf_op jit(solution)/shard_map/ppermute | solution.py:567
  50.3 9.2 %collective-permute-start.18 = (bf16[256,512]{1,0:T(8,128)(2,1)S(1)}, bf16[256,512]{1,0:T(8,128)(2,1)S(1)}, u32[]{:S(2)}, u32[]{:S(2)}) collective-permute-start(bf16[256,512]{1,0:T(8,128)(2,1)S(1)} %shard_map.92), channel_id=1, source_target_pairs={{0,2},{2,0},{1,3},{3,1},{4,6},{6,4},{5,7},{7,5},{8,10},{10,8},{9,1... | collective-permute-start | bytes 786440 | tf_op jit(solution)/shard_map/ppermute | solution.py:568
  51.9 12.4 %collective-permute-start.16 = (bf16[256,512]{1,0:T(8,128)(2,1)S(1)}, bf16[256,512]{1,0:T(8,128)(2,1)S(1)}, u32[]{:S(2)}, u32[]{:S(2)}) collective-permute-start(bf16[256,512]{1,0:T(8,128)(2,1)S(1)} %shard_map.91), channel_id=1, source_target_pairs={{0,2},{2,0},{1,3},{3,1},{4,6},{6,4},{5,7},{7,5},{8,10},{10,8},{9,1... | collective-permute-start | bytes 786440 | tf_op jit(solution)/shard_map/ppermute | solution.py:568
  53.9 10.4 %collective-permute-start.14 = (bf16[256,1024]{1,0:T(8,128)(2,1)S(1)}, bf16[256,1024]{1,0:T(8,128)(2,1)S(1)}, u32[]{:S(2)}, u32[]{:S(2)}) collective-permute-start(bf16[256,1024]{1,0:T(8,128)(2,1)S(1)} %get-tuple-element.58), channel_id=1, source_target_pairs={{0,1},{1,0},{2,3},{3,2},{4,5},{5,4},{6,7},{7,6},{8,9},{9,8},{10,11... | collective-permute-start | bytes 1572872 | tf_op jit(solution)/shard_map/ppermute | solution.py:571

commit v5 on v4

--- a/solution.py
+++ b/solution.py
@@ -98,6 +98,7 @@
     near, far = list(range(1, half)), list(range(half, n_peers))
     if back:
         return [0, near[0]] + far[:3] + [near[1]] + far[3:] + near[2:]
+    far = far[2:] + far[:2]
     return [0, near[0], far[0], near[1], far[1]] + near[2:] + far[2:]
 
 

time: 65.4 us -> 66.3 us (1.014)
  waiting for transfers between devices: 20 us -> 27 us
  starting transfers between devices: 32.7 us -> 26.5 us
    ppermute x14, waiting for transfers between devices: 9.24 us -> 16.3 us  [exchange(): lax.ppermute(block, 'seq', [(i, i ^ slot) for i in range(n_peers)])]
    ppermute x14, starting transfers between devices: 29.9 us -> 23.7 us  [exchange(): lax.ppermute(block, 'seq', [(i, i ^ slot) for i in range(n_peers)])]
  transfers between devices with their start and end apart: 19 -> 19, of which waited for: 10 -> 12; matrix products, arithmetic and copies ran while one was open for 0% -> 0% of each run, Pallas kernels for 11% -> 10%
where the time goes in v5:
time: 66.3 us; the launch traced here: 66.1 us
  waiting for transfers between devices  27 us (41%)
  starting transfers between devices  26.5 us (40%)
  Pallas kernels  12.4 us (19%)
    ppermute x14, starting transfers between devices, exchange(): lax.ppermute(block, 'seq', [(i, i ^ slot) for i in range(n_peers)])  23.7 us
    ppermute x14, waiting for transfers between devices, exchange(): lax.ppermute(block, 'seq', [(i, i ^ slot) for i in range(n_peers)])  16.3 us
    ppermute x2, waiting for transfers between devices, body(): lax.ppermute(add(*pair), 'fsdp', across)  10.4 us
    pallas_call x1, Pallas kernels, spectra(): pl.pallas_call(functools.partial(spectra_kernel, n_peers), in_specs=[pl.B...  3.09 us
    pallas_call x1, Pallas kernels, conv_fast(): pl.pallas_call(conv_kernel, in_specs=[whole] * 6, out_specs=[whole] * n_b...  2.59 us
    ppermute x2, starting transfers between devices, body(): lax.ppermute(add(*pair), 'fsdp', across)  2.16 us
    pallas_call x1, Pallas kernels, pre(): pl.pallas_call(functools.partial(pre_kernel, n_peers), in_specs=[pl.Block...  1.77 us
    pallas_call x1, Pallas kernels, gate_early(): pl.pallas_call(functools.partial(gate_early_kernel, n_peers), in_specs=[w...  1.73 us
  transfers between devices with their start and end apart: 19, of which 12 were waited for; matrix products, arithmetic and copies ran while one was open for 0% of the time, Pallas kernels for 10%

profile of v5, /device:TPU:0, one launch (start us, length us, event | category | flops | bytes accessed | tf_op | source)
XLA Modules:
  0.0 66.1 jit_solution(16886567553410316007)
XLA Ops:
  0.0 1.8 %shard_map.82 = (bf16[256,256]{1,0:T(8,128)(2,1)S(1)}, bf16[256,256]{1,0:T(8,128)(2,1)S(1)}, bf16[256,256]{1,0:T(8,128)(2,1)S(1)}, bf16[256,256]{1,0:T(8,128)(2,...) custom-call(bf16[256,1024]{1,0:T(8,128)(2,1)} %keys_ref.3, ...), custom_call_target="tpu_custom_call" | custom-call | flops 262144 | bytes 3145728 | tf_op jit(solution)/shard_map/pallas_call | solution.py:78
  1.8 3.0 %collective-permute-start = (bf16[256,256]{1,0:T(8,128)(2,1)S(1)}, bf16[256,256]{1,0:T(8,128)(2,1)S(1)}, u32[]{:S(2)}, u32[]{:S(2)}) collective-permute-start(bf16[256,256]{1,0:T(8,128)(2,1)S(1)} %get-tuple-element.35), channel_id=1, source_target_pairs={{0,4},{4,0},{8,12},{12,8},{16,20},{20,16},{24,28},{28,24},{1,5},{5... | collective-permute-start | bytes 393224 | tf_op jit(solution)/shard_map/ppermute | solution.py:107
  4.8 3.6 %collective-permute-start.1 = (bf16[256,256]{1,0:T(8,128)(2,1)S(1)}, bf16[256,256]{1,0:T(8,128)(2,1)S(1)}, u32[]{:S(2)}, u32[]{:S(2)}) collective-permute-start(bf16[256,256]{1,0:T(8,128)(2,1)S(1)} %get-tuple-element.36), channel_id=1, source_target_pairs={{0,24},{4,28},{8,16},{12,20},{16,8},{20,12},{24,0},{28,4},{1,25},{... | collective-permute-start | bytes 393224 | tf_op jit(solution)/shard_map/ppermute | solution.py:107
  8.4 0.8 %collective-permute-start.3 = (bf16[256,256]{1,0:T(8,128)(2,1)S(1)}, bf16[256,256]{1,0:T(8,128)(2,1)S(1)}, u32[]{:S(2)}, u32[]{:S(2)}) collective-permute-start(bf16[256,256]{1,0:T(8,128)(2,1)S(1)} %get-tuple-element.38), channel_id=1, source_target_pairs={{0,28},{4,24},{8,20},{12,16},{16,12},{20,8},{24,4},{28,0},{1,29},{... | collective-permute-start | bytes 393224 | tf_op jit(solution)/shard_map/ppermute | solution.py:107
  9.3 1.4 %collective-permute-start.4 = (bf16[256,256]{1,0:T(8,128)(2,1)S(1)}, bf16[256,256]{1,0:T(8,128)(2,1)S(1)}, u32[]{:S(2)}, u32[]{:S(2)}) collective-permute-start(bf16[256,256]{1,0:T(8,128)(2,1)S(1)} %get-tuple-element.39), channel_id=1, source_target_pairs={{0,12},{4,8},{8,4},{12,0},{16,28},{20,24},{24,20},{28,16},{1,13},{... | collective-permute-start | bytes 393224 | tf_op jit(solution)/shard_map/ppermute | solution.py:107
  10.7 3.0 %collective-permute-start.5 = (bf16[256,256]{1,0:T(8,128)(2,1)S(1)}, bf16[256,256]{1,0:T(8,128)(2,1)S(1)}, u32[]{:S(2)}, u32[]{:S(2)}) collective-permute-start(bf16[256,256]{1,0:T(8,128)(2,1)S(1)} %get-tuple-element.44), channel_id=1, source_target_pairs={{0,16},{4,20},{8,24},{12,28},{16,0},{20,4},{24,8},{28,12},{1,17},{... | collective-permute-start | bytes 393224 | tf_op jit(solution)/shard_map/ppermute | solution.py:107
  13.7 2.5 %collective-permute-start.6 = (bf16[256,256]{1,0:T(8,128)(2,1)S(1)}, bf16[256,256]{1,0:T(8,128)(2,1)S(1)}, u32[]{:S(2)}, u32[]{:S(2)}) collective-permute-start(bf16[256,256]{1,0:T(8,128)(2,1)S(1)} %get-tuple-element.45), channel_id=1, source_target_pairs={{0,20},{4,16},{8,28},{12,24},{16,4},{20,0},{24,12},{28,8},{1,21},{... | collective-permute-start | bytes 393224 | tf_op jit(solution)/shard_map/ppermute | solution.py:107
  16.3 1.5 %collective-permute-done.2.refs_3_ = bf16[256,256]{1,0:T(8,128)(2,1)S(1)} collective-permute-done((bf16[256,256]{1,0:T(8,128)(2,1)S(1)}, bf16[256,256]{1,0:T(8,128)(2,1)S(1)}, u32[]{:S(2)}, u32[]{:S(2)}) %collective-permute-start.2) | collective-permute-done | bytes 131104 | tf_op jit(solution)/shard_map/ppermute | solution.py:107
  17.7 0.6 collective-permute-done.3.refs_4_
  18.3 2.6 %collective-permute-done.4.refs_5_ = bf16[256,256]{1,0:T(8,128)(2,1)S(1)} collective-permute-done((bf16[256,256]{1,0:T(8,128)(2,1)S(1)}, bf16[256,256]{1,0:T(8,128)(2,1)S(1)}, u32[]{:S(2)}, u32[]{:S(2)}) %collective-permute-start.4) | collective-permute-done | bytes 131104 | tf_op jit(solution)/shard_map/ppermute | solution.py:107
  21.0 3.1 %shard_map.83 = (bf16[512,512]{1,0:T(8,128)(2,1)S(1)}, bf16[256,1536]{1,0:T(8,128)(2,1)S(1)}, f32[8,512,256]{2,1,0:T(8,128)S(1)}, f32[8,512,128]{2,1,0:T(8,128)S(1)}) custom-call(bf16[512,512]{1,0:T(8,128)(2,1)} %constant.4.clone.fwd_hbm, bf16[256,1536]{1,0:T(8,128)(2,1)} %constant.5.clone.bwd_hbm, bf16[256,256]{1,0:T(8,128)(2,1)S(1)} %get-tuple-element.34.refs_0_, ...), custom_call_target="tpu_custom_call" | custom-call | flops 805306368 | bytes 4194304 | tf_op jit(solution)/shard_map/pallas_call | solution.py:174
  24.1 4.5 %collective-permute-done.5.refs_0_ = bf16[256,256]{1,0:T(8,128)(2,1)S(1)} collective-permute-done((bf16[256,256]{1,0:T(8,128)(2,1)S(1)}, bf16[256,256]{1,0:T(8,128)(2,1)S(1)}, u32[]{:S(2)}, u32[]{:S(2)}) %collective-permute-start.5) | collective-permute-done | bytes 131104 | tf_op jit(solution)/shard_map/ppermute | solution.py:107
  28.6 1.8 %collective-permute-done.6.refs_1_ = bf16[256,256]{1,0:T(8,128)(2,1)S(1)} collective-permute-done((bf16[256,256]{1,0:T(8,128)(2,1)S(1)}, bf16[256,256]{1,0:T(8,128)(2,1)S(1)}, u32[]{:S(2)}, u32[]{:S(2)}) %collective-permute-start.6) | collective-permute-done | bytes 131104 | tf_op jit(solution)/shard_map/ppermute | solution.py:107
  30.4 2.6 %shard_map.84 = (bf16[256,128]{1,0:T(8,128)(2,1)S(1)}, bf16[256,128]{1,0:T(8,128)(2,1)S(1)}, bf16[256,128]{1,0:T(8,128)(2,1)S(1)}, bf16[256,128]{1,0:T(8,128)(2,...) custom-call(bf16[512,512]{1,0:T(8,128)(2,1)S(1)} %get-tuple-element., ...), custom_call_target="tpu_custom_call" | custom-call | flops 1073741824 | bytes 4194304 | tf_op jit(solution)/shard_map/pallas_call | solution.py:262
  33.0 1.6 %collective-permute-start.7 = (bf16[256,128]{1,0:T(8,128)(2,1)S(1)}, bf16[256,128]{1,0:T(8,128)(2,1)S(1)}, u32[]{:S(2)}, u32[]{:S(2)}) collective-permute-start(bf16[256,128]{1,0:T(8,128)(2,1)S(1)} %get-tuple-element.47), channel_id=1, source_target_pairs={{0,4},{4,0},{8,12},{12,8},{16,20},{20,16},{24,28},{28,24},{1,5},{5... | collective-permute-start | bytes 196616 | tf_op jit(solution)/shard_map/ppermute | solution.py:107
  34.6 2.9 %collective-permute-start.9 = (bf16[256,128]{1,0:T(8,128)(2,1)S(1)}, bf16[256,128]{1,0:T(8,128)(2,1)S(1)}, u32[]{:S(2)}, u32[]{:S(2)}) collective-permute-start(bf16[256,128]{1,0:T(8,128)(2,1)S(1)} %get-tuple-element.49), channel_id=1, source_target_pairs={{0,20},{4,16},{8,28},{12,24},{16,4},{20,0},{24,12},{28,8},{1,21},{... | collective-permute-start | bytes 196616 | tf_op jit(solution)/shard_map/ppermute | solution.py:107
  37.4 2.6 %collective-permute-start.10 = (bf16[256,128]{1,0:T(8,128)(2,1)S(1)}, bf16[256,128]{1,0:T(8,128)(2,1)S(1)}, u32[]{:S(2)}, u32[]{:S(2)}) collective-permute-start(bf16[256,128]{1,0:T(8,128)(2,1)S(1)} %get-tuple-element.50), channel_id=1, source_target_pairs={{0,24},{4,28},{8,16},{12,20},{16,8},{20,12},{24,0},{28,4},{1,25},{... | collective-permute-start | bytes 196616 | tf_op jit(solution)/shard_map/ppermute | solution.py:107
  40.1 2.1 %collective-permute-start.12 = (bf16[256,128]{1,0:T(8,128)(2,1)S(1)}, bf16[256,128]{1,0:T(8,128)(2,1)S(1)}, u32[]{:S(2)}, u32[]{:S(2)}) collective-permute-start(bf16[256,128]{1,0:T(8,128)(2,1)S(1)} %get-tuple-element.54), channel_id=1, source_target_pairs={{0,28},{4,24},{8,20},{12,16},{16,12},{20,8},{24,4},{28,0},{1,29},{... | collective-permute-start | bytes 196616 | tf_op jit(solution)/shard_map/ppermute | solution.py:107
  42.2 1.9 %collective-permute-done.8.refs_2_ = bf16[256,128]{1,0:T(8,128)(2,1)S(1)} collective-permute-done((bf16[256,128]{1,0:T(8,128)(2,1)S(1)}, bf16[256,128]{1,0:T(8,128)(2,1)S(1)}, u32[]{:S(2)}, u32[]{:S(2)}) %collective-permute-start.8) | collective-permute-done | bytes 65568 | tf_op jit(solution)/shard_map/ppermute | solution.py:107
  44.1 1.8 %collective-permute-done.9.refs_3_ = bf16[256,128]{1,0:T(8,128)(2,1)S(1)} collective-permute-done((bf16[256,128]{1,0:T(8,128)(2,1)S(1)}, bf16[256,128]{1,0:T(8,128)(2,1)S(1)}, u32[]{:S(2)}, u32[]{:S(2)}) %collective-permute-start.9) | collective-permute-done | bytes 65568 | tf_op jit(solution)/shard_map/ppermute | solution.py:107
  45.9 0.4 collective-permute-done.11.refs_5_
  46.4 1.7 %shard_map.85 = (bf16[256,1024]{1,0:T(8,128)(2,1)S(1)}, f32[256,1024]{1,0:T(8,128)S(1)}, f32[256,1024]{1,0:T(8,128)S(1)}) custom-call(bf16[256,1024]{1,0:T(8,128)(2,1)S(1)} %copy-done.3, bf16[256,1024]{1,0:T(8,128)(2,1)S(1)} %copy-done.1, bf16[256,1024]{1,0:T(8,128)(2,1)S(1)} %copy-done.2, f32[1,1024]{1,0:T(1,128)S(1)} %bitcast.1, ...), custom_call_target="tpu_custom_call" | custom-call | flops 1073741824 | bytes 2621440 | tf_op jit(solution)/shard_map/pallas_call | solution.py:343
  48.1 1.1 %collective-permute-done.13.refs_1_ = bf16[256,128]{1,0:T(8,128)(2,1)S(1)} collective-permute-done((bf16[256,128]{1,0:T(8,128)(2,1)S(1)}, bf16[256,128]{1,0:T(8,128)(2,1)S(1)}, u32[]{:S(2)}, u32[]{:S(2)}) %collective-permute-start.13) | collective-permute-done | bytes 65568 | tf_op jit(solution)/shard_map/ppermute | solution.py:107
  49.9 0.5 collective-permute-start.15
  50.4 0.3 shard_map.89
  50.8 0.4 collective-permute-done.17.arrived_ref
  51.2 1.5 %collective-permute-start.18 = (bf16[256,512]{1,0:T(8,128)(2,1)S(1)}, bf16[256,512]{1,0:T(8,128)(2,1)S(1)}, u32[]{:S(2)}, u32[]{:S(2)}) collective-permute-start(bf16[256,512]{1,0:T(8,128)(2,1)S(1)} %shard_map.92), channel_id=1, source_target_pairs={{0,2},{2,0},{1,3},{3,1},{4,6},{6,4},{5,7},{7,5},{8,10},{10,8},{9,1... | collective-permute-start | bytes 786440 | tf_op jit(solution)/shard_map/ppermute | solution.py:569
  52.8 0.6 collective-permute-start.16
  53.5 1.3 %shard_map.88 = (bf16[256,1024]{1,0:T(8,128)(2,1)S(1)}, f32[256,1024]{1,0:T(8,128)S(1)}) custom-call(bf16[256,1024]{1,0:T(8,128)(2,1)S(1)} %shard_map.87.gated_ref, bf16[1024,4096]{1,0:T(8,128)(2,1)S(1)} %copy-done), custom_call_target="tpu_custom_call" | custom-call | flops 1073741824 | bytes 4194304 | tf_op jit(solution)/shard_map/pallas_call | solution.py:446
  54.9 5.5 %collective-permute-done.18.refs_1_ = bf16[256,512]{1,0:T(8,128)(2,1)S(1)} collective-permute-done((bf16[256,512]{1,0:T(8,128)(2,1)S(1)}, bf16[256,512]{1,0:T(8,128)(2,1)S(1)}, u32[]{:S(2)}, u32[]{:S(2)}) %collective-permute-start.18) | collective-permute-done | bytes 262176 | tf_op jit(solution)/shard_map/ppermute | solution.py:569
  60.4 4.8 %collective-permute-done.16.refs_0_ = bf16[256,512]{1,0:T(8,128)(2,1)S(1)} collective-permute-done((bf16[256,512]{1,0:T(8,128)(2,1)S(1)}, bf16[256,512]{1,0:T(8,128)(2,1)S(1)}, u32[]{:S(2)}, u32[]{:S(2)}) %collective-permute-start.16) | collective-permute-done | bytes 262176 | tf_op jit(solution)/shard_map/ppermute | solution.py:569
  65.3 0.9 %shard_map.94 = bf16[256,1024]{1,0:T(8,128)(2,1)} custom-call(f32[256,1024]{1,0:T(8,128)S(1)} %get-tuple-element.57.own_ref, bf16[256,1024]{1,0:T(8,128)(2,1)S(1)} %collective-permute-done.14.near_ref, bf16[256,512]{1,0:T(8,128)(2,1)S(1)} %collective-permute-done.16.refs_0_, bf16[256,512]{1,0:T(8,128)(2,1)S(1)} %collective-permute-done.18.refs_1_, ...), custom_call_target="tpu_custom_call" | custom-call | flops 262144 | bytes 2097152 | tf_op jit(solution)/shard_map/pallas_call | solution.py:513
  (29 shorter events, 0.9 us)
Async XLA Ops:
  1.8 8.9 %collective-permute-start = (bf16[256,256]{1,0:T(8,128)(2,1)S(1)}, bf16[256,256]{1,0:T(8,128)(2,1)S(1)}, u32[]{:S(2)}, u32[]{:S(2)}) collective-permute-start(bf16[256,256]{1,0:T(8,128)(2,1)S(1)} %get-tuple-element.35), channel_id=1, source_target_pairs={{0,4},{4,0},{8,12},{12,8},{16,20},{20,16},{24,28},{28,24},{1,5},{5... | collective-permute-start | bytes 393224 | tf_op jit(solution)/shard_map/ppermute | solution.py:107
  4.8 8.9 %collective-permute-start.1 = (bf16[256,256]{1,0:T(8,128)(2,1)S(1)}, bf16[256,256]{1,0:T(8,128)(2,1)S(1)}, u32[]{:S(2)}, u32[]{:S(2)}) collective-permute-start(bf16[256,256]{1,0:T(8,128)(2,1)S(1)} %get-tuple-element.36), channel_id=1, source_target_pairs={{0,24},{4,28},{8,16},{12,20},{16,8},{20,12},{24,0},{28,4},{1,25},{... | collective-permute-start | bytes 393224 | tf_op jit(solution)/shard_map/ppermute | solution.py:107
  8.4 9.3 %collective-permute-start.2 = (bf16[256,256]{1,0:T(8,128)(2,1)S(1)}, bf16[256,256]{1,0:T(8,128)(2,1)S(1)}, u32[]{:S(2)}, u32[]{:S(2)}) collective-permute-start(bf16[256,256]{1,0:T(8,128)(2,1)S(1)} %get-tuple-element.37), channel_id=1, source_target_pairs={{0,8},{4,12},{8,0},{12,4},{16,24},{20,28},{24,16},{28,20},{1,9},{5... | collective-permute-start | bytes 393224 | tf_op jit(solution)/shard_map/ppermute | solution.py:107
  8.4 9.9 %collective-permute-start.3 = (bf16[256,256]{1,0:T(8,128)(2,1)S(1)}, bf16[256,256]{1,0:T(8,128)(2,1)S(1)}, u32[]{:S(2)}, u32[]{:S(2)}) collective-permute-start(bf16[256,256]{1,0:T(8,128)(2,1)S(1)} %get-tuple-element.38), channel_id=1, source_target_pairs={{0,28},{4,24},{8,20},{12,16},{16,12},{20,8},{24,4},{28,0},{1,29},{... | collective-permute-start | bytes 393224 | tf_op jit(solution)/shard_map/ppermute | solution.py:107
  9.3 11.7 %collective-permute-start.4 = (bf16[256,256]{1,0:T(8,128)(2,1)S(1)}, bf16[256,256]{1,0:T(8,128)(2,1)S(1)}, u32[]{:S(2)}, u32[]{:S(2)}) collective-permute-start(bf16[256,256]{1,0:T(8,128)(2,1)S(1)} %get-tuple-element.39), channel_id=1, source_target_pairs={{0,12},{4,8},{8,4},{12,0},{16,28},{20,24},{24,20},{28,16},{1,13},{... | collective-permute-start | bytes 393224 | tf_op jit(solution)/shard_map/ppermute | solution.py:107
  10.7 18.0 %collective-permute-start.5 = (bf16[256,256]{1,0:T(8,128)(2,1)S(1)}, bf16[256,256]{1,0:T(8,128)(2,1)S(1)}, u32[]{:S(2)}, u32[]{:S(2)}) collective-permute-start(bf16[256,256]{1,0:T(8,128)(2,1)S(1)} %get-tuple-element.44), channel_id=1, source_target_pairs={{0,16},{4,20},{8,24},{12,28},{16,0},{20,4},{24,8},{28,12},{1,17},{... | collective-permute-start | bytes 393224 | tf_op jit(solution)/shard_map/ppermute | solution.py:107
  13.7 16.7 %collective-permute-start.6 = (bf16[256,256]{1,0:T(8,128)(2,1)S(1)}, bf16[256,256]{1,0:T(8,128)(2,1)S(1)}, u32[]{:S(2)}, u32[]{:S(2)}) collective-permute-start(bf16[256,256]{1,0:T(8,128)(2,1)S(1)} %get-tuple-element.45), channel_id=1, source_target_pairs={{0,20},{4,16},{8,28},{12,24},{16,4},{20,0},{24,12},{28,8},{1,21},{... | collective-permute-start | bytes 393224 | tf_op jit(solution)/shard_map/ppermute | solution.py:107
  21.0 25.4 %copy-start = (bf16[1024,4096]{1,0:T(8,128)(2,1)S(1)}, bf16[1024,4096]{1,0:T(8,128)(2,1)}, u32[]{:S(2)}) copy-start(bf16[1024,4096]{1,0:T(8,128)(2,1)} %weight_ref.9) | copy-start | bytes 25165828
  24.1 22.3 %copy-start.1 = (bf16[256,1024]{1,0:T(8,128)(2,1)S(1)}, bf16[256,1024]{1,0:T(8,128)(2,1)}, u32[]{:S(2)}) copy-start(bf16[256,1024]{1,0:T(8,128)(2,1)} %keys_ref.3) | copy-start | bytes 1572868
  24.1 22.3 %copy-start.2 = (bf16[256,1024]{1,0:T(8,128)(2,1)S(1)}, bf16[256,1024]{1,0:T(8,128)(2,1)}, u32[]{:S(2)}) copy-start(bf16[256,1024]{1,0:T(8,128)(2,1)} %values_ref.3) | copy-start | bytes 1572868
  24.1 22.3 %copy-start.3 = (bf16[256,1024]{1,0:T(8,128)(2,1)S(1)}, bf16[256,1024]{1,0:T(8,128)(2,1)}, u32[]{:S(2)}) copy-start(bf16[256,1024]{1,0:T(8,128)(2,1)} %queries_ref.3) | copy-start | bytes 1572868
  24.1 22.3 %copy-start.4 = (f32[1024]{0:T(1024)S(1)}, f32[1024]{0:T(1024)}, u32[]{:S(2)}) copy-start(f32[1024]{0:T(1024)} %param.12) | copy-start | bytes 12292
  33.0 7.1 %collective-permute-start.7 = (bf16[256,128]{1,0:T(8,128)(2,1)S(1)}, bf16[256,128]{1,0:T(8,128)(2,1)S(1)}, u32[]{:S(2)}, u32[]{:S(2)}) collective-permute-start(bf16[256,128]{1,0:T(8,128)(2,1)S(1)} %get-tuple-element.47), channel_id=1, source_target_pairs={{0,4},{4,0},{8,12},{12,8},{16,20},{20,16},{24,28},{28,24},{1,5},{5... | collective-permute-start | bytes 196616 | tf_op jit(solution)/shard_map/ppermute | solution.py:107
  34.6 9.5 %collective-permute-start.8 = (bf16[256,128]{1,0:T(8,128)(2,1)S(1)}, bf16[256,128]{1,0:T(8,128)(2,1)S(1)}, u32[]{:S(2)}, u32[]{:S(2)}) collective-permute-start(bf16[256,128]{1,0:T(8,128)(2,1)S(1)} %get-tuple-element.48), channel_id=1, source_target_pairs={{0,16},{4,20},{8,24},{12,28},{16,0},{20,4},{24,8},{28,12},{1,17},{... | collective-permute-start | bytes 196616 | tf_op jit(solution)/shard_map/ppermute | solution.py:107
  34.6 11.3 %collective-permute-start.9 = (bf16[256,128]{1,0:T(8,128)(2,1)S(1)}, bf16[256,128]{1,0:T(8,128)(2,1)S(1)}, u32[]{:S(2)}, u32[]{:S(2)}) collective-permute-start(bf16[256,128]{1,0:T(8,128)(2,1)S(1)} %get-tuple-element.49), channel_id=1, source_target_pairs={{0,20},{4,16},{8,28},{12,24},{16,4},{20,0},{24,12},{28,8},{1,21},{... | collective-permute-start | bytes 196616 | tf_op jit(solution)/shard_map/ppermute | solution.py:107
  37.4 8.5 %collective-permute-start.10 = (bf16[256,128]{1,0:T(8,128)(2,1)S(1)}, bf16[256,128]{1,0:T(8,128)(2,1)S(1)}, u32[]{:S(2)}, u32[]{:S(2)}) collective-permute-start(bf16[256,128]{1,0:T(8,128)(2,1)S(1)} %get-tuple-element.50), channel_id=1, source_target_pairs={{0,24},{4,28},{8,16},{12,20},{16,8},{20,12},{24,0},{28,4},{1,25},{... | collective-permute-start | bytes 196616 | tf_op jit(solution)/shard_map/ppermute | solution.py:107
  40.1 6.3 %collective-permute-start.11 = (bf16[256,128]{1,0:T(8,128)(2,1)S(1)}, bf16[256,128]{1,0:T(8,128)(2,1)S(1)}, u32[]{:S(2)}, u32[]{:S(2)}) collective-permute-start(bf16[256,128]{1,0:T(8,128)(2,1)S(1)} %get-tuple-element.51), channel_id=1, source_target_pairs={{0,8},{4,12},{8,0},{12,4},{16,24},{20,28},{24,16},{28,20},{1,9},{5... | collective-permute-start | bytes 196616 | tf_op jit(solution)/shard_map/ppermute | solution.py:107
  40.1 8.0 %collective-permute-start.12 = (bf16[256,128]{1,0:T(8,128)(2,1)S(1)}, bf16[256,128]{1,0:T(8,128)(2,1)S(1)}, u32[]{:S(2)}, u32[]{:S(2)}) collective-permute-start(bf16[256,128]{1,0:T(8,128)(2,1)S(1)} %get-tuple-element.54), channel_id=1, source_target_pairs={{0,28},{4,24},{8,20},{12,16},{16,12},{20,8},{24,4},{28,0},{1,29},{... | collective-permute-start | bytes 196616 | tf_op jit(solution)/shard_map/ppermute | solution.py:107
  44.1 5.2 %collective-permute-start.13 = (bf16[256,128]{1,0:T(8,128)(2,1)S(1)}, bf16[256,128]{1,0:T(8,128)(2,1)S(1)}, u32[]{:S(2)}, u32[]{:S(2)}) collective-permute-start(bf16[256,128]{1,0:T(8,128)(2,1)S(1)} %get-tuple-element.55), channel_id=1, source_target_pairs={{0,12},{4,8},{8,4},{12,0},{16,28},{20,24},{24,20},{28,16},{1,13},{... | collective-permute-start | bytes 196616 | tf_op jit(solution)/shard_map/ppermute | solution.py:107
  49.6 1.6 %collective-permute-start.17 = (bf16[256,512]{1,0:T(8,128)(2,1)S(1)}, bf16[256,512]{1,0:T(8,128)(2,1)S(1)}, u32[]{:S(2)}, u32[]{:S(2)}) collective-permute-start(bf16[256,512]{1,0:T(8,128)(2,1)S(1)} %get-tuple-element.62), channel_id=1, source_target_pairs={{0,1},{1,0},{2,3},{3,2},{4,5},{5,4},{6,7},{7,6},{8,9},{9,8},{10,11... | collective-permute-start | bytes 786440 | tf_op jit(solution)/shard_map/ppermute | solution.py:568
  49.9 2.9 %collective-permute-start.15 = (bf16[256,512]{1,0:T(8,128)(2,1)S(1)}, bf16[256,512]{1,0:T(8,128)(2,1)S(1)}, u32[]{:S(2)}, u32[]{:S(2)}) collective-permute-start(bf16[256,512]{1,0:T(8,128)(2,1)S(1)} %shard_map.90), channel_id=1, source_target_pairs={{0,1},{1,0},{2,3},{3,2},{4,5},{5,4},{6,7},{7,6},{8,9},{9,8},{10,11... | collective-permute-start | bytes 786440 | tf_op jit(solution)/shard_map/ppermute | solution.py:568
  51.2 9.2 %collective-permute-start.18 = (bf16[256,512]{1,0:T(8,128)(2,1)S(1)}, bf16[256,512]{1,0:T(8,128)(2,1)S(1)}, u32[]{:S(2)}, u32[]{:S(2)}) collective-permute-start(bf16[256,512]{1,0:T(8,128)(2,1)S(1)} %shard_map.92), channel_id=1, source_target_pairs={{0,2},{2,0},{1,3},{3,1},{4,6},{6,4},{5,7},{7,5},{8,10},{10,8},{9,1... | collective-permute-start | bytes 786440 | tf_op jit(solution)/shard_map/ppermute | solution.py:569
  52.8 12.4 %collective-permute-start.16 = (bf16[256,512]{1,0:T(8,128)(2,1)S(1)}, bf16[256,512]{1,0:T(8,128)(2,1)S(1)}, u32[]{:S(2)}, u32[]{:S(2)}) collective-permute-start(bf16[256,512]{1,0:T(8,128)(2,1)S(1)} %shard_map.91), channel_id=1, source_target_pairs={{0,2},{2,0},{1,3},{3,1},{4,6},{6,4},{5,7},{7,5},{8,10},{10,8},{9,1... | collective-permute-start | bytes 786440 | tf_op jit(solution)/shard_map/ppermute | solution.py:569
  54.8 10.4 %collective-permute-start.14 = (bf16[256,1024]{1,0:T(8,128)(2,1)S(1)}, bf16[256,1024]{1,0:T(8,128)(2,1)S(1)}, u32[]{:S(2)}, u32[]{:S(2)}) collective-permute-start(bf16[256,1024]{1,0:T(8,128)(2,1)S(1)} %get-tuple-element.58), channel_id=1, source_target_pairs={{0,1},{1,0},{2,3},{3,2},{4,5},{5,4},{6,7},{7,6},{8,9},{9,8},{10,11... | collective-permute-start | bytes 1572872 | tf_op jit(solution)/shard_map/ppermute | solution.py:572

commit v6 on v4

--- a/solution.py
+++ b/solution.py
@@ -97,6 +97,7 @@
     half = n_peers // 2
     near, far = list(range(1, half)), list(range(half, n_peers))
     if back:
+        far = far[2:] + far[:2]
         return [0, near[0]] + far[:3] + [near[1]] + far[3:] + near[2:]
     return [0, near[0], far[0], near[1], far[1]] + near[2:] + far[2:]
 

time: 65.4 us -> 65.7 us (level)
  waiting for transfers between devices: 20 us -> 21 us
  starting transfers between devices: 32.7 us -> 31.9 us
    ppermute x14, waiting for transfers between devices: 9.24 us -> 10.3 us  [exchange(): lax.ppermute(block, 'seq', [(i, i ^ slot) for i in range(n_peers)])]
    ppermute x14, starting transfers between devices: 29.9 us -> 29.1 us  [exchange(): lax.ppermute(block, 'seq', [(i, i ^ slot) for i in range(n_peers)])]
  transfers between devices with their start and end apart: 19 -> 19, of which waited for: 10 -> 9; matrix products, arithmetic and copies ran while one was open for 0% -> 0% of each run, Pallas kernels for 11% -> 11%
where the time goes in v6:
time: 65.7 us; the launch traced here: 65.5 us
  starting transfers between devices  31.9 us (49%)
  waiting for transfers between devices  21 us (32%)
  Pallas kernels  12.3 us (19%)
    ppermute x14, starting transfers between devices, exchange(): lax.ppermute(block, 'seq', [(i, i ^ slot) for i in range(n_peers)])  29.1 us
    ppermute x2, waiting for transfers between devices, body(): lax.ppermute(add(*pair), 'fsdp', across)  10.3 us
    ppermute x14, waiting for transfers between devices, exchange(): lax.ppermute(block, 'seq', [(i, i ^ slot) for i in range(n_peers)])  10.3 us
    pallas_call x1, Pallas kernels, spectra(): pl.pallas_call(functools.partial(spectra_kernel, n_peers), in_specs=[pl.B...  3.37 us
    pallas_call x1, Pallas kernels, conv_fast(): pl.pallas_call(conv_kernel, in_specs=[whole] * 6, out_specs=[whole] * n_b...  2.26 us
    ppermute x2, starting transfers between devices, body(): lax.ppermute(add(*pair), 'fsdp', across)  2.16 us
    pallas_call x1, Pallas kernels, pre(): pl.pallas_call(functools.partial(pre_kernel, n_peers), in_specs=[pl.Block...  1.77 us
    pallas_call x1, Pallas kernels, gate_early(): pl.pallas_call(functools.partial(gate_early_kernel, n_peers), in_specs=[w...  1.73 us
  transfers between devices with their start and end apart: 19, of which 9 were waited for; matrix products, arithmetic and copies ran while one was open for 0% of the time, Pallas kernels for 11%

profile of v6, /device:TPU:0, one launch (start us, length us, event | category | flops | bytes accessed | tf_op | source)
XLA Modules:
  0.0 65.5 jit_solution(3113952444214758700)
XLA Ops:
  0.0 1.8 %shard_map.82 = (bf16[256,256]{1,0:T(8,128)(2,1)S(1)}, bf16[256,256]{1,0:T(8,128)(2,1)S(1)}, bf16[256,256]{1,0:T(8,128)(2,1)S(1)}, bf16[256,256]{1,0:T(8,128)(2,...) custom-call(bf16[256,1024]{1,0:T(8,128)(2,1)} %keys_ref.3, ...), custom_call_target="tpu_custom_call" | custom-call | flops 262144 | bytes 3145728 | tf_op jit(solution)/shard_map/pallas_call | solution.py:78
  1.8 3.0 %collective-permute-start = (bf16[256,256]{1,0:T(8,128)(2,1)S(1)}, bf16[256,256]{1,0:T(8,128)(2,1)S(1)}, u32[]{:S(2)}, u32[]{:S(2)}) collective-permute-start(bf16[256,256]{1,0:T(8,128)(2,1)S(1)} %get-tuple-element.35), channel_id=1, source_target_pairs={{0,4},{4,0},{8,12},{12,8},{16,20},{20,16},{24,28},{28,24},{1,5},{5... | collective-permute-start | bytes 393224 | tf_op jit(solution)/shard_map/ppermute | solution.py:107
  4.8 2.6 %collective-permute-start.1 = (bf16[256,256]{1,0:T(8,128)(2,1)S(1)}, bf16[256,256]{1,0:T(8,128)(2,1)S(1)}, u32[]{:S(2)}, u32[]{:S(2)}) collective-permute-start(bf16[256,256]{1,0:T(8,128)(2,1)S(1)} %get-tuple-element.36), channel_id=1, source_target_pairs={{0,16},{4,20},{8,24},{12,28},{16,0},{20,4},{24,8},{28,12},{1,17},{... | collective-permute-start | bytes 393224 | tf_op jit(solution)/shard_map/ppermute | solution.py:107
  7.4 1.6 %collective-permute-start.2 = (bf16[256,256]{1,0:T(8,128)(2,1)S(1)}, bf16[256,256]{1,0:T(8,128)(2,1)S(1)}, u32[]{:S(2)}, u32[]{:S(2)}) collective-permute-start(bf16[256,256]{1,0:T(8,128)(2,1)S(1)} %get-tuple-element.37), channel_id=1, source_target_pairs={{0,8},{4,12},{8,0},{12,4},{16,24},{20,28},{24,16},{28,20},{1,9},{5... | collective-permute-start | bytes 393224 | tf_op jit(solution)/shard_map/ppermute | solution.py:107
  9.3 1.4 %collective-permute-start.4 = (bf16[256,256]{1,0:T(8,128)(2,1)S(1)}, bf16[256,256]{1,0:T(8,128)(2,1)S(1)}, u32[]{:S(2)}, u32[]{:S(2)}) collective-permute-start(bf16[256,256]{1,0:T(8,128)(2,1)S(1)} %get-tuple-element.39), channel_id=1, source_target_pairs={{0,12},{4,8},{8,4},{12,0},{16,28},{20,24},{24,20},{28,16},{1,13},{... | collective-permute-start | bytes 393224 | tf_op jit(solution)/shard_map/ppermute | solution.py:107
  10.7 3.6 %collective-permute-start.5 = (bf16[256,256]{1,0:T(8,128)(2,1)S(1)}, bf16[256,256]{1,0:T(8,128)(2,1)S(1)}, u32[]{:S(2)}, u32[]{:S(2)}) collective-permute-start(bf16[256,256]{1,0:T(8,128)(2,1)S(1)} %get-tuple-element.44), channel_id=1, source_target_pairs={{0,24},{4,28},{8,16},{12,20},{16,8},{20,12},{24,0},{28,4},{1,25},{... | collective-permute-start | bytes 393224 | tf_op jit(solution)/shard_map/ppermute | solution.py:107
  14.3 1.9 %collective-permute-done.1.refs_2_ = bf16[256,256]{1,0:T(8,128)(2,1)S(1)} collective-permute-done((bf16[256,256]{1,0:T(8,128)(2,1)S(1)}, bf16[256,256]{1,0:T(8,128)(2,1)S(1)}, u32[]{:S(2)}, u32[]{:S(2)}) %collective-permute-start.1) | collective-permute-done | bytes 131104 | tf_op jit(solution)/shard_map/ppermute | solution.py:107
  16.1 2.4 %collective-permute-start.6 = (bf16[256,256]{1,0:T(8,128)(2,1)S(1)}, bf16[256,256]{1,0:T(8,128)(2,1)S(1)}, u32[]{:S(2)}, u32[]{:S(2)}) collective-permute-start(bf16[256,256]{1,0:T(8,128)(2,1)S(1)} %get-tuple-element.45), channel_id=1, source_target_pairs={{0,28},{4,24},{8,20},{12,16},{16,12},{20,8},{24,4},{28,0},{1,29},{... | collective-permute-start | bytes 393224 | tf_op jit(solution)/shard_map/ppermute | solution.py:107
  18.5 1.9 %collective-permute-done.3.refs_4_ = bf16[256,256]{1,0:T(8,128)(2,1)S(1)} collective-permute-done((bf16[256,256]{1,0:T(8,128)(2,1)S(1)}, bf16[256,256]{1,0:T(8,128)(2,1)S(1)}, u32[]{:S(2)}, u32[]{:S(2)}) %collective-permute-start.3) | collective-permute-done | bytes 131104 | tf_op jit(solution)/shard_map/ppermute | solution.py:107
  20.4 3.4 %shard_map.83 = (bf16[512,512]{1,0:T(8,128)(2,1)S(1)}, bf16[256,1536]{1,0:T(8,128)(2,1)S(1)}, f32[8,512,256]{2,1,0:T(8,128)S(1)}, f32[8,512,128]{2,1,0:T(8,128)S(1)}) custom-call(bf16[512,512]{1,0:T(8,128)(2,1)} %constant.4.clone.fwd_hbm, bf16[256,1536]{1,0:T(8,128)(2,1)} %constant.5.clone.bwd_hbm, bf16[256,256]{1,0:T(8,128)(2,1)S(1)} %get-tuple-element.34.refs_0_, ...), custom_call_target="tpu_custom_call" | custom-call | flops 805306368 | bytes 4194304 | tf_op jit(solution)/shard_map/pallas_call | solution.py:174
  23.9 0.5 collective-permute-done.5.refs_0_
  24.4 1.4 %collective-permute-done.6.refs_1_ = bf16[256,256]{1,0:T(8,128)(2,1)S(1)} collective-permute-done((bf16[256,256]{1,0:T(8,128)(2,1)S(1)}, bf16[256,256]{1,0:T(8,128)(2,1)S(1)}, u32[]{:S(2)}, u32[]{:S(2)}) %collective-permute-start.6) | collective-permute-done | bytes 131104 | tf_op jit(solution)/shard_map/ppermute | solution.py:107
  25.8 2.3 %shard_map.84 = (bf16[256,128]{1,0:T(8,128)(2,1)S(1)}, bf16[256,128]{1,0:T(8,128)(2,1)S(1)}, bf16[256,128]{1,0:T(8,128)(2,1)S(1)}, bf16[256,128]{1,0:T(8,128)(2,...) custom-call(bf16[512,512]{1,0:T(8,128)(2,1)S(1)} %get-tuple-element., ...), custom_call_target="tpu_custom_call" | custom-call | flops 1073741824 | bytes 4194304 | tf_op jit(solution)/shard_map/pallas_call | solution.py:262
  28.0 5.1 %collective-permute-start.7 = (bf16[256,128]{1,0:T(8,128)(2,1)S(1)}, bf16[256,128]{1,0:T(8,128)(2,1)S(1)}, u32[]{:S(2)}, u32[]{:S(2)}) collective-permute-start(bf16[256,128]{1,0:T(8,128)(2,1)S(1)} %get-tuple-element.47), channel_id=1, source_target_pairs={{0,4},{4,0},{8,12},{12,8},{16,20},{20,16},{24,28},{28,24},{1,5},{5... | collective-permute-start | bytes 196616 | tf_op jit(solution)/shard_map/ppermute | solution.py:107
  33.1 2.6 %collective-permute-start.8 = (bf16[256,128]{1,0:T(8,128)(2,1)S(1)}, bf16[256,128]{1,0:T(8,128)(2,1)S(1)}, u32[]{:S(2)}, u32[]{:S(2)}) collective-permute-start(bf16[256,128]{1,0:T(8,128)(2,1)S(1)} %get-tuple-element.48), channel_id=1, source_target_pairs={{0,24},{4,28},{8,16},{12,20},{16,8},{20,12},{24,0},{28,4},{1,25},{... | collective-permute-start | bytes 196616 | tf_op jit(solution)/shard_map/ppermute | solution.py:107
  35.8 0.7 %collective-permute-start.9 = (bf16[256,128]{1,0:T(8,128)(2,1)S(1)}, bf16[256,128]{1,0:T(8,128)(2,1)S(1)}, u32[]{:S(2)}, u32[]{:S(2)}) collective-permute-start(bf16[256,128]{1,0:T(8,128)(2,1)S(1)} %get-tuple-element.49), channel_id=1, source_target_pairs={{0,28},{4,24},{8,20},{12,16},{16,12},{20,8},{24,4},{28,0},{1,29},{... | collective-permute-start | bytes 196616 | tf_op jit(solution)/shard_map/ppermute | solution.py:107
  36.5 2.7 %collective-permute-start.10 = (bf16[256,128]{1,0:T(8,128)(2,1)S(1)}, bf16[256,128]{1,0:T(8,128)(2,1)S(1)}, u32[]{:S(2)}, u32[]{:S(2)}) collective-permute-start(bf16[256,128]{1,0:T(8,128)(2,1)S(1)} %get-tuple-element.50), channel_id=1, source_target_pairs={{0,16},{4,20},{8,24},{12,28},{16,0},{20,4},{24,8},{28,12},{1,17},{... | collective-permute-start | bytes 196616 | tf_op jit(solution)/shard_map/ppermute | solution.py:107
  39.2 0.9 %collective-permute-start.11 = (bf16[256,128]{1,0:T(8,128)(2,1)S(1)}, bf16[256,128]{1,0:T(8,128)(2,1)S(1)}, u32[]{:S(2)}, u32[]{:S(2)}) collective-permute-start(bf16[256,128]{1,0:T(8,128)(2,1)S(1)} %get-tuple-element.51), channel_id=1, source_target_pairs={{0,8},{4,12},{8,0},{12,4},{16,24},{20,28},{24,16},{28,20},{1,9},{5... | collective-permute-start | bytes 196616 | tf_op jit(solution)/shard_map/ppermute | solution.py:107
  40.1 1.5 %collective-permute-start.12 = (bf16[256,128]{1,0:T(8,128)(2,1)S(1)}, bf16[256,128]{1,0:T(8,128)(2,1)S(1)}, u32[]{:S(2)}, u32[]{:S(2)}) collective-permute-start(bf16[256,128]{1,0:T(8,128)(2,1)S(1)} %get-tuple-element.54), channel_id=1, source_target_pairs={{0,20},{4,16},{8,28},{12,24},{16,4},{20,0},{24,12},{28,8},{1,21},{... | collective-permute-start | bytes 196616 | tf_op jit(solution)/shard_map/ppermute | solution.py:107
  41.6 0.7 %collective-permute-start.13 = (bf16[256,128]{1,0:T(8,128)(2,1)S(1)}, bf16[256,128]{1,0:T(8,128)(2,1)S(1)}, u32[]{:S(2)}, u32[]{:S(2)}) collective-permute-start(bf16[256,128]{1,0:T(8,128)(2,1)S(1)} %get-tuple-element.55), channel_id=1, source_target_pairs={{0,12},{4,8},{8,4},{12,0},{16,28},{20,24},{24,20},{28,16},{1,13},{... | collective-permute-start | bytes 196616 | tf_op jit(solution)/shard_map/ppermute | solution.py:107
  42.3 0.9 %collective-permute-done.9.refs_3_ = bf16[256,128]{1,0:T(8,128)(2,1)S(1)} collective-permute-done((bf16[256,128]{1,0:T(8,128)(2,1)S(1)}, bf16[256,128]{1,0:T(8,128)(2,1)S(1)}, u32[]{:S(2)}, u32[]{:S(2)}) %collective-permute-start.9) | collective-permute-done | bytes 65568 | tf_op jit(solution)/shard_map/ppermute | solution.py:107
  43.2 3.7 %collective-permute-done.10.refs_4_ = bf16[256,128]{1,0:T(8,128)(2,1)S(1)} collective-permute-done((bf16[256,128]{1,0:T(8,128)(2,1)S(1)}, bf16[256,128]{1,0:T(8,128)(2,1)S(1)}, u32[]{:S(2)}, u32[]{:S(2)}) %collective-permute-start.10) | collective-permute-done | bytes 65568 | tf_op jit(solution)/shard_map/ppermute | solution.py:107
  46.9 1.7 %shard_map.85 = (bf16[256,1024]{1,0:T(8,128)(2,1)S(1)}, f32[256,1024]{1,0:T(8,128)S(1)}, f32[256,1024]{1,0:T(8,128)S(1)}) custom-call(bf16[256,1024]{1,0:T(8,128)(2,1)S(1)} %copy-done.3, bf16[256,1024]{1,0:T(8,128)(2,1)S(1)} %copy-done.1, bf16[256,1024]{1,0:T(8,128)(2,1)S(1)} %copy-done.2, f32[1,1024]{1,0:T(1,128)S(1)} %bitcast.1, ...), custom_call_target="tpu_custom_call" | custom-call | flops 1073741824 | bytes 2621440 | tf_op jit(solution)/shard_map/pallas_call | solution.py:343
  48.7 0.3 shard_map.86
  49.3 0.5 collective-permute-start.15
  50.2 0.4 collective-permute-done.17.arrived_ref
  50.6 1.6 %collective-permute-start.18 = (bf16[256,512]{1,0:T(8,128)(2,1)S(1)}, bf16[256,512]{1,0:T(8,128)(2,1)S(1)}, u32[]{:S(2)}, u32[]{:S(2)}) collective-permute-start(bf16[256,512]{1,0:T(8,128)(2,1)S(1)} %shard_map.92), channel_id=1, source_target_pairs={{0,2},{2,0},{1,3},{3,1},{4,6},{6,4},{5,7},{7,5},{8,10},{10,8},{9,1... | collective-permute-start | bytes 786440 | tf_op jit(solution)/shard_map/ppermute | solution.py:569
  52.3 0.6 collective-permute-start.16
  52.9 1.3 %shard_map.88 = (bf16[256,1024]{1,0:T(8,128)(2,1)S(1)}, f32[256,1024]{1,0:T(8,128)S(1)}) custom-call(bf16[256,1024]{1,0:T(8,128)(2,1)S(1)} %shard_map.87.gated_ref, bf16[1024,4096]{1,0:T(8,128)(2,1)S(1)} %copy-done), custom_call_target="tpu_custom_call" | custom-call | flops 1073741824 | bytes 4194304 | tf_op jit(solution)/shard_map/pallas_call | solution.py:446
  54.3 5.5 %collective-permute-done.18.refs_1_ = bf16[256,512]{1,0:T(8,128)(2,1)S(1)} collective-permute-done((bf16[256,512]{1,0:T(8,128)(2,1)S(1)}, bf16[256,512]{1,0:T(8,128)(2,1)S(1)}, u32[]{:S(2)}, u32[]{:S(2)}) %collective-permute-start.18) | collective-permute-done | bytes 262176 | tf_op jit(solution)/shard_map/ppermute | solution.py:569
  59.8 4.8 %collective-permute-done.16.refs_0_ = bf16[256,512]{1,0:T(8,128)(2,1)S(1)} collective-permute-done((bf16[256,512]{1,0:T(8,128)(2,1)S(1)}, bf16[256,512]{1,0:T(8,128)(2,1)S(1)}, u32[]{:S(2)}, u32[]{:S(2)}) %collective-permute-start.16) | collective-permute-done | bytes 262176 | tf_op jit(solution)/shard_map/ppermute | solution.py:569
  64.7 0.9 %shard_map.94 = bf16[256,1024]{1,0:T(8,128)(2,1)} custom-call(f32[256,1024]{1,0:T(8,128)S(1)} %get-tuple-element.57.own_ref, bf16[256,1024]{1,0:T(8,128)(2,1)S(1)} %collective-permute-done.14.near_ref, bf16[256,512]{1,0:T(8,128)(2,1)S(1)} %collective-permute-done.16.refs_0_, bf16[256,512]{1,0:T(8,128)(2,1)S(1)} %collective-permute-done.18.refs_1_, ...), custom_call_target="tpu_custom_call" | custom-call | flops 262144 | bytes 2097152 | tf_op jit(solution)/shard_map/pallas_call | solution.py:513
  (29 shorter events, 1.2 us)
Async XLA Ops:
  1.8 8.9 %collective-permute-start = (bf16[256,256]{1,0:T(8,128)(2,1)S(1)}, bf16[256,256]{1,0:T(8,128)(2,1)S(1)}, u32[]{:S(2)}, u32[]{:S(2)}) collective-permute-start(bf16[256,256]{1,0:T(8,128)(2,1)S(1)} %get-tuple-element.35), channel_id=1, source_target_pairs={{0,4},{4,0},{8,12},{12,8},{16,20},{20,16},{24,28},{28,24},{1,5},{5... | collective-permute-start | bytes 393224 | tf_op jit(solution)/shard_map/ppermute | solution.py:107
  4.8 11.3 %collective-permute-start.1 = (bf16[256,256]{1,0:T(8,128)(2,1)S(1)}, bf16[256,256]{1,0:T(8,128)(2,1)S(1)}, u32[]{:S(2)}, u32[]{:S(2)}) collective-permute-start(bf16[256,256]{1,0:T(8,128)(2,1)S(1)} %get-tuple-element.36), channel_id=1, source_target_pairs={{0,16},{4,20},{8,24},{12,28},{16,0},{20,4},{24,8},{28,12},{1,17},{... | collective-permute-start | bytes 393224 | tf_op jit(solution)/shard_map/ppermute | solution.py:107
  7.4 11.1 %collective-permute-start.2 = (bf16[256,256]{1,0:T(8,128)(2,1)S(1)}, bf16[256,256]{1,0:T(8,128)(2,1)S(1)}, u32[]{:S(2)}, u32[]{:S(2)}) collective-permute-start(bf16[256,256]{1,0:T(8,128)(2,1)S(1)} %get-tuple-element.37), channel_id=1, source_target_pairs={{0,8},{4,12},{8,0},{12,4},{16,24},{20,28},{24,16},{28,20},{1,9},{5... | collective-permute-start | bytes 393224 | tf_op jit(solution)/shard_map/ppermute | solution.py:107
  9.0 11.5 %collective-permute-start.3 = (bf16[256,256]{1,0:T(8,128)(2,1)S(1)}, bf16[256,256]{1,0:T(8,128)(2,1)S(1)}, u32[]{:S(2)}, u32[]{:S(2)}) collective-permute-start(bf16[256,256]{1,0:T(8,128)(2,1)S(1)} %get-tuple-element.38), channel_id=1, source_target_pairs={{0,20},{4,16},{8,28},{12,24},{16,4},{20,0},{24,12},{28,8},{1,21},{... | collective-permute-start | bytes 393224 | tf_op jit(solution)/shard_map/ppermute | solution.py:107
  9.3 11.2 %collective-permute-start.4 = (bf16[256,256]{1,0:T(8,128)(2,1)S(1)}, bf16[256,256]{1,0:T(8,128)(2,1)S(1)}, u32[]{:S(2)}, u32[]{:S(2)}) collective-permute-start(bf16[256,256]{1,0:T(8,128)(2,1)S(1)} %get-tuple-element.39), channel_id=1, source_target_pairs={{0,12},{4,8},{8,4},{12,0},{16,28},{20,24},{24,20},{28,16},{1,13},{... | collective-permute-start | bytes 393224 | tf_op jit(solution)/shard_map/ppermute | solution.py:107
  10.7 13.7 %collective-permute-start.5 = (bf16[256,256]{1,0:T(8,128)(2,1)S(1)}, bf16[256,256]{1,0:T(8,128)(2,1)S(1)}, u32[]{:S(2)}, u32[]{:S(2)}) collective-permute-start(bf16[256,256]{1,0:T(8,128)(2,1)S(1)} %get-tuple-element.44), channel_id=1, source_target_pairs={{0,24},{4,28},{8,16},{12,20},{16,8},{20,12},{24,0},{28,4},{1,25},{... | collective-permute-start | bytes 393224 | tf_op jit(solution)/shard_map/ppermute | solution.py:107
  16.1 9.6 %collective-permute-start.6 = (bf16[256,256]{1,0:T(8,128)(2,1)S(1)}, bf16[256,256]{1,0:T(8,128)(2,1)S(1)}, u32[]{:S(2)}, u32[]{:S(2)}) collective-permute-start(bf16[256,256]{1,0:T(8,128)(2,1)S(1)} %get-tuple-element.45), channel_id=1, source_target_pairs={{0,28},{4,24},{8,20},{12,16},{16,12},{20,8},{24,4},{28,0},{1,29},{... | collective-permute-start | bytes 393224 | tf_op jit(solution)/shard_map/ppermute | solution.py:107
  20.4 26.4 %copy-start = (bf16[1024,4096]{1,0:T(8,128)(2,1)S(1)}, bf16[1024,4096]{1,0:T(8,128)(2,1)}, u32[]{:S(2)}) copy-start(bf16[1024,4096]{1,0:T(8,128)(2,1)} %weight_ref.9) | copy-start | bytes 25165828
  23.8 23.1 %copy-start.1 = (bf16[256,1024]{1,0:T(8,128)(2,1)S(1)}, bf16[256,1024]{1,0:T(8,128)(2,1)}, u32[]{:S(2)}) copy-start(bf16[256,1024]{1,0:T(8,128)(2,1)} %keys_ref.3) | copy-start | bytes 1572868
  23.8 23.0 %copy-start.2 = (bf16[256,1024]{1,0:T(8,128)(2,1)S(1)}, bf16[256,1024]{1,0:T(8,128)(2,1)}, u32[]{:S(2)}) copy-start(bf16[256,1024]{1,0:T(8,128)(2,1)} %values_ref.3) | copy-start | bytes 1572868
  23.8 23.0 %copy-start.3 = (bf16[256,1024]{1,0:T(8,128)(2,1)S(1)}, bf16[256,1024]{1,0:T(8,128)(2,1)}, u32[]{:S(2)}) copy-start(bf16[256,1024]{1,0:T(8,128)(2,1)} %queries_ref.3) | copy-start | bytes 1572868
  23.9 23.0 %copy-start.4 = (f32[1024]{0:T(1024)S(1)}, f32[1024]{0:T(1024)}, u32[]{:S(2)}) copy-start(f32[1024]{0:T(1024)} %param.12) | copy-start | bytes 12292
  28.0 12.1 %collective-permute-start.7 = (bf16[256,128]{1,0:T(8,128)(2,1)S(1)}, bf16[256,128]{1,0:T(8,128)(2,1)S(1)}, u32[]{:S(2)}, u32[]{:S(2)}) collective-permute-start(bf16[256,128]{1,0:T(8,128)(2,1)S(1)} %get-tuple-element.47), channel_id=1, source_target_pairs={{0,4},{4,0},{8,12},{12,8},{16,20},{20,16},{24,28},{28,24},{1,5},{5... | collective-permute-start | bytes 196616 | tf_op jit(solution)/shard_map/ppermute | solution.py:107
  33.1 8.5 %collective-permute-start.8 = (bf16[256,128]{1,0:T(8,128)(2,1)S(1)}, bf16[256,128]{1,0:T(8,128)(2,1)S(1)}, u32[]{:S(2)}, u32[]{:S(2)}) collective-permute-start(bf16[256,128]{1,0:T(8,128)(2,1)S(1)} %get-tuple-element.48), channel_id=1, source_target_pairs={{0,24},{4,28},{8,16},{12,20},{16,8},{20,12},{24,0},{28,4},{1,25},{... | collective-permute-start | bytes 196616 | tf_op jit(solution)/shard_map/ppermute | solution.py:107
  35.8 7.4 %collective-permute-start.9 = (bf16[256,128]{1,0:T(8,128)(2,1)S(1)}, bf16[256,128]{1,0:T(8,128)(2,1)S(1)}, u32[]{:S(2)}, u32[]{:S(2)}) collective-permute-start(bf16[256,128]{1,0:T(8,128)(2,1)S(1)} %get-tuple-element.49), channel_id=1, source_target_pairs={{0,28},{4,24},{8,20},{12,16},{16,12},{20,8},{24,4},{28,0},{1,29},{... | collective-permute-start | bytes 196616 | tf_op jit(solution)/shard_map/ppermute | solution.py:107
  36.5 10.4 %collective-permute-start.10 = (bf16[256,128]{1,0:T(8,128)(2,1)S(1)}, bf16[256,128]{1,0:T(8,128)(2,1)S(1)}, u32[]{:S(2)}, u32[]{:S(2)}) collective-permute-start(bf16[256,128]{1,0:T(8,128)(2,1)S(1)} %get-tuple-element.50), channel_id=1, source_target_pairs={{0,16},{4,20},{8,24},{12,28},{16,0},{20,4},{24,8},{28,12},{1,17},{... | collective-permute-start | bytes 196616 | tf_op jit(solution)/shard_map/ppermute | solution.py:107
  39.2 7.7 %collective-permute-start.11 = (bf16[256,128]{1,0:T(8,128)(2,1)S(1)}, bf16[256,128]{1,0:T(8,128)(2,1)S(1)}, u32[]{:S(2)}, u32[]{:S(2)}) collective-permute-start(bf16[256,128]{1,0:T(8,128)(2,1)S(1)} %get-tuple-element.51), channel_id=1, source_target_pairs={{0,8},{4,12},{8,0},{12,4},{16,24},{20,28},{24,16},{28,20},{1,9},{5... | collective-permute-start | bytes 196616 | tf_op jit(solution)/shard_map/ppermute | solution.py:107
  40.1 8.5 %collective-permute-start.12 = (bf16[256,128]{1,0:T(8,128)(2,1)S(1)}, bf16[256,128]{1,0:T(8,128)(2,1)S(1)}, u32[]{:S(2)}, u32[]{:S(2)}) collective-permute-start(bf16[256,128]{1,0:T(8,128)(2,1)S(1)} %get-tuple-element.54), channel_id=1, source_target_pairs={{0,20},{4,16},{8,28},{12,24},{16,4},{20,0},{24,12},{28,8},{1,21},{... | collective-permute-start | bytes 196616 | tf_op jit(solution)/shard_map/ppermute | solution.py:107
  41.6 7.1 %collective-permute-start.13 = (bf16[256,128]{1,0:T(8,128)(2,1)S(1)}, bf16[256,128]{1,0:T(8,128)(2,1)S(1)}, u32[]{:S(2)}, u32[]{:S(2)}) collective-permute-start(bf16[256,128]{1,0:T(8,128)(2,1)S(1)} %get-tuple-element.55), channel_id=1, source_target_pairs={{0,12},{4,8},{8,4},{12,0},{16,28},{20,24},{24,20},{28,16},{1,13},{... | collective-permute-start | bytes 196616 | tf_op jit(solution)/shard_map/ppermute | solution.py:107
  49.0 1.6 %collective-permute-start.17 = (bf16[256,512]{1,0:T(8,128)(2,1)S(1)}, bf16[256,512]{1,0:T(8,128)(2,1)S(1)}, u32[]{:S(2)}, u32[]{:S(2)}) collective-permute-start(bf16[256,512]{1,0:T(8,128)(2,1)S(1)} %get-tuple-element.62), channel_id=1, source_target_pairs={{0,1},{1,0},{2,3},{3,2},{4,5},{5,4},{6,7},{7,6},{8,9},{9,8},{10,11... | collective-permute-start | bytes 786440 | tf_op jit(solution)/shard_map/ppermute | solution.py:568
  49.3 2.9 %collective-permute-start.15 = (bf16[256,512]{1,0:T(8,128)(2,1)S(1)}, bf16[256,512]{1,0:T(8,128)(2,1)S(1)}, u32[]{:S(2)}, u32[]{:S(2)}) collective-permute-start(bf16[256,512]{1,0:T(8,128)(2,1)S(1)} %shard_map.90), channel_id=1, source_target_pairs={{0,1},{1,0},{2,3},{3,2},{4,5},{5,4},{6,7},{7,6},{8,9},{9,8},{10,11... | collective-permute-start | bytes 786440 | tf_op jit(solution)/shard_map/ppermute | solution.py:568
  50.6 9.2 %collective-permute-start.18 = (bf16[256,512]{1,0:T(8,128)(2,1)S(1)}, bf16[256,512]{1,0:T(8,128)(2,1)S(1)}, u32[]{:S(2)}, u32[]{:S(2)}) collective-permute-start(bf16[256,512]{1,0:T(8,128)(2,1)S(1)} %shard_map.92), channel_id=1, source_target_pairs={{0,2},{2,0},{1,3},{3,1},{4,6},{6,4},{5,7},{7,5},{8,10},{10,8},{9,1... | collective-permute-start | bytes 786440 | tf_op jit(solution)/shard_map/ppermute | solution.py:569
  52.3 12.4 %collective-permute-start.16 = (bf16[256,512]{1,0:T(8,128)(2,1)S(1)}, bf16[256,512]{1,0:T(8,128)(2,1)S(1)}, u32[]{:S(2)}, u32[]{:S(2)}) collective-permute-start(bf16[256,512]{1,0:T(8,128)(2,1)S(1)} %shard_map.91), channel_id=1, source_target_pairs={{0,2},{2,0},{1,3},{3,1},{4,6},{6,4},{5,7},{7,5},{8,10},{10,8},{9,1... | collective-permute-start | bytes 786440 | tf_op jit(solution)/shard_map/ppermute | solution.py:569
  54.2 10.4 %collective-permute-start.14 = (bf16[256,1024]{1,0:T(8,128)(2,1)S(1)}, bf16[256,1024]{1,0:T(8,128)(2,1)S(1)}, u32[]{:S(2)}, u32[]{:S(2)}) collective-permute-start(bf16[256,1024]{1,0:T(8,128)(2,1)S(1)} %get-tuple-element.58), channel_id=1, source_target_pairs={{0,1},{1,0},{2,3},{3,2},{4,5},{5,4},{6,7},{7,6},{8,9},{9,8},{10,11... | collective-permute-start | bytes 1572872 | tf_op jit(solution)/shard_map/ppermute | solution.py:572

commit v7 on v4

--- a/solution.py
+++ b/solution.py
@@ -97,7 +97,7 @@
     half = n_peers // 2
     near, far = list(range(1, half)), list(range(half, n_peers))
     if back:
-        return [0, near[0]] + far[:3] + [near[1]] + far[3:] + near[2:]
+        return [0, near[0]] + far[2:] + near[1:] + far[:2]
     return [0, near[0], far[0], near[1], far[1]] + near[2:] + far[2:]
 
 

time: 65.4 us -> 65.9 us (level)
  waiting for transfers between devices: 20 us -> 21.3 us
  starting transfers between devices: 32.7 us -> 31.9 us
    ppermute x14, waiting for transfers between devices: 9.24 us -> 10.6 us  [exchange(): lax.ppermute(block, 'seq', [(i, i ^ slot) for i in range(n_peers)])]
    ppermute x14, starting transfers between devices: 29.9 us -> 29.1 us  [exchange(): lax.ppermute(block, 'seq', [(i, i ^ slot) for i in range(n_peers)])]
  transfers between devices with their start and end apart: 19 -> 19, of which waited for: 10 -> 11; matrix products, arithmetic and copies ran while one was open for 0% -> 0% of each run, Pallas kernels for 11% -> 11%
where the time goes in v7:
time: 65.9 us; the launch traced here: 65.8 us
  starting transfers between devices  31.9 us (48%)
  waiting for transfers between devices  21.3 us (32%)
  Pallas kernels  12.3 us (19%)
    ppermute x14, starting transfers between devices, exchange(): lax.ppermute(block, 'seq', [(i, i ^ slot) for i in range(n_peers)])  29.1 us
    ppermute x14, waiting for transfers between devices, exchange(): lax.ppermute(block, 'seq', [(i, i ^ slot) for i in range(n_peers)])  10.6 us
    ppermute x2, waiting for transfers between devices, body(): lax.ppermute(add(*pair), 'fsdp', across)  10.4 us
    pallas_call x1, Pallas kernels, spectra(): pl.pallas_call(functools.partial(spectra_kernel, n_peers), in_specs=[pl.B...  3.37 us
    pallas_call x1, Pallas kernels, conv_fast(): pl.pallas_call(conv_kernel, in_specs=[whole] * 6, out_specs=[whole] * n_b...  2.26 us
    ppermute x2, starting transfers between devices, body(): lax.ppermute(add(*pair), 'fsdp', across)  2.16 us
    pallas_call x1, Pallas kernels, pre(): pl.pallas_call(functools.partial(pre_kernel, n_peers), in_specs=[pl.Block...  1.77 us
    pallas_call x1, Pallas kernels, gate_early(): pl.pallas_call(functools.partial(gate_early_kernel, n_peers), in_specs=[w...  1.73 us
  transfers between devices with their start and end apart: 19, of which 11 were waited for; matrix products, arithmetic and copies ran while one was open for 0% of the time, Pallas kernels for 11%

profile of v7, /device:TPU:0, one launch (start us, length us, event | category | flops | bytes accessed | tf_op | source)
XLA Modules:
  0.0 65.8 jit_solution(12666598406202445369)
XLA Ops:
  0.0 1.8 %shard_map.82 = (bf16[256,256]{1,0:T(8,128)(2,1)S(1)}, bf16[256,256]{1,0:T(8,128)(2,1)S(1)}, bf16[256,256]{1,0:T(8,128)(2,1)S(1)}, bf16[256,256]{1,0:T(8,128)(2,...) custom-call(bf16[256,1024]{1,0:T(8,128)(2,1)} %keys_ref.3, ...), custom_call_target="tpu_custom_call" | custom-call | flops 262144 | bytes 3145728 | tf_op jit(solution)/shard_map/pallas_call | solution.py:78
  1.8 3.0 %collective-permute-start = (bf16[256,256]{1,0:T(8,128)(2,1)S(1)}, bf16[256,256]{1,0:T(8,128)(2,1)S(1)}, u32[]{:S(2)}, u32[]{:S(2)}) collective-permute-start(bf16[256,256]{1,0:T(8,128)(2,1)S(1)} %get-tuple-element.35), channel_id=1, source_target_pairs={{0,4},{4,0},{8,12},{12,8},{16,20},{20,16},{24,28},{28,24},{1,5},{5... | collective-permute-start | bytes 393224 | tf_op jit(solution)/shard_map/ppermute | solution.py:106
  4.8 2.6 %collective-permute-start.1 = (bf16[256,256]{1,0:T(8,128)(2,1)S(1)}, bf16[256,256]{1,0:T(8,128)(2,1)S(1)}, u32[]{:S(2)}, u32[]{:S(2)}) collective-permute-start(bf16[256,256]{1,0:T(8,128)(2,1)S(1)} %get-tuple-element.36), channel_id=1, source_target_pairs={{0,16},{4,20},{8,24},{12,28},{16,0},{20,4},{24,8},{28,12},{1,17},{... | collective-permute-start | bytes 393224 | tf_op jit(solution)/shard_map/ppermute | solution.py:106
  7.4 1.6 %collective-permute-start.2 = (bf16[256,256]{1,0:T(8,128)(2,1)S(1)}, bf16[256,256]{1,0:T(8,128)(2,1)S(1)}, u32[]{:S(2)}, u32[]{:S(2)}) collective-permute-start(bf16[256,256]{1,0:T(8,128)(2,1)S(1)} %get-tuple-element.37), channel_id=1, source_target_pairs={{0,8},{4,12},{8,0},{12,4},{16,24},{20,28},{24,16},{28,20},{1,9},{5... | collective-permute-start | bytes 393224 | tf_op jit(solution)/shard_map/ppermute | solution.py:106
  9.3 1.4 %collective-permute-start.4 = (bf16[256,256]{1,0:T(8,128)(2,1)S(1)}, bf16[256,256]{1,0:T(8,128)(2,1)S(1)}, u32[]{:S(2)}, u32[]{:S(2)}) collective-permute-start(bf16[256,256]{1,0:T(8,128)(2,1)S(1)} %get-tuple-element.39), channel_id=1, source_target_pairs={{0,12},{4,8},{8,4},{12,0},{16,28},{20,24},{24,20},{28,16},{1,13},{... | collective-permute-start | bytes 393224 | tf_op jit(solution)/shard_map/ppermute | solution.py:106
  10.7 3.6 %collective-permute-start.5 = (bf16[256,256]{1,0:T(8,128)(2,1)S(1)}, bf16[256,256]{1,0:T(8,128)(2,1)S(1)}, u32[]{:S(2)}, u32[]{:S(2)}) collective-permute-start(bf16[256,256]{1,0:T(8,128)(2,1)S(1)} %get-tuple-element.44), channel_id=1, source_target_pairs={{0,24},{4,28},{8,16},{12,20},{16,8},{20,12},{24,0},{28,4},{1,25},{... | collective-permute-start | bytes 393224 | tf_op jit(solution)/shard_map/ppermute | solution.py:106
  14.3 1.9 %collective-permute-done.1.refs_2_ = bf16[256,256]{1,0:T(8,128)(2,1)S(1)} collective-permute-done((bf16[256,256]{1,0:T(8,128)(2,1)S(1)}, bf16[256,256]{1,0:T(8,128)(2,1)S(1)}, u32[]{:S(2)}, u32[]{:S(2)}) %collective-permute-start.1) | collective-permute-done | bytes 131104 | tf_op jit(solution)/shard_map/ppermute | solution.py:106
  16.1 2.4 %collective-permute-start.6 = (bf16[256,256]{1,0:T(8,128)(2,1)S(1)}, bf16[256,256]{1,0:T(8,128)(2,1)S(1)}, u32[]{:S(2)}, u32[]{:S(2)}) collective-permute-start(bf16[256,256]{1,0:T(8,128)(2,1)S(1)} %get-tuple-element.45), channel_id=1, source_target_pairs={{0,28},{4,24},{8,20},{12,16},{16,12},{20,8},{24,4},{28,0},{1,29},{... | collective-permute-start | bytes 393224 | tf_op jit(solution)/shard_map/ppermute | solution.py:106
  18.5 1.9 %collective-permute-done.3.refs_4_ = bf16[256,256]{1,0:T(8,128)(2,1)S(1)} collective-permute-done((bf16[256,256]{1,0:T(8,128)(2,1)S(1)}, bf16[256,256]{1,0:T(8,128)(2,1)S(1)}, u32[]{:S(2)}, u32[]{:S(2)}) %collective-permute-start.3) | collective-permute-done | bytes 131104 | tf_op jit(solution)/shard_map/ppermute | solution.py:106
  20.4 3.4 %shard_map.83 = (bf16[512,512]{1,0:T(8,128)(2,1)S(1)}, bf16[256,1536]{1,0:T(8,128)(2,1)S(1)}, f32[8,512,256]{2,1,0:T(8,128)S(1)}, f32[8,512,128]{2,1,0:T(8,128)S(1)}) custom-call(bf16[512,512]{1,0:T(8,128)(2,1)} %constant.4.clone.fwd_hbm, bf16[256,1536]{1,0:T(8,128)(2,1)} %constant.5.clone.bwd_hbm, bf16[256,256]{1,0:T(8,128)(2,1)S(1)} %get-tuple-element.34.refs_0_, ...), custom_call_target="tpu_custom_call" | custom-call | flops 805306368 | bytes 4194304 | tf_op jit(solution)/shard_map/pallas_call | solution.py:173
  23.9 0.5 collective-permute-done.5.refs_0_
  24.4 1.4 %collective-permute-done.6.refs_1_ = bf16[256,256]{1,0:T(8,128)(2,1)S(1)} collective-permute-done((bf16[256,256]{1,0:T(8,128)(2,1)S(1)}, bf16[256,256]{1,0:T(8,128)(2,1)S(1)}, u32[]{:S(2)}, u32[]{:S(2)}) %collective-permute-start.6) | collective-permute-done | bytes 131104 | tf_op jit(solution)/shard_map/ppermute | solution.py:106
  25.8 2.3 %shard_map.84 = (bf16[256,128]{1,0:T(8,128)(2,1)S(1)}, bf16[256,128]{1,0:T(8,128)(2,1)S(1)}, bf16[256,128]{1,0:T(8,128)(2,1)S(1)}, bf16[256,128]{1,0:T(8,128)(2,...) custom-call(bf16[512,512]{1,0:T(8,128)(2,1)S(1)} %get-tuple-element., ...), custom_call_target="tpu_custom_call" | custom-call | flops 1073741824 | bytes 4194304 | tf_op jit(solution)/shard_map/pallas_call | solution.py:261
  28.0 5.1 %collective-permute-start.7 = (bf16[256,128]{1,0:T(8,128)(2,1)S(1)}, bf16[256,128]{1,0:T(8,128)(2,1)S(1)}, u32[]{:S(2)}, u32[]{:S(2)}) collective-permute-start(bf16[256,128]{1,0:T(8,128)(2,1)S(1)} %get-tuple-element.47), channel_id=1, source_target_pairs={{0,4},{4,0},{8,12},{12,8},{16,20},{20,16},{24,28},{28,24},{1,5},{5... | collective-permute-start | bytes 196616 | tf_op jit(solution)/shard_map/ppermute | solution.py:106
  33.1 2.6 %collective-permute-start.8 = (bf16[256,128]{1,0:T(8,128)(2,1)S(1)}, bf16[256,128]{1,0:T(8,128)(2,1)S(1)}, u32[]{:S(2)}, u32[]{:S(2)}) collective-permute-start(bf16[256,128]{1,0:T(8,128)(2,1)S(1)} %get-tuple-element.48), channel_id=1, source_target_pairs={{0,24},{4,28},{8,16},{12,20},{16,8},{20,12},{24,0},{28,4},{1,25},{... | collective-permute-start | bytes 196616 | tf_op jit(solution)/shard_map/ppermute | solution.py:106
  35.8 0.7 %collective-permute-start.9 = (bf16[256,128]{1,0:T(8,128)(2,1)S(1)}, bf16[256,128]{1,0:T(8,128)(2,1)S(1)}, u32[]{:S(2)}, u32[]{:S(2)}) collective-permute-start(bf16[256,128]{1,0:T(8,128)(2,1)S(1)} %get-tuple-element.49), channel_id=1, source_target_pairs={{0,28},{4,24},{8,20},{12,16},{16,12},{20,8},{24,4},{28,0},{1,29},{... | collective-permute-start | bytes 196616 | tf_op jit(solution)/shard_map/ppermute | solution.py:106
  36.5 1.3 %collective-permute-start.10 = (bf16[256,128]{1,0:T(8,128)(2,1)S(1)}, bf16[256,128]{1,0:T(8,128)(2,1)S(1)}, u32[]{:S(2)}, u32[]{:S(2)}) collective-permute-start(bf16[256,128]{1,0:T(8,128)(2,1)S(1)} %get-tuple-element.50), channel_id=1, source_target_pairs={{0,8},{4,12},{8,0},{12,4},{16,24},{20,28},{24,16},{28,20},{1,9},{5... | collective-permute-start | bytes 196616 | tf_op jit(solution)/shard_map/ppermute | solution.py:106
  37.8 2.1 %collective-permute-start.11 = (bf16[256,128]{1,0:T(8,128)(2,1)S(1)}, bf16[256,128]{1,0:T(8,128)(2,1)S(1)}, u32[]{:S(2)}, u32[]{:S(2)}) collective-permute-start(bf16[256,128]{1,0:T(8,128)(2,1)S(1)} %get-tuple-element.51), channel_id=1, source_target_pairs={{0,12},{4,8},{8,4},{12,0},{16,28},{20,24},{24,20},{28,16},{1,13},{... | collective-permute-start | bytes 196616 | tf_op jit(solution)/shard_map/ppermute | solution.py:106
  39.9 2.3 %collective-permute-start.12 = (bf16[256,128]{1,0:T(8,128)(2,1)S(1)}, bf16[256,128]{1,0:T(8,128)(2,1)S(1)}, u32[]{:S(2)}, u32[]{:S(2)}) collective-permute-start(bf16[256,128]{1,0:T(8,128)(2,1)S(1)} %get-tuple-element.54), channel_id=1, source_target_pairs={{0,16},{4,20},{8,24},{12,28},{16,0},{20,4},{24,8},{28,12},{1,17},{... | collective-permute-start | bytes 196616 | tf_op jit(solution)/shard_map/ppermute | solution.py:106
  42.3 1.1 %collective-permute-done.9.refs_3_ = bf16[256,128]{1,0:T(8,128)(2,1)S(1)} collective-permute-done((bf16[256,128]{1,0:T(8,128)(2,1)S(1)}, bf16[256,128]{1,0:T(8,128)(2,1)S(1)}, u32[]{:S(2)}, u32[]{:S(2)}) %collective-permute-start.9) | collective-permute-done | bytes 65568 | tf_op jit(solution)/shard_map/ppermute | solution.py:106
  43.4 1.2 %collective-permute-done.11.refs_5_ = bf16[256,128]{1,0:T(8,128)(2,1)S(1)} collective-permute-done((bf16[256,128]{1,0:T(8,128)(2,1)S(1)}, bf16[256,128]{1,0:T(8,128)(2,1)S(1)}, u32[]{:S(2)}, u32[]{:S(2)}) %collective-permute-start.11) | collective-permute-done | bytes 65568 | tf_op jit(solution)/shard_map/ppermute | solution.py:106
  44.6 1.7 %shard_map.85 = (bf16[256,1024]{1,0:T(8,128)(2,1)S(1)}, f32[256,1024]{1,0:T(8,128)S(1)}, f32[256,1024]{1,0:T(8,128)S(1)}) custom-call(bf16[256,1024]{1,0:T(8,128)(2,1)S(1)} %copy-done.3, bf16[256,1024]{1,0:T(8,128)(2,1)S(1)} %copy-done.1, bf16[256,1024]{1,0:T(8,128)(2,1)S(1)} %copy-done.2, f32[1,1024]{1,0:T(1,128)S(1)} %bitcast.1, ...), custom_call_target="tpu_custom_call" | custom-call | flops 1073741824 | bytes 2621440 | tf_op jit(solution)/shard_map/pallas_call | solution.py:342
  46.3 0.3 collective-permute-done.12.refs_0_
  46.7 2.2 %collective-permute-done.13.refs_1_ = bf16[256,128]{1,0:T(8,128)(2,1)S(1)} collective-permute-done((bf16[256,128]{1,0:T(8,128)(2,1)S(1)}, bf16[256,128]{1,0:T(8,128)(2,1)S(1)}, u32[]{:S(2)}, u32[]{:S(2)}) %collective-permute-start.13) | collective-permute-done | bytes 65568 | tf_op jit(solution)/shard_map/ppermute | solution.py:106
  49.6 0.5 collective-permute-start.15
  50.4 0.4 collective-permute-done.17.arrived_ref
  50.9 1.6 %collective-permute-start.18 = (bf16[256,512]{1,0:T(8,128)(2,1)S(1)}, bf16[256,512]{1,0:T(8,128)(2,1)S(1)}, u32[]{:S(2)}, u32[]{:S(2)}) collective-permute-start(bf16[256,512]{1,0:T(8,128)(2,1)S(1)} %shard_map.92), channel_id=1, source_target_pairs={{0,2},{2,0},{1,3},{3,1},{4,6},{6,4},{5,7},{7,5},{8,10},{10,8},{9,1... | collective-permute-start | bytes 786440 | tf_op jit(solution)/shard_map/ppermute | solution.py:568
  52.5 0.6 collective-permute-start.16
  53.2 1.3 %shard_map.88 = (bf16[256,1024]{1,0:T(8,128)(2,1)S(1)}, f32[256,1024]{1,0:T(8,128)S(1)}) custom-call(bf16[256,1024]{1,0:T(8,128)(2,1)S(1)} %shard_map.87.gated_ref, bf16[1024,4096]{1,0:T(8,128)(2,1)S(1)} %copy-done), custom_call_target="tpu_custom_call" | custom-call | flops 1073741824 | bytes 4194304 | tf_op jit(solution)/shard_map/pallas_call | solution.py:445
  54.6 5.5 %collective-permute-done.18.refs_1_ = bf16[256,512]{1,0:T(8,128)(2,1)S(1)} collective-permute-done((bf16[256,512]{1,0:T(8,128)(2,1)S(1)}, bf16[256,512]{1,0:T(8,128)(2,1)S(1)}, u32[]{:S(2)}, u32[]{:S(2)}) %collective-permute-start.18) | collective-permute-done | bytes 262176 | tf_op jit(solution)/shard_map/ppermute | solution.py:568
  60.1 4.8 %collective-permute-done.16.refs_0_ = bf16[256,512]{1,0:T(8,128)(2,1)S(1)} collective-permute-done((bf16[256,512]{1,0:T(8,128)(2,1)S(1)}, bf16[256,512]{1,0:T(8,128)(2,1)S(1)}, u32[]{:S(2)}, u32[]{:S(2)}) %collective-permute-start.16) | collective-permute-done | bytes 262176 | tf_op jit(solution)/shard_map/ppermute | solution.py:568
  64.9 0.9 %shard_map.94 = bf16[256,1024]{1,0:T(8,128)(2,1)} custom-call(f32[256,1024]{1,0:T(8,128)S(1)} %get-tuple-element.57.own_ref, bf16[256,1024]{1,0:T(8,128)(2,1)S(1)} %collective-permute-done.14.near_ref, bf16[256,512]{1,0:T(8,128)(2,1)S(1)} %collective-permute-done.16.refs_0_, bf16[256,512]{1,0:T(8,128)(2,1)S(1)} %collective-permute-done.18.refs_1_, ...), custom_call_target="tpu_custom_call" | custom-call | flops 262144 | bytes 2097152 | tf_op jit(solution)/shard_map/pallas_call | solution.py:512
  (29 shorter events, 1.7 us)
Async XLA Ops:
  1.8 8.9 %collective-permute-start = (bf16[256,256]{1,0:T(8,128)(2,1)S(1)}, bf16[256,256]{1,0:T(8,128)(2,1)S(1)}, u32[]{:S(2)}, u32[]{:S(2)}) collective-permute-start(bf16[256,256]{1,0:T(8,128)(2,1)S(1)} %get-tuple-element.35), channel_id=1, source_target_pairs={{0,4},{4,0},{8,12},{12,8},{16,20},{20,16},{24,28},{28,24},{1,5},{5... | collective-permute-start | bytes 393224 | tf_op jit(solution)/shard_map/ppermute | solution.py:106
  4.8 11.3 %collective-permute-start.1 = (bf16[256,256]{1,0:T(8,128)(2,1)S(1)}, bf16[256,256]{1,0:T(8,128)(2,1)S(1)}, u32[]{:S(2)}, u32[]{:S(2)}) collective-permute-start(bf16[256,256]{1,0:T(8,128)(2,1)S(1)} %get-tuple-element.36), channel_id=1, source_target_pairs={{0,16},{4,20},{8,24},{12,28},{16,0},{20,4},{24,8},{28,12},{1,17},{... | collective-permute-start | bytes 393224 | tf_op jit(solution)/shard_map/ppermute | solution.py:106
  7.4 11.1 %collective-permute-start.2 = (bf16[256,256]{1,0:T(8,128)(2,1)S(1)}, bf16[256,256]{1,0:T(8,128)(2,1)S(1)}, u32[]{:S(2)}, u32[]{:S(2)}) collective-permute-start(bf16[256,256]{1,0:T(8,128)(2,1)S(1)} %get-tuple-element.37), channel_id=1, source_target_pairs={{0,8},{4,12},{8,0},{12,4},{16,24},{20,28},{24,16},{28,20},{1,9},{5... | collective-permute-start | bytes 393224 | tf_op jit(solution)/shard_map/ppermute | solution.py:106
  9.0 11.5 %collective-permute-start.3 = (bf16[256,256]{1,0:T(8,128)(2,1)S(1)}, bf16[256,256]{1,0:T(8,128)(2,1)S(1)}, u32[]{:S(2)}, u32[]{:S(2)}) collective-permute-start(bf16[256,256]{1,0:T(8,128)(2,1)S(1)} %get-tuple-element.38), channel_id=1, source_target_pairs={{0,20},{4,16},{8,28},{12,24},{16,4},{20,0},{24,12},{28,8},{1,21},{... | collective-permute-start | bytes 393224 | tf_op jit(solution)/shard_map/ppermute | solution.py:106
  9.3 11.2 %collective-permute-start.4 = (bf16[256,256]{1,0:T(8,128)(2,1)S(1)}, bf16[256,256]{1,0:T(8,128)(2,1)S(1)}, u32[]{:S(2)}, u32[]{:S(2)}) collective-permute-start(bf16[256,256]{1,0:T(8,128)(2,1)S(1)} %get-tuple-element.39), channel_id=1, source_target_pairs={{0,12},{4,8},{8,4},{12,0},{16,28},{20,24},{24,20},{28,16},{1,13},{... | collective-permute-start | bytes 393224 | tf_op jit(solution)/shard_map/ppermute | solution.py:106
  10.7 13.7 %collective-permute-start.5 = (bf16[256,256]{1,0:T(8,128)(2,1)S(1)}, bf16[256,256]{1,0:T(8,128)(2,1)S(1)}, u32[]{:S(2)}, u32[]{:S(2)}) collective-permute-start(bf16[256,256]{1,0:T(8,128)(2,1)S(1)} %get-tuple-element.44), channel_id=1, source_target_pairs={{0,24},{4,28},{8,16},{12,20},{16,8},{20,12},{24,0},{28,4},{1,25},{... | collective-permute-start | bytes 393224 | tf_op jit(solution)/shard_map/ppermute | solution.py:106
  16.1 9.6 %collective-permute-start.6 = (bf16[256,256]{1,0:T(8,128)(2,1)S(1)}, bf16[256,256]{1,0:T(8,128)(2,1)S(1)}, u32[]{:S(2)}, u32[]{:S(2)}) collective-permute-start(bf16[256,256]{1,0:T(8,128)(2,1)S(1)} %get-tuple-element.45), channel_id=1, source_target_pairs={{0,28},{4,24},{8,20},{12,16},{16,12},{20,8},{24,4},{28,0},{1,29},{... | collective-permute-start | bytes 393224 | tf_op jit(solution)/shard_map/ppermute | solution.py:106
  20.4 24.1 %copy-start = (bf16[1024,4096]{1,0:T(8,128)(2,1)S(1)}, bf16[1024,4096]{1,0:T(8,128)(2,1)}, u32[]{:S(2)}) copy-start(bf16[1024,4096]{1,0:T(8,128)(2,1)} %weight_ref.9) | copy-start | bytes 25165828
  23.8 20.8 %copy-start.1 = (bf16[256,1024]{1,0:T(8,128)(2,1)S(1)}, bf16[256,1024]{1,0:T(8,128)(2,1)}, u32[]{:S(2)}) copy-start(bf16[256,1024]{1,0:T(8,128)(2,1)} %keys_ref.3) | copy-start | bytes 1572868
  23.8 20.8 %copy-start.2 = (bf16[256,1024]{1,0:T(8,128)(2,1)S(1)}, bf16[256,1024]{1,0:T(8,128)(2,1)}, u32[]{:S(2)}) copy-start(bf16[256,1024]{1,0:T(8,128)(2,1)} %values_ref.3) | copy-start | bytes 1572868
  23.8 20.7 %copy-start.3 = (bf16[256,1024]{1,0:T(8,128)(2,1)S(1)}, bf16[256,1024]{1,0:T(8,128)(2,1)}, u32[]{:S(2)}) copy-start(bf16[256,1024]{1,0:T(8,128)(2,1)} %queries_ref.3) | copy-start | bytes 1572868
  23.9 20.7 %copy-start.4 = (f32[1024]{0:T(1024)S(1)}, f32[1024]{0:T(1024)}, u32[]{:S(2)}) copy-start(f32[1024]{0:T(1024)} %param.12) | copy-start | bytes 12292
  28.0 11.8 %collective-permute-start.7 = (bf16[256,128]{1,0:T(8,128)(2,1)S(1)}, bf16[256,128]{1,0:T(8,128)(2,1)S(1)}, u32[]{:S(2)}, u32[]{:S(2)}) collective-permute-start(bf16[256,128]{1,0:T(8,128)(2,1)S(1)} %get-tuple-element.47), channel_id=1, source_target_pairs={{0,4},{4,0},{8,12},{12,8},{16,20},{20,16},{24,28},{28,24},{1,5},{5... | collective-permute-start | bytes 196616 | tf_op jit(solution)/shard_map/ppermute | solution.py:106
  33.1 9.0 %collective-permute-start.8 = (bf16[256,128]{1,0:T(8,128)(2,1)S(1)}, bf16[256,128]{1,0:T(8,128)(2,1)S(1)}, u32[]{:S(2)}, u32[]{:S(2)}) collective-permute-start(bf16[256,128]{1,0:T(8,128)(2,1)S(1)} %get-tuple-element.48), channel_id=1, source_target_pairs={{0,24},{4,28},{8,16},{12,20},{16,8},{20,12},{24,0},{28,4},{1,25},{... | collective-permute-start | bytes 196616 | tf_op jit(solution)/shard_map/ppermute | solution.py:106
  35.8 7.6 %collective-permute-start.9 = (bf16[256,128]{1,0:T(8,128)(2,1)S(1)}, bf16[256,128]{1,0:T(8,128)(2,1)S(1)}, u32[]{:S(2)}, u32[]{:S(2)}) collective-permute-start(bf16[256,128]{1,0:T(8,128)(2,1)S(1)} %get-tuple-element.49), channel_id=1, source_target_pairs={{0,28},{4,24},{8,20},{12,16},{16,12},{20,8},{24,4},{28,0},{1,29},{... | collective-permute-start | bytes 196616 | tf_op jit(solution)/shard_map/ppermute | solution.py:106
  36.5 6.9 %collective-permute-start.10 = (bf16[256,128]{1,0:T(8,128)(2,1)S(1)}, bf16[256,128]{1,0:T(8,128)(2,1)S(1)}, u32[]{:S(2)}, u32[]{:S(2)}) collective-permute-start(bf16[256,128]{1,0:T(8,128)(2,1)S(1)} %get-tuple-element.50), channel_id=1, source_target_pairs={{0,8},{4,12},{8,0},{12,4},{16,24},{20,28},{24,16},{28,20},{1,9},{5... | collective-permute-start | bytes 196616 | tf_op jit(solution)/shard_map/ppermute | solution.py:106
  37.8 6.8 %collective-permute-start.11 = (bf16[256,128]{1,0:T(8,128)(2,1)S(1)}, bf16[256,128]{1,0:T(8,128)(2,1)S(1)}, u32[]{:S(2)}, u32[]{:S(2)}) collective-permute-start(bf16[256,128]{1,0:T(8,128)(2,1)S(1)} %get-tuple-element.51), channel_id=1, source_target_pairs={{0,12},{4,8},{8,4},{12,0},{16,28},{20,24},{24,20},{28,16},{1,13},{... | collective-permute-start | bytes 196616 | tf_op jit(solution)/shard_map/ppermute | solution.py:106
  39.9 6.8 %collective-permute-start.12 = (bf16[256,128]{1,0:T(8,128)(2,1)S(1)}, bf16[256,128]{1,0:T(8,128)(2,1)S(1)}, u32[]{:S(2)}, u32[]{:S(2)}) collective-permute-start(bf16[256,128]{1,0:T(8,128)(2,1)S(1)} %get-tuple-element.54), channel_id=1, source_target_pairs={{0,16},{4,20},{8,24},{12,28},{16,0},{20,4},{24,8},{28,12},{1,17},{... | collective-permute-start | bytes 196616 | tf_op jit(solution)/shard_map/ppermute | solution.py:106
  42.1 6.8 %collective-permute-start.13 = (bf16[256,128]{1,0:T(8,128)(2,1)S(1)}, bf16[256,128]{1,0:T(8,128)(2,1)S(1)}, u32[]{:S(2)}, u32[]{:S(2)}) collective-permute-start(bf16[256,128]{1,0:T(8,128)(2,1)S(1)} %get-tuple-element.55), channel_id=1, source_target_pairs={{0,20},{4,16},{8,28},{12,24},{16,4},{20,0},{24,12},{28,8},{1,21},{... | collective-permute-start | bytes 196616 | tf_op jit(solution)/shard_map/ppermute | solution.py:106
  49.2 1.6 %collective-permute-start.17 = (bf16[256,512]{1,0:T(8,128)(2,1)S(1)}, bf16[256,512]{1,0:T(8,128)(2,1)S(1)}, u32[]{:S(2)}, u32[]{:S(2)}) collective-permute-start(bf16[256,512]{1,0:T(8,128)(2,1)S(1)} %get-tuple-element.62), channel_id=1, source_target_pairs={{0,1},{1,0},{2,3},{3,2},{4,5},{5,4},{6,7},{7,6},{8,9},{9,8},{10,11... | collective-permute-start | bytes 786440 | tf_op jit(solution)/shard_map/ppermute | solution.py:567
  49.6 2.9 %collective-permute-start.15 = (bf16[256,512]{1,0:T(8,128)(2,1)S(1)}, bf16[256,512]{1,0:T(8,128)(2,1)S(1)}, u32[]{:S(2)}, u32[]{:S(2)}) collective-permute-start(bf16[256,512]{1,0:T(8,128)(2,1)S(1)} %shard_map.90), channel_id=1, source_target_pairs={{0,1},{1,0},{2,3},{3,2},{4,5},{5,4},{6,7},{7,6},{8,9},{9,8},{10,11... | collective-permute-start | bytes 786440 | tf_op jit(solution)/shard_map/ppermute | solution.py:567
  50.9 9.2 %collective-permute-start.18 = (bf16[256,512]{1,0:T(8,128)(2,1)S(1)}, bf16[256,512]{1,0:T(8,128)(2,1)S(1)}, u32[]{:S(2)}, u32[]{:S(2)}) collective-permute-start(bf16[256,512]{1,0:T(8,128)(2,1)S(1)} %shard_map.92), channel_id=1, source_target_pairs={{0,2},{2,0},{1,3},{3,1},{4,6},{6,4},{5,7},{7,5},{8,10},{10,8},{9,1... | collective-permute-start | bytes 786440 | tf_op jit(solution)/shard_map/ppermute | solution.py:568
  52.5 12.4 %collective-permute-start.16 = (bf16[256,512]{1,0:T(8,128)(2,1)S(1)}, bf16[256,512]{1,0:T(8,128)(2,1)S(1)}, u32[]{:S(2)}, u32[]{:S(2)}) collective-permute-start(bf16[256,512]{1,0:T(8,128)(2,1)S(1)} %shard_map.91), channel_id=1, source_target_pairs={{0,2},{2,0},{1,3},{3,1},{4,6},{6,4},{5,7},{7,5},{8,10},{10,8},{9,1... | collective-permute-start | bytes 786440 | tf_op jit(solution)/shard_map/ppermute | solution.py:568
  54.5 10.4 %collective-permute-start.14 = (bf16[256,1024]{1,0:T(8,128)(2,1)S(1)}, bf16[256,1024]{1,0:T(8,128)(2,1)S(1)}, u32[]{:S(2)}, u32[]{:S(2)}) collective-permute-start(bf16[256,1024]{1,0:T(8,128)(2,1)S(1)} %get-tuple-element.58), channel_id=1, source_target_pairs={{0,1},{1,0},{2,3},{3,2},{4,5},{5,4},{6,7},{7,6},{8,9},{9,8},{10,11... | collective-permute-start | bytes 1572872 | tf_op jit(solution)/shard_map/ppermute | solution.py:571

commit v8 on v7

--- a/solution.py
+++ b/solution.py
@@ -98,7 +98,7 @@
     near, far = list(range(1, half)), list(range(half, n_peers))
     if back:
         return [0, near[0]] + far[2:] + near[1:] + far[:2]
-    return [0, near[0], far[0], near[1], far[1]] + near[2:] + far[2:]
+    return [0, far[0], near[0]] + near[:0:-1] + far[1:]
 
 
 def exchange(blocks, n_peers, back):

time: 65.9 us -> 64.9 us (0.985)
  no operation moved by 1% of the time
where the time goes in v8:
time: 64.9 us; the launch traced here: 64.8 us
  starting transfers between devices  31.4 us (48%)
  waiting for transfers between devices  20.8 us (32%)
  Pallas kernels  12.3 us (19%)
    ppermute x14, starting transfers between devices, exchange(): lax.ppermute(block, 'seq', [(i, i ^ slot) for i in range(n_peers)])  28.6 us
    ppermute x2, waiting for transfers between devices, body(): lax.ppermute(add(*pair), 'fsdp', across)  10.4 us
    ppermute x14, waiting for transfers between devices, exchange(): lax.ppermute(block, 'seq', [(i, i ^ slot) for i in range(n_peers)])  10 us
    pallas_call x1, Pallas kernels, spectra(): pl.pallas_call(functools.partial(spectra_kernel, n_peers), in_specs=[pl.B...  3.36 us
    pallas_call x1, Pallas kernels, conv_fast(): pl.pallas_call(conv_kernel, in_specs=[whole] * 6, out_specs=[whole] * n_b...  2.26 us
    ppermute x2, starting transfers between devices, body(): lax.ppermute(add(*pair), 'fsdp', across)  2.16 us
    pallas_call x1, Pallas kernels, pre(): pl.pallas_call(functools.partial(pre_kernel, n_peers), in_specs=[pl.Block...  1.77 us
    pallas_call x1, Pallas kernels, gate_early(): pl.pallas_call(functools.partial(gate_early_kernel, n_peers), in_specs=[w...  1.73 us
  transfers between devices with their start and end apart: 19, of which 11 were waited for; matrix products, arithmetic and copies ran while one was open for 0% of the time, Pallas kernels for 11%

profile of v8, /device:TPU:0, one launch (start us, length us, event | category | flops | bytes accessed | tf_op | source)
XLA Modules:
  0.0 64.8 jit_solution(12653015547225341765)
XLA Ops:
  0.0 1.8 %shard_map.82 = (bf16[256,256]{1,0:T(8,128)(2,1)S(1)}, bf16[256,256]{1,0:T(8,128)(2,1)S(1)}, bf16[256,256]{1,0:T(8,128)(2,1)S(1)}, bf16[256,256]{1,0:T(8,128)(2,...) custom-call(bf16[256,1024]{1,0:T(8,128)(2,1)} %keys_ref.3, ...), custom_call_target="tpu_custom_call" | custom-call | flops 262144 | bytes 3145728 | tf_op jit(solution)/shard_map/pallas_call | solution.py:78
  1.8 4.1 %collective-permute-start = (bf16[256,256]{1,0:T(8,128)(2,1)S(1)}, bf16[256,256]{1,0:T(8,128)(2,1)S(1)}, u32[]{:S(2)}, u32[]{:S(2)}) collective-permute-start(bf16[256,256]{1,0:T(8,128)(2,1)S(1)} %get-tuple-element.35), channel_id=1, source_target_pairs={{0,16},{4,20},{8,24},{12,28},{16,0},{20,4},{24,8},{28,12},{1,17},{... | collective-permute-start | bytes 393224 | tf_op jit(solution)/shard_map/ppermute | solution.py:106
  5.9 1.5 %collective-permute-start.1 = (bf16[256,256]{1,0:T(8,128)(2,1)S(1)}, bf16[256,256]{1,0:T(8,128)(2,1)S(1)}, u32[]{:S(2)}, u32[]{:S(2)}) collective-permute-start(bf16[256,256]{1,0:T(8,128)(2,1)S(1)} %get-tuple-element.36), channel_id=1, source_target_pairs={{0,4},{4,0},{8,12},{12,8},{16,20},{20,16},{24,28},{28,24},{1,5},{5... | collective-permute-start | bytes 393224 | tf_op jit(solution)/shard_map/ppermute | solution.py:106
  7.4 1.5 %collective-permute-start.2 = (bf16[256,256]{1,0:T(8,128)(2,1)S(1)}, bf16[256,256]{1,0:T(8,128)(2,1)S(1)}, u32[]{:S(2)}, u32[]{:S(2)}) collective-permute-start(bf16[256,256]{1,0:T(8,128)(2,1)S(1)} %get-tuple-element.37), channel_id=1, source_target_pairs={{0,12},{4,8},{8,4},{12,0},{16,28},{20,24},{24,20},{28,16},{1,13},{... | collective-permute-start | bytes 393224 | tf_op jit(solution)/shard_map/ppermute | solution.py:106
  9.4 1.3 %collective-permute-start.4 = (bf16[256,256]{1,0:T(8,128)(2,1)S(1)}, bf16[256,256]{1,0:T(8,128)(2,1)S(1)}, u32[]{:S(2)}, u32[]{:S(2)}) collective-permute-start(bf16[256,256]{1,0:T(8,128)(2,1)S(1)} %get-tuple-element.39), channel_id=1, source_target_pairs={{0,20},{4,16},{8,28},{12,24},{16,4},{20,0},{24,12},{28,8},{1,21},{... | collective-permute-start | bytes 393224 | tf_op jit(solution)/shard_map/ppermute | solution.py:106
  10.7 1.6 %collective-permute-done.refs_1_ = bf16[256,256]{1,0:T(8,128)(2,1)S(1)} collective-permute-done((bf16[256,256]{1,0:T(8,128)(2,1)S(1)}, bf16[256,256]{1,0:T(8,128)(2,1)S(1)}, u32[]{:S(2)}, u32[]{:S(2)}) %collective-permute-start) | collective-permute-done | bytes 131104 | tf_op jit(solution)/shard_map/ppermute | solution.py:106
  12.3 3.6 %collective-permute-start.5 = (bf16[256,256]{1,0:T(8,128)(2,1)S(1)}, bf16[256,256]{1,0:T(8,128)(2,1)S(1)}, u32[]{:S(2)}, u32[]{:S(2)}) collective-permute-start(bf16[256,256]{1,0:T(8,128)(2,1)S(1)} %get-tuple-element.44), channel_id=1, source_target_pairs={{0,24},{4,28},{8,16},{12,20},{16,8},{20,12},{24,0},{28,4},{1,25},{... | collective-permute-start | bytes 393224 | tf_op jit(solution)/shard_map/ppermute | solution.py:106
  15.9 1.8 %collective-permute-start.6 = (bf16[256,256]{1,0:T(8,128)(2,1)S(1)}, bf16[256,256]{1,0:T(8,128)(2,1)S(1)}, u32[]{:S(2)}, u32[]{:S(2)}) collective-permute-start(bf16[256,256]{1,0:T(8,128)(2,1)S(1)} %get-tuple-element.45), channel_id=1, source_target_pairs={{0,28},{4,24},{8,20},{12,16},{16,12},{20,8},{24,4},{28,0},{1,29},{... | collective-permute-start | bytes 393224 | tf_op jit(solution)/shard_map/ppermute | solution.py:106
  17.7 0.8 %collective-permute-done.2.refs_3_ = bf16[256,256]{1,0:T(8,128)(2,1)S(1)} collective-permute-done((bf16[256,256]{1,0:T(8,128)(2,1)S(1)}, bf16[256,256]{1,0:T(8,128)(2,1)S(1)}, u32[]{:S(2)}, u32[]{:S(2)}) %collective-permute-start.2) | collective-permute-done | bytes 131104 | tf_op jit(solution)/shard_map/ppermute | solution.py:106
  18.5 0.9 %collective-permute-done.3.refs_4_ = bf16[256,256]{1,0:T(8,128)(2,1)S(1)} collective-permute-done((bf16[256,256]{1,0:T(8,128)(2,1)S(1)}, bf16[256,256]{1,0:T(8,128)(2,1)S(1)}, u32[]{:S(2)}, u32[]{:S(2)}) %collective-permute-start.3) | collective-permute-done | bytes 131104 | tf_op jit(solution)/shard_map/ppermute | solution.py:106
  19.5 3.4 %shard_map.83 = (bf16[512,512]{1,0:T(8,128)(2,1)S(1)}, bf16[256,1536]{1,0:T(8,128)(2,1)S(1)}, f32[8,512,256]{2,1,0:T(8,128)S(1)}, f32[8,512,128]{2,1,0:T(8,128)S(1)}) custom-call(bf16[512,512]{1,0:T(8,128)(2,1)} %constant.4.clone.fwd_hbm, bf16[256,1536]{1,0:T(8,128)(2,1)} %constant.5.clone.bwd_hbm, bf16[256,256]{1,0:T(8,128)(2,1)S(1)} %get-tuple-element.34.refs_0_, ...), custom_call_target="tpu_custom_call" | custom-call | flops 805306368 | bytes 4194304 | tf_op jit(solution)/shard_map/pallas_call | solution.py:173
  22.9 2.8 %collective-permute-done.6.refs_1_ = bf16[256,256]{1,0:T(8,128)(2,1)S(1)} collective-permute-done((bf16[256,256]{1,0:T(8,128)(2,1)S(1)}, bf16[256,256]{1,0:T(8,128)(2,1)S(1)}, u32[]{:S(2)}, u32[]{:S(2)}) %collective-permute-start.6) | collective-permute-done | bytes 131104 | tf_op jit(solution)/shard_map/ppermute | solution.py:106
  25.7 2.3 %shard_map.84 = (bf16[256,128]{1,0:T(8,128)(2,1)S(1)}, bf16[256,128]{1,0:T(8,128)(2,1)S(1)}, bf16[256,128]{1,0:T(8,128)(2,1)S(1)}, bf16[256,128]{1,0:T(8,128)(2,...) custom-call(bf16[512,512]{1,0:T(8,128)(2,1)S(1)} %get-tuple-element., ...), custom_call_target="tpu_custom_call" | custom-call | flops 1073741824 | bytes 4194304 | tf_op jit(solution)/shard_map/pallas_call | solution.py:261
  28.0 5.1 %collective-permute-start.7 = (bf16[256,128]{1,0:T(8,128)(2,1)S(1)}, bf16[256,128]{1,0:T(8,128)(2,1)S(1)}, u32[]{:S(2)}, u32[]{:S(2)}) collective-permute-start(bf16[256,128]{1,0:T(8,128)(2,1)S(1)} %get-tuple-element.47), channel_id=1, source_target_pairs={{0,4},{4,0},{8,12},{12,8},{16,20},{20,16},{24,28},{28,24},{1,5},{5... | collective-permute-start | bytes 196616 | tf_op jit(solution)/shard_map/ppermute | solution.py:106
  33.1 1.9 %collective-permute-start.8 = (bf16[256,128]{1,0:T(8,128)(2,1)S(1)}, bf16[256,128]{1,0:T(8,128)(2,1)S(1)}, u32[]{:S(2)}, u32[]{:S(2)}) collective-permute-start(bf16[256,128]{1,0:T(8,128)(2,1)S(1)} %get-tuple-element.48), channel_id=1, source_target_pairs={{0,24},{4,28},{8,16},{12,20},{16,8},{20,12},{24,0},{28,4},{1,25},{... | collective-permute-start | bytes 196616 | tf_op jit(solution)/shard_map/ppermute | solution.py:106
  34.9 1.5 %collective-permute-start.9 = (bf16[256,128]{1,0:T(8,128)(2,1)S(1)}, bf16[256,128]{1,0:T(8,128)(2,1)S(1)}, u32[]{:S(2)}, u32[]{:S(2)}) collective-permute-start(bf16[256,128]{1,0:T(8,128)(2,1)S(1)} %get-tuple-element.49), channel_id=1, source_target_pairs={{0,28},{4,24},{8,20},{12,16},{16,12},{20,8},{24,4},{28,0},{1,29},{... | collective-permute-start | bytes 196616 | tf_op jit(solution)/shard_map/ppermute | solution.py:106
  36.4 1.1 %collective-permute-start.10 = (bf16[256,128]{1,0:T(8,128)(2,1)S(1)}, bf16[256,128]{1,0:T(8,128)(2,1)S(1)}, u32[]{:S(2)}, u32[]{:S(2)}) collective-permute-start(bf16[256,128]{1,0:T(8,128)(2,1)S(1)} %get-tuple-element.50), channel_id=1, source_target_pairs={{0,8},{4,12},{8,0},{12,4},{16,24},{20,28},{24,16},{28,20},{1,9},{5... | collective-permute-start | bytes 196616 | tf_op jit(solution)/shard_map/ppermute | solution.py:106
  37.5 2.3 %collective-permute-start.11 = (bf16[256,128]{1,0:T(8,128)(2,1)S(1)}, bf16[256,128]{1,0:T(8,128)(2,1)S(1)}, u32[]{:S(2)}, u32[]{:S(2)}) collective-permute-start(bf16[256,128]{1,0:T(8,128)(2,1)S(1)} %get-tuple-element.51), channel_id=1, source_target_pairs={{0,12},{4,8},{8,4},{12,0},{16,28},{20,24},{24,20},{28,16},{1,13},{... | collective-permute-start | bytes 196616 | tf_op jit(solution)/shard_map/ppermute | solution.py:106
  39.8 1.1 %collective-permute-start.12 = (bf16[256,128]{1,0:T(8,128)(2,1)S(1)}, bf16[256,128]{1,0:T(8,128)(2,1)S(1)}, u32[]{:S(2)}, u32[]{:S(2)}) collective-permute-start(bf16[256,128]{1,0:T(8,128)(2,1)S(1)} %get-tuple-element.54), channel_id=1, source_target_pairs={{0,16},{4,20},{8,24},{12,28},{16,0},{20,4},{24,8},{28,12},{1,17},{... | collective-permute-start | bytes 196616 | tf_op jit(solution)/shard_map/ppermute | solution.py:106
  41.0 1.3 %collective-permute-start.13 = (bf16[256,128]{1,0:T(8,128)(2,1)S(1)}, bf16[256,128]{1,0:T(8,128)(2,1)S(1)}, u32[]{:S(2)}, u32[]{:S(2)}) collective-permute-start(bf16[256,128]{1,0:T(8,128)(2,1)S(1)} %get-tuple-element.55), channel_id=1, source_target_pairs={{0,20},{4,16},{8,28},{12,24},{16,4},{20,0},{24,12},{28,8},{1,21},{... | collective-permute-start | bytes 196616 | tf_op jit(solution)/shard_map/ppermute | solution.py:106
  42.2 0.5 collective-permute-done.9.refs_3_
  42.7 1.9 %collective-permute-done.11.refs_5_ = bf16[256,128]{1,0:T(8,128)(2,1)S(1)} collective-permute-done((bf16[256,128]{1,0:T(8,128)(2,1)S(1)}, bf16[256,128]{1,0:T(8,128)(2,1)S(1)}, u32[]{:S(2)}, u32[]{:S(2)}) %collective-permute-start.11) | collective-permute-done | bytes 65568 | tf_op jit(solution)/shard_map/ppermute | solution.py:106
  44.6 1.7 %shard_map.85 = (bf16[256,1024]{1,0:T(8,128)(2,1)S(1)}, f32[256,1024]{1,0:T(8,128)S(1)}, f32[256,1024]{1,0:T(8,128)S(1)}) custom-call(bf16[256,1024]{1,0:T(8,128)(2,1)S(1)} %copy-done.3, bf16[256,1024]{1,0:T(8,128)(2,1)S(1)} %copy-done.1, bf16[256,1024]{1,0:T(8,128)(2,1)S(1)} %copy-done.2, f32[1,1024]{1,0:T(1,128)S(1)} %bitcast.1, ...), custom_call_target="tpu_custom_call" | custom-call | flops 1073741824 | bytes 2621440 | tf_op jit(solution)/shard_map/pallas_call | solution.py:342
  46.4 1.0 %collective-permute-done.12.refs_0_ = bf16[256,128]{1,0:T(8,128)(2,1)S(1)} collective-permute-done((bf16[256,128]{1,0:T(8,128)(2,1)S(1)}, bf16[256,128]{1,0:T(8,128)(2,1)S(1)}, u32[]{:S(2)}, u32[]{:S(2)}) %collective-permute-start.12) | collective-permute-done | bytes 65568 | tf_op jit(solution)/shard_map/ppermute | solution.py:106
  47.4 0.5 collective-permute-done.13.refs_1_
  48.5 0.5 collective-permute-start.15
  49.8 1.6 %collective-permute-start.18 = (bf16[256,512]{1,0:T(8,128)(2,1)S(1)}, bf16[256,512]{1,0:T(8,128)(2,1)S(1)}, u32[]{:S(2)}, u32[]{:S(2)}) collective-permute-start(bf16[256,512]{1,0:T(8,128)(2,1)S(1)} %shard_map.92), channel_id=1, source_target_pairs={{0,2},{2,0},{1,3},{3,1},{4,6},{6,4},{5,7},{7,5},{8,10},{10,8},{9,1... | collective-permute-start | bytes 786440 | tf_op jit(solution)/shard_map/ppermute | solution.py:568
  51.5 0.6 collective-permute-start.16
  52.1 1.3 %shard_map.88 = (bf16[256,1024]{1,0:T(8,128)(2,1)S(1)}, f32[256,1024]{1,0:T(8,128)S(1)}) custom-call(bf16[256,1024]{1,0:T(8,128)(2,1)S(1)} %shard_map.87.gated_ref, bf16[1024,4096]{1,0:T(8,128)(2,1)S(1)} %copy-done), custom_call_target="tpu_custom_call" | custom-call | flops 1073741824 | bytes 4194304 | tf_op jit(solution)/shard_map/pallas_call | solution.py:445
  53.5 5.5 %collective-permute-done.18.refs_1_ = bf16[256,512]{1,0:T(8,128)(2,1)S(1)} collective-permute-done((bf16[256,512]{1,0:T(8,128)(2,1)S(1)}, bf16[256,512]{1,0:T(8,128)(2,1)S(1)}, u32[]{:S(2)}, u32[]{:S(2)}) %collective-permute-start.18) | collective-permute-done | bytes 262176 | tf_op jit(solution)/shard_map/ppermute | solution.py:568
  59.1 4.8 %collective-permute-done.16.refs_0_ = bf16[256,512]{1,0:T(8,128)(2,1)S(1)} collective-permute-done((bf16[256,512]{1,0:T(8,128)(2,1)S(1)}, bf16[256,512]{1,0:T(8,128)(2,1)S(1)}, u32[]{:S(2)}, u32[]{:S(2)}) %collective-permute-start.16) | collective-permute-done | bytes 262176 | tf_op jit(solution)/shard_map/ppermute | solution.py:568
  63.9 0.9 %shard_map.94 = bf16[256,1024]{1,0:T(8,128)(2,1)} custom-call(f32[256,1024]{1,0:T(8,128)S(1)} %get-tuple-element.57.own_ref, bf16[256,1024]{1,0:T(8,128)(2,1)S(1)} %collective-permute-done.14.near_ref, bf16[256,512]{1,0:T(8,128)(2,1)S(1)} %collective-permute-done.16.refs_0_, bf16[256,512]{1,0:T(8,128)(2,1)S(1)} %collective-permute-done.18.refs_1_, ...), custom_call_target="tpu_custom_call" | custom-call | flops 262144 | bytes 2097152 | tf_op jit(solution)/shard_map/pallas_call | solution.py:512
  (29 shorter events, 2.1 us)
Async XLA Ops:
  1.8 10.5 %collective-permute-start = (bf16[256,256]{1,0:T(8,128)(2,1)S(1)}, bf16[256,256]{1,0:T(8,128)(2,1)S(1)}, u32[]{:S(2)}, u32[]{:S(2)}) collective-permute-start(bf16[256,256]{1,0:T(8,128)(2,1)S(1)} %get-tuple-element.35), channel_id=1, source_target_pairs={{0,16},{4,20},{8,24},{12,28},{16,0},{20,4},{24,8},{28,12},{1,17},{... | collective-permute-start | bytes 393224 | tf_op jit(solution)/shard_map/ppermute | solution.py:106
  5.9 10.0 %collective-permute-start.1 = (bf16[256,256]{1,0:T(8,128)(2,1)S(1)}, bf16[256,256]{1,0:T(8,128)(2,1)S(1)}, u32[]{:S(2)}, u32[]{:S(2)}) collective-permute-start(bf16[256,256]{1,0:T(8,128)(2,1)S(1)} %get-tuple-element.36), channel_id=1, source_target_pairs={{0,4},{4,0},{8,12},{12,8},{16,20},{20,16},{24,28},{28,24},{1,5},{5... | collective-permute-start | bytes 393224 | tf_op jit(solution)/shard_map/ppermute | solution.py:106
  7.4 11.1 %collective-permute-start.2 = (bf16[256,256]{1,0:T(8,128)(2,1)S(1)}, bf16[256,256]{1,0:T(8,128)(2,1)S(1)}, u32[]{:S(2)}, u32[]{:S(2)}) collective-permute-start(bf16[256,256]{1,0:T(8,128)(2,1)S(1)} %get-tuple-element.37), channel_id=1, source_target_pairs={{0,12},{4,8},{8,4},{12,0},{16,28},{20,24},{24,20},{28,16},{1,13},{... | collective-permute-start | bytes 393224 | tf_op jit(solution)/shard_map/ppermute | solution.py:106
  8.9 10.6 %collective-permute-start.3 = (bf16[256,256]{1,0:T(8,128)(2,1)S(1)}, bf16[256,256]{1,0:T(8,128)(2,1)S(1)}, u32[]{:S(2)}, u32[]{:S(2)}) collective-permute-start(bf16[256,256]{1,0:T(8,128)(2,1)S(1)} %get-tuple-element.38), channel_id=1, source_target_pairs={{0,8},{4,12},{8,0},{12,4},{16,24},{20,28},{24,16},{28,20},{1,9},{5... | collective-permute-start | bytes 393224 | tf_op jit(solution)/shard_map/ppermute | solution.py:106
  9.4 10.1 %collective-permute-start.4 = (bf16[256,256]{1,0:T(8,128)(2,1)S(1)}, bf16[256,256]{1,0:T(8,128)(2,1)S(1)}, u32[]{:S(2)}, u32[]{:S(2)}) collective-permute-start(bf16[256,256]{1,0:T(8,128)(2,1)S(1)} %get-tuple-element.39), channel_id=1, source_target_pairs={{0,20},{4,16},{8,28},{12,24},{16,4},{20,0},{24,12},{28,8},{1,21},{... | collective-permute-start | bytes 393224 | tf_op jit(solution)/shard_map/ppermute | solution.py:106
  12.3 10.6 %collective-permute-start.5 = (bf16[256,256]{1,0:T(8,128)(2,1)S(1)}, bf16[256,256]{1,0:T(8,128)(2,1)S(1)}, u32[]{:S(2)}, u32[]{:S(2)}) collective-permute-start(bf16[256,256]{1,0:T(8,128)(2,1)S(1)} %get-tuple-element.44), channel_id=1, source_target_pairs={{0,24},{4,28},{8,16},{12,20},{16,8},{20,12},{24,0},{28,4},{1,25},{... | collective-permute-start | bytes 393224 | tf_op jit(solution)/shard_map/ppermute | solution.py:106
  15.9 9.8 %collective-permute-start.6 = (bf16[256,256]{1,0:T(8,128)(2,1)S(1)}, bf16[256,256]{1,0:T(8,128)(2,1)S(1)}, u32[]{:S(2)}, u32[]{:S(2)}) collective-permute-start(bf16[256,256]{1,0:T(8,128)(2,1)S(1)} %get-tuple-element.45), channel_id=1, source_target_pairs={{0,28},{4,24},{8,20},{12,16},{16,12},{20,8},{24,4},{28,0},{1,29},{... | collective-permute-start | bytes 393224 | tf_op jit(solution)/shard_map/ppermute | solution.py:106
  19.5 25.1 %copy-start = (bf16[1024,4096]{1,0:T(8,128)(2,1)S(1)}, bf16[1024,4096]{1,0:T(8,128)(2,1)}, u32[]{:S(2)}) copy-start(bf16[1024,4096]{1,0:T(8,128)(2,1)} %weight_ref.9) | copy-start | bytes 25165828
  22.8 21.8 %copy-start.1 = (bf16[256,1024]{1,0:T(8,128)(2,1)S(1)}, bf16[256,1024]{1,0:T(8,128)(2,1)}, u32[]{:S(2)}) copy-start(bf16[256,1024]{1,0:T(8,128)(2,1)} %keys_ref.3) | copy-start | bytes 1572868
  22.9 21.8 %copy-start.2 = (bf16[256,1024]{1,0:T(8,128)(2,1)S(1)}, bf16[256,1024]{1,0:T(8,128)(2,1)}, u32[]{:S(2)}) copy-start(bf16[256,1024]{1,0:T(8,128)(2,1)} %values_ref.3) | copy-start | bytes 1572868
  22.9 21.7 %copy-start.3 = (bf16[256,1024]{1,0:T(8,128)(2,1)S(1)}, bf16[256,1024]{1,0:T(8,128)(2,1)}, u32[]{:S(2)}) copy-start(bf16[256,1024]{1,0:T(8,128)(2,1)} %queries_ref.3) | copy-start | bytes 1572868
  22.9 21.7 %copy-start.4 = (f32[1024]{0:T(1024)S(1)}, f32[1024]{0:T(1024)}, u32[]{:S(2)}) copy-start(f32[1024]{0:T(1024)} %param.12) | copy-start | bytes 12292
  28.0 11.8 %collective-permute-start.7 = (bf16[256,128]{1,0:T(8,128)(2,1)S(1)}, bf16[256,128]{1,0:T(8,128)(2,1)S(1)}, u32[]{:S(2)}, u32[]{:S(2)}) collective-permute-start(bf16[256,128]{1,0:T(8,128)(2,1)S(1)} %get-tuple-element.47), channel_id=1, source_target_pairs={{0,4},{4,0},{8,12},{12,8},{16,20},{20,16},{24,28},{28,24},{1,5},{5... | collective-permute-start | bytes 196616 | tf_op jit(solution)/shard_map/ppermute | solution.py:106
  33.1 7.9 %collective-permute-start.8 = (bf16[256,128]{1,0:T(8,128)(2,1)S(1)}, bf16[256,128]{1,0:T(8,128)(2,1)S(1)}, u32[]{:S(2)}, u32[]{:S(2)}) collective-permute-start(bf16[256,128]{1,0:T(8,128)(2,1)S(1)} %get-tuple-element.48), channel_id=1, source_target_pairs={{0,24},{4,28},{8,16},{12,20},{16,8},{20,12},{24,0},{28,4},{1,25},{... | collective-permute-start | bytes 196616 | tf_op jit(solution)/shard_map/ppermute | solution.py:106
  34.9 7.8 %collective-permute-start.9 = (bf16[256,128]{1,0:T(8,128)(2,1)S(1)}, bf16[256,128]{1,0:T(8,128)(2,1)S(1)}, u32[]{:S(2)}, u32[]{:S(2)}) collective-permute-start(bf16[256,128]{1,0:T(8,128)(2,1)S(1)} %get-tuple-element.49), channel_id=1, source_target_pairs={{0,28},{4,24},{8,20},{12,16},{16,12},{20,8},{24,4},{28,0},{1,29},{... | collective-permute-start | bytes 196616 | tf_op jit(solution)/shard_map/ppermute | solution.py:106
  36.4 6.3 %collective-permute-start.10 = (bf16[256,128]{1,0:T(8,128)(2,1)S(1)}, bf16[256,128]{1,0:T(8,128)(2,1)S(1)}, u32[]{:S(2)}, u32[]{:S(2)}) collective-permute-start(bf16[256,128]{1,0:T(8,128)(2,1)S(1)} %get-tuple-element.50), channel_id=1, source_target_pairs={{0,8},{4,12},{8,0},{12,4},{16,24},{20,28},{24,16},{28,20},{1,9},{5... | collective-permute-start | bytes 196616 | tf_op jit(solution)/shard_map/ppermute | solution.py:106
  37.5 7.1 %collective-permute-start.11 = (bf16[256,128]{1,0:T(8,128)(2,1)S(1)}, bf16[256,128]{1,0:T(8,128)(2,1)S(1)}, u32[]{:S(2)}, u32[]{:S(2)}) collective-permute-start(bf16[256,128]{1,0:T(8,128)(2,1)S(1)} %get-tuple-element.51), channel_id=1, source_target_pairs={{0,12},{4,8},{8,4},{12,0},{16,28},{20,24},{24,20},{28,16},{1,13},{... | collective-permute-start | bytes 196616 | tf_op jit(solution)/shard_map/ppermute | solution.py:106
  39.8 7.6 %collective-permute-start.12 = (bf16[256,128]{1,0:T(8,128)(2,1)S(1)}, bf16[256,128]{1,0:T(8,128)(2,1)S(1)}, u32[]{:S(2)}, u32[]{:S(2)}) collective-permute-start(bf16[256,128]{1,0:T(8,128)(2,1)S(1)} %get-tuple-element.54), channel_id=1, source_target_pairs={{0,16},{4,20},{8,24},{12,28},{16,0},{20,4},{24,8},{28,12},{1,17},{... | collective-permute-start | bytes 196616 | tf_op jit(solution)/shard_map/ppermute | solution.py:106
  41.0 6.9 %collective-permute-start.13 = (bf16[256,128]{1,0:T(8,128)(2,1)S(1)}, bf16[256,128]{1,0:T(8,128)(2,1)S(1)}, u32[]{:S(2)}, u32[]{:S(2)}) collective-permute-start(bf16[256,128]{1,0:T(8,128)(2,1)S(1)} %get-tuple-element.55), channel_id=1, source_target_pairs={{0,20},{4,16},{8,28},{12,24},{16,4},{20,0},{24,12},{28,8},{1,21},{... | collective-permute-start | bytes 196616 | tf_op jit(solution)/shard_map/ppermute | solution.py:106
  48.2 1.6 %collective-permute-start.17 = (bf16[256,512]{1,0:T(8,128)(2,1)S(1)}, bf16[256,512]{1,0:T(8,128)(2,1)S(1)}, u32[]{:S(2)}, u32[]{:S(2)}) collective-permute-start(bf16[256,512]{1,0:T(8,128)(2,1)S(1)} %get-tuple-element.62), channel_id=1, source_target_pairs={{0,1},{1,0},{2,3},{3,2},{4,5},{5,4},{6,7},{7,6},{8,9},{9,8},{10,11... | collective-permute-start | bytes 786440 | tf_op jit(solution)/shard_map/ppermute | solution.py:567
  48.5 2.9 %collective-permute-start.15 = (bf16[256,512]{1,0:T(8,128)(2,1)S(1)}, bf16[256,512]{1,0:T(8,128)(2,1)S(1)}, u32[]{:S(2)}, u32[]{:S(2)}) collective-permute-start(bf16[256,512]{1,0:T(8,128)(2,1)S(1)} %shard_map.90), channel_id=1, source_target_pairs={{0,1},{1,0},{2,3},{3,2},{4,5},{5,4},{6,7},{7,6},{8,9},{9,8},{10,11... | collective-permute-start | bytes 786440 | tf_op jit(solution)/shard_map/ppermute | solution.py:567
  49.8 9.2 %collective-permute-start.18 = (bf16[256,512]{1,0:T(8,128)(2,1)S(1)}, bf16[256,512]{1,0:T(8,128)(2,1)S(1)}, u32[]{:S(2)}, u32[]{:S(2)}) collective-permute-start(bf16[256,512]{1,0:T(8,128)(2,1)S(1)} %shard_map.92), channel_id=1, source_target_pairs={{0,2},{2,0},{1,3},{3,1},{4,6},{6,4},{5,7},{7,5},{8,10},{10,8},{9,1... | collective-permute-start | bytes 786440 | tf_op jit(solution)/shard_map/ppermute | solution.py:568
  51.5 12.4 %collective-permute-start.16 = (bf16[256,512]{1,0:T(8,128)(2,1)S(1)}, bf16[256,512]{1,0:T(8,128)(2,1)S(1)}, u32[]{:S(2)}, u32[]{:S(2)}) collective-permute-start(bf16[256,512]{1,0:T(8,128)(2,1)S(1)} %shard_map.91), channel_id=1, source_target_pairs={{0,2},{2,0},{1,3},{3,1},{4,6},{6,4},{5,7},{7,5},{8,10},{10,8},{9,1... | collective-permute-start | bytes 786440 | tf_op jit(solution)/shard_map/ppermute | solution.py:568
  53.4 10.4 %collective-permute-start.14 = (bf16[256,1024]{1,0:T(8,128)(2,1)S(1)}, bf16[256,1024]{1,0:T(8,128)(2,1)S(1)}, u32[]{:S(2)}, u32[]{:S(2)}) collective-permute-start(bf16[256,1024]{1,0:T(8,128)(2,1)S(1)} %get-tuple-element.58), channel_id=1, source_target_pairs={{0,1},{1,0},{2,3},{3,2},{4,5},{5,4},{6,7},{7,6},{8,9},{9,8},{10,11... | collective-permute-start | bytes 1572872 | tf_op jit(solution)/shard_map/ppermute | solution.py:571

commit v9 on v8

--- a/solution.py
+++ b/solution.py
@@ -98,7 +98,7 @@
     near, far = list(range(1, half)), list(range(half, n_peers))
     if back:
         return [0, near[0]] + far[2:] + near[1:] + far[:2]
-    return [0, far[0], near[0]] + near[:0:-1] + far[1:]
+    return [0, far[0]] + near[::-1] + far[1:]
 
 
 def exchange(blocks, n_peers, back):

time: 64.9 us -> 64.7 us (level)
  waiting for transfers between devices: 20.8 us -> 19.1 us
  starting transfers between devices: 31.4 us -> 33 us
    ppermute x14, waiting for transfers between devices: 10 us -> 8.33 us  [exchange(): lax.ppermute(block, 'seq', [(i, i ^ slot) for i in range(n_peers)])]
    ppermute x14, starting transfers between devices: 28.6 us -> 30.1 us  [exchange(): lax.ppermute(block, 'seq', [(i, i ^ slot) for i in range(n_peers)])]
  transfers between devices with their start and end apart: 19 -> 19, of which waited for: 11 -> 9; matrix products, arithmetic and copies ran while one was open for 0% -> 0% of each run, Pallas kernels for 11% -> 11%
where the time goes in v9:
time: 64.7 us; the launch traced here: 64.6 us
  starting transfers between devices  33 us (51%)
  waiting for transfers between devices  19.1 us (30%)
  Pallas kernels  12.3 us (19%)
    ppermute x14, starting transfers between devices, exchange(): lax.ppermute(block, 'seq', [(i, i ^ slot) for i in range(n_peers)])  30.1 us
    ppermute x2, waiting for transfers between devices, body(): lax.ppermute(add(*pair), 'fsdp', across)  10.4 us
    ppermute x14, waiting for transfers between devices, exchange(): lax.ppermute(block, 'seq', [(i, i ^ slot) for i in range(n_peers)])  8.33 us
    pallas_call x1, Pallas kernels, spectra(): pl.pallas_call(functools.partial(spectra_kernel, n_peers), in_specs=[pl.B...  3.37 us
    pallas_call x1, Pallas kernels, conv_fast(): pl.pallas_call(conv_kernel, in_specs=[whole] * 6, out_specs=[whole] * n_b...  2.26 us
    ppermute x2, starting transfers between devices, body(): lax.ppermute(add(*pair), 'fsdp', across)  2.16 us
    pallas_call x1, Pallas kernels, pre(): pl.pallas_call(functools.partial(pre_kernel, n_peers), in_specs=[pl.Block...  1.77 us
    pallas_call x1, Pallas kernels, gate_early(): pl.pallas_call(functools.partial(gate_early_kernel, n_peers), in_specs=[w...  1.73 us
  transfers between devices with their start and end apart: 19, of which 9 were waited for; matrix products, arithmetic and copies ran while one was open for 0% of the time, Pallas kernels for 11%

profile of v9, /device:TPU:0, one launch (start us, length us, event | category | flops | bytes accessed | tf_op | source)
XLA Modules:
  0.0 64.6 jit_solution(15515865207879973793)
XLA Ops:
  0.0 1.8 %shard_map.82 = (bf16[256,256]{1,0:T(8,128)(2,1)S(1)}, bf16[256,256]{1,0:T(8,128)(2,1)S(1)}, bf16[256,256]{1,0:T(8,128)(2,1)S(1)}, bf16[256,256]{1,0:T(8,128)(2,...) custom-call(bf16[256,1024]{1,0:T(8,128)(2,1)} %keys_ref.3, ...), custom_call_target="tpu_custom_call" | custom-call | flops 262144 | bytes 3145728 | tf_op jit(solution)/shard_map/pallas_call | solution.py:78
  1.8 4.1 %collective-permute-start = (bf16[256,256]{1,0:T(8,128)(2,1)S(1)}, bf16[256,256]{1,0:T(8,128)(2,1)S(1)}, u32[]{:S(2)}, u32[]{:S(2)}) collective-permute-start(bf16[256,256]{1,0:T(8,128)(2,1)S(1)} %get-tuple-element.35), channel_id=1, source_target_pairs={{0,16},{4,20},{8,24},{12,28},{16,0},{20,4},{24,8},{28,12},{1,17},{... | collective-permute-start | bytes 393224 | tf_op jit(solution)/shard_map/ppermute | solution.py:106
  5.9 2.5 %collective-permute-start.1 = (bf16[256,256]{1,0:T(8,128)(2,1)S(1)}, bf16[256,256]{1,0:T(8,128)(2,1)S(1)}, u32[]{:S(2)}, u32[]{:S(2)}) collective-permute-start(bf16[256,256]{1,0:T(8,128)(2,1)S(1)} %get-tuple-element.36), channel_id=1, source_target_pairs={{0,12},{4,8},{8,4},{12,0},{16,28},{20,24},{24,20},{28,16},{1,13},{... | collective-permute-start | bytes 393224 | tf_op jit(solution)/shard_map/ppermute | solution.py:106
  8.4 0.4 collective-permute-start.2
  8.9 0.5 collective-permute-start.3
  9.4 1.3 %collective-permute-start.4 = (bf16[256,256]{1,0:T(8,128)(2,1)S(1)}, bf16[256,256]{1,0:T(8,128)(2,1)S(1)}, u32[]{:S(2)}, u32[]{:S(2)}) collective-permute-start(bf16[256,256]{1,0:T(8,128)(2,1)S(1)} %get-tuple-element.39), channel_id=1, source_target_pairs={{0,20},{4,16},{8,28},{12,24},{16,4},{20,0},{24,12},{28,8},{1,21},{... | collective-permute-start | bytes 393224 | tf_op jit(solution)/shard_map/ppermute | solution.py:106
  10.7 1.6 %collective-permute-done.refs_1_ = bf16[256,256]{1,0:T(8,128)(2,1)S(1)} collective-permute-done((bf16[256,256]{1,0:T(8,128)(2,1)S(1)}, bf16[256,256]{1,0:T(8,128)(2,1)S(1)}, u32[]{:S(2)}, u32[]{:S(2)}) %collective-permute-start) | collective-permute-done | bytes 131104 | tf_op jit(solution)/shard_map/ppermute | solution.py:106
  12.3 3.6 %collective-permute-start.5 = (bf16[256,256]{1,0:T(8,128)(2,1)S(1)}, bf16[256,256]{1,0:T(8,128)(2,1)S(1)}, u32[]{:S(2)}, u32[]{:S(2)}) collective-permute-start(bf16[256,256]{1,0:T(8,128)(2,1)S(1)} %get-tuple-element.44), channel_id=1, source_target_pairs={{0,24},{4,28},{8,16},{12,20},{16,8},{20,12},{24,0},{28,4},{1,25},{... | collective-permute-start | bytes 393224 | tf_op jit(solution)/shard_map/ppermute | solution.py:106
  15.9 1.8 %collective-permute-done.1.refs_2_ = bf16[256,256]{1,0:T(8,128)(2,1)S(1)} collective-permute-done((bf16[256,256]{1,0:T(8,128)(2,1)S(1)}, bf16[256,256]{1,0:T(8,128)(2,1)S(1)}, u32[]{:S(2)}, u32[]{:S(2)}) %collective-permute-start.1) | collective-permute-done | bytes 131104 | tf_op jit(solution)/shard_map/ppermute | solution.py:106
  17.7 3.2 %collective-permute-start.6 = (bf16[256,256]{1,0:T(8,128)(2,1)S(1)}, bf16[256,256]{1,0:T(8,128)(2,1)S(1)}, u32[]{:S(2)}, u32[]{:S(2)}) collective-permute-start(bf16[256,256]{1,0:T(8,128)(2,1)S(1)} %get-tuple-element.45), channel_id=1, source_target_pairs={{0,28},{4,24},{8,20},{12,16},{16,12},{20,8},{24,4},{28,0},{1,29},{... | collective-permute-start | bytes 393224 | tf_op jit(solution)/shard_map/ppermute | solution.py:106
  20.9 3.4 %shard_map.83 = (bf16[512,512]{1,0:T(8,128)(2,1)S(1)}, bf16[256,1536]{1,0:T(8,128)(2,1)S(1)}, f32[8,512,256]{2,1,0:T(8,128)S(1)}, f32[8,512,128]{2,1,0:T(8,128)S(1)}) custom-call(bf16[512,512]{1,0:T(8,128)(2,1)} %constant.4.clone.fwd_hbm, bf16[256,1536]{1,0:T(8,128)(2,1)} %constant.5.clone.bwd_hbm, bf16[256,256]{1,0:T(8,128)(2,1)S(1)} %get-tuple-element.34.refs_0_, ...), custom_call_target="tpu_custom_call" | custom-call | flops 805306368 | bytes 4194304 | tf_op jit(solution)/shard_map/pallas_call | solution.py:173
  24.3 1.3 %collective-permute-done.6.refs_1_ = bf16[256,256]{1,0:T(8,128)(2,1)S(1)} collective-permute-done((bf16[256,256]{1,0:T(8,128)(2,1)S(1)}, bf16[256,256]{1,0:T(8,128)(2,1)S(1)}, u32[]{:S(2)}, u32[]{:S(2)}) %collective-permute-start.6) | collective-permute-done | bytes 131104 | tf_op jit(solution)/shard_map/ppermute | solution.py:106
  25.6 2.3 %shard_map.84 = (bf16[256,128]{1,0:T(8,128)(2,1)S(1)}, bf16[256,128]{1,0:T(8,128)(2,1)S(1)}, bf16[256,128]{1,0:T(8,128)(2,1)S(1)}, bf16[256,128]{1,0:T(8,128)(2,...) custom-call(bf16[512,512]{1,0:T(8,128)(2,1)S(1)} %get-tuple-element., ...), custom_call_target="tpu_custom_call" | custom-call | flops 1073741824 | bytes 4194304 | tf_op jit(solution)/shard_map/pallas_call | solution.py:261
  27.9 5.2 %collective-permute-start.7 = (bf16[256,128]{1,0:T(8,128)(2,1)S(1)}, bf16[256,128]{1,0:T(8,128)(2,1)S(1)}, u32[]{:S(2)}, u32[]{:S(2)}) collective-permute-start(bf16[256,128]{1,0:T(8,128)(2,1)S(1)} %get-tuple-element.47), channel_id=1, source_target_pairs={{0,4},{4,0},{8,12},{12,8},{16,20},{20,16},{24,28},{28,24},{1,5},{5... | collective-permute-start | bytes 196616 | tf_op jit(solution)/shard_map/ppermute | solution.py:106
  33.1 1.1 %collective-permute-start.8 = (bf16[256,128]{1,0:T(8,128)(2,1)S(1)}, bf16[256,128]{1,0:T(8,128)(2,1)S(1)}, u32[]{:S(2)}, u32[]{:S(2)}) collective-permute-start(bf16[256,128]{1,0:T(8,128)(2,1)S(1)} %get-tuple-element.48), channel_id=1, source_target_pairs={{0,24},{4,28},{8,16},{12,20},{16,8},{20,12},{24,0},{28,4},{1,25},{... | collective-permute-start | bytes 196616 | tf_op jit(solution)/shard_map/ppermute | solution.py:106
  34.1 2.3 %collective-permute-start.9 = (bf16[256,128]{1,0:T(8,128)(2,1)S(1)}, bf16[256,128]{1,0:T(8,128)(2,1)S(1)}, u32[]{:S(2)}, u32[]{:S(2)}) collective-permute-start(bf16[256,128]{1,0:T(8,128)(2,1)S(1)} %get-tuple-element.49), channel_id=1, source_target_pairs={{0,28},{4,24},{8,20},{12,16},{16,12},{20,8},{24,4},{28,0},{1,29},{... | collective-permute-start | bytes 196616 | tf_op jit(solution)/shard_map/ppermute | solution.py:106
  36.4 1.1 %collective-permute-start.10 = (bf16[256,128]{1,0:T(8,128)(2,1)S(1)}, bf16[256,128]{1,0:T(8,128)(2,1)S(1)}, u32[]{:S(2)}, u32[]{:S(2)}) collective-permute-start(bf16[256,128]{1,0:T(8,128)(2,1)S(1)} %get-tuple-element.50), channel_id=1, source_target_pairs={{0,8},{4,12},{8,0},{12,4},{16,24},{20,28},{24,16},{28,20},{1,9},{5... | collective-permute-start | bytes 196616 | tf_op jit(solution)/shard_map/ppermute | solution.py:106
  37.5 2.3 %collective-permute-start.11 = (bf16[256,128]{1,0:T(8,128)(2,1)S(1)}, bf16[256,128]{1,0:T(8,128)(2,1)S(1)}, u32[]{:S(2)}, u32[]{:S(2)}) collective-permute-start(bf16[256,128]{1,0:T(8,128)(2,1)S(1)} %get-tuple-element.51), channel_id=1, source_target_pairs={{0,12},{4,8},{8,4},{12,0},{16,28},{20,24},{24,20},{28,16},{1,13},{... | collective-permute-start | bytes 196616 | tf_op jit(solution)/shard_map/ppermute | solution.py:106
  39.8 1.1 %collective-permute-start.12 = (bf16[256,128]{1,0:T(8,128)(2,1)S(1)}, bf16[256,128]{1,0:T(8,128)(2,1)S(1)}, u32[]{:S(2)}, u32[]{:S(2)}) collective-permute-start(bf16[256,128]{1,0:T(8,128)(2,1)S(1)} %get-tuple-element.54), channel_id=1, source_target_pairs={{0,16},{4,20},{8,24},{12,28},{16,0},{20,4},{24,8},{28,12},{1,17},{... | collective-permute-start | bytes 196616 | tf_op jit(solution)/shard_map/ppermute | solution.py:106
  41.0 1.3 %collective-permute-start.13 = (bf16[256,128]{1,0:T(8,128)(2,1)S(1)}, bf16[256,128]{1,0:T(8,128)(2,1)S(1)}, u32[]{:S(2)}, u32[]{:S(2)}) collective-permute-start(bf16[256,128]{1,0:T(8,128)(2,1)S(1)} %get-tuple-element.55), channel_id=1, source_target_pairs={{0,20},{4,16},{8,28},{12,24},{16,4},{20,0},{24,12},{28,8},{1,21},{... | collective-permute-start | bytes 196616 | tf_op jit(solution)/shard_map/ppermute | solution.py:106
  42.3 1.5 %collective-permute-done.11.refs_5_ = bf16[256,128]{1,0:T(8,128)(2,1)S(1)} collective-permute-done((bf16[256,128]{1,0:T(8,128)(2,1)S(1)}, bf16[256,128]{1,0:T(8,128)(2,1)S(1)}, u32[]{:S(2)}, u32[]{:S(2)}) %collective-permute-start.11) | collective-permute-done | bytes 65568 | tf_op jit(solution)/shard_map/ppermute | solution.py:106
  43.7 1.7 %shard_map.85 = (bf16[256,1024]{1,0:T(8,128)(2,1)S(1)}, f32[256,1024]{1,0:T(8,128)S(1)}, f32[256,1024]{1,0:T(8,128)S(1)}) custom-call(bf16[256,1024]{1,0:T(8,128)(2,1)S(1)} %copy-done.3, bf16[256,1024]{1,0:T(8,128)(2,1)S(1)} %copy-done.1, bf16[256,1024]{1,0:T(8,128)(2,1)S(1)} %copy-done.2, f32[1,1024]{1,0:T(1,128)S(1)} %bitcast.1, ...), custom_call_target="tpu_custom_call" | custom-call | flops 1073741824 | bytes 2621440 | tf_op jit(solution)/shard_map/pallas_call | solution.py:342
  45.5 1.1 %collective-permute-done.12.refs_0_ = bf16[256,128]{1,0:T(8,128)(2,1)S(1)} collective-permute-done((bf16[256,128]{1,0:T(8,128)(2,1)S(1)}, bf16[256,128]{1,0:T(8,128)(2,1)S(1)}, u32[]{:S(2)}, u32[]{:S(2)}) %collective-permute-start.12) | collective-permute-done | bytes 65568 | tf_op jit(solution)/shard_map/ppermute | solution.py:106
  46.6 1.1 %collective-permute-done.13.refs_1_ = bf16[256,128]{1,0:T(8,128)(2,1)S(1)} collective-permute-done((bf16[256,128]{1,0:T(8,128)(2,1)S(1)}, bf16[256,128]{1,0:T(8,128)(2,1)S(1)}, u32[]{:S(2)}, u32[]{:S(2)}) %collective-permute-start.13) | collective-permute-done | bytes 65568 | tf_op jit(solution)/shard_map/ppermute | solution.py:106
  48.3 0.5 collective-permute-start.15
  49.2 0.4 collective-permute-done.17.arrived_ref
  49.7 1.6 %collective-permute-start.18 = (bf16[256,512]{1,0:T(8,128)(2,1)S(1)}, bf16[256,512]{1,0:T(8,128)(2,1)S(1)}, u32[]{:S(2)}, u32[]{:S(2)}) collective-permute-start(bf16[256,512]{1,0:T(8,128)(2,1)S(1)} %shard_map.92), channel_id=1, source_target_pairs={{0,2},{2,0},{1,3},{3,1},{4,6},{6,4},{5,7},{7,5},{8,10},{10,8},{9,1... | collective-permute-start | bytes 786440 | tf_op jit(solution)/shard_map/ppermute | solution.py:568
  51.3 0.6 collective-permute-start.16
  52.0 1.3 %shard_map.88 = (bf16[256,1024]{1,0:T(8,128)(2,1)S(1)}, f32[256,1024]{1,0:T(8,128)S(1)}) custom-call(bf16[256,1024]{1,0:T(8,128)(2,1)S(1)} %shard_map.87.gated_ref, bf16[1024,4096]{1,0:T(8,128)(2,1)S(1)} %copy-done), custom_call_target="tpu_custom_call" | custom-call | flops 1073741824 | bytes 4194304 | tf_op jit(solution)/shard_map/pallas_call | solution.py:445
  53.3 5.5 %collective-permute-done.18.refs_1_ = bf16[256,512]{1,0:T(8,128)(2,1)S(1)} collective-permute-done((bf16[256,512]{1,0:T(8,128)(2,1)S(1)}, bf16[256,512]{1,0:T(8,128)(2,1)S(1)}, u32[]{:S(2)}, u32[]{:S(2)}) %collective-permute-start.18) | collective-permute-done | bytes 262176 | tf_op jit(solution)/shard_map/ppermute | solution.py:568
  58.9 4.8 %collective-permute-done.16.refs_0_ = bf16[256,512]{1,0:T(8,128)(2,1)S(1)} collective-permute-done((bf16[256,512]{1,0:T(8,128)(2,1)S(1)}, bf16[256,512]{1,0:T(8,128)(2,1)S(1)}, u32[]{:S(2)}, u32[]{:S(2)}) %collective-permute-start.16) | collective-permute-done | bytes 262176 | tf_op jit(solution)/shard_map/ppermute | solution.py:568
  63.7 0.9 %shard_map.94 = bf16[256,1024]{1,0:T(8,128)(2,1)} custom-call(f32[256,1024]{1,0:T(8,128)S(1)} %get-tuple-element.57.own_ref, bf16[256,1024]{1,0:T(8,128)(2,1)S(1)} %collective-permute-done.14.near_ref, bf16[256,512]{1,0:T(8,128)(2,1)S(1)} %collective-permute-done.16.refs_0_, bf16[256,512]{1,0:T(8,128)(2,1)S(1)} %collective-permute-done.18.refs_1_, ...), custom_call_target="tpu_custom_call" | custom-call | flops 262144 | bytes 2097152 | tf_op jit(solution)/shard_map/pallas_call | solution.py:512
  (29 shorter events, 1.2 us)
Async XLA Ops:
  1.8 10.5 %collective-permute-start = (bf16[256,256]{1,0:T(8,128)(2,1)S(1)}, bf16[256,256]{1,0:T(8,128)(2,1)S(1)}, u32[]{:S(2)}, u32[]{:S(2)}) collective-permute-start(bf16[256,256]{1,0:T(8,128)(2,1)S(1)} %get-tuple-element.35), channel_id=1, source_target_pairs={{0,16},{4,20},{8,24},{12,28},{16,0},{20,4},{24,8},{28,12},{1,17},{... | collective-permute-start | bytes 393224 | tf_op jit(solution)/shard_map/ppermute | solution.py:106
  5.9 11.8 %collective-permute-start.1 = (bf16[256,256]{1,0:T(8,128)(2,1)S(1)}, bf16[256,256]{1,0:T(8,128)(2,1)S(1)}, u32[]{:S(2)}, u32[]{:S(2)}) collective-permute-start(bf16[256,256]{1,0:T(8,128)(2,1)S(1)} %get-tuple-element.36), channel_id=1, source_target_pairs={{0,12},{4,8},{8,4},{12,0},{16,28},{20,24},{24,20},{28,16},{1,13},{... | collective-permute-start | bytes 393224 | tf_op jit(solution)/shard_map/ppermute | solution.py:106
  8.4 12.5 %collective-permute-start.2 = (bf16[256,256]{1,0:T(8,128)(2,1)S(1)}, bf16[256,256]{1,0:T(8,128)(2,1)S(1)}, u32[]{:S(2)}, u32[]{:S(2)}) collective-permute-start(bf16[256,256]{1,0:T(8,128)(2,1)S(1)} %get-tuple-element.37), channel_id=1, source_target_pairs={{0,8},{4,12},{8,0},{12,4},{16,24},{20,28},{24,16},{28,20},{1,9},{5... | collective-permute-start | bytes 393224 | tf_op jit(solution)/shard_map/ppermute | solution.py:106
  8.9 12.0 %collective-permute-start.3 = (bf16[256,256]{1,0:T(8,128)(2,1)S(1)}, bf16[256,256]{1,0:T(8,128)(2,1)S(1)}, u32[]{:S(2)}, u32[]{:S(2)}) collective-permute-start(bf16[256,256]{1,0:T(8,128)(2,1)S(1)} %get-tuple-element.38), channel_id=1, source_target_pairs={{0,4},{4,0},{8,12},{12,8},{16,20},{20,16},{24,28},{28,24},{1,5},{5... | collective-permute-start | bytes 393224 | tf_op jit(solution)/shard_map/ppermute | solution.py:106
  9.4 11.5 %collective-permute-start.4 = (bf16[256,256]{1,0:T(8,128)(2,1)S(1)}, bf16[256,256]{1,0:T(8,128)(2,1)S(1)}, u32[]{:S(2)}, u32[]{:S(2)}) collective-permute-start(bf16[256,256]{1,0:T(8,128)(2,1)S(1)} %get-tuple-element.39), channel_id=1, source_target_pairs={{0,20},{4,16},{8,28},{12,24},{16,4},{20,0},{24,12},{28,8},{1,21},{... | collective-permute-start | bytes 393224 | tf_op jit(solution)/shard_map/ppermute | solution.py:106
  12.3 12.0 %collective-permute-start.5 = (bf16[256,256]{1,0:T(8,128)(2,1)S(1)}, bf16[256,256]{1,0:T(8,128)(2,1)S(1)}, u32[]{:S(2)}, u32[]{:S(2)}) collective-permute-start(bf16[256,256]{1,0:T(8,128)(2,1)S(1)} %get-tuple-element.44), channel_id=1, source_target_pairs={{0,24},{4,28},{8,16},{12,20},{16,8},{20,12},{24,0},{28,4},{1,25},{... | collective-permute-start | bytes 393224 | tf_op jit(solution)/shard_map/ppermute | solution.py:106
  17.7 7.9 %collective-permute-start.6 = (bf16[256,256]{1,0:T(8,128)(2,1)S(1)}, bf16[256,256]{1,0:T(8,128)(2,1)S(1)}, u32[]{:S(2)}, u32[]{:S(2)}) collective-permute-start(bf16[256,256]{1,0:T(8,128)(2,1)S(1)} %get-tuple-element.45), channel_id=1, source_target_pairs={{0,28},{4,24},{8,20},{12,16},{16,12},{20,8},{24,4},{28,0},{1,29},{... | collective-permute-start | bytes 393224 | tf_op jit(solution)/shard_map/ppermute | solution.py:106
  20.9 22.8 %copy-start = (bf16[1024,4096]{1,0:T(8,128)(2,1)S(1)}, bf16[1024,4096]{1,0:T(8,128)(2,1)}, u32[]{:S(2)}) copy-start(bf16[1024,4096]{1,0:T(8,128)(2,1)} %weight_ref.9) | copy-start | bytes 25165828
  24.3 19.4 %copy-start.1 = (bf16[256,1024]{1,0:T(8,128)(2,1)S(1)}, bf16[256,1024]{1,0:T(8,128)(2,1)}, u32[]{:S(2)}) copy-start(bf16[256,1024]{1,0:T(8,128)(2,1)} %keys_ref.3) | copy-start | bytes 1572868
  24.3 19.4 %copy-start.2 = (bf16[256,1024]{1,0:T(8,128)(2,1)S(1)}, bf16[256,1024]{1,0:T(8,128)(2,1)}, u32[]{:S(2)}) copy-start(bf16[256,1024]{1,0:T(8,128)(2,1)} %values_ref.3) | copy-start | bytes 1572868
  24.3 19.4 %copy-start.3 = (bf16[256,1024]{1,0:T(8,128)(2,1)S(1)}, bf16[256,1024]{1,0:T(8,128)(2,1)}, u32[]{:S(2)}) copy-start(bf16[256,1024]{1,0:T(8,128)(2,1)} %queries_ref.3) | copy-start | bytes 1572868
  24.3 19.4 %copy-start.4 = (f32[1024]{0:T(1024)S(1)}, f32[1024]{0:T(1024)}, u32[]{:S(2)}) copy-start(f32[1024]{0:T(1024)} %param.12) | copy-start | bytes 12292
  27.9 11.9 %collective-permute-start.7 = (bf16[256,128]{1,0:T(8,128)(2,1)S(1)}, bf16[256,128]{1,0:T(8,128)(2,1)S(1)}, u32[]{:S(2)}, u32[]{:S(2)}) collective-permute-start(bf16[256,128]{1,0:T(8,128)(2,1)S(1)} %get-tuple-element.47), channel_id=1, source_target_pairs={{0,4},{4,0},{8,12},{12,8},{16,20},{20,16},{24,28},{28,24},{1,5},{5... | collective-permute-start | bytes 196616 | tf_op jit(solution)/shard_map/ppermute | solution.py:106
  33.1 7.9 %collective-permute-start.8 = (bf16[256,128]{1,0:T(8,128)(2,1)S(1)}, bf16[256,128]{1,0:T(8,128)(2,1)S(1)}, u32[]{:S(2)}, u32[]{:S(2)}) collective-permute-start(bf16[256,128]{1,0:T(8,128)(2,1)S(1)} %get-tuple-element.48), channel_id=1, source_target_pairs={{0,24},{4,28},{8,16},{12,20},{16,8},{20,12},{24,0},{28,4},{1,25},{... | collective-permute-start | bytes 196616 | tf_op jit(solution)/shard_map/ppermute | solution.py:106
  34.1 8.1 %collective-permute-start.9 = (bf16[256,128]{1,0:T(8,128)(2,1)S(1)}, bf16[256,128]{1,0:T(8,128)(2,1)S(1)}, u32[]{:S(2)}, u32[]{:S(2)}) collective-permute-start(bf16[256,128]{1,0:T(8,128)(2,1)S(1)} %get-tuple-element.49), channel_id=1, source_target_pairs={{0,28},{4,24},{8,20},{12,16},{16,12},{20,8},{24,4},{28,0},{1,29},{... | collective-permute-start | bytes 196616 | tf_op jit(solution)/shard_map/ppermute | solution.py:106
  36.4 5.9 %collective-permute-start.10 = (bf16[256,128]{1,0:T(8,128)(2,1)S(1)}, bf16[256,128]{1,0:T(8,128)(2,1)S(1)}, u32[]{:S(2)}, u32[]{:S(2)}) collective-permute-start(bf16[256,128]{1,0:T(8,128)(2,1)S(1)} %get-tuple-element.50), channel_id=1, source_target_pairs={{0,8},{4,12},{8,0},{12,4},{16,24},{20,28},{24,16},{28,20},{1,9},{5... | collective-permute-start | bytes 196616 | tf_op jit(solution)/shard_map/ppermute | solution.py:106
  37.5 6.2 %collective-permute-start.11 = (bf16[256,128]{1,0:T(8,128)(2,1)S(1)}, bf16[256,128]{1,0:T(8,128)(2,1)S(1)}, u32[]{:S(2)}, u32[]{:S(2)}) collective-permute-start(bf16[256,128]{1,0:T(8,128)(2,1)S(1)} %get-tuple-element.51), channel_id=1, source_target_pairs={{0,12},{4,8},{8,4},{12,0},{16,28},{20,24},{24,20},{28,16},{1,13},{... | collective-permute-start | bytes 196616 | tf_op jit(solution)/shard_map/ppermute | solution.py:106
  39.8 6.7 %collective-permute-start.12 = (bf16[256,128]{1,0:T(8,128)(2,1)S(1)}, bf16[256,128]{1,0:T(8,128)(2,1)S(1)}, u32[]{:S(2)}, u32[]{:S(2)}) collective-permute-start(bf16[256,128]{1,0:T(8,128)(2,1)S(1)} %get-tuple-element.54), channel_id=1, source_target_pairs={{0,16},{4,20},{8,24},{12,28},{16,0},{20,4},{24,8},{28,12},{1,17},{... | collective-permute-start | bytes 196616 | tf_op jit(solution)/shard_map/ppermute | solution.py:106
  41.0 6.8 %collective-permute-start.13 = (bf16[256,128]{1,0:T(8,128)(2,1)S(1)}, bf16[256,128]{1,0:T(8,128)(2,1)S(1)}, u32[]{:S(2)}, u32[]{:S(2)}) collective-permute-start(bf16[256,128]{1,0:T(8,128)(2,1)S(1)} %get-tuple-element.55), channel_id=1, source_target_pairs={{0,20},{4,16},{8,28},{12,24},{16,4},{20,0},{24,12},{28,8},{1,21},{... | collective-permute-start | bytes 196616 | tf_op jit(solution)/shard_map/ppermute | solution.py:106
  48.0 1.6 %collective-permute-start.17 = (bf16[256,512]{1,0:T(8,128)(2,1)S(1)}, bf16[256,512]{1,0:T(8,128)(2,1)S(1)}, u32[]{:S(2)}, u32[]{:S(2)}) collective-permute-start(bf16[256,512]{1,0:T(8,128)(2,1)S(1)} %get-tuple-element.62), channel_id=1, source_target_pairs={{0,1},{1,0},{2,3},{3,2},{4,5},{5,4},{6,7},{7,6},{8,9},{9,8},{10,11... | collective-permute-start | bytes 786440 | tf_op jit(solution)/shard_map/ppermute | solution.py:567
  48.3 2.9 %collective-permute-start.15 = (bf16[256,512]{1,0:T(8,128)(2,1)S(1)}, bf16[256,512]{1,0:T(8,128)(2,1)S(1)}, u32[]{:S(2)}, u32[]{:S(2)}) collective-permute-start(bf16[256,512]{1,0:T(8,128)(2,1)S(1)} %shard_map.90), channel_id=1, source_target_pairs={{0,1},{1,0},{2,3},{3,2},{4,5},{5,4},{6,7},{7,6},{8,9},{9,8},{10,11... | collective-permute-start | bytes 786440 | tf_op jit(solution)/shard_map/ppermute | solution.py:567
  49.7 9.2 %collective-permute-start.18 = (bf16[256,512]{1,0:T(8,128)(2,1)S(1)}, bf16[256,512]{1,0:T(8,128)(2,1)S(1)}, u32[]{:S(2)}, u32[]{:S(2)}) collective-permute-start(bf16[256,512]{1,0:T(8,128)(2,1)S(1)} %shard_map.92), channel_id=1, source_target_pairs={{0,2},{2,0},{1,3},{3,1},{4,6},{6,4},{5,7},{7,5},{8,10},{10,8},{9,1... | collective-permute-start | bytes 786440 | tf_op jit(solution)/shard_map/ppermute | solution.py:568
  51.3 12.4 %collective-permute-start.16 = (bf16[256,512]{1,0:T(8,128)(2,1)S(1)}, bf16[256,512]{1,0:T(8,128)(2,1)S(1)}, u32[]{:S(2)}, u32[]{:S(2)}) collective-permute-start(bf16[256,512]{1,0:T(8,128)(2,1)S(1)} %shard_map.91), channel_id=1, source_target_pairs={{0,2},{2,0},{1,3},{3,1},{4,6},{6,4},{5,7},{7,5},{8,10},{10,8},{9,1... | collective-permute-start | bytes 786440 | tf_op jit(solution)/shard_map/ppermute | solution.py:568
  53.3 10.4 %collective-permute-start.14 = (bf16[256,1024]{1,0:T(8,128)(2,1)S(1)}, bf16[256,1024]{1,0:T(8,128)(2,1)S(1)}, u32[]{:S(2)}, u32[]{:S(2)}) collective-permute-start(bf16[256,1024]{1,0:T(8,128)(2,1)S(1)} %get-tuple-element.58), channel_id=1, source_target_pairs={{0,1},{1,0},{2,3},{3,2},{4,5},{5,4},{6,7},{7,6},{8,9},{9,8},{10,11... | collective-permute-start | bytes 1572872 | tf_op jit(solution)/shard_map/ppermute | solution.py:571

commit v10 on v8

--- a/solution.py
+++ b/solution.py
@@ -148,44 +148,59 @@
                 part_ref[i, pl.ds(row + part * rows, step)] = total[part]
 
 
-def spectra_kernel(n_peers, fwd_hbm, bwd_hbm, *refs):
-    *in_refs, fwd_ref, bwd_ref, spec_ref, part_ref, sem = refs
+def tables_kernel(fwd_hbm, bwd_hbm, *refs):
+    fwd_ref, bwd_ref, sem = refs[-3:]
     copies = [
         pltpu.make_async_copy(fwd_hbm, fwd_ref, sem.at[0]),
         pltpu.make_async_copy(bwd_hbm, bwd_ref, sem.at[1]),
     ]
     for copy in copies:
         copy.start()
-    copies[0].wait()
+    for copy in copies:
+        copy.wait()
+
+
+def load_tables(fwd, bwd, after):
+    whole = pl.BlockSpec(memory_space=pltpu.VMEM)
+    args = [pltpu.with_memory_space_constraint(a, pltpu.HBM) for a in (fwd, bwd)]
+    return pl.pallas_call(
+        tables_kernel,
+        in_specs=[pl.BlockSpec(memory_space=pltpu.HBM)] * 2
+        + [pl.BlockSpec(memory_space=pl.ANY)] * len(after),
+        out_specs=[whole] * 2,
+        out_shape=[jax.ShapeDtypeStruct(t.shape, BF16) for t in (fwd, bwd)],
+        scratch_shapes=[pltpu.SemaphoreType.DMA((2,))],
+        compiler_params=pltpu.CompilerParams(vmem_limit_bytes=SMALL_VMEM),
+        cost_estimate=pl.CostEstimate(flops=10**6, bytes_accessed=3 * 2**20, transcendentals=0),
+    )(*args, *after)
+
+
+def spectra_kernel(n_peers, fwd_ref, *refs):
+    *in_refs, spec_ref, part_ref = refs
     for slot, in_ref in zip(slots_of(n_peers, False), in_refs):
         spec_ref[peer_of(slot)] = block_spectrum(fwd_ref[...], in_ref[...])
     for pair in range(n_peers // 2):
         pl.when(late_place(n_peers) == pair)(
             functools.partial(mix_early, pair, STEP, spec_ref, part_ref)
         )
-    copies[1].wait()
-
-
-def spectra(received, fwd, bwd, n_peers):
+
+
+def spectra(received, fwd, n_peers):
     rows, width = received[0].shape
     whole = pl.BlockSpec(memory_space=pltpu.VMEM)
-    args = [pltpu.with_memory_space_constraint(a, pltpu.HBM) for a in (fwd, bwd)]
     return pl.pallas_call(
         functools.partial(spectra_kernel, n_peers),
-        in_specs=[pl.BlockSpec(memory_space=pltpu.HBM)] * 2 + [whole] * len(received),
-        out_specs=[whole] * 4,
+        in_specs=[whole] * (1 + len(received)),
+        out_specs=[whole] * 2,
         out_shape=[
-            jax.ShapeDtypeStruct(fwd.shape, BF16),
-            jax.ShapeDtypeStruct(bwd.shape, BF16),
             jax.ShapeDtypeStruct((n_peers, 2 * rows, width), F32),
             jax.ShapeDtypeStruct((n_peers, 2 * rows, width // 2), F32),
         ],
-        scratch_shapes=[pltpu.SemaphoreType.DMA((2,))],
         compiler_params=pltpu.CompilerParams(vmem_limit_bytes=CONV_VMEM),
         cost_estimate=pl.CostEstimate(
             flops=8 * len(received) * rows * rows * width, bytes_accessed=4 * 2**20, transcendentals=0
         ),
-    )(*args, *received)
+    )(fwd, *received)
 
 
 def mix_late(pair, step, first, last, sign, spec_ref, part_ref, late_ref, turned):
@@ -537,7 +552,8 @@
     if chans % 128 == 0 and n_peers == 8:
         blocks = pre(keys, values, filters, n_peers)
         received = exchange(blocks, n_peers, False)
-        fwd, bwd, early, part = spectra(received[:-2], fwd, bwd, n_peers)
+        fwd, bwd = load_tables(fwd, bwd, received[1:2])
+        early, part = spectra(received[:-2], fwd, n_peers)
         back = exchange(conv_fast(early, part, received[-2:], fwd, bwd), n_peers, True)
         slots = slots_of(n_peers, True)[-2:]
         gated, send_part, own_part = gate_early(

time: 64.9 us -> 64.8 us (level)
    pallas_call x1 -> x2, Pallas kernels: 3.36 us -> 3.46 us  [the longest x1 2.15 us: spectra(): pl.pallas_call(functools.partial(spectra_kernel, n_peers), in_specs=[whol...]
  transfers between devices with their start and end apart: 19 -> 19, of which waited for: 11 -> 9; matrix products, arithmetic and copies ran while one was open for 0% -> 0% of each run, Pallas kernels for 11% -> 11%
where the time goes in v10:
time: 64.8 us; the launch traced here: 64.6 us
  starting transfers between devices  31.2 us (48%)
  waiting for transfers between devices  20.8 us (32%)
  Pallas kernels  12.4 us (19%)
    ppermute x14, starting transfers between devices, exchange(): lax.ppermute(block, 'seq', [(i, i ^ slot) for i in range(n_peers)])  28.3 us
    ppermute x2, waiting for transfers between devices, body(): lax.ppermute(add(*pair), 'fsdp', across)  10.3 us
    ppermute x14, waiting for transfers between devices, exchange(): lax.ppermute(block, 'seq', [(i, i ^ slot) for i in range(n_peers)])  10.1 us
    pallas_call x1, Pallas kernels, conv_fast(): pl.pallas_call(conv_kernel, in_specs=[whole] * 6, out_specs=[whole] * n_b...  2.23 us
    ppermute x2, starting transfers between devices, body(): lax.ppermute(add(*pair), 'fsdp', across)  2.16 us
    pallas_call x1, Pallas kernels, spectra(): pl.pallas_call(functools.partial(spectra_kernel, n_peers), in_specs=[whol...  2.15 us
    pallas_call x1, Pallas kernels, pre(): pl.pallas_call(functools.partial(pre_kernel, n_peers), in_specs=[pl.Block...  1.77 us
    pallas_call x1, Pallas kernels, gate_early(): pl.pallas_call(functools.partial(gate_early_kernel, n_peers), in_specs=[w...  1.73 us
  transfers between devices with their start and end apart: 19, of which 9 were waited for; matrix products, arithmetic and copies ran while one was open for 0% of the time, Pallas kernels for 11%

profile of v10, /device:TPU:0, one launch (start us, length us, event | category | flops | bytes accessed | tf_op | source)
XLA Modules:
  0.0 64.6 jit_solution(10291881809545620281)
XLA Ops:
  0.0 1.8 %shard_map.82 = (bf16[256,256]{1,0:T(8,128)(2,1)S(1)}, bf16[256,256]{1,0:T(8,128)(2,1)S(1)}, bf16[256,256]{1,0:T(8,128)(2,1)S(1)}, bf16[256,256]{1,0:T(8,128)(2,...) custom-call(bf16[256,1024]{1,0:T(8,128)(2,1)} %keys_ref.3, ...), custom_call_target="tpu_custom_call" | custom-call | flops 262144 | bytes 3145728 | tf_op jit(solution)/shard_map/pallas_call | solution.py:78
  1.8 4.1 %collective-permute-start = (bf16[256,256]{1,0:T(8,128)(2,1)S(1)}, bf16[256,256]{1,0:T(8,128)(2,1)S(1)}, u32[]{:S(2)}, u32[]{:S(2)}) collective-permute-start(bf16[256,256]{1,0:T(8,128)(2,1)S(1)} %get-tuple-element.34), channel_id=1, source_target_pairs={{0,16},{4,20},{8,24},{12,28},{16,0},{20,4},{24,8},{28,12},{1,17},{... | collective-permute-start | bytes 393224 | tf_op jit(solution)/shard_map/ppermute | solution.py:106
  5.9 1.5 %collective-permute-start.1 = (bf16[256,256]{1,0:T(8,128)(2,1)S(1)}, bf16[256,256]{1,0:T(8,128)(2,1)S(1)}, u32[]{:S(2)}, u32[]{:S(2)}) collective-permute-start(bf16[256,256]{1,0:T(8,128)(2,1)S(1)} %get-tuple-element.38), channel_id=1, source_target_pairs={{0,4},{4,0},{8,12},{12,8},{16,20},{20,16},{24,28},{28,24},{1,5},{5... | collective-permute-start | bytes 393224 | tf_op jit(solution)/shard_map/ppermute | solution.py:106
  7.4 1.5 %collective-permute-start.2 = (bf16[256,256]{1,0:T(8,128)(2,1)S(1)}, bf16[256,256]{1,0:T(8,128)(2,1)S(1)}, u32[]{:S(2)}, u32[]{:S(2)}) collective-permute-start(bf16[256,256]{1,0:T(8,128)(2,1)S(1)} %get-tuple-element.39), channel_id=1, source_target_pairs={{0,12},{4,8},{8,4},{12,0},{16,28},{20,24},{24,20},{28,16},{1,13},{... | collective-permute-start | bytes 393224 | tf_op jit(solution)/shard_map/ppermute | solution.py:106
  8.9 0.4 collective-permute-start.3
  9.4 1.3 %collective-permute-start.4 = (bf16[256,256]{1,0:T(8,128)(2,1)S(1)}, bf16[256,256]{1,0:T(8,128)(2,1)S(1)}, u32[]{:S(2)}, u32[]{:S(2)}) collective-permute-start(bf16[256,256]{1,0:T(8,128)(2,1)S(1)} %get-tuple-element.41), channel_id=1, source_target_pairs={{0,20},{4,16},{8,28},{12,24},{16,4},{20,0},{24,12},{28,8},{1,21},{... | collective-permute-start | bytes 393224 | tf_op jit(solution)/shard_map/ppermute | solution.py:106
  10.7 1.6 %collective-permute-done.refs_0_.refs_1_ = bf16[256,256]{1,0:T(8,128)(2,1)S(1)} collective-permute-done((bf16[256,256]{1,0:T(8,128)(2,1)S(1)}, bf16[256,256]{1,0:T(8,128)(2,1)S(1)}, u32[]{:S(2)}, u32[]{:S(2)}) %collective-permute-start) | collective-permute-done | bytes 131104 | tf_op jit(solution)/shard_map/ppermute | solution.py:106
  12.3 3.6 %collective-permute-start.5 = (bf16[256,256]{1,0:T(8,128)(2,1)S(1)}, bf16[256,256]{1,0:T(8,128)(2,1)S(1)}, u32[]{:S(2)}, u32[]{:S(2)}) collective-permute-start(bf16[256,256]{1,0:T(8,128)(2,1)S(1)} %get-tuple-element.44), channel_id=1, source_target_pairs={{0,24},{4,28},{8,16},{12,20},{16,8},{20,12},{24,0},{28,4},{1,25},{... | collective-permute-start | bytes 393224 | tf_op jit(solution)/shard_map/ppermute | solution.py:106
  15.9 1.8 %collective-permute-start.6 = (bf16[256,256]{1,0:T(8,128)(2,1)S(1)}, bf16[256,256]{1,0:T(8,128)(2,1)S(1)}, u32[]{:S(2)}, u32[]{:S(2)}) collective-permute-start(bf16[256,256]{1,0:T(8,128)(2,1)S(1)} %get-tuple-element.45), channel_id=1, source_target_pairs={{0,28},{4,24},{8,20},{12,16},{16,12},{20,8},{24,4},{28,0},{1,29},{... | collective-permute-start | bytes 393224 | tf_op jit(solution)/shard_map/ppermute | solution.py:106
  17.7 1.3 %shard_map.83 = (bf16[512,512]{1,0:T(8,128)(2,1)S(1)}, bf16[256,1536]{1,0:T(8,128)(2,1)S(1)}) custom-call(bf16[512,512]{1,0:T(8,128)(2,1)} %constant.4.clone.fwd_hbm, bf16[256,1536]{1,0:T(8,128)(2,1)} %constant.5.clone.bwd_hbm, bf16[256,256]{1,0:T(8,128)(2,1)S(1)} %collective-permute-done.refs_0_.refs_1_), custom_call_target="tpu_custom_call" | custom-call | flops 1000000 | bytes 3145728 | tf_op jit(solution)/shard_map/pallas_call | solution.py:166
  19.5 2.2 %shard_map.84 = (f32[8,512,256]{2,1,0:T(8,128)S(1)}, f32[8,512,128]{2,1,0:T(8,128)S(1)}) custom-call(bf16[512,512]{1,0:T(8,128)(2,1)S(1)} %get-tuple-element.35.fwd_ref, bf16[256,256]{1,0:T(8,128)(2,1)S(1)} %get-tuple-element.37.refs_0_, bf16[256,256]{1,0:T(8,128)(2,1)S(1)} %collective-permute-done.refs_0_.refs_1_, ...), custom_call_target="tpu_custom_call" | custom-call | flops 805306368 | bytes 4194304 | tf_op jit(solution)/shard_map/pallas_call | solution.py:191
  21.7 1.0 %collective-permute-done.5.refs_0_ = bf16[256,256]{1,0:T(8,128)(2,1)S(1)} collective-permute-done((bf16[256,256]{1,0:T(8,128)(2,1)S(1)}, bf16[256,256]{1,0:T(8,128)(2,1)S(1)}, u32[]{:S(2)}, u32[]{:S(2)}) %collective-permute-start.5) | collective-permute-done | bytes 131104 | tf_op jit(solution)/shard_map/ppermute | solution.py:106
  22.7 3.0 %collective-permute-done.6.refs_1_ = bf16[256,256]{1,0:T(8,128)(2,1)S(1)} collective-permute-done((bf16[256,256]{1,0:T(8,128)(2,1)S(1)}, bf16[256,256]{1,0:T(8,128)(2,1)S(1)}, u32[]{:S(2)}, u32[]{:S(2)}) %collective-permute-start.6) | collective-permute-done | bytes 131104 | tf_op jit(solution)/shard_map/ppermute | solution.py:106
  25.7 2.2 %shard_map.85 = (bf16[256,128]{1,0:T(8,128)(2,1)S(1)}, bf16[256,128]{1,0:T(8,128)(2,1)S(1)}, bf16[256,128]{1,0:T(8,128)(2,1)S(1)}, bf16[256,128]{1,0:T(8,128)(2,...) custom-call(bf16[512,512]{1,0:T(8,128)(2,1)S(1)} %get-tuple-element., ...), custom_call_target="tpu_custom_call" | custom-call | flops 1073741824 | bytes 4194304 | tf_op jit(solution)/shard_map/pallas_call | solution.py:276
  27.9 3.9 %collective-permute-start.7 = (bf16[256,128]{1,0:T(8,128)(2,1)S(1)}, bf16[256,128]{1,0:T(8,128)(2,1)S(1)}, u32[]{:S(2)}, u32[]{:S(2)}) collective-permute-start(bf16[256,128]{1,0:T(8,128)(2,1)S(1)} %get-tuple-element.47), channel_id=1, source_target_pairs={{0,4},{4,0},{8,12},{12,8},{16,20},{20,16},{24,28},{28,24},{1,5},{5... | collective-permute-start | bytes 196616 | tf_op jit(solution)/shard_map/ppermute | solution.py:106
  31.8 1.9 %collective-permute-start.8 = (bf16[256,128]{1,0:T(8,128)(2,1)S(1)}, bf16[256,128]{1,0:T(8,128)(2,1)S(1)}, u32[]{:S(2)}, u32[]{:S(2)}) collective-permute-start(bf16[256,128]{1,0:T(8,128)(2,1)S(1)} %get-tuple-element.48), channel_id=1, source_target_pairs={{0,24},{4,28},{8,16},{12,20},{16,8},{20,12},{24,0},{28,4},{1,25},{... | collective-permute-start | bytes 196616 | tf_op jit(solution)/shard_map/ppermute | solution.py:106
  33.7 1.5 %collective-permute-start.9 = (bf16[256,128]{1,0:T(8,128)(2,1)S(1)}, bf16[256,128]{1,0:T(8,128)(2,1)S(1)}, u32[]{:S(2)}, u32[]{:S(2)}) collective-permute-start(bf16[256,128]{1,0:T(8,128)(2,1)S(1)} %get-tuple-element.49), channel_id=1, source_target_pairs={{0,28},{4,24},{8,20},{12,16},{16,12},{20,8},{24,4},{28,0},{1,29},{... | collective-permute-start | bytes 196616 | tf_op jit(solution)/shard_map/ppermute | solution.py:106
  35.2 2.3 %collective-permute-start.10 = (bf16[256,128]{1,0:T(8,128)(2,1)S(1)}, bf16[256,128]{1,0:T(8,128)(2,1)S(1)}, u32[]{:S(2)}, u32[]{:S(2)}) collective-permute-start(bf16[256,128]{1,0:T(8,128)(2,1)S(1)} %get-tuple-element.50), channel_id=1, source_target_pairs={{0,8},{4,12},{8,0},{12,4},{16,24},{20,28},{24,16},{28,20},{1,9},{5... | collective-permute-start | bytes 196616 | tf_op jit(solution)/shard_map/ppermute | solution.py:106
  37.5 1.1 %collective-permute-start.11 = (bf16[256,128]{1,0:T(8,128)(2,1)S(1)}, bf16[256,128]{1,0:T(8,128)(2,1)S(1)}, u32[]{:S(2)}, u32[]{:S(2)}) collective-permute-start(bf16[256,128]{1,0:T(8,128)(2,1)S(1)} %get-tuple-element.51), channel_id=1, source_target_pairs={{0,12},{4,8},{8,4},{12,0},{16,28},{20,24},{24,20},{28,16},{1,13},{... | collective-permute-start | bytes 196616 | tf_op jit(solution)/shard_map/ppermute | solution.py:106
  38.6 2.4 %collective-permute-start.12 = (bf16[256,128]{1,0:T(8,128)(2,1)S(1)}, bf16[256,128]{1,0:T(8,128)(2,1)S(1)}, u32[]{:S(2)}, u32[]{:S(2)}) collective-permute-start(bf16[256,128]{1,0:T(8,128)(2,1)S(1)} %get-tuple-element.54), channel_id=1, source_target_pairs={{0,16},{4,20},{8,24},{12,28},{16,0},{20,4},{24,8},{28,12},{1,17},{... | collective-permute-start | bytes 196616 | tf_op jit(solution)/shard_map/ppermute | solution.py:106
  40.9 1.0 %collective-permute-start.13 = (bf16[256,128]{1,0:T(8,128)(2,1)S(1)}, bf16[256,128]{1,0:T(8,128)(2,1)S(1)}, u32[]{:S(2)}, u32[]{:S(2)}) collective-permute-start(bf16[256,128]{1,0:T(8,128)(2,1)S(1)} %get-tuple-element.55), channel_id=1, source_target_pairs={{0,20},{4,16},{8,28},{12,24},{16,4},{20,0},{24,12},{28,8},{1,21},{... | collective-permute-start | bytes 196616 | tf_op jit(solution)/shard_map/ppermute | solution.py:106
  42.0 1.7 %collective-permute-done.11.refs_5_ = bf16[256,128]{1,0:T(8,128)(2,1)S(1)} collective-permute-done((bf16[256,128]{1,0:T(8,128)(2,1)S(1)}, bf16[256,128]{1,0:T(8,128)(2,1)S(1)}, u32[]{:S(2)}, u32[]{:S(2)}) %collective-permute-start.11) | collective-permute-done | bytes 65568 | tf_op jit(solution)/shard_map/ppermute | solution.py:106
  43.7 1.7 %shard_map.86 = (bf16[256,1024]{1,0:T(8,128)(2,1)S(1)}, f32[256,1024]{1,0:T(8,128)S(1)}, f32[256,1024]{1,0:T(8,128)S(1)}) custom-call(bf16[256,1024]{1,0:T(8,128)(2,1)S(1)} %copy-done.3, bf16[256,1024]{1,0:T(8,128)(2,1)S(1)} %copy-done.1, bf16[256,1024]{1,0:T(8,128)(2,1)S(1)} %copy-done.2, f32[1,1024]{1,0:T(1,128)S(1)} %bitcast.1, ...), custom_call_target="tpu_custom_call" | custom-call | flops 1073741824 | bytes 2621440 | tf_op jit(solution)/shard_map/pallas_call | solution.py:357
  45.4 2.3 %collective-permute-done.13.refs_1_ = bf16[256,128]{1,0:T(8,128)(2,1)S(1)} collective-permute-done((bf16[256,128]{1,0:T(8,128)(2,1)S(1)}, bf16[256,128]{1,0:T(8,128)(2,1)S(1)}, u32[]{:S(2)}, u32[]{:S(2)}) %collective-permute-start.13) | collective-permute-done | bytes 65568 | tf_op jit(solution)/shard_map/ppermute | solution.py:106
  48.4 0.6 collective-permute-start.15
  49.3 0.4 collective-permute-done.17.arrived_ref
  49.7 1.6 %collective-permute-start.18 = (bf16[256,512]{1,0:T(8,128)(2,1)S(1)}, bf16[256,512]{1,0:T(8,128)(2,1)S(1)}, u32[]{:S(2)}, u32[]{:S(2)}) collective-permute-start(bf16[256,512]{1,0:T(8,128)(2,1)S(1)} %shard_map.93), channel_id=1, source_target_pairs={{0,2},{2,0},{1,3},{3,1},{4,6},{6,4},{5,7},{7,5},{8,10},{10,8},{9,1... | collective-permute-start | bytes 786440 | tf_op jit(solution)/shard_map/ppermute | solution.py:584
  51.3 0.6 collective-permute-start.16
  52.0 1.3 %shard_map.89 = (bf16[256,1024]{1,0:T(8,128)(2,1)S(1)}, f32[256,1024]{1,0:T(8,128)S(1)}) custom-call(bf16[256,1024]{1,0:T(8,128)(2,1)S(1)} %shard_map.88.gated_ref, bf16[1024,4096]{1,0:T(8,128)(2,1)S(1)} %copy-done), custom_call_target="tpu_custom_call" | custom-call | flops 1073741824 | bytes 4194304 | tf_op jit(solution)/shard_map/pallas_call | solution.py:460
  53.4 5.5 %collective-permute-done.18.refs_1_ = bf16[256,512]{1,0:T(8,128)(2,1)S(1)} collective-permute-done((bf16[256,512]{1,0:T(8,128)(2,1)S(1)}, bf16[256,512]{1,0:T(8,128)(2,1)S(1)}, u32[]{:S(2)}, u32[]{:S(2)}) %collective-permute-start.18) | collective-permute-done | bytes 262176 | tf_op jit(solution)/shard_map/ppermute | solution.py:584
  58.9 4.8 %collective-permute-done.16.refs_0_ = bf16[256,512]{1,0:T(8,128)(2,1)S(1)} collective-permute-done((bf16[256,512]{1,0:T(8,128)(2,1)S(1)}, bf16[256,512]{1,0:T(8,128)(2,1)S(1)}, u32[]{:S(2)}, u32[]{:S(2)}) %collective-permute-start.16) | collective-permute-done | bytes 262176 | tf_op jit(solution)/shard_map/ppermute | solution.py:584
  63.7 0.9 %shard_map.95 = bf16[256,1024]{1,0:T(8,128)(2,1)} custom-call(f32[256,1024]{1,0:T(8,128)S(1)} %get-tuple-element.57.own_ref, bf16[256,1024]{1,0:T(8,128)(2,1)S(1)} %collective-permute-done.14.near_ref, bf16[256,512]{1,0:T(8,128)(2,1)S(1)} %collective-permute-done.16.refs_0_, bf16[256,512]{1,0:T(8,128)(2,1)S(1)} %collective-permute-done.18.refs_1_, ...), custom_call_target="tpu_custom_call" | custom-call | flops 262144 | bytes 2097152 | tf_op jit(solution)/shard_map/pallas_call | solution.py:527
  (30 shorter events, 1.6 us)
Async XLA Ops:
  1.8 10.5 %collective-permute-start = (bf16[256,256]{1,0:T(8,128)(2,1)S(1)}, bf16[256,256]{1,0:T(8,128)(2,1)S(1)}, u32[]{:S(2)}, u32[]{:S(2)}) collective-permute-start(bf16[256,256]{1,0:T(8,128)(2,1)S(1)} %get-tuple-element.34), channel_id=1, source_target_pairs={{0,16},{4,20},{8,24},{12,28},{16,0},{20,4},{24,8},{28,12},{1,17},{... | collective-permute-start | bytes 393224 | tf_op jit(solution)/shard_map/ppermute | solution.py:106
  5.9 10.0 %collective-permute-start.1 = (bf16[256,256]{1,0:T(8,128)(2,1)S(1)}, bf16[256,256]{1,0:T(8,128)(2,1)S(1)}, u32[]{:S(2)}, u32[]{:S(2)}) collective-permute-start(bf16[256,256]{1,0:T(8,128)(2,1)S(1)} %get-tuple-element.38), channel_id=1, source_target_pairs={{0,4},{4,0},{8,12},{12,8},{16,20},{20,16},{24,28},{28,24},{1,5},{5... | collective-permute-start | bytes 393224 | tf_op jit(solution)/shard_map/ppermute | solution.py:106
  7.4 11.7 %collective-permute-start.2 = (bf16[256,256]{1,0:T(8,128)(2,1)S(1)}, bf16[256,256]{1,0:T(8,128)(2,1)S(1)}, u32[]{:S(2)}, u32[]{:S(2)}) collective-permute-start(bf16[256,256]{1,0:T(8,128)(2,1)S(1)} %get-tuple-element.39), channel_id=1, source_target_pairs={{0,12},{4,8},{8,4},{12,0},{16,28},{20,24},{24,20},{28,16},{1,13},{... | collective-permute-start | bytes 393224 | tf_op jit(solution)/shard_map/ppermute | solution.py:106
  8.9 10.6 %collective-permute-start.3 = (bf16[256,256]{1,0:T(8,128)(2,1)S(1)}, bf16[256,256]{1,0:T(8,128)(2,1)S(1)}, u32[]{:S(2)}, u32[]{:S(2)}) collective-permute-start(bf16[256,256]{1,0:T(8,128)(2,1)S(1)} %get-tuple-element.40), channel_id=1, source_target_pairs={{0,8},{4,12},{8,0},{12,4},{16,24},{20,28},{24,16},{28,20},{1,9},{5... | collective-permute-start | bytes 393224 | tf_op jit(solution)/shard_map/ppermute | solution.py:106
  9.4 10.1 %collective-permute-start.4 = (bf16[256,256]{1,0:T(8,128)(2,1)S(1)}, bf16[256,256]{1,0:T(8,128)(2,1)S(1)}, u32[]{:S(2)}, u32[]{:S(2)}) collective-permute-start(bf16[256,256]{1,0:T(8,128)(2,1)S(1)} %get-tuple-element.41), channel_id=1, source_target_pairs={{0,20},{4,16},{8,28},{12,24},{16,4},{20,0},{24,12},{28,8},{1,21},{... | collective-permute-start | bytes 393224 | tf_op jit(solution)/shard_map/ppermute | solution.py:106
  12.3 10.4 %collective-permute-start.5 = (bf16[256,256]{1,0:T(8,128)(2,1)S(1)}, bf16[256,256]{1,0:T(8,128)(2,1)S(1)}, u32[]{:S(2)}, u32[]{:S(2)}) collective-permute-start(bf16[256,256]{1,0:T(8,128)(2,1)S(1)} %get-tuple-element.44), channel_id=1, source_target_pairs={{0,24},{4,28},{8,16},{12,20},{16,8},{20,12},{24,0},{28,4},{1,25},{... | collective-permute-start | bytes 393224 | tf_op jit(solution)/shard_map/ppermute | solution.py:106
  15.9 9.8 %collective-permute-start.6 = (bf16[256,256]{1,0:T(8,128)(2,1)S(1)}, bf16[256,256]{1,0:T(8,128)(2,1)S(1)}, u32[]{:S(2)}, u32[]{:S(2)}) collective-permute-start(bf16[256,256]{1,0:T(8,128)(2,1)S(1)} %get-tuple-element.45), channel_id=1, source_target_pairs={{0,28},{4,24},{8,20},{12,16},{16,12},{20,8},{24,4},{28,0},{1,29},{... | collective-permute-start | bytes 393224 | tf_op jit(solution)/shard_map/ppermute | solution.py:106
  19.5 24.2 %copy-start = (bf16[1024,4096]{1,0:T(8,128)(2,1)S(1)}, bf16[1024,4096]{1,0:T(8,128)(2,1)}, u32[]{:S(2)}) copy-start(bf16[1024,4096]{1,0:T(8,128)(2,1)} %weight_ref.9) | copy-start | bytes 25165828
  21.6 22.0 %copy-start.1 = (bf16[256,1024]{1,0:T(8,128)(2,1)S(1)}, bf16[256,1024]{1,0:T(8,128)(2,1)}, u32[]{:S(2)}) copy-start(bf16[256,1024]{1,0:T(8,128)(2,1)} %keys_ref.3) | copy-start | bytes 1572868
  21.7 22.0 %copy-start.2 = (bf16[256,1024]{1,0:T(8,128)(2,1)S(1)}, bf16[256,1024]{1,0:T(8,128)(2,1)}, u32[]{:S(2)}) copy-start(bf16[256,1024]{1,0:T(8,128)(2,1)} %values_ref.3) | copy-start | bytes 1572868
  21.7 22.0 %copy-start.3 = (bf16[256,1024]{1,0:T(8,128)(2,1)S(1)}, bf16[256,1024]{1,0:T(8,128)(2,1)}, u32[]{:S(2)}) copy-start(bf16[256,1024]{1,0:T(8,128)(2,1)} %queries_ref.3) | copy-start | bytes 1572868
  21.7 22.0 %copy-start.4 = (f32[1024]{0:T(1024)S(1)}, f32[1024]{0:T(1024)}, u32[]{:S(2)}) copy-start(f32[1024]{0:T(1024)} %param.12) | copy-start | bytes 12292
  27.9 10.6 %collective-permute-start.7 = (bf16[256,128]{1,0:T(8,128)(2,1)S(1)}, bf16[256,128]{1,0:T(8,128)(2,1)S(1)}, u32[]{:S(2)}, u32[]{:S(2)}) collective-permute-start(bf16[256,128]{1,0:T(8,128)(2,1)S(1)} %get-tuple-element.47), channel_id=1, source_target_pairs={{0,4},{4,0},{8,12},{12,8},{16,20},{20,16},{24,28},{28,24},{1,5},{5... | collective-permute-start | bytes 196616 | tf_op jit(solution)/shard_map/ppermute | solution.py:106
  31.8 9.1 %collective-permute-start.8 = (bf16[256,128]{1,0:T(8,128)(2,1)S(1)}, bf16[256,128]{1,0:T(8,128)(2,1)S(1)}, u32[]{:S(2)}, u32[]{:S(2)}) collective-permute-start(bf16[256,128]{1,0:T(8,128)(2,1)S(1)} %get-tuple-element.48), channel_id=1, source_target_pairs={{0,24},{4,28},{8,16},{12,20},{16,8},{20,12},{24,0},{28,4},{1,25},{... | collective-permute-start | bytes 196616 | tf_op jit(solution)/shard_map/ppermute | solution.py:106
  33.7 8.3 %collective-permute-start.9 = (bf16[256,128]{1,0:T(8,128)(2,1)S(1)}, bf16[256,128]{1,0:T(8,128)(2,1)S(1)}, u32[]{:S(2)}, u32[]{:S(2)}) collective-permute-start(bf16[256,128]{1,0:T(8,128)(2,1)S(1)} %get-tuple-element.49), channel_id=1, source_target_pairs={{0,28},{4,24},{8,20},{12,16},{16,12},{20,8},{24,4},{28,0},{1,29},{... | collective-permute-start | bytes 196616 | tf_op jit(solution)/shard_map/ppermute | solution.py:106
  35.2 6.8 %collective-permute-start.10 = (bf16[256,128]{1,0:T(8,128)(2,1)S(1)}, bf16[256,128]{1,0:T(8,128)(2,1)S(1)}, u32[]{:S(2)}, u32[]{:S(2)}) collective-permute-start(bf16[256,128]{1,0:T(8,128)(2,1)S(1)} %get-tuple-element.50), channel_id=1, source_target_pairs={{0,8},{4,12},{8,0},{12,4},{16,24},{20,28},{24,16},{28,20},{1,9},{5... | collective-permute-start | bytes 196616 | tf_op jit(solution)/shard_map/ppermute | solution.py:106
  37.5 6.1 %collective-permute-start.11 = (bf16[256,128]{1,0:T(8,128)(2,1)S(1)}, bf16[256,128]{1,0:T(8,128)(2,1)S(1)}, u32[]{:S(2)}, u32[]{:S(2)}) collective-permute-start(bf16[256,128]{1,0:T(8,128)(2,1)S(1)} %get-tuple-element.51), channel_id=1, source_target_pairs={{0,12},{4,8},{8,4},{12,0},{16,28},{20,24},{24,20},{28,16},{1,13},{... | collective-permute-start | bytes 196616 | tf_op jit(solution)/shard_map/ppermute | solution.py:106
  38.6 6.8 %collective-permute-start.12 = (bf16[256,128]{1,0:T(8,128)(2,1)S(1)}, bf16[256,128]{1,0:T(8,128)(2,1)S(1)}, u32[]{:S(2)}, u32[]{:S(2)}) collective-permute-start(bf16[256,128]{1,0:T(8,128)(2,1)S(1)} %get-tuple-element.54), channel_id=1, source_target_pairs={{0,16},{4,20},{8,24},{12,28},{16,0},{20,4},{24,8},{28,12},{1,17},{... | collective-permute-start | bytes 196616 | tf_op jit(solution)/shard_map/ppermute | solution.py:106
  40.9 6.8 %collective-permute-start.13 = (bf16[256,128]{1,0:T(8,128)(2,1)S(1)}, bf16[256,128]{1,0:T(8,128)(2,1)S(1)}, u32[]{:S(2)}, u32[]{:S(2)}) collective-permute-start(bf16[256,128]{1,0:T(8,128)(2,1)S(1)} %get-tuple-element.55), channel_id=1, source_target_pairs={{0,20},{4,16},{8,28},{12,24},{16,4},{20,0},{24,12},{28,8},{1,21},{... | collective-permute-start | bytes 196616 | tf_op jit(solution)/shard_map/ppermute | solution.py:106
  48.1 1.6 %collective-permute-start.17 = (bf16[256,512]{1,0:T(8,128)(2,1)S(1)}, bf16[256,512]{1,0:T(8,128)(2,1)S(1)}, u32[]{:S(2)}, u32[]{:S(2)}) collective-permute-start(bf16[256,512]{1,0:T(8,128)(2,1)S(1)} %get-tuple-element.62), channel_id=1, source_target_pairs={{0,1},{1,0},{2,3},{3,2},{4,5},{5,4},{6,7},{7,6},{8,9},{9,8},{10,11... | collective-permute-start | bytes 786440 | tf_op jit(solution)/shard_map/ppermute | solution.py:583
  48.4 2.9 %collective-permute-start.15 = (bf16[256,512]{1,0:T(8,128)(2,1)S(1)}, bf16[256,512]{1,0:T(8,128)(2,1)S(1)}, u32[]{:S(2)}, u32[]{:S(2)}) collective-permute-start(bf16[256,512]{1,0:T(8,128)(2,1)S(1)} %shard_map.91), channel_id=1, source_target_pairs={{0,1},{1,0},{2,3},{3,2},{4,5},{5,4},{6,7},{7,6},{8,9},{9,8},{10,11... | collective-permute-start | bytes 786440 | tf_op jit(solution)/shard_map/ppermute | solution.py:583
  49.7 9.2 %collective-permute-start.18 = (bf16[256,512]{1,0:T(8,128)(2,1)S(1)}, bf16[256,512]{1,0:T(8,128)(2,1)S(1)}, u32[]{:S(2)}, u32[]{:S(2)}) collective-permute-start(bf16[256,512]{1,0:T(8,128)(2,1)S(1)} %shard_map.93), channel_id=1, source_target_pairs={{0,2},{2,0},{1,3},{3,1},{4,6},{6,4},{5,7},{7,5},{8,10},{10,8},{9,1... | collective-permute-start | bytes 786440 | tf_op jit(solution)/shard_map/ppermute | solution.py:584
  51.3 12.4 %collective-permute-start.16 = (bf16[256,512]{1,0:T(8,128)(2,1)S(1)}, bf16[256,512]{1,0:T(8,128)(2,1)S(1)}, u32[]{:S(2)}, u32[]{:S(2)}) collective-permute-start(bf16[256,512]{1,0:T(8,128)(2,1)S(1)} %shard_map.92), channel_id=1, source_target_pairs={{0,2},{2,0},{1,3},{3,1},{4,6},{6,4},{5,7},{7,5},{8,10},{10,8},{9,1... | collective-permute-start | bytes 786440 | tf_op jit(solution)/shard_map/ppermute | solution.py:584
  53.3 10.4 %collective-permute-start.14 = (bf16[256,1024]{1,0:T(8,128)(2,1)S(1)}, bf16[256,1024]{1,0:T(8,128)(2,1)S(1)}, u32[]{:S(2)}, u32[]{:S(2)}) collective-permute-start(bf16[256,1024]{1,0:T(8,128)(2,1)S(1)} %get-tuple-element.58), channel_id=1, source_target_pairs={{0,1},{1,0},{2,3},{3,2},{4,5},{5,4},{6,7},{7,6},{8,9},{9,8},{10,11... | collective-permute-start | bytes 1572872 | tf_op jit(solution)/shard_map/ppermute | solution.py:587

commit v11 on v10

--- a/solution.py
+++ b/solution.py
@@ -97,7 +97,7 @@
     half = n_peers // 2
     near, far = list(range(1, half)), list(range(half, n_peers))
     if back:
-        return [0, near[0]] + far[2:] + near[1:] + far[:2]
+        return [0, near[0], far[2], far[0], far[1], near[1], far[3]] + near[2:]
     return [0, far[0], near[0]] + near[:0:-1] + far[1:]
 
 

time: 64.8 us -> 64.6 us (level)
  waiting for transfers between devices: 20.8 us -> 20 us
    ppermute x14, waiting for transfers between devices: 10.1 us -> 9.25 us  [exchange(): lax.ppermute(block, 'seq', [(i, i ^ slot) for i in range(n_peers)])]
where the time goes in v11:
time: 64.6 us; the launch traced here: 64.5 us
  starting transfers between devices  31.8 us (49%)
  waiting for transfers between devices  20 us (31%)
  Pallas kernels  12.4 us (19%)
    ppermute x14, starting transfers between devices, exchange(): lax.ppermute(block, 'seq', [(i, i ^ slot) for i in range(n_peers)])  29 us
    ppermute x2, waiting for transfers between devices, body(): lax.ppermute(add(*pair), 'fsdp', across)  10.4 us
    ppermute x14, waiting for transfers between devices, exchange(): lax.ppermute(block, 'seq', [(i, i ^ slot) for i in range(n_peers)])  9.25 us
    pallas_call x1, Pallas kernels, conv_fast(): pl.pallas_call(conv_kernel, in_specs=[whole] * 6, out_specs=[whole] * n_b...  2.23 us
    ppermute x2, starting transfers between devices, body(): lax.ppermute(add(*pair), 'fsdp', across)  2.16 us
    pallas_call x1, Pallas kernels, spectra(): pl.pallas_call(functools.partial(spectra_kernel, n_peers), in_specs=[whol...  2.15 us
    pallas_call x1, Pallas kernels, pre(): pl.pallas_call(functools.partial(pre_kernel, n_peers), in_specs=[pl.Block...  1.77 us
    pallas_call x1, Pallas kernels, gate_early(): pl.pallas_call(functools.partial(gate_early_kernel, n_peers), in_specs=[w...  1.73 us
  transfers between devices with their start and end apart: 19, of which 9 were waited for; matrix products, arithmetic and copies ran while one was open for 0% of the time, Pallas kernels for 11%

profile of v11, /device:TPU:0, one launch (start us, length us, event | category | flops | bytes accessed | tf_op | source)
XLA Modules:
  0.0 64.5 jit_solution(10710466571372058305)
XLA Ops:
  0.0 1.8 %shard_map.82 = (bf16[256,256]{1,0:T(8,128)(2,1)S(1)}, bf16[256,256]{1,0:T(8,128)(2,1)S(1)}, bf16[256,256]{1,0:T(8,128)(2,1)S(1)}, bf16[256,256]{1,0:T(8,128)(2,...) custom-call(bf16[256,1024]{1,0:T(8,128)(2,1)} %keys_ref.3, ...), custom_call_target="tpu_custom_call" | custom-call | flops 262144 | bytes 3145728 | tf_op jit(solution)/shard_map/pallas_call | solution.py:78
  1.8 4.1 %collective-permute-start = (bf16[256,256]{1,0:T(8,128)(2,1)S(1)}, bf16[256,256]{1,0:T(8,128)(2,1)S(1)}, u32[]{:S(2)}, u32[]{:S(2)}) collective-permute-start(bf16[256,256]{1,0:T(8,128)(2,1)S(1)} %get-tuple-element.34), channel_id=1, source_target_pairs={{0,16},{4,20},{8,24},{12,28},{16,0},{20,4},{24,8},{28,12},{1,17},{... | collective-permute-start | bytes 393224 | tf_op jit(solution)/shard_map/ppermute | solution.py:106
  5.9 1.5 %collective-permute-start.1 = (bf16[256,256]{1,0:T(8,128)(2,1)S(1)}, bf16[256,256]{1,0:T(8,128)(2,1)S(1)}, u32[]{:S(2)}, u32[]{:S(2)}) collective-permute-start(bf16[256,256]{1,0:T(8,128)(2,1)S(1)} %get-tuple-element.38), channel_id=1, source_target_pairs={{0,4},{4,0},{8,12},{12,8},{16,20},{20,16},{24,28},{28,24},{1,5},{5... | collective-permute-start | bytes 393224 | tf_op jit(solution)/shard_map/ppermute | solution.py:106
  7.4 1.5 %collective-permute-start.2 = (bf16[256,256]{1,0:T(8,128)(2,1)S(1)}, bf16[256,256]{1,0:T(8,128)(2,1)S(1)}, u32[]{:S(2)}, u32[]{:S(2)}) collective-permute-start(bf16[256,256]{1,0:T(8,128)(2,1)S(1)} %get-tuple-element.39), channel_id=1, source_target_pairs={{0,12},{4,8},{8,4},{12,0},{16,28},{20,24},{24,20},{28,16},{1,13},{... | collective-permute-start | bytes 393224 | tf_op jit(solution)/shard_map/ppermute | solution.py:106
  8.9 0.4 collective-permute-start.3
  9.4 1.3 %collective-permute-start.4 = (bf16[256,256]{1,0:T(8,128)(2,1)S(1)}, bf16[256,256]{1,0:T(8,128)(2,1)S(1)}, u32[]{:S(2)}, u32[]{:S(2)}) collective-permute-start(bf16[256,256]{1,0:T(8,128)(2,1)S(1)} %get-tuple-element.41), channel_id=1, source_target_pairs={{0,20},{4,16},{8,28},{12,24},{16,4},{20,0},{24,12},{28,8},{1,21},{... | collective-permute-start | bytes 393224 | tf_op jit(solution)/shard_map/ppermute | solution.py:106
  10.7 1.6 %collective-permute-done.refs_0_.refs_1_ = bf16[256,256]{1,0:T(8,128)(2,1)S(1)} collective-permute-done((bf16[256,256]{1,0:T(8,128)(2,1)S(1)}, bf16[256,256]{1,0:T(8,128)(2,1)S(1)}, u32[]{:S(2)}, u32[]{:S(2)}) %collective-permute-start) | collective-permute-done | bytes 131104 | tf_op jit(solution)/shard_map/ppermute | solution.py:106
  12.3 3.6 %collective-permute-start.5 = (bf16[256,256]{1,0:T(8,128)(2,1)S(1)}, bf16[256,256]{1,0:T(8,128)(2,1)S(1)}, u32[]{:S(2)}, u32[]{:S(2)}) collective-permute-start(bf16[256,256]{1,0:T(8,128)(2,1)S(1)} %get-tuple-element.44), channel_id=1, source_target_pairs={{0,24},{4,28},{8,16},{12,20},{16,8},{20,12},{24,0},{28,4},{1,25},{... | collective-permute-start | bytes 393224 | tf_op jit(solution)/shard_map/ppermute | solution.py:106
  15.9 1.8 %collective-permute-start.6 = (bf16[256,256]{1,0:T(8,128)(2,1)S(1)}, bf16[256,256]{1,0:T(8,128)(2,1)S(1)}, u32[]{:S(2)}, u32[]{:S(2)}) collective-permute-start(bf16[256,256]{1,0:T(8,128)(2,1)S(1)} %get-tuple-element.45), channel_id=1, source_target_pairs={{0,28},{4,24},{8,20},{12,16},{16,12},{20,8},{24,4},{28,0},{1,29},{... | collective-permute-start | bytes 393224 | tf_op jit(solution)/shard_map/ppermute | solution.py:106
  17.7 1.3 %shard_map.83 = (bf16[512,512]{1,0:T(8,128)(2,1)S(1)}, bf16[256,1536]{1,0:T(8,128)(2,1)S(1)}) custom-call(bf16[512,512]{1,0:T(8,128)(2,1)} %constant.4.clone.fwd_hbm, bf16[256,1536]{1,0:T(8,128)(2,1)} %constant.5.clone.bwd_hbm, bf16[256,256]{1,0:T(8,128)(2,1)S(1)} %collective-permute-done.refs_0_.refs_1_), custom_call_target="tpu_custom_call" | custom-call | flops 1000000 | bytes 3145728 | tf_op jit(solution)/shard_map/pallas_call | solution.py:166
  19.5 2.2 %shard_map.84 = (f32[8,512,256]{2,1,0:T(8,128)S(1)}, f32[8,512,128]{2,1,0:T(8,128)S(1)}) custom-call(bf16[512,512]{1,0:T(8,128)(2,1)S(1)} %get-tuple-element.35.fwd_ref, bf16[256,256]{1,0:T(8,128)(2,1)S(1)} %get-tuple-element.37.refs_0_, bf16[256,256]{1,0:T(8,128)(2,1)S(1)} %collective-permute-done.refs_0_.refs_1_, ...), custom_call_target="tpu_custom_call" | custom-call | flops 805306368 | bytes 4194304 | tf_op jit(solution)/shard_map/pallas_call | solution.py:191
  21.7 1.0 %collective-permute-done.5.refs_0_ = bf16[256,256]{1,0:T(8,128)(2,1)S(1)} collective-permute-done((bf16[256,256]{1,0:T(8,128)(2,1)S(1)}, bf16[256,256]{1,0:T(8,128)(2,1)S(1)}, u32[]{:S(2)}, u32[]{:S(2)}) %collective-permute-start.5) | collective-permute-done | bytes 131104 | tf_op jit(solution)/shard_map/ppermute | solution.py:106
  22.7 3.0 %collective-permute-done.6.refs_1_ = bf16[256,256]{1,0:T(8,128)(2,1)S(1)} collective-permute-done((bf16[256,256]{1,0:T(8,128)(2,1)S(1)}, bf16[256,256]{1,0:T(8,128)(2,1)S(1)}, u32[]{:S(2)}, u32[]{:S(2)}) %collective-permute-start.6) | collective-permute-done | bytes 131104 | tf_op jit(solution)/shard_map/ppermute | solution.py:106
  25.7 2.2 %shard_map.85 = (bf16[256,128]{1,0:T(8,128)(2,1)S(1)}, bf16[256,128]{1,0:T(8,128)(2,1)S(1)}, bf16[256,128]{1,0:T(8,128)(2,1)S(1)}, bf16[256,128]{1,0:T(8,128)(2,...) custom-call(bf16[512,512]{1,0:T(8,128)(2,1)S(1)} %get-tuple-element., ...), custom_call_target="tpu_custom_call" | custom-call | flops 1073741824 | bytes 4194304 | tf_op jit(solution)/shard_map/pallas_call | solution.py:276
  27.9 3.9 %collective-permute-start.7 = (bf16[256,128]{1,0:T(8,128)(2,1)S(1)}, bf16[256,128]{1,0:T(8,128)(2,1)S(1)}, u32[]{:S(2)}, u32[]{:S(2)}) collective-permute-start(bf16[256,128]{1,0:T(8,128)(2,1)S(1)} %get-tuple-element.47), channel_id=1, source_target_pairs={{0,4},{4,0},{8,12},{12,8},{16,20},{20,16},{24,28},{28,24},{1,5},{5... | collective-permute-start | bytes 196616 | tf_op jit(solution)/shard_map/ppermute | solution.py:106
  31.8 1.9 %collective-permute-start.8 = (bf16[256,128]{1,0:T(8,128)(2,1)S(1)}, bf16[256,128]{1,0:T(8,128)(2,1)S(1)}, u32[]{:S(2)}, u32[]{:S(2)}) collective-permute-start(bf16[256,128]{1,0:T(8,128)(2,1)S(1)} %get-tuple-element.48), channel_id=1, source_target_pairs={{0,24},{4,28},{8,16},{12,20},{16,8},{20,12},{24,0},{28,4},{1,25},{... | collective-permute-start | bytes 196616 | tf_op jit(solution)/shard_map/ppermute | solution.py:106
  33.7 2.7 %collective-permute-start.9 = (bf16[256,128]{1,0:T(8,128)(2,1)S(1)}, bf16[256,128]{1,0:T(8,128)(2,1)S(1)}, u32[]{:S(2)}, u32[]{:S(2)}) collective-permute-start(bf16[256,128]{1,0:T(8,128)(2,1)S(1)} %get-tuple-element.49), channel_id=1, source_target_pairs={{0,16},{4,20},{8,24},{12,28},{16,0},{20,4},{24,8},{28,12},{1,17},{... | collective-permute-start | bytes 196616 | tf_op jit(solution)/shard_map/ppermute | solution.py:106
  36.4 0.6 collective-permute-start.10
  36.9 3.5 %collective-permute-start.11 = (bf16[256,128]{1,0:T(8,128)(2,1)S(1)}, bf16[256,128]{1,0:T(8,128)(2,1)S(1)}, u32[]{:S(2)}, u32[]{:S(2)}) collective-permute-start(bf16[256,128]{1,0:T(8,128)(2,1)S(1)} %get-tuple-element.51), channel_id=1, source_target_pairs={{0,8},{4,12},{8,0},{12,4},{16,24},{20,28},{24,16},{28,20},{1,9},{5... | collective-permute-start | bytes 196616 | tf_op jit(solution)/shard_map/ppermute | solution.py:106
  40.4 1.2 %collective-permute-start.12 = (bf16[256,128]{1,0:T(8,128)(2,1)S(1)}, bf16[256,128]{1,0:T(8,128)(2,1)S(1)}, u32[]{:S(2)}, u32[]{:S(2)}) collective-permute-start(bf16[256,128]{1,0:T(8,128)(2,1)S(1)} %get-tuple-element.54), channel_id=1, source_target_pairs={{0,28},{4,24},{8,20},{12,16},{16,12},{20,8},{24,4},{28,0},{1,29},{... | collective-permute-start | bytes 196616 | tf_op jit(solution)/shard_map/ppermute | solution.py:106
  41.7 0.9 %collective-permute-start.13 = (bf16[256,128]{1,0:T(8,128)(2,1)S(1)}, bf16[256,128]{1,0:T(8,128)(2,1)S(1)}, u32[]{:S(2)}, u32[]{:S(2)}) collective-permute-start(bf16[256,128]{1,0:T(8,128)(2,1)S(1)} %get-tuple-element.55), channel_id=1, source_target_pairs={{0,12},{4,8},{8,4},{12,0},{16,28},{20,24},{24,20},{28,16},{1,13},{... | collective-permute-start | bytes 196616 | tf_op jit(solution)/shard_map/ppermute | solution.py:106
  42.6 1.2 %collective-permute-done.9.refs_3_ = bf16[256,128]{1,0:T(8,128)(2,1)S(1)} collective-permute-done((bf16[256,128]{1,0:T(8,128)(2,1)S(1)}, bf16[256,128]{1,0:T(8,128)(2,1)S(1)}, u32[]{:S(2)}, u32[]{:S(2)}) %collective-permute-start.9) | collective-permute-done | bytes 65568 | tf_op jit(solution)/shard_map/ppermute | solution.py:106
  43.8 1.9 %collective-permute-done.10.refs_4_ = bf16[256,128]{1,0:T(8,128)(2,1)S(1)} collective-permute-done((bf16[256,128]{1,0:T(8,128)(2,1)S(1)}, bf16[256,128]{1,0:T(8,128)(2,1)S(1)}, u32[]{:S(2)}, u32[]{:S(2)}) %collective-permute-start.10) | collective-permute-done | bytes 65568 | tf_op jit(solution)/shard_map/ppermute | solution.py:106
  45.8 1.7 %shard_map.86 = (bf16[256,1024]{1,0:T(8,128)(2,1)S(1)}, f32[256,1024]{1,0:T(8,128)S(1)}, f32[256,1024]{1,0:T(8,128)S(1)}) custom-call(bf16[256,1024]{1,0:T(8,128)(2,1)S(1)} %copy-done.3, bf16[256,1024]{1,0:T(8,128)(2,1)S(1)} %copy-done.1, bf16[256,1024]{1,0:T(8,128)(2,1)S(1)} %copy-done.2, f32[1,1024]{1,0:T(1,128)S(1)} %bitcast.1, ...), custom_call_target="tpu_custom_call" | custom-call | flops 1073741824 | bytes 2621440 | tf_op jit(solution)/shard_map/pallas_call | solution.py:357
  48.2 0.5 collective-permute-start.15
  49.1 0.4 collective-permute-done.17.arrived_ref
  49.5 1.6 %collective-permute-start.18 = (bf16[256,512]{1,0:T(8,128)(2,1)S(1)}, bf16[256,512]{1,0:T(8,128)(2,1)S(1)}, u32[]{:S(2)}, u32[]{:S(2)}) collective-permute-start(bf16[256,512]{1,0:T(8,128)(2,1)S(1)} %shard_map.93), channel_id=1, source_target_pairs={{0,2},{2,0},{1,3},{3,1},{4,6},{6,4},{5,7},{7,5},{8,10},{10,8},{9,1... | collective-permute-start | bytes 786440 | tf_op jit(solution)/shard_map/ppermute | solution.py:584
  51.2 0.6 collective-permute-start.16
  51.8 1.3 %shard_map.89 = (bf16[256,1024]{1,0:T(8,128)(2,1)S(1)}, f32[256,1024]{1,0:T(8,128)S(1)}) custom-call(bf16[256,1024]{1,0:T(8,128)(2,1)S(1)} %shard_map.88.gated_ref, bf16[1024,4096]{1,0:T(8,128)(2,1)S(1)} %copy-done), custom_call_target="tpu_custom_call" | custom-call | flops 1073741824 | bytes 4194304 | tf_op jit(solution)/shard_map/pallas_call | solution.py:460
  53.2 5.5 %collective-permute-done.18.refs_1_ = bf16[256,512]{1,0:T(8,128)(2,1)S(1)} collective-permute-done((bf16[256,512]{1,0:T(8,128)(2,1)S(1)}, bf16[256,512]{1,0:T(8,128)(2,1)S(1)}, u32[]{:S(2)}, u32[]{:S(2)}) %collective-permute-start.18) | collective-permute-done | bytes 262176 | tf_op jit(solution)/shard_map/ppermute | solution.py:584
  58.8 4.8 %collective-permute-done.16.refs_0_ = bf16[256,512]{1,0:T(8,128)(2,1)S(1)} collective-permute-done((bf16[256,512]{1,0:T(8,128)(2,1)S(1)}, bf16[256,512]{1,0:T(8,128)(2,1)S(1)}, u32[]{:S(2)}, u32[]{:S(2)}) %collective-permute-start.16) | collective-permute-done | bytes 262176 | tf_op jit(solution)/shard_map/ppermute | solution.py:584
  63.6 0.9 %shard_map.95 = bf16[256,1024]{1,0:T(8,128)(2,1)} custom-call(f32[256,1024]{1,0:T(8,128)S(1)} %get-tuple-element.57.own_ref, bf16[256,1024]{1,0:T(8,128)(2,1)S(1)} %collective-permute-done.14.near_ref, bf16[256,512]{1,0:T(8,128)(2,1)S(1)} %collective-permute-done.16.refs_0_, bf16[256,512]{1,0:T(8,128)(2,1)S(1)} %collective-permute-done.18.refs_1_, ...), custom_call_target="tpu_custom_call" | custom-call | flops 262144 | bytes 2097152 | tf_op jit(solution)/shard_map/pallas_call | solution.py:527
  (30 shorter events, 1.6 us)
Async XLA Ops:
  1.8 10.5 %collective-permute-start = (bf16[256,256]{1,0:T(8,128)(2,1)S(1)}, bf16[256,256]{1,0:T(8,128)(2,1)S(1)}, u32[]{:S(2)}, u32[]{:S(2)}) collective-permute-start(bf16[256,256]{1,0:T(8,128)(2,1)S(1)} %get-tuple-element.34), channel_id=1, source_target_pairs={{0,16},{4,20},{8,24},{12,28},{16,0},{20,4},{24,8},{28,12},{1,17},{... | collective-permute-start | bytes 393224 | tf_op jit(solution)/shard_map/ppermute | solution.py:106
  5.9 10.0 %collective-permute-start.1 = (bf16[256,256]{1,0:T(8,128)(2,1)S(1)}, bf16[256,256]{1,0:T(8,128)(2,1)S(1)}, u32[]{:S(2)}, u32[]{:S(2)}) collective-permute-start(bf16[256,256]{1,0:T(8,128)(2,1)S(1)} %get-tuple-element.38), channel_id=1, source_target_pairs={{0,4},{4,0},{8,12},{12,8},{16,20},{20,16},{24,28},{28,24},{1,5},{5... | collective-permute-start | bytes 393224 | tf_op jit(solution)/shard_map/ppermute | solution.py:106
  7.4 11.7 %collective-permute-start.2 = (bf16[256,256]{1,0:T(8,128)(2,1)S(1)}, bf16[256,256]{1,0:T(8,128)(2,1)S(1)}, u32[]{:S(2)}, u32[]{:S(2)}) collective-permute-start(bf16[256,256]{1,0:T(8,128)(2,1)S(1)} %get-tuple-element.39), channel_id=1, source_target_pairs={{0,12},{4,8},{8,4},{12,0},{16,28},{20,24},{24,20},{28,16},{1,13},{... | collective-permute-start | bytes 393224 | tf_op jit(solution)/shard_map/ppermute | solution.py:106
  8.9 10.6 %collective-permute-start.3 = (bf16[256,256]{1,0:T(8,128)(2,1)S(1)}, bf16[256,256]{1,0:T(8,128)(2,1)S(1)}, u32[]{:S(2)}, u32[]{:S(2)}) collective-permute-start(bf16[256,256]{1,0:T(8,128)(2,1)S(1)} %get-tuple-element.40), channel_id=1, source_target_pairs={{0,8},{4,12},{8,0},{12,4},{16,24},{20,28},{24,16},{28,20},{1,9},{5... | collective-permute-start | bytes 393224 | tf_op jit(solution)/shard_map/ppermute | solution.py:106
  9.4 10.1 %collective-permute-start.4 = (bf16[256,256]{1,0:T(8,128)(2,1)S(1)}, bf16[256,256]{1,0:T(8,128)(2,1)S(1)}, u32[]{:S(2)}, u32[]{:S(2)}) collective-permute-start(bf16[256,256]{1,0:T(8,128)(2,1)S(1)} %get-tuple-element.41), channel_id=1, source_target_pairs={{0,20},{4,16},{8,28},{12,24},{16,4},{20,0},{24,12},{28,8},{1,21},{... | collective-permute-start | bytes 393224 | tf_op jit(solution)/shard_map/ppermute | solution.py:106
  12.3 10.4 %collective-permute-start.5 = (bf16[256,256]{1,0:T(8,128)(2,1)S(1)}, bf16[256,256]{1,0:T(8,128)(2,1)S(1)}, u32[]{:S(2)}, u32[]{:S(2)}) collective-permute-start(bf16[256,256]{1,0:T(8,128)(2,1)S(1)} %get-tuple-element.44), channel_id=1, source_target_pairs={{0,24},{4,28},{8,16},{12,20},{16,8},{20,12},{24,0},{28,4},{1,25},{... | collective-permute-start | bytes 393224 | tf_op jit(solution)/shard_map/ppermute | solution.py:106
  15.9 9.8 %collective-permute-start.6 = (bf16[256,256]{1,0:T(8,128)(2,1)S(1)}, bf16[256,256]{1,0:T(8,128)(2,1)S(1)}, u32[]{:S(2)}, u32[]{:S(2)}) collective-permute-start(bf16[256,256]{1,0:T(8,128)(2,1)S(1)} %get-tuple-element.45), channel_id=1, source_target_pairs={{0,28},{4,24},{8,20},{12,16},{16,12},{20,8},{24,4},{28,0},{1,29},{... | collective-permute-start | bytes 393224 | tf_op jit(solution)/shard_map/ppermute | solution.py:106
  19.5 26.3 %copy-start = (bf16[1024,4096]{1,0:T(8,128)(2,1)S(1)}, bf16[1024,4096]{1,0:T(8,128)(2,1)}, u32[]{:S(2)}) copy-start(bf16[1024,4096]{1,0:T(8,128)(2,1)} %weight_ref.9) | copy-start | bytes 25165828
  21.6 24.1 %copy-start.1 = (bf16[256,1024]{1,0:T(8,128)(2,1)S(1)}, bf16[256,1024]{1,0:T(8,128)(2,1)}, u32[]{:S(2)}) copy-start(bf16[256,1024]{1,0:T(8,128)(2,1)} %keys_ref.3) | copy-start | bytes 1572868
  21.7 24.1 %copy-start.2 = (bf16[256,1024]{1,0:T(8,128)(2,1)S(1)}, bf16[256,1024]{1,0:T(8,128)(2,1)}, u32[]{:S(2)}) copy-start(bf16[256,1024]{1,0:T(8,128)(2,1)} %values_ref.3) | copy-start | bytes 1572868
  21.7 24.1 %copy-start.3 = (bf16[256,1024]{1,0:T(8,128)(2,1)S(1)}, bf16[256,1024]{1,0:T(8,128)(2,1)}, u32[]{:S(2)}) copy-start(bf16[256,1024]{1,0:T(8,128)(2,1)} %queries_ref.3) | copy-start | bytes 1572868
  21.7 24.1 %copy-start.4 = (f32[1024]{0:T(1024)S(1)}, f32[1024]{0:T(1024)}, u32[]{:S(2)}) copy-start(f32[1024]{0:T(1024)} %param.12) | copy-start | bytes 12292
  27.9 12.5 %collective-permute-start.7 = (bf16[256,128]{1,0:T(8,128)(2,1)S(1)}, bf16[256,128]{1,0:T(8,128)(2,1)S(1)}, u32[]{:S(2)}, u32[]{:S(2)}) collective-permute-start(bf16[256,128]{1,0:T(8,128)(2,1)S(1)} %get-tuple-element.47), channel_id=1, source_target_pairs={{0,4},{4,0},{8,12},{12,8},{16,20},{20,16},{24,28},{28,24},{1,5},{5... | collective-permute-start | bytes 196616 | tf_op jit(solution)/shard_map/ppermute | solution.py:106
  31.8 9.8 %collective-permute-start.8 = (bf16[256,128]{1,0:T(8,128)(2,1)S(1)}, bf16[256,128]{1,0:T(8,128)(2,1)S(1)}, u32[]{:S(2)}, u32[]{:S(2)}) collective-permute-start(bf16[256,128]{1,0:T(8,128)(2,1)S(1)} %get-tuple-element.48), channel_id=1, source_target_pairs={{0,24},{4,28},{8,16},{12,20},{16,8},{20,12},{24,0},{28,4},{1,25},{... | collective-permute-start | bytes 196616 | tf_op jit(solution)/shard_map/ppermute | solution.py:106
  33.7 10.1 %collective-permute-start.9 = (bf16[256,128]{1,0:T(8,128)(2,1)S(1)}, bf16[256,128]{1,0:T(8,128)(2,1)S(1)}, u32[]{:S(2)}, u32[]{:S(2)}) collective-permute-start(bf16[256,128]{1,0:T(8,128)(2,1)S(1)} %get-tuple-element.49), channel_id=1, source_target_pairs={{0,16},{4,20},{8,24},{12,28},{16,0},{20,4},{24,8},{28,12},{1,17},{... | collective-permute-start | bytes 196616 | tf_op jit(solution)/shard_map/ppermute | solution.py:106
  36.4 9.4 %collective-permute-start.10 = (bf16[256,128]{1,0:T(8,128)(2,1)S(1)}, bf16[256,128]{1,0:T(8,128)(2,1)S(1)}, u32[]{:S(2)}, u32[]{:S(2)}) collective-permute-start(bf16[256,128]{1,0:T(8,128)(2,1)S(1)} %get-tuple-element.50), channel_id=1, source_target_pairs={{0,20},{4,16},{8,28},{12,24},{16,4},{20,0},{24,12},{28,8},{1,21},{... | collective-permute-start | bytes 196616 | tf_op jit(solution)/shard_map/ppermute | solution.py:106
  36.9 8.8 %collective-permute-start.11 = (bf16[256,128]{1,0:T(8,128)(2,1)S(1)}, bf16[256,128]{1,0:T(8,128)(2,1)S(1)}, u32[]{:S(2)}, u32[]{:S(2)}) collective-permute-start(bf16[256,128]{1,0:T(8,128)(2,1)S(1)} %get-tuple-element.51), channel_id=1, source_target_pairs={{0,8},{4,12},{8,0},{12,4},{16,24},{20,28},{24,16},{28,20},{1,9},{5... | collective-permute-start | bytes 196616 | tf_op jit(solution)/shard_map/ppermute | solution.py:106
  40.4 7.1 %collective-permute-start.12 = (bf16[256,128]{1,0:T(8,128)(2,1)S(1)}, bf16[256,128]{1,0:T(8,128)(2,1)S(1)}, u32[]{:S(2)}, u32[]{:S(2)}) collective-permute-start(bf16[256,128]{1,0:T(8,128)(2,1)S(1)} %get-tuple-element.54), channel_id=1, source_target_pairs={{0,28},{4,24},{8,20},{12,16},{16,12},{20,8},{24,4},{28,0},{1,29},{... | collective-permute-start | bytes 196616 | tf_op jit(solution)/shard_map/ppermute | solution.py:106
  41.7 5.9 %collective-permute-start.13 = (bf16[256,128]{1,0:T(8,128)(2,1)S(1)}, bf16[256,128]{1,0:T(8,128)(2,1)S(1)}, u32[]{:S(2)}, u32[]{:S(2)}) collective-permute-start(bf16[256,128]{1,0:T(8,128)(2,1)S(1)} %get-tuple-element.55), channel_id=1, source_target_pairs={{0,12},{4,8},{8,4},{12,0},{16,28},{20,24},{24,20},{28,16},{1,13},{... | collective-permute-start | bytes 196616 | tf_op jit(solution)/shard_map/ppermute | solution.py:106
  47.9 1.6 %collective-permute-start.17 = (bf16[256,512]{1,0:T(8,128)(2,1)S(1)}, bf16[256,512]{1,0:T(8,128)(2,1)S(1)}, u32[]{:S(2)}, u32[]{:S(2)}) collective-permute-start(bf16[256,512]{1,0:T(8,128)(2,1)S(1)} %get-tuple-element.62), channel_id=1, source_target_pairs={{0,1},{1,0},{2,3},{3,2},{4,5},{5,4},{6,7},{7,6},{8,9},{9,8},{10,11... | collective-permute-start | bytes 786440 | tf_op jit(solution)/shard_map/ppermute | solution.py:583
  48.2 2.9 %collective-permute-start.15 = (bf16[256,512]{1,0:T(8,128)(2,1)S(1)}, bf16[256,512]{1,0:T(8,128)(2,1)S(1)}, u32[]{:S(2)}, u32[]{:S(2)}) collective-permute-start(bf16[256,512]{1,0:T(8,128)(2,1)S(1)} %shard_map.91), channel_id=1, source_target_pairs={{0,1},{1,0},{2,3},{3,2},{4,5},{5,4},{6,7},{7,6},{8,9},{9,8},{10,11... | collective-permute-start | bytes 786440 | tf_op jit(solution)/shard_map/ppermute | solution.py:583
  49.5 9.2 %collective-permute-start.18 = (bf16[256,512]{1,0:T(8,128)(2,1)S(1)}, bf16[256,512]{1,0:T(8,128)(2,1)S(1)}, u32[]{:S(2)}, u32[]{:S(2)}) collective-permute-start(bf16[256,512]{1,0:T(8,128)(2,1)S(1)} %shard_map.93), channel_id=1, source_target_pairs={{0,2},{2,0},{1,3},{3,1},{4,6},{6,4},{5,7},{7,5},{8,10},{10,8},{9,1... | collective-permute-start | bytes 786440 | tf_op jit(solution)/shard_map/ppermute | solution.py:584
  51.2 12.4 %collective-permute-start.16 = (bf16[256,512]{1,0:T(8,128)(2,1)S(1)}, bf16[256,512]{1,0:T(8,128)(2,1)S(1)}, u32[]{:S(2)}, u32[]{:S(2)}) collective-permute-start(bf16[256,512]{1,0:T(8,128)(2,1)S(1)} %shard_map.92), channel_id=1, source_target_pairs={{0,2},{2,0},{1,3},{3,1},{4,6},{6,4},{5,7},{7,5},{8,10},{10,8},{9,1... | collective-permute-start | bytes 786440 | tf_op jit(solution)/shard_map/ppermute | solution.py:584
  53.1 10.4 %collective-permute-start.14 = (bf16[256,1024]{1,0:T(8,128)(2,1)S(1)}, bf16[256,1024]{1,0:T(8,128)(2,1)S(1)}, u32[]{:S(2)}, u32[]{:S(2)}) collective-permute-start(bf16[256,1024]{1,0:T(8,128)(2,1)S(1)} %get-tuple-element.58), channel_id=1, source_target_pairs={{0,1},{1,0},{2,3},{3,2},{4,5},{5,4},{6,7},{7,6},{8,9},{9,8},{10,11... | collective-permute-start | bytes 1572872 | tf_op jit(solution)/shard_map/ppermute | solution.py:587

commit v12 on v11

--- a/solution.py
+++ b/solution.py
@@ -97,7 +97,7 @@
     half = n_peers // 2
     near, far = list(range(1, half)), list(range(half, n_peers))
     if back:
-        return [0, near[0], far[2], far[0], far[1], near[1], far[3]] + near[2:]
+        return [0, near[0], far[2], far[0], near[1], far[1], far[3]] + near[2:]
     return [0, far[0], near[0]] + near[:0:-1] + far[1:]
 
 
@@ -555,12 +555,12 @@
         fwd, bwd = load_tables(fwd, bwd, received[1:2])
         early, part = spectra(received[:-2], fwd, n_peers)
         back = exchange(conv_fast(early, part, received[-2:], fwd, bwd), n_peers, True)
-        slots = slots_of(n_peers, True)[-2:]
+        slots = slots_of(n_peers, True)[-3:]
         gated, send_part, own_part = gate_early(
-            queries, keys, values, skip, out_weight, back[:-2], n_peers
+            queries, keys, values, skip, out_weight, back[:-3], n_peers
         )
         late, last = gate_late(
-            queries, keys, values, skip, out_weight, send_part, back[-2:], slots, sends[-1]
+            queries, keys, values, skip, out_weight, send_part, back[-3:], slots, sends[-1]
         )
         sent = [
             *(late_project(out_weight, late, send_part, slots, [s], BF16)[0] for s in sends[:-1]),

time: 64.6 us -> 64.7 us (level)
  starting transfers between devices: 31.8 us -> 31.1 us
    ppermute x14, waiting for transfers between devices: 9.25 us -> 9.96 us  [exchange(): lax.ppermute(block, 'seq', [(i, i ^ slot) for i in range(n_peers)])]
    ppermute x14, starting transfers between devices: 29 us -> 28.3 us  [exchange(): lax.ppermute(block, 'seq', [(i, i ^ slot) for i in range(n_peers)])]
  transfers between devices with their start and end apart: 19 -> 19, of which waited for: 9 -> 10; matrix products, arithmetic and copies ran while one was open for 0% -> 0% of each run, Pallas kernels for 11% -> 11%
where the time goes in v12:
time: 64.7 us; the launch traced here: 64.5 us
  starting transfers between devices  31.1 us (48%)
  waiting for transfers between devices  20.5 us (32%)
  Pallas kernels  12.6 us (19%)
    ppermute x14, starting transfers between devices, exchange(): lax.ppermute(block, 'seq', [(i, i ^ slot) for i in range(n_peers)])  28.3 us
    ppermute x2, waiting for transfers between devices, body(): lax.ppermute(add(*pair), 'fsdp', across)  10.4 us
    ppermute x14, waiting for transfers between devices, exchange(): lax.ppermute(block, 'seq', [(i, i ^ slot) for i in range(n_peers)])  9.96 us
    pallas_call x1, Pallas kernels, conv_fast(): pl.pallas_call(conv_kernel, in_specs=[whole] * 6, out_specs=[whole] * n_b...  2.23 us
    ppermute x2, starting transfers between devices, body(): lax.ppermute(add(*pair), 'fsdp', across)  2.16 us
    pallas_call x1, Pallas kernels, spectra(): pl.pallas_call(functools.partial(spectra_kernel, n_peers), in_specs=[whol...  2.15 us
    pallas_call x1, Pallas kernels, pre(): pl.pallas_call(functools.partial(pre_kernel, n_peers), in_specs=[pl.Block...  1.77 us
    pallas_call x1, Pallas kernels, gate_early(): pl.pallas_call(functools.partial(gate_early_kernel, n_peers), in_specs=[w...  1.67 us
  transfers between devices with their start and end apart: 19, of which 10 were waited for; matrix products, arithmetic and copies ran while one was open for 0% of the time, Pallas kernels for 11%

profile of v12, /device:TPU:0, one launch (start us, length us, event | category | flops | bytes accessed | tf_op | source)
XLA Modules:
  0.0 64.5 jit_solution(905195399509728959)
XLA Ops:
  0.0 1.8 %shard_map.82 = (bf16[256,256]{1,0:T(8,128)(2,1)S(1)}, bf16[256,256]{1,0:T(8,128)(2,1)S(1)}, bf16[256,256]{1,0:T(8,128)(2,1)S(1)}, bf16[256,256]{1,0:T(8,128)(2,...) custom-call(bf16[256,1024]{1,0:T(8,128)(2,1)} %keys_ref.3, ...), custom_call_target="tpu_custom_call" | custom-call | flops 262144 | bytes 3145728 | tf_op jit(solution)/shard_map/pallas_call | solution.py:78
  1.8 4.1 %collective-permute-start = (bf16[256,256]{1,0:T(8,128)(2,1)S(1)}, bf16[256,256]{1,0:T(8,128)(2,1)S(1)}, u32[]{:S(2)}, u32[]{:S(2)}) collective-permute-start(bf16[256,256]{1,0:T(8,128)(2,1)S(1)} %get-tuple-element.34), channel_id=1, source_target_pairs={{0,16},{4,20},{8,24},{12,28},{16,0},{20,4},{24,8},{28,12},{1,17},{... | collective-permute-start | bytes 393224 | tf_op jit(solution)/shard_map/ppermute | solution.py:106
  5.9 1.5 %collective-permute-start.1 = (bf16[256,256]{1,0:T(8,128)(2,1)S(1)}, bf16[256,256]{1,0:T(8,128)(2,1)S(1)}, u32[]{:S(2)}, u32[]{:S(2)}) collective-permute-start(bf16[256,256]{1,0:T(8,128)(2,1)S(1)} %get-tuple-element.38), channel_id=1, source_target_pairs={{0,4},{4,0},{8,12},{12,8},{16,20},{20,16},{24,28},{28,24},{1,5},{5... | collective-permute-start | bytes 393224 | tf_op jit(solution)/shard_map/ppermute | solution.py:106
  7.4 1.5 %collective-permute-start.2 = (bf16[256,256]{1,0:T(8,128)(2,1)S(1)}, bf16[256,256]{1,0:T(8,128)(2,1)S(1)}, u32[]{:S(2)}, u32[]{:S(2)}) collective-permute-start(bf16[256,256]{1,0:T(8,128)(2,1)S(1)} %get-tuple-element.39), channel_id=1, source_target_pairs={{0,12},{4,8},{8,4},{12,0},{16,28},{20,24},{24,20},{28,16},{1,13},{... | collective-permute-start | bytes 393224 | tf_op jit(solution)/shard_map/ppermute | solution.py:106
  8.9 0.4 collective-permute-start.3
  9.4 1.3 %collective-permute-start.4 = (bf16[256,256]{1,0:T(8,128)(2,1)S(1)}, bf16[256,256]{1,0:T(8,128)(2,1)S(1)}, u32[]{:S(2)}, u32[]{:S(2)}) collective-permute-start(bf16[256,256]{1,0:T(8,128)(2,1)S(1)} %get-tuple-element.41), channel_id=1, source_target_pairs={{0,20},{4,16},{8,28},{12,24},{16,4},{20,0},{24,12},{28,8},{1,21},{... | collective-permute-start | bytes 393224 | tf_op jit(solution)/shard_map/ppermute | solution.py:106
  10.7 1.6 %collective-permute-done.refs_0_.refs_1_ = bf16[256,256]{1,0:T(8,128)(2,1)S(1)} collective-permute-done((bf16[256,256]{1,0:T(8,128)(2,1)S(1)}, bf16[256,256]{1,0:T(8,128)(2,1)S(1)}, u32[]{:S(2)}, u32[]{:S(2)}) %collective-permute-start) | collective-permute-done | bytes 131104 | tf_op jit(solution)/shard_map/ppermute | solution.py:106
  12.3 3.6 %collective-permute-start.5 = (bf16[256,256]{1,0:T(8,128)(2,1)S(1)}, bf16[256,256]{1,0:T(8,128)(2,1)S(1)}, u32[]{:S(2)}, u32[]{:S(2)}) collective-permute-start(bf16[256,256]{1,0:T(8,128)(2,1)S(1)} %get-tuple-element.44), channel_id=1, source_target_pairs={{0,24},{4,28},{8,16},{12,20},{16,8},{20,12},{24,0},{28,4},{1,25},{... | collective-permute-start | bytes 393224 | tf_op jit(solution)/shard_map/ppermute | solution.py:106
  15.9 1.8 %collective-permute-start.6 = (bf16[256,256]{1,0:T(8,128)(2,1)S(1)}, bf16[256,256]{1,0:T(8,128)(2,1)S(1)}, u32[]{:S(2)}, u32[]{:S(2)}) collective-permute-start(bf16[256,256]{1,0:T(8,128)(2,1)S(1)} %get-tuple-element.45), channel_id=1, source_target_pairs={{0,28},{4,24},{8,20},{12,16},{16,12},{20,8},{24,4},{28,0},{1,29},{... | collective-permute-start | bytes 393224 | tf_op jit(solution)/shard_map/ppermute | solution.py:106
  17.7 1.3 %shard_map.83 = (bf16[512,512]{1,0:T(8,128)(2,1)S(1)}, bf16[256,1536]{1,0:T(8,128)(2,1)S(1)}) custom-call(bf16[512,512]{1,0:T(8,128)(2,1)} %constant.4.clone.fwd_hbm, bf16[256,1536]{1,0:T(8,128)(2,1)} %constant.5.clone.bwd_hbm, bf16[256,256]{1,0:T(8,128)(2,1)S(1)} %collective-permute-done.refs_0_.refs_1_), custom_call_target="tpu_custom_call" | custom-call | flops 1000000 | bytes 3145728 | tf_op jit(solution)/shard_map/pallas_call | solution.py:166
  19.5 2.2 %shard_map.84 = (f32[8,512,256]{2,1,0:T(8,128)S(1)}, f32[8,512,128]{2,1,0:T(8,128)S(1)}) custom-call(bf16[512,512]{1,0:T(8,128)(2,1)S(1)} %get-tuple-element.35.fwd_ref, bf16[256,256]{1,0:T(8,128)(2,1)S(1)} %get-tuple-element.37.refs_0_, bf16[256,256]{1,0:T(8,128)(2,1)S(1)} %collective-permute-done.refs_0_.refs_1_, ...), custom_call_target="tpu_custom_call" | custom-call | flops 805306368 | bytes 4194304 | tf_op jit(solution)/shard_map/pallas_call | solution.py:191
  21.7 1.0 %collective-permute-done.5.refs_0_ = bf16[256,256]{1,0:T(8,128)(2,1)S(1)} collective-permute-done((bf16[256,256]{1,0:T(8,128)(2,1)S(1)}, bf16[256,256]{1,0:T(8,128)(2,1)S(1)}, u32[]{:S(2)}, u32[]{:S(2)}) %collective-permute-start.5) | collective-permute-done | bytes 131104 | tf_op jit(solution)/shard_map/ppermute | solution.py:106
  22.7 3.0 %collective-permute-done.6.refs_1_ = bf16[256,256]{1,0:T(8,128)(2,1)S(1)} collective-permute-done((bf16[256,256]{1,0:T(8,128)(2,1)S(1)}, bf16[256,256]{1,0:T(8,128)(2,1)S(1)}, u32[]{:S(2)}, u32[]{:S(2)}) %collective-permute-start.6) | collective-permute-done | bytes 131104 | tf_op jit(solution)/shard_map/ppermute | solution.py:106
  25.7 2.2 %shard_map.85 = (bf16[256,128]{1,0:T(8,128)(2,1)S(1)}, bf16[256,128]{1,0:T(8,128)(2,1)S(1)}, bf16[256,128]{1,0:T(8,128)(2,1)S(1)}, bf16[256,128]{1,0:T(8,128)(2,...) custom-call(bf16[512,512]{1,0:T(8,128)(2,1)S(1)} %get-tuple-element., ...), custom_call_target="tpu_custom_call" | custom-call | flops 1073741824 | bytes 4194304 | tf_op jit(solution)/shard_map/pallas_call | solution.py:276
  27.9 3.9 %collective-permute-start.7 = (bf16[256,128]{1,0:T(8,128)(2,1)S(1)}, bf16[256,128]{1,0:T(8,128)(2,1)S(1)}, u32[]{:S(2)}, u32[]{:S(2)}) collective-permute-start(bf16[256,128]{1,0:T(8,128)(2,1)S(1)} %get-tuple-element.47), channel_id=1, source_target_pairs={{0,4},{4,0},{8,12},{12,8},{16,20},{20,16},{24,28},{28,24},{1,5},{5... | collective-permute-start | bytes 196616 | tf_op jit(solution)/shard_map/ppermute | solution.py:106
  31.8 1.9 %collective-permute-start.8 = (bf16[256,128]{1,0:T(8,128)(2,1)S(1)}, bf16[256,128]{1,0:T(8,128)(2,1)S(1)}, u32[]{:S(2)}, u32[]{:S(2)}) collective-permute-start(bf16[256,128]{1,0:T(8,128)(2,1)S(1)} %get-tuple-element.48), channel_id=1, source_target_pairs={{0,24},{4,28},{8,16},{12,20},{16,8},{20,12},{24,0},{28,4},{1,25},{... | collective-permute-start | bytes 196616 | tf_op jit(solution)/shard_map/ppermute | solution.py:106
  33.7 2.7 %collective-permute-start.9 = (bf16[256,128]{1,0:T(8,128)(2,1)S(1)}, bf16[256,128]{1,0:T(8,128)(2,1)S(1)}, u32[]{:S(2)}, u32[]{:S(2)}) collective-permute-start(bf16[256,128]{1,0:T(8,128)(2,1)S(1)} %get-tuple-element.49), channel_id=1, source_target_pairs={{0,16},{4,20},{8,24},{12,28},{16,0},{20,4},{24,8},{28,12},{1,17},{... | collective-permute-start | bytes 196616 | tf_op jit(solution)/shard_map/ppermute | solution.py:106
  36.5 3.9 %collective-permute-start.11 = (bf16[256,128]{1,0:T(8,128)(2,1)S(1)}, bf16[256,128]{1,0:T(8,128)(2,1)S(1)}, u32[]{:S(2)}, u32[]{:S(2)}) collective-permute-start(bf16[256,128]{1,0:T(8,128)(2,1)S(1)} %get-tuple-element.53), channel_id=1, source_target_pairs={{0,20},{4,16},{8,28},{12,24},{16,4},{20,0},{24,12},{28,8},{1,21},{... | collective-permute-start | bytes 196616 | tf_op jit(solution)/shard_map/ppermute | solution.py:106
  40.4 1.2 %collective-permute-start.12 = (bf16[256,128]{1,0:T(8,128)(2,1)S(1)}, bf16[256,128]{1,0:T(8,128)(2,1)S(1)}, u32[]{:S(2)}, u32[]{:S(2)}) collective-permute-start(bf16[256,128]{1,0:T(8,128)(2,1)S(1)} %get-tuple-element.54), channel_id=1, source_target_pairs={{0,28},{4,24},{8,20},{12,16},{16,12},{20,8},{24,4},{28,0},{1,29},{... | collective-permute-start | bytes 196616 | tf_op jit(solution)/shard_map/ppermute | solution.py:106
  41.9 0.5 collective-permute-done.9.refs_3_
  42.5 1.7 %shard_map.86 = (bf16[256,1024]{1,0:T(8,128)(2,1)S(1)}, f32[256,1024]{1,0:T(8,128)S(1)}, f32[256,1024]{1,0:T(8,128)S(1)}) custom-call(bf16[256,1024]{1,0:T(8,128)(2,1)S(1)} %copy-done.3, bf16[256,1024]{1,0:T(8,128)(2,1)S(1)} %copy-done.1, bf16[256,1024]{1,0:T(8,128)(2,1)S(1)} %copy-done.2, f32[1,1024]{1,0:T(1,128)S(1)} %bitcast.1, ...), custom_call_target="tpu_custom_call" | custom-call | flops 1073741824 | bytes 2621440 | tf_op jit(solution)/shard_map/pallas_call | solution.py:357
  44.1 1.5 %collective-permute-done.11.refs_0_ = bf16[256,128]{1,0:T(8,128)(2,1)S(1)} collective-permute-done((bf16[256,128]{1,0:T(8,128)(2,1)S(1)}, bf16[256,128]{1,0:T(8,128)(2,1)S(1)}, u32[]{:S(2)}, u32[]{:S(2)}) %collective-permute-start.11) | collective-permute-done | bytes 65568 | tf_op jit(solution)/shard_map/ppermute | solution.py:106
  45.7 1.8 %collective-permute-done.12.refs_1_ = bf16[256,128]{1,0:T(8,128)(2,1)S(1)} collective-permute-done((bf16[256,128]{1,0:T(8,128)(2,1)S(1)}, bf16[256,128]{1,0:T(8,128)(2,1)S(1)}, u32[]{:S(2)}, u32[]{:S(2)}) %collective-permute-start.12) | collective-permute-done | bytes 65568 | tf_op jit(solution)/shard_map/ppermute | solution.py:106
  47.5 0.4 shard_map.87
  48.3 0.5 collective-permute-start.15
  48.9 0.4 shard_map.90
  49.6 1.6 %collective-permute-start.18 = (bf16[256,512]{1,0:T(8,128)(2,1)S(1)}, bf16[256,512]{1,0:T(8,128)(2,1)S(1)}, u32[]{:S(2)}, u32[]{:S(2)}) collective-permute-start(bf16[256,512]{1,0:T(8,128)(2,1)S(1)} %shard_map.93), channel_id=1, source_target_pairs={{0,2},{2,0},{1,3},{3,1},{4,6},{6,4},{5,7},{7,5},{8,10},{10,8},{9,1... | collective-permute-start | bytes 786440 | tf_op jit(solution)/shard_map/ppermute | solution.py:584
  51.2 0.6 collective-permute-start.16
  51.9 1.3 %shard_map.89 = (bf16[256,1024]{1,0:T(8,128)(2,1)S(1)}, f32[256,1024]{1,0:T(8,128)S(1)}) custom-call(bf16[256,1024]{1,0:T(8,128)(2,1)S(1)} %shard_map.88.gated_ref, bf16[1024,4096]{1,0:T(8,128)(2,1)S(1)} %copy-done), custom_call_target="tpu_custom_call" | custom-call | flops 1073741824 | bytes 4194304 | tf_op jit(solution)/shard_map/pallas_call | solution.py:460
  53.3 5.5 %collective-permute-done.18.refs_1_ = bf16[256,512]{1,0:T(8,128)(2,1)S(1)} collective-permute-done((bf16[256,512]{1,0:T(8,128)(2,1)S(1)}, bf16[256,512]{1,0:T(8,128)(2,1)S(1)}, u32[]{:S(2)}, u32[]{:S(2)}) %collective-permute-start.18) | collective-permute-done | bytes 262176 | tf_op jit(solution)/shard_map/ppermute | solution.py:584
  58.8 4.8 %collective-permute-done.16.refs_0_ = bf16[256,512]{1,0:T(8,128)(2,1)S(1)} collective-permute-done((bf16[256,512]{1,0:T(8,128)(2,1)S(1)}, bf16[256,512]{1,0:T(8,128)(2,1)S(1)}, u32[]{:S(2)}, u32[]{:S(2)}) %collective-permute-start.16) | collective-permute-done | bytes 262176 | tf_op jit(solution)/shard_map/ppermute | solution.py:584
  63.7 0.9 %shard_map.95 = bf16[256,1024]{1,0:T(8,128)(2,1)} custom-call(f32[256,1024]{1,0:T(8,128)S(1)} %get-tuple-element.57.own_ref, bf16[256,1024]{1,0:T(8,128)(2,1)S(1)} %collective-permute-done.14.near_ref, bf16[256,512]{1,0:T(8,128)(2,1)S(1)} %collective-permute-done.16.refs_0_, bf16[256,512]{1,0:T(8,128)(2,1)S(1)} %collective-permute-done.18.refs_1_, ...), custom_call_target="tpu_custom_call" | custom-call | flops 262144 | bytes 2097152 | tf_op jit(solution)/shard_map/pallas_call | solution.py:527
  (30 shorter events, 1.8 us)
Async XLA Ops:
  1.8 10.5 %collective-permute-start = (bf16[256,256]{1,0:T(8,128)(2,1)S(1)}, bf16[256,256]{1,0:T(8,128)(2,1)S(1)}, u32[]{:S(2)}, u32[]{:S(2)}) collective-permute-start(bf16[256,256]{1,0:T(8,128)(2,1)S(1)} %get-tuple-element.34), channel_id=1, source_target_pairs={{0,16},{4,20},{8,24},{12,28},{16,0},{20,4},{24,8},{28,12},{1,17},{... | collective-permute-start | bytes 393224 | tf_op jit(solution)/shard_map/ppermute | solution.py:106
  5.9 10.0 %collective-permute-start.1 = (bf16[256,256]{1,0:T(8,128)(2,1)S(1)}, bf16[256,256]{1,0:T(8,128)(2,1)S(1)}, u32[]{:S(2)}, u32[]{:S(2)}) collective-permute-start(bf16[256,256]{1,0:T(8,128)(2,1)S(1)} %get-tuple-element.38), channel_id=1, source_target_pairs={{0,4},{4,0},{8,12},{12,8},{16,20},{20,16},{24,28},{28,24},{1,5},{5... | collective-permute-start | bytes 393224 | tf_op jit(solution)/shard_map/ppermute | solution.py:106
  7.4 11.7 %collective-permute-start.2 = (bf16[256,256]{1,0:T(8,128)(2,1)S(1)}, bf16[256,256]{1,0:T(8,128)(2,1)S(1)}, u32[]{:S(2)}, u32[]{:S(2)}) collective-permute-start(bf16[256,256]{1,0:T(8,128)(2,1)S(1)} %get-tuple-element.39), channel_id=1, source_target_pairs={{0,12},{4,8},{8,4},{12,0},{16,28},{20,24},{24,20},{28,16},{1,13},{... | collective-permute-start | bytes 393224 | tf_op jit(solution)/shard_map/ppermute | solution.py:106
  8.9 10.6 %collective-permute-start.3 = (bf16[256,256]{1,0:T(8,128)(2,1)S(1)}, bf16[256,256]{1,0:T(8,128)(2,1)S(1)}, u32[]{:S(2)}, u32[]{:S(2)}) collective-permute-start(bf16[256,256]{1,0:T(8,128)(2,1)S(1)} %get-tuple-element.40), channel_id=1, source_target_pairs={{0,8},{4,12},{8,0},{12,4},{16,24},{20,28},{24,16},{28,20},{1,9},{5... | collective-permute-start | bytes 393224 | tf_op jit(solution)/shard_map/ppermute | solution.py:106
  9.4 10.1 %collective-permute-start.4 = (bf16[256,256]{1,0:T(8,128)(2,1)S(1)}, bf16[256,256]{1,0:T(8,128)(2,1)S(1)}, u32[]{:S(2)}, u32[]{:S(2)}) collective-permute-start(bf16[256,256]{1,0:T(8,128)(2,1)S(1)} %get-tuple-element.41), channel_id=1, source_target_pairs={{0,20},{4,16},{8,28},{12,24},{16,4},{20,0},{24,12},{28,8},{1,21},{... | collective-permute-start | bytes 393224 | tf_op jit(solution)/shard_map/ppermute | solution.py:106
  12.3 10.4 %collective-permute-start.5 = (bf16[256,256]{1,0:T(8,128)(2,1)S(1)}, bf16[256,256]{1,0:T(8,128)(2,1)S(1)}, u32[]{:S(2)}, u32[]{:S(2)}) collective-permute-start(bf16[256,256]{1,0:T(8,128)(2,1)S(1)} %get-tuple-element.44), channel_id=1, source_target_pairs={{0,24},{4,28},{8,16},{12,20},{16,8},{20,12},{24,0},{28,4},{1,25},{... | collective-permute-start | bytes 393224 | tf_op jit(solution)/shard_map/ppermute | solution.py:106
  15.9 9.8 %collective-permute-start.6 = (bf16[256,256]{1,0:T(8,128)(2,1)S(1)}, bf16[256,256]{1,0:T(8,128)(2,1)S(1)}, u32[]{:S(2)}, u32[]{:S(2)}) collective-permute-start(bf16[256,256]{1,0:T(8,128)(2,1)S(1)} %get-tuple-element.45), channel_id=1, source_target_pairs={{0,28},{4,24},{8,20},{12,16},{16,12},{20,8},{24,4},{28,0},{1,29},{... | collective-permute-start | bytes 393224 | tf_op jit(solution)/shard_map/ppermute | solution.py:106
  19.5 23.0 %copy-start = (bf16[1024,4096]{1,0:T(8,128)(2,1)S(1)}, bf16[1024,4096]{1,0:T(8,128)(2,1)}, u32[]{:S(2)}) copy-start(bf16[1024,4096]{1,0:T(8,128)(2,1)} %weight_ref.9) | copy-start | bytes 25165828
  21.6 20.8 %copy-start.1 = (bf16[256,1024]{1,0:T(8,128)(2,1)S(1)}, bf16[256,1024]{1,0:T(8,128)(2,1)}, u32[]{:S(2)}) copy-start(bf16[256,1024]{1,0:T(8,128)(2,1)} %keys_ref.3) | copy-start | bytes 1572868
  21.7 20.8 %copy-start.2 = (bf16[256,1024]{1,0:T(8,128)(2,1)S(1)}, bf16[256,1024]{1,0:T(8,128)(2,1)}, u32[]{:S(2)}) copy-start(bf16[256,1024]{1,0:T(8,128)(2,1)} %values_ref.3) | copy-start | bytes 1572868
  21.7 20.8 %copy-start.3 = (bf16[256,1024]{1,0:T(8,128)(2,1)S(1)}, bf16[256,1024]{1,0:T(8,128)(2,1)}, u32[]{:S(2)}) copy-start(bf16[256,1024]{1,0:T(8,128)(2,1)} %queries_ref.3) | copy-start | bytes 1572868
  21.7 20.8 %copy-start.4 = (f32[1024]{0:T(1024)S(1)}, f32[1024]{0:T(1024)}, u32[]{:S(2)}) copy-start(f32[1024]{0:T(1024)} %param.12) | copy-start | bytes 12292
  27.9 12.5 %collective-permute-start.7 = (bf16[256,128]{1,0:T(8,128)(2,1)S(1)}, bf16[256,128]{1,0:T(8,128)(2,1)S(1)}, u32[]{:S(2)}, u32[]{:S(2)}) collective-permute-start(bf16[256,128]{1,0:T(8,128)(2,1)S(1)} %get-tuple-element.47), channel_id=1, source_target_pairs={{0,4},{4,0},{8,12},{12,8},{16,20},{20,16},{24,28},{28,24},{1,5},{5... | collective-permute-start | bytes 196616 | tf_op jit(solution)/shard_map/ppermute | solution.py:106
  31.8 9.8 %collective-permute-start.8 = (bf16[256,128]{1,0:T(8,128)(2,1)S(1)}, bf16[256,128]{1,0:T(8,128)(2,1)S(1)}, u32[]{:S(2)}, u32[]{:S(2)}) collective-permute-start(bf16[256,128]{1,0:T(8,128)(2,1)S(1)} %get-tuple-element.48), channel_id=1, source_target_pairs={{0,24},{4,28},{8,16},{12,20},{16,8},{20,12},{24,0},{28,4},{1,25},{... | collective-permute-start | bytes 196616 | tf_op jit(solution)/shard_map/ppermute | solution.py:106
  33.7 8.7 %collective-permute-start.9 = (bf16[256,128]{1,0:T(8,128)(2,1)S(1)}, bf16[256,128]{1,0:T(8,128)(2,1)S(1)}, u32[]{:S(2)}, u32[]{:S(2)}) collective-permute-start(bf16[256,128]{1,0:T(8,128)(2,1)S(1)} %get-tuple-element.49), channel_id=1, source_target_pairs={{0,16},{4,20},{8,24},{12,28},{16,0},{20,4},{24,8},{28,12},{1,17},{... | collective-permute-start | bytes 196616 | tf_op jit(solution)/shard_map/ppermute | solution.py:106
  36.4 6.1 %collective-permute-start.10 = (bf16[256,128]{1,0:T(8,128)(2,1)S(1)}, bf16[256,128]{1,0:T(8,128)(2,1)S(1)}, u32[]{:S(2)}, u32[]{:S(2)}) collective-permute-start(bf16[256,128]{1,0:T(8,128)(2,1)S(1)} %get-tuple-element.50), channel_id=1, source_target_pairs={{0,8},{4,12},{8,0},{12,4},{16,24},{20,28},{24,16},{28,20},{1,9},{5... | collective-permute-start | bytes 196616 | tf_op jit(solution)/shard_map/ppermute | solution.py:106
  36.5 9.1 %collective-permute-start.11 = (bf16[256,128]{1,0:T(8,128)(2,1)S(1)}, bf16[256,128]{1,0:T(8,128)(2,1)S(1)}, u32[]{:S(2)}, u32[]{:S(2)}) collective-permute-start(bf16[256,128]{1,0:T(8,128)(2,1)S(1)} %get-tuple-element.53), channel_id=1, source_target_pairs={{0,20},{4,16},{8,28},{12,24},{16,4},{20,0},{24,12},{28,8},{1,21},{... | collective-permute-start | bytes 196616 | tf_op jit(solution)/shard_map/ppermute | solution.py:106
  40.4 7.1 %collective-permute-start.12 = (bf16[256,128]{1,0:T(8,128)(2,1)S(1)}, bf16[256,128]{1,0:T(8,128)(2,1)S(1)}, u32[]{:S(2)}, u32[]{:S(2)}) collective-permute-start(bf16[256,128]{1,0:T(8,128)(2,1)S(1)} %get-tuple-element.54), channel_id=1, source_target_pairs={{0,28},{4,24},{8,20},{12,16},{16,12},{20,8},{24,4},{28,0},{1,29},{... | collective-permute-start | bytes 196616 | tf_op jit(solution)/shard_map/ppermute | solution.py:106
  41.7 5.9 %collective-permute-start.13 = (bf16[256,128]{1,0:T(8,128)(2,1)S(1)}, bf16[256,128]{1,0:T(8,128)(2,1)S(1)}, u32[]{:S(2)}, u32[]{:S(2)}) collective-permute-start(bf16[256,128]{1,0:T(8,128)(2,1)S(1)} %get-tuple-element.55), channel_id=1, source_target_pairs={{0,12},{4,8},{8,4},{12,0},{16,28},{20,24},{24,20},{28,16},{1,13},{... | collective-permute-start | bytes 196616 | tf_op jit(solution)/shard_map/ppermute | solution.py:106
  47.9 1.6 %collective-permute-start.17 = (bf16[256,512]{1,0:T(8,128)(2,1)S(1)}, bf16[256,512]{1,0:T(8,128)(2,1)S(1)}, u32[]{:S(2)}, u32[]{:S(2)}) collective-permute-start(bf16[256,512]{1,0:T(8,128)(2,1)S(1)} %get-tuple-element.62), channel_id=1, source_target_pairs={{0,1},{1,0},{2,3},{3,2},{4,5},{5,4},{6,7},{7,6},{8,9},{9,8},{10,11... | collective-permute-start | bytes 786440 | tf_op jit(solution)/shard_map/ppermute | solution.py:583
  48.3 2.8 %collective-permute-start.15 = (bf16[256,512]{1,0:T(8,128)(2,1)S(1)}, bf16[256,512]{1,0:T(8,128)(2,1)S(1)}, u32[]{:S(2)}, u32[]{:S(2)}) collective-permute-start(bf16[256,512]{1,0:T(8,128)(2,1)S(1)} %shard_map.91), channel_id=1, source_target_pairs={{0,1},{1,0},{2,3},{3,2},{4,5},{5,4},{6,7},{7,6},{8,9},{9,8},{10,11... | collective-permute-start | bytes 786440 | tf_op jit(solution)/shard_map/ppermute | solution.py:583
  49.6 9.2 %collective-permute-start.18 = (bf16[256,512]{1,0:T(8,128)(2,1)S(1)}, bf16[256,512]{1,0:T(8,128)(2,1)S(1)}, u32[]{:S(2)}, u32[]{:S(2)}) collective-permute-start(bf16[256,512]{1,0:T(8,128)(2,1)S(1)} %shard_map.93), channel_id=1, source_target_pairs={{0,2},{2,0},{1,3},{3,1},{4,6},{6,4},{5,7},{7,5},{8,10},{10,8},{9,1... | collective-permute-start | bytes 786440 | tf_op jit(solution)/shard_map/ppermute | solution.py:584
  51.2 12.4 %collective-permute-start.16 = (bf16[256,512]{1,0:T(8,128)(2,1)S(1)}, bf16[256,512]{1,0:T(8,128)(2,1)S(1)}, u32[]{:S(2)}, u32[]{:S(2)}) collective-permute-start(bf16[256,512]{1,0:T(8,128)(2,1)S(1)} %shard_map.92), channel_id=1, source_target_pairs={{0,2},{2,0},{1,3},{3,1},{4,6},{6,4},{5,7},{7,5},{8,10},{10,8},{9,1... | collective-permute-start | bytes 786440 | tf_op jit(solution)/shard_map/ppermute | solution.py:584
  53.2 10.4 %collective-permute-start.14 = (bf16[256,1024]{1,0:T(8,128)(2,1)S(1)}, bf16[256,1024]{1,0:T(8,128)(2,1)S(1)}, u32[]{:S(2)}, u32[]{:S(2)}) collective-permute-start(bf16[256,1024]{1,0:T(8,128)(2,1)S(1)} %get-tuple-element.58), channel_id=1, source_target_pairs={{0,1},{1,0},{2,3},{3,2},{4,5},{5,4},{6,7},{7,6},{8,9},{9,8},{10,11... | collective-permute-start | bytes 1572872 | tf_op jit(solution)/shard_map/ppermute | solution.py:587

commit v13 on v11

--- a/solution.py
+++ b/solution.py
@@ -203,31 +203,70 @@
     )(fwd, *received)
 
 
-def mix_late(pair, step, first, last, sign, spec_ref, part_ref, late_ref, turned):
+def add_block(total, place, new, others, row, step, rows, chans):
+    n_blocks = len(total)
+    x_at, f_at = slice(0, chans), slice(chans, 2 * chans)
+    x_new, f_new = load(new, (), row, step, rows, x_at), load(new, (), row, step, rows, f_at)
+    for j, (ref, at) in others.items():
+        if j + place < n_blocks:
+            x_j = load(ref, at, row, step, rows, x_at)
+            f_j = load(ref, at, row, step, rows, f_at)
+            total[j + place] = plus(total[j + place], times(f_new, x_j))
+            total[j + place] = plus(total[j + place], times(f_j, x_new))
+    if 2 * place < n_blocks:
+        total[2 * place] = plus(total[2 * place], times(f_new, x_new))
+
+
+def early_blocks(place, n_blocks, spec_ref):
+    return {j: (spec_ref, (j,)) for j in range(n_blocks) if j // 2 != place // 2}
+
+
+def mix_middle(place, step, spec_ref, part_ref, new_ref, out_ref):
     n_blocks, rows, chans = spec_ref.shape[0], spec_ref.shape[1] // 2, spec_ref.shape[2] // 2
-    early = [j for j in range(n_blocks) if j // 2 != pair]
-    x_at, f_at = slice(0, chans), slice(chans, 2 * chans)
+    others = early_blocks(place, n_blocks, spec_ref)
+
+    @pl.loop(0, rows // step)
+    def _(t):
+        row = pl.multiple_of(t * step, step)
+        total = [load(part_ref, (i,), row, step, rows, slice(0, chans)) for i in range(n_blocks)]
+        add_block(total, place, new_ref, others, row, step, rows, chans)
+        for i in range(n_blocks):
+            for part in range(2):
+                out_ref[i, pl.ds(row + part * rows, step)] = total[i][part]
+
+
+def middle_kernel(fwd_ref, spec_ref, part_ref, in_ref, new_ref, out_ref):
+    n_blocks = spec_ref.shape[0]
+    new_ref[...] = block_spectrum(fwd_ref[...], in_ref[...])
+    mine = peer_of(slots_of(n_blocks, False)[-2])
+    for place in range(n_blocks):
+        pl.when(mine == place)(
+            functools.partial(mix_middle, place, STEP, spec_ref, part_ref, new_ref, out_ref)
+        )
+
+
+def middle(early, part, block, fwd):
+    whole = pl.BlockSpec(memory_space=pltpu.VMEM)
+    return pl.pallas_call(
+        middle_kernel,
+        in_specs=[whole] * 4,
+        out_specs=[whole] * 2,
+        out_shape=[jax.ShapeDtypeStruct(a.shape, F32) for a in (early[0], part)],
+        compiler_params=pltpu.CompilerParams(vmem_limit_bytes=CONV_VMEM),
+        cost_estimate=pl.CostEstimate(flops=10**9, bytes_accessed=4 * 2**20, transcendentals=0),
+    )(fwd, early, part, block)
+
+
+def mix_last(place, step, first, last, sign, spec_ref, part_ref, next_ref, new_ref, turned):
+    n_blocks, rows, chans = spec_ref.shape[0], spec_ref.shape[1] // 2, spec_ref.shape[2] // 2
+    others = early_blocks(place, n_blocks, spec_ref)
+    others[place ^ 1] = (next_ref, ())
 
     @pl.loop(first // step, last // step)
     def _(t):
         row = pl.multiple_of(t * step, step)
-        late = [2 * pair, 2 * pair + 1]
-        signal = {j: load(late_ref, (j % 2,), row, step, rows, x_at) for j in late}
-        filt = {j: load(late_ref, (j % 2,), row, step, rows, f_at) for j in late}
         total = [load(part_ref, (i,), row, step, rows, slice(0, chans)) for i in range(n_blocks)]
-        for b in early:
-            if b + late[0] >= n_blocks:
-                continue
-            x_b = load(spec_ref, (b,), row, step, rows, x_at)
-            f_b = load(spec_ref, (b,), row, step, rows, f_at)
-            for j in late:
-                if b + j < n_blocks:
-                    total[b + j] = plus(total[b + j], times(filt[j], x_b))
-                    total[b + j] = plus(total[b + j], times(f_b, signal[j]))
-        for j in late:
-            for d in late:
-                if j + d < n_blocks:
-                    total[j + d] = plus(total[j + d], times(filt[d], signal[j]))
+        add_block(total, place, new_ref, others, row, step, rows, chans)
         for i in range(n_blocks):
             value = total[i]
             if i > 0:
@@ -244,20 +283,18 @@
                     turned[i // 2, pl.ds(row + (2 * c + part) * rows, step), lanes] = piece
 
 
-def conv_kernel(fwd_ref, bwd_ref, spec_ref, part_ref, *refs):
-    *refs, late_ref, turned = refs
-    n_blocks = spec_ref.shape[0]
-    in_refs, out_refs = refs[:-n_blocks], refs[-n_blocks:]
-    rows, chans = in_refs[0].shape[0], in_refs[0].shape[1] // 2
-    for slot, in_ref in zip(slots_of(n_blocks, False)[-2:], in_refs):
-        late_ref[lax.bitwise_and(peer_of(slot), 1)] = block_spectrum(fwd_ref[...], in_ref[...])
-
-    def mix(pair):
+def conv_kernel(fwd_ref, bwd_ref, spec_ref, part_ref, next_ref, in_ref, *refs):
+    *out_refs, new_ref, turned = refs
+    n_blocks, rows, chans = spec_ref.shape[0], in_ref.shape[0], in_ref.shape[1] // 2
+    new_ref[...] = block_spectrum(fwd_ref[...], in_ref[...])
+
+    def mix(place):
         for first, last, sign in ((0, rows // 2, 1), (rows // 2, rows, -1)):
-            mix_late(pair, STEP, first, last, sign, spec_ref, part_ref, late_ref, turned)
-
-    for pair in range(n_blocks // 2):
-        pl.when(late_place(n_blocks) == pair)(functools.partial(mix, pair))
+            mix_last(place, STEP, first, last, sign, spec_ref, part_ref, next_ref, new_ref, turned)
+
+    mine = peer_of(slots_of(n_blocks, False)[-1])
+    for place in range(n_blocks):
+        pl.when(mine == place)(functools.partial(mix, place))
 
     odd = lax.bitwise_and(lax.axis_index("seq"), 1) == 1
     by_slot = dict(zip(slots_of(n_blocks, True), out_refs))
@@ -272,6 +309,7 @@
 def conv_fast(early, part, late, fwd, bwd):
     n_blocks = early.shape[0]
     rows, chans = late[0].shape[0], late[0].shape[1] // 2
+    late_spec, part = middle(early, part, late[0], fwd)
     whole = pl.BlockSpec(memory_space=pltpu.VMEM)
     return pl.pallas_call(
         conv_kernel,
@@ -279,14 +317,14 @@
         out_specs=[whole] * n_blocks,
         out_shape=[jax.ShapeDtypeStruct((rows, chans), BF16)] * n_blocks,
         scratch_shapes=[
-            pltpu.VMEM((2, 2 * rows, 2 * chans), F32),
+            pltpu.VMEM((2 * rows, 2 * chans), F32),
             pltpu.VMEM((n_blocks // 2, 6 * rows, 2 * chans), BF16),
         ],
         compiler_params=pltpu.CompilerParams(vmem_limit_bytes=CONV_VMEM),
         cost_estimate=pl.CostEstimate(
             flops=16 * n_blocks * rows * rows * chans, bytes_accessed=4 * 2**20, transcendentals=0
         ),
-    )(fwd, bwd, early, part, *late)
+    )(fwd, bwd, early, part, late_spec, late[1])
 
 
 def conv_plain(received, fwd, bwd):
@@ -552,7 +590,7 @@
     if chans % 128 == 0 and n_peers == 8:
         blocks = pre(keys, values, filters, n_peers)
         received = exchange(blocks, n_peers, False)
-        fwd, bwd = load_tables(fwd, bwd, received[1:2])
+        fwd, bwd = load_tables(fwd, bwd, received[3:4])
         early, part = spectra(received[:-2], fwd, n_peers)
         back = exchange(conv_fast(early, part, received[-2:], fwd, bwd), n_peers, True)
         slots = slots_of(n_peers, True)[-2:]

time: 64.6 us -> 65.1 us (level)
  waiting for transfers between devices: 20 us -> 22.3 us
  starting transfers between devices: 31.8 us -> 29.6 us
    ppermute x14, waiting for transfers between devices: 9.25 us -> 11.5 us  [exchange(): lax.ppermute(block, 'seq', [(i, i ^ slot) for i in range(n_peers)])]
    ppermute x14, starting transfers between devices: 29 us -> 26.7 us  [exchange(): lax.ppermute(block, 'seq', [(i, i ^ slot) for i in range(n_peers)])]
    pallas_call x0 -> x1, Pallas kernels: none -> 0.69 us  [middle(): pl.pallas_call(middle_kernel, in_specs=[whole] * 4, out_specs=[whole] * 2...]
  transfers between devices with their start and end apart: 19 -> 19, of which waited for: 9 -> 8; matrix products, arithmetic and copies ran while one was open for 0% -> 0% of each run, Pallas kernels for 11% -> 12%
where the time goes in v13:
time: 65.1 us; the launch traced here: 64.9 us
  starting transfers between devices  29.6 us (45%)
  waiting for transfers between devices  22.3 us (34%)
  Pallas kernels  12.8 us (20%)
    ppermute x14, starting transfers between devices, exchange(): lax.ppermute(block, 'seq', [(i, i ^ slot) for i in range(n_peers)])  26.7 us
    ppermute x14, waiting for transfers between devices, exchange(): lax.ppermute(block, 'seq', [(i, i ^ slot) for i in range(n_peers)])  11.5 us
    ppermute x2, waiting for transfers between devices, body(): lax.ppermute(add(*pair), 'fsdp', across)  10.4 us
    ppermute x2, starting transfers between devices, body(): lax.ppermute(add(*pair), 'fsdp', across)  2.16 us
    pallas_call x1, Pallas kernels, spectra(): pl.pallas_call(functools.partial(spectra_kernel, n_peers), in_specs=[whol...  2.15 us
    pallas_call x1, Pallas kernels, conv_fast(): pl.pallas_call(conv_kernel, in_specs=[whole] * 6, out_specs=[whole] * n_b...  1.94 us
    pallas_call x1, Pallas kernels, pre(): pl.pallas_call(functools.partial(pre_kernel, n_peers), in_specs=[pl.Block...  1.77 us
    pallas_call x1, Pallas kernels, gate_early(): pl.pallas_call(functools.partial(gate_early_kernel, n_peers), in_specs=[w...  1.73 us
  transfers between devices with their start and end apart: 19, of which 8 were waited for; matrix products, arithmetic and copies ran while one was open for 0% of the time, Pallas kernels for 12%

profile of v13, /device:TPU:0, one launch (start us, length us, event | category | flops | bytes accessed | tf_op | source)
XLA Modules:
  0.0 64.9 jit_solution(5355869152409659230)
XLA Ops:
  0.0 1.8 %shard_map.82 = (bf16[256,256]{1,0:T(8,128)(2,1)S(1)}, bf16[256,256]{1,0:T(8,128)(2,1)S(1)}, bf16[256,256]{1,0:T(8,128)(2,1)S(1)}, bf16[256,256]{1,0:T(8,128)(2,...) custom-call(bf16[256,1024]{1,0:T(8,128)(2,1)} %keys_ref.3, ...), custom_call_target="tpu_custom_call" | custom-call | flops 262144 | bytes 3145728 | tf_op jit(solution)/shard_map/pallas_call | solution.py:78
  1.8 4.0 %collective-permute-start = (bf16[256,256]{1,0:T(8,128)(2,1)S(1)}, bf16[256,256]{1,0:T(8,128)(2,1)S(1)}, u32[]{:S(2)}, u32[]{:S(2)}) collective-permute-start(bf16[256,256]{1,0:T(8,128)(2,1)S(1)} %get-tuple-element.36), channel_id=1, source_target_pairs={{0,12},{4,8},{8,4},{12,0},{16,28},{20,24},{24,20},{28,16},{1,13},{... | collective-permute-start | bytes 393224 | tf_op jit(solution)/shard_map/ppermute | solution.py:106
  5.8 2.6 %collective-permute-start.1 = (bf16[256,256]{1,0:T(8,128)(2,1)S(1)}, bf16[256,256]{1,0:T(8,128)(2,1)S(1)}, u32[]{:S(2)}, u32[]{:S(2)}) collective-permute-start(bf16[256,256]{1,0:T(8,128)(2,1)S(1)} %get-tuple-element.40), channel_id=1, source_target_pairs={{0,16},{4,20},{8,24},{12,28},{16,0},{20,4},{24,8},{28,12},{1,17},{... | collective-permute-start | bytes 393224 | tf_op jit(solution)/shard_map/ppermute | solution.py:106
  8.4 0.5 collective-permute-start.2
  8.9 0.4 collective-permute-start.3
  9.4 1.3 %collective-permute-start.4 = (bf16[256,256]{1,0:T(8,128)(2,1)S(1)}, bf16[256,256]{1,0:T(8,128)(2,1)S(1)}, u32[]{:S(2)}, u32[]{:S(2)}) collective-permute-start(bf16[256,256]{1,0:T(8,128)(2,1)S(1)} %get-tuple-element.43), channel_id=1, source_target_pairs={{0,20},{4,16},{8,28},{12,24},{16,4},{20,0},{24,12},{28,8},{1,21},{... | collective-permute-start | bytes 393224 | tf_op jit(solution)/shard_map/ppermute | solution.py:106
  10.7 0.6 collective-permute-done.refs_0_.refs_3_
  11.2 5.4 %collective-permute-start.5 = (bf16[256,256]{1,0:T(8,128)(2,1)S(1)}, bf16[256,256]{1,0:T(8,128)(2,1)S(1)}, u32[]{:S(2)}, u32[]{:S(2)}) collective-permute-start(bf16[256,256]{1,0:T(8,128)(2,1)S(1)} %get-tuple-element.46), channel_id=1, source_target_pairs={{0,24},{4,28},{8,16},{12,20},{16,8},{20,12},{24,0},{28,4},{1,25},{... | collective-permute-start | bytes 393224 | tf_op jit(solution)/shard_map/ppermute | solution.py:106
  16.7 1.3 %shard_map.83 = (bf16[512,512]{1,0:T(8,128)(2,1)S(1)}, bf16[256,1536]{1,0:T(8,128)(2,1)S(1)}) custom-call(bf16[512,512]{1,0:T(8,128)(2,1)} %constant.4.clone.fwd_hbm, bf16[256,1536]{1,0:T(8,128)(2,1)} %constant.5.clone.bwd_hbm, bf16[256,256]{1,0:T(8,128)(2,1)S(1)} %collective-permute-done.refs_0_.refs_3_), custom_call_target="tpu_custom_call" | custom-call | flops 1000000 | bytes 3145728 | tf_op jit(solution)/shard_map/pallas_call | solution.py:166
  18.0 1.0 %collective-permute-start.6 = (bf16[256,256]{1,0:T(8,128)(2,1)S(1)}, bf16[256,256]{1,0:T(8,128)(2,1)S(1)}, u32[]{:S(2)}, u32[]{:S(2)}) collective-permute-start(bf16[256,256]{1,0:T(8,128)(2,1)S(1)} %get-tuple-element.49), channel_id=1, source_target_pairs={{0,28},{4,24},{8,20},{12,16},{16,12},{20,8},{24,4},{28,0},{1,29},{... | collective-permute-start | bytes 393224 | tf_op jit(solution)/shard_map/ppermute | solution.py:106
  19.0 7.4 %collective-permute-done.4.refs_5_ = bf16[256,256]{1,0:T(8,128)(2,1)S(1)} collective-permute-done((bf16[256,256]{1,0:T(8,128)(2,1)S(1)}, bf16[256,256]{1,0:T(8,128)(2,1)S(1)}, u32[]{:S(2)}, u32[]{:S(2)}) %collective-permute-start.4) | collective-permute-done | bytes 131104 | tf_op jit(solution)/shard_map/ppermute | solution.py:106
  26.4 2.1 %shard_map.84 = (f32[8,512,256]{2,1,0:T(8,128)S(1)}, f32[8,512,128]{2,1,0:T(8,128)S(1)}) custom-call(bf16[512,512]{1,0:T(8,128)(2,1)S(1)} %get-tuple-element.37.fwd_ref, bf16[256,256]{1,0:T(8,128)(2,1)S(1)} %get-tuple-element.39.refs_0_, bf16[256,256]{1,0:T(8,128)(2,1)S(1)} %collective-permute-done.1.refs_1_, ...), custom_call_target="tpu_custom_call" | custom-call | flops 805306368 | bytes 4194304 | tf_op jit(solution)/shard_map/pallas_call | solution.py:191
  28.6 0.7 %shard_map.85 = (f32[512,256]{1,0:T(8,128)S(1)}, f32[8,512,128]{2,1,0:T(8,128)S(1)}) custom-call(bf16[512,512]{1,0:T(8,128)(2,1)S(1)} %get-tuple-element.37.fwd_ref, f32[8,512,256]{2,1,0:T(8,128)S(1)} %get-tuple-element.44.spec_ref, f32[8,512,128]{2,1,0:T(8,128)S(1)} %get-tuple-element.45.part_ref, bf16[256,256]{1,0:T(8,128)(2,1)S(1)} %collective-permute-done.5.in_ref), custom_call_target="tpu_custom_call" | custom-call | flops 1000000000 | bytes 4194304 | tf_op jit(solution)/shard_map/pallas_call | solution.py:250
  29.3 1.9 %shard_map.86 = (bf16[256,128]{1,0:T(8,128)(2,1)S(1)}, bf16[256,128]{1,0:T(8,128)(2,1)S(1)}, bf16[256,128]{1,0:T(8,128)(2,1)S(1)}, bf16[256,128]{1,0:T(8,128)(2,...) custom-call(bf16[512,512]{1,0:T(8,128)(2,1)S(1)} %get-tuple-element., ...), custom_call_target="tpu_custom_call" | custom-call | flops 1073741824 | bytes 4194304 | tf_op jit(solution)/shard_map/pallas_call | solution.py:314
  31.3 1.6 %collective-permute-start.7 = (bf16[256,128]{1,0:T(8,128)(2,1)S(1)}, bf16[256,128]{1,0:T(8,128)(2,1)S(1)}, u32[]{:S(2)}, u32[]{:S(2)}) collective-permute-start(bf16[256,128]{1,0:T(8,128)(2,1)S(1)} %get-tuple-element.51), channel_id=1, source_target_pairs={{0,4},{4,0},{8,12},{12,8},{16,20},{20,16},{24,28},{28,24},{1,5},{5... | collective-permute-start | bytes 196616 | tf_op jit(solution)/shard_map/ppermute | solution.py:106
  32.9 3.2 %collective-permute-start.8 = (bf16[256,128]{1,0:T(8,128)(2,1)S(1)}, bf16[256,128]{1,0:T(8,128)(2,1)S(1)}, u32[]{:S(2)}, u32[]{:S(2)}) collective-permute-start(bf16[256,128]{1,0:T(8,128)(2,1)S(1)} %get-tuple-element.52), channel_id=1, source_target_pairs={{0,24},{4,28},{8,16},{12,20},{16,8},{20,12},{24,0},{28,4},{1,25},{... | collective-permute-start | bytes 196616 | tf_op jit(solution)/shard_map/ppermute | solution.py:106
  36.1 1.1 %collective-permute-start.9 = (bf16[256,128]{1,0:T(8,128)(2,1)S(1)}, bf16[256,128]{1,0:T(8,128)(2,1)S(1)}, u32[]{:S(2)}, u32[]{:S(2)}) collective-permute-start(bf16[256,128]{1,0:T(8,128)(2,1)S(1)} %get-tuple-element.53), channel_id=1, source_target_pairs={{0,16},{4,20},{8,24},{12,28},{16,0},{20,4},{24,8},{28,12},{1,17},{... | collective-permute-start | bytes 196616 | tf_op jit(solution)/shard_map/ppermute | solution.py:106
  37.2 1.7 %collective-permute-start.10 = (bf16[256,128]{1,0:T(8,128)(2,1)S(1)}, bf16[256,128]{1,0:T(8,128)(2,1)S(1)}, u32[]{:S(2)}, u32[]{:S(2)}) collective-permute-start(bf16[256,128]{1,0:T(8,128)(2,1)S(1)} %get-tuple-element.54), channel_id=1, source_target_pairs={{0,20},{4,16},{8,28},{12,24},{16,4},{20,0},{24,12},{28,8},{1,21},{... | collective-permute-start | bytes 196616 | tf_op jit(solution)/shard_map/ppermute | solution.py:106
  38.9 1.3 %collective-permute-start.11 = (bf16[256,128]{1,0:T(8,128)(2,1)S(1)}, bf16[256,128]{1,0:T(8,128)(2,1)S(1)}, u32[]{:S(2)}, u32[]{:S(2)}) collective-permute-start(bf16[256,128]{1,0:T(8,128)(2,1)S(1)} %get-tuple-element.55), channel_id=1, source_target_pairs={{0,8},{4,12},{8,0},{12,4},{16,24},{20,28},{24,16},{28,20},{1,9},{5... | collective-permute-start | bytes 196616 | tf_op jit(solution)/shard_map/ppermute | solution.py:106
  40.2 2.2 %collective-permute-start.12 = (bf16[256,128]{1,0:T(8,128)(2,1)S(1)}, bf16[256,128]{1,0:T(8,128)(2,1)S(1)}, u32[]{:S(2)}, u32[]{:S(2)}) collective-permute-start(bf16[256,128]{1,0:T(8,128)(2,1)S(1)} %get-tuple-element.58), channel_id=1, source_target_pairs={{0,28},{4,24},{8,20},{12,16},{16,12},{20,8},{24,4},{28,0},{1,29},{... | collective-permute-start | bytes 196616 | tf_op jit(solution)/shard_map/ppermute | solution.py:106
  42.7 2.7 %collective-permute-done.9.refs_3_ = bf16[256,128]{1,0:T(8,128)(2,1)S(1)} collective-permute-done((bf16[256,128]{1,0:T(8,128)(2,1)S(1)}, bf16[256,128]{1,0:T(8,128)(2,1)S(1)}, u32[]{:S(2)}, u32[]{:S(2)}) %collective-permute-start.9) | collective-permute-done | bytes 65568 | tf_op jit(solution)/shard_map/ppermute | solution.py:106
  45.3 0.6 collective-permute-done.10.refs_4_
  46.0 1.7 %shard_map.87 = (bf16[256,1024]{1,0:T(8,128)(2,1)S(1)}, f32[256,1024]{1,0:T(8,128)S(1)}, f32[256,1024]{1,0:T(8,128)S(1)}) custom-call(bf16[256,1024]{1,0:T(8,128)(2,1)S(1)} %copy-done.2, bf16[256,1024]{1,0:T(8,128)(2,1)S(1)} %copy-done, bf16[256,1024]{1,0:T(8,128)(2,1)S(1)} %copy-done.1, f32[1,1024]{1,0:T(1,128)S(1)} %bitcast.3, ...), custom_call_target="tpu_custom_call" | custom-call | flops 1073741824 | bytes 2621440 | tf_op jit(solution)/shard_map/pallas_call | solution.py:395
  47.7 0.3 collective-permute-done.13.refs_1_
  48.7 0.5 collective-permute-start.15
  49.5 0.4 collective-permute-done.17.arrived_ref
  50.0 1.6 %collective-permute-start.18 = (bf16[256,512]{1,0:T(8,128)(2,1)S(1)}, bf16[256,512]{1,0:T(8,128)(2,1)S(1)}, u32[]{:S(2)}, u32[]{:S(2)}) collective-permute-start(bf16[256,512]{1,0:T(8,128)(2,1)S(1)} %shard_map.94), channel_id=1, source_target_pairs={{0,2},{2,0},{1,3},{3,1},{4,6},{6,4},{5,7},{7,5},{8,10},{10,8},{9,1... | collective-permute-start | bytes 786440 | tf_op jit(solution)/shard_map/ppermute | solution.py:622
  51.7 0.6 collective-permute-start.16
  52.3 1.3 %shard_map.90 = (bf16[256,1024]{1,0:T(8,128)(2,1)S(1)}, f32[256,1024]{1,0:T(8,128)S(1)}) custom-call(bf16[256,1024]{1,0:T(8,128)(2,1)S(1)} %shard_map.89.gated_ref, bf16[1024,4096]{1,0:T(8,128)(2,1)S(1)} %bitcast.2), custom_call_target="tpu_custom_call" | custom-call | flops 1073741824 | bytes 4194304 | tf_op jit(solution)/shard_map/pallas_call | solution.py:498
  53.7 5.6 %collective-permute-done.18.refs_1_ = bf16[256,512]{1,0:T(8,128)(2,1)S(1)} collective-permute-done((bf16[256,512]{1,0:T(8,128)(2,1)S(1)}, bf16[256,512]{1,0:T(8,128)(2,1)S(1)}, u32[]{:S(2)}, u32[]{:S(2)}) %collective-permute-start.18) | collective-permute-done | bytes 262176 | tf_op jit(solution)/shard_map/ppermute | solution.py:622
  59.2 4.8 %collective-permute-done.16.refs_0_ = bf16[256,512]{1,0:T(8,128)(2,1)S(1)} collective-permute-done((bf16[256,512]{1,0:T(8,128)(2,1)S(1)}, bf16[256,512]{1,0:T(8,128)(2,1)S(1)}, u32[]{:S(2)}, u32[]{:S(2)}) %collective-permute-start.16) | collective-permute-done | bytes 262176 | tf_op jit(solution)/shard_map/ppermute | solution.py:622
  64.1 0.9 %shard_map.96 = bf16[256,1024]{1,0:T(8,128)(2,1)} custom-call(f32[256,1024]{1,0:T(8,128)S(1)} %get-tuple-element.61.own_ref, bf16[256,1024]{1,0:T(8,128)(2,1)S(1)} %collective-permute-done.14.near_ref, bf16[256,512]{1,0:T(8,128)(2,1)S(1)} %collective-permute-done.16.refs_0_, bf16[256,512]{1,0:T(8,128)(2,1)S(1)} %collective-permute-done.18.refs_1_, ...), custom_call_target="tpu_custom_call" | custom-call | flops 262144 | bytes 2097152 | tf_op jit(solution)/shard_map/pallas_call | solution.py:565
  (34 shorter events, 1.4 us)
Async XLA Ops:
  1.8 9.4 %collective-permute-start = (bf16[256,256]{1,0:T(8,128)(2,1)S(1)}, bf16[256,256]{1,0:T(8,128)(2,1)S(1)}, u32[]{:S(2)}, u32[]{:S(2)}) collective-permute-start(bf16[256,256]{1,0:T(8,128)(2,1)S(1)} %get-tuple-element.36), channel_id=1, source_target_pairs={{0,12},{4,8},{8,4},{12,0},{16,28},{20,24},{24,20},{28,16},{1,13},{... | collective-permute-start | bytes 393224 | tf_op jit(solution)/shard_map/ppermute | solution.py:106
  5.8 12.2 %collective-permute-start.1 = (bf16[256,256]{1,0:T(8,128)(2,1)S(1)}, bf16[256,256]{1,0:T(8,128)(2,1)S(1)}, u32[]{:S(2)}, u32[]{:S(2)}) collective-permute-start(bf16[256,256]{1,0:T(8,128)(2,1)S(1)} %get-tuple-element.40), channel_id=1, source_target_pairs={{0,16},{4,20},{8,24},{12,28},{16,0},{20,4},{24,8},{28,12},{1,17},{... | collective-permute-start | bytes 393224 | tf_op jit(solution)/shard_map/ppermute | solution.py:106
  8.4 10.6 %collective-permute-start.2 = (bf16[256,256]{1,0:T(8,128)(2,1)S(1)}, bf16[256,256]{1,0:T(8,128)(2,1)S(1)}, u32[]{:S(2)}, u32[]{:S(2)}) collective-permute-start(bf16[256,256]{1,0:T(8,128)(2,1)S(1)} %get-tuple-element.41), channel_id=1, source_target_pairs={{0,4},{4,0},{8,12},{12,8},{16,20},{20,16},{24,28},{28,24},{1,5},{5... | collective-permute-start | bytes 393224 | tf_op jit(solution)/shard_map/ppermute | solution.py:106
  8.9 10.1 %collective-permute-start.3 = (bf16[256,256]{1,0:T(8,128)(2,1)S(1)}, bf16[256,256]{1,0:T(8,128)(2,1)S(1)}, u32[]{:S(2)}, u32[]{:S(2)}) collective-permute-start(bf16[256,256]{1,0:T(8,128)(2,1)S(1)} %get-tuple-element.42), channel_id=1, source_target_pairs={{0,8},{4,12},{8,0},{12,4},{16,24},{20,28},{24,16},{28,20},{1,9},{5... | collective-permute-start | bytes 393224 | tf_op jit(solution)/shard_map/ppermute | solution.py:106
  9.4 17.0 %collective-permute-start.4 = (bf16[256,256]{1,0:T(8,128)(2,1)S(1)}, bf16[256,256]{1,0:T(8,128)(2,1)S(1)}, u32[]{:S(2)}, u32[]{:S(2)}) collective-permute-start(bf16[256,256]{1,0:T(8,128)(2,1)S(1)} %get-tuple-element.43), channel_id=1, source_target_pairs={{0,20},{4,16},{8,28},{12,24},{16,4},{20,0},{24,12},{28,8},{1,21},{... | collective-permute-start | bytes 393224 | tf_op jit(solution)/shard_map/ppermute | solution.py:106
  11.2 17.3 %collective-permute-start.5 = (bf16[256,256]{1,0:T(8,128)(2,1)S(1)}, bf16[256,256]{1,0:T(8,128)(2,1)S(1)}, u32[]{:S(2)}, u32[]{:S(2)}) collective-permute-start(bf16[256,256]{1,0:T(8,128)(2,1)S(1)} %get-tuple-element.46), channel_id=1, source_target_pairs={{0,24},{4,28},{8,16},{12,20},{16,8},{20,12},{24,0},{28,4},{1,25},{... | collective-permute-start | bytes 393224 | tf_op jit(solution)/shard_map/ppermute | solution.py:106
  18.0 11.3 %collective-permute-start.6 = (bf16[256,256]{1,0:T(8,128)(2,1)S(1)}, bf16[256,256]{1,0:T(8,128)(2,1)S(1)}, u32[]{:S(2)}, u32[]{:S(2)}) collective-permute-start(bf16[256,256]{1,0:T(8,128)(2,1)S(1)} %get-tuple-element.49), channel_id=1, source_target_pairs={{0,28},{4,24},{8,20},{12,16},{16,12},{20,8},{24,4},{28,0},{1,29},{... | collective-permute-start | bytes 393224 | tf_op jit(solution)/shard_map/ppermute | solution.py:106
  28.5 17.4 %slice-start = ((s8[8388608]{0:T(1024)(128)(4,1)}), s8[4194304]{0:T(1024)(128)(4,1)S(1)}, s32[]{:S(2)}) async-start(s8[8388608]{0:T(1024)(128)(4,1)} %bitcast.1), calls=%async_computation | async-start | bytes 8388608
  29.2 16.7 %copy-start = (bf16[256,1024]{1,0:T(8,128)(2,1)S(1)}, bf16[256,1024]{1,0:T(8,128)(2,1)}, u32[]{:S(2)}) copy-start(bf16[256,1024]{1,0:T(8,128)(2,1)} %keys_ref.3) | copy-start | bytes 1572868
  29.3 16.7 %copy-start.1 = (bf16[256,1024]{1,0:T(8,128)(2,1)S(1)}, bf16[256,1024]{1,0:T(8,128)(2,1)}, u32[]{:S(2)}) copy-start(bf16[256,1024]{1,0:T(8,128)(2,1)} %values_ref.3) | copy-start | bytes 1572868
  29.3 16.7 %copy-start.2 = (bf16[256,1024]{1,0:T(8,128)(2,1)S(1)}, bf16[256,1024]{1,0:T(8,128)(2,1)}, u32[]{:S(2)}) copy-start(bf16[256,1024]{1,0:T(8,128)(2,1)} %queries_ref.3) | copy-start | bytes 1572868
  29.3 16.6 %copy-start.3 = (f32[1024]{0:T(1024)S(1)}, f32[1024]{0:T(1024)}, u32[]{:S(2)}) copy-start(f32[1024]{0:T(1024)} %param.12) | copy-start | bytes 12292
  29.3 16.6 %slice-start.1 = ((s8[8388608]{0:T(1024)(128)(4,1)}), s8[4194304]{0:T(1024)(128)(4,1)S(1)}, s32[]{:S(2)}) async-start(s8[8388608]{0:T(1024)(128)(4,1)} %bitcast.1), calls=%async_computation.1 | async-start | bytes 8388608
  31.3 9.0 %collective-permute-start.7 = (bf16[256,128]{1,0:T(8,128)(2,1)S(1)}, bf16[256,128]{1,0:T(8,128)(2,1)S(1)}, u32[]{:S(2)}, u32[]{:S(2)}) collective-permute-start(bf16[256,128]{1,0:T(8,128)(2,1)S(1)} %get-tuple-element.51), channel_id=1, source_target_pairs={{0,4},{4,0},{8,12},{12,8},{16,20},{20,16},{24,28},{28,24},{1,5},{5... | collective-permute-start | bytes 196616 | tf_op jit(solution)/shard_map/ppermute | solution.py:106
  32.9 9.6 %collective-permute-start.8 = (bf16[256,128]{1,0:T(8,128)(2,1)S(1)}, bf16[256,128]{1,0:T(8,128)(2,1)S(1)}, u32[]{:S(2)}, u32[]{:S(2)}) collective-permute-start(bf16[256,128]{1,0:T(8,128)(2,1)S(1)} %get-tuple-element.52), channel_id=1, source_target_pairs={{0,24},{4,28},{8,16},{12,20},{16,8},{20,12},{24,0},{28,4},{1,25},{... | collective-permute-start | bytes 196616 | tf_op jit(solution)/shard_map/ppermute | solution.py:106
  36.1 9.2 %collective-permute-start.9 = (bf16[256,128]{1,0:T(8,128)(2,1)S(1)}, bf16[256,128]{1,0:T(8,128)(2,1)S(1)}, u32[]{:S(2)}, u32[]{:S(2)}) collective-permute-start(bf16[256,128]{1,0:T(8,128)(2,1)S(1)} %get-tuple-element.53), channel_id=1, source_target_pairs={{0,16},{4,20},{8,24},{12,28},{16,0},{20,4},{24,8},{28,12},{1,17},{... | collective-permute-start | bytes 196616 | tf_op jit(solution)/shard_map/ppermute | solution.py:106
  37.2 8.7 %collective-permute-start.10 = (bf16[256,128]{1,0:T(8,128)(2,1)S(1)}, bf16[256,128]{1,0:T(8,128)(2,1)S(1)}, u32[]{:S(2)}, u32[]{:S(2)}) collective-permute-start(bf16[256,128]{1,0:T(8,128)(2,1)S(1)} %get-tuple-element.54), channel_id=1, source_target_pairs={{0,20},{4,16},{8,28},{12,24},{16,4},{20,0},{24,12},{28,8},{1,21},{... | collective-permute-start | bytes 196616 | tf_op jit(solution)/shard_map/ppermute | solution.py:106
  38.9 7.0 %collective-permute-start.11 = (bf16[256,128]{1,0:T(8,128)(2,1)S(1)}, bf16[256,128]{1,0:T(8,128)(2,1)S(1)}, u32[]{:S(2)}, u32[]{:S(2)}) collective-permute-start(bf16[256,128]{1,0:T(8,128)(2,1)S(1)} %get-tuple-element.55), channel_id=1, source_target_pairs={{0,8},{4,12},{8,0},{12,4},{16,24},{20,28},{24,16},{28,20},{1,9},{5... | collective-permute-start | bytes 196616 | tf_op jit(solution)/shard_map/ppermute | solution.py:106
  40.2 7.5 %collective-permute-start.12 = (bf16[256,128]{1,0:T(8,128)(2,1)S(1)}, bf16[256,128]{1,0:T(8,128)(2,1)S(1)}, u32[]{:S(2)}, u32[]{:S(2)}) collective-permute-start(bf16[256,128]{1,0:T(8,128)(2,1)S(1)} %get-tuple-element.58), channel_id=1, source_target_pairs={{0,28},{4,24},{8,20},{12,16},{16,12},{20,8},{24,4},{28,0},{1,29},{... | collective-permute-start | bytes 196616 | tf_op jit(solution)/shard_map/ppermute | solution.py:106
  42.5 5.6 %collective-permute-start.13 = (bf16[256,128]{1,0:T(8,128)(2,1)S(1)}, bf16[256,128]{1,0:T(8,128)(2,1)S(1)}, u32[]{:S(2)}, u32[]{:S(2)}) collective-permute-start(bf16[256,128]{1,0:T(8,128)(2,1)S(1)} %get-tuple-element.59), channel_id=1, source_target_pairs={{0,12},{4,8},{8,4},{12,0},{16,28},{20,24},{24,20},{28,16},{1,13},{... | collective-permute-start | bytes 196616 | tf_op jit(solution)/shard_map/ppermute | solution.py:106
  48.4 1.6 %collective-permute-start.17 = (bf16[256,512]{1,0:T(8,128)(2,1)S(1)}, bf16[256,512]{1,0:T(8,128)(2,1)S(1)}, u32[]{:S(2)}, u32[]{:S(2)}) collective-permute-start(bf16[256,512]{1,0:T(8,128)(2,1)S(1)} %get-tuple-element.66), channel_id=1, source_target_pairs={{0,1},{1,0},{2,3},{3,2},{4,5},{5,4},{6,7},{7,6},{8,9},{9,8},{10,11... | collective-permute-start | bytes 786440 | tf_op jit(solution)/shard_map/ppermute | solution.py:621
  48.7 2.9 %collective-permute-start.15 = (bf16[256,512]{1,0:T(8,128)(2,1)S(1)}, bf16[256,512]{1,0:T(8,128)(2,1)S(1)}, u32[]{:S(2)}, u32[]{:S(2)}) collective-permute-start(bf16[256,512]{1,0:T(8,128)(2,1)S(1)} %shard_map.92), channel_id=1, source_target_pairs={{0,1},{1,0},{2,3},{3,2},{4,5},{5,4},{6,7},{7,6},{8,9},{9,8},{10,11... | collective-permute-start | bytes 786440 | tf_op jit(solution)/shard_map/ppermute | solution.py:621
  50.0 9.2 %collective-permute-start.18 = (bf16[256,512]{1,0:T(8,128)(2,1)S(1)}, bf16[256,512]{1,0:T(8,128)(2,1)S(1)}, u32[]{:S(2)}, u32[]{:S(2)}) collective-permute-start(bf16[256,512]{1,0:T(8,128)(2,1)S(1)} %shard_map.94), channel_id=1, source_target_pairs={{0,2},{2,0},{1,3},{3,1},{4,6},{6,4},{5,7},{7,5},{8,10},{10,8},{9,1... | collective-permute-start | bytes 786440 | tf_op jit(solution)/shard_map/ppermute | solution.py:622
  51.7 12.4 %collective-permute-start.16 = (bf16[256,512]{1,0:T(8,128)(2,1)S(1)}, bf16[256,512]{1,0:T(8,128)(2,1)S(1)}, u32[]{:S(2)}, u32[]{:S(2)}) collective-permute-start(bf16[256,512]{1,0:T(8,128)(2,1)S(1)} %shard_map.93), channel_id=1, source_target_pairs={{0,2},{2,0},{1,3},{3,1},{4,6},{6,4},{5,7},{7,5},{8,10},{10,8},{9,1... | collective-permute-start | bytes 786440 | tf_op jit(solution)/shard_map/ppermute | solution.py:622
  53.6 10.5 %collective-permute-start.14 = (bf16[256,1024]{1,0:T(8,128)(2,1)S(1)}, bf16[256,1024]{1,0:T(8,128)(2,1)S(1)}, u32[]{:S(2)}, u32[]{:S(2)}) collective-permute-start(bf16[256,1024]{1,0:T(8,128)(2,1)S(1)} %get-tuple-element.62), channel_id=1, source_target_pairs={{0,1},{1,0},{2,3},{3,2},{4,5},{5,4},{6,7},{7,6},{8,9},{9,8},{10,11... | collective-permute-start | bytes 1572872 | tf_op jit(solution)/shard_map/ppermute | solution.py:625

commit v14 on v13

--- a/solution.py
+++ b/solution.py
@@ -590,7 +590,7 @@
     if chans % 128 == 0 and n_peers == 8:
         blocks = pre(keys, values, filters, n_peers)
         received = exchange(blocks, n_peers, False)
-        fwd, bwd = load_tables(fwd, bwd, received[3:4])
+        fwd, bwd = load_tables(fwd, bwd, received[1:2])
         early, part = spectra(received[:-2], fwd, n_peers)
         back = exchange(conv_fast(early, part, received[-2:], fwd, bwd), n_peers, True)
         slots = slots_of(n_peers, True)[-2:]

time: 65.1 us -> 64.7 us (level)
  waiting for transfers between devices: 22.3 us -> 19.8 us
  starting transfers between devices: 29.6 us -> 31.7 us
    ppermute x14, waiting for transfers between devices: 11.5 us -> 8.97 us  [exchange(): lax.ppermute(block, 'seq', [(i, i ^ slot) for i in range(n_peers)])]
    ppermute x14, starting transfers between devices: 26.7 us -> 28.9 us  [exchange(): lax.ppermute(block, 'seq', [(i, i ^ slot) for i in range(n_peers)])]
  transfers between devices with their start and end apart: 19 -> 19, of which waited for: 8 -> 9; matrix products, arithmetic and copies ran while one was open for 0% -> 0% of each run, Pallas kernels for 12% -> 12%
where the time goes in v14:
time: 64.7 us; the launch traced here: 64.5 us
  starting transfers between devices  31.7 us (49%)
  waiting for transfers between devices  19.8 us (31%)
  Pallas kernels  12.8 us (20%)
    ppermute x14, starting transfers between devices, exchange(): lax.ppermute(block, 'seq', [(i, i ^ slot) for i in range(n_peers)])  28.9 us
    ppermute x2, waiting for transfers between devices, body(): lax.ppermute(add(*pair), 'fsdp', across)  10.4 us
    ppermute x14, waiting for transfers between devices, exchange(): lax.ppermute(block, 'seq', [(i, i ^ slot) for i in range(n_peers)])  8.97 us
    pallas_call x1, Pallas kernels, spectra(): pl.pallas_call(functools.partial(spectra_kernel, n_peers), in_specs=[whol...  2.16 us
    ppermute x2, starting transfers between devices, body(): lax.ppermute(add(*pair), 'fsdp', across)  2.16 us
    pallas_call x1, Pallas kernels, conv_fast(): pl.pallas_call(conv_kernel, in_specs=[whole] * 6, out_specs=[whole] * n_b...  1.93 us
    pallas_call x1, Pallas kernels, pre(): pl.pallas_call(functools.partial(pre_kernel, n_peers), in_specs=[pl.Block...  1.77 us
    pallas_call x1, Pallas kernels, gate_early(): pl.pallas_call(functools.partial(gate_early_kernel, n_peers), in_specs=[w...  1.73 us
  transfers between devices with their start and end apart: 19, of which 9 were waited for; matrix products, arithmetic and copies ran while one was open for 0% of the time, Pallas kernels for 12%

profile of v14, /device:TPU:0, one launch (start us, length us, event | category | flops | bytes accessed | tf_op | source)
XLA Modules:
  0.0 64.5 jit_solution(15315105246910628444)
XLA Ops:
  0.0 1.8 %shard_map.82 = (bf16[256,256]{1,0:T(8,128)(2,1)S(1)}, bf16[256,256]{1,0:T(8,128)(2,1)S(1)}, bf16[256,256]{1,0:T(8,128)(2,1)S(1)}, bf16[256,256]{1,0:T(8,128)(2,...) custom-call(bf16[256,1024]{1,0:T(8,128)(2,1)} %keys_ref.3, ...), custom_call_target="tpu_custom_call" | custom-call | flops 262144 | bytes 3145728 | tf_op jit(solution)/shard_map/pallas_call | solution.py:78
  1.8 4.1 %collective-permute-start = (bf16[256,256]{1,0:T(8,128)(2,1)S(1)}, bf16[256,256]{1,0:T(8,128)(2,1)S(1)}, u32[]{:S(2)}, u32[]{:S(2)}) collective-permute-start(bf16[256,256]{1,0:T(8,128)(2,1)S(1)} %get-tuple-element.36), channel_id=1, source_target_pairs={{0,16},{4,20},{8,24},{12,28},{16,0},{20,4},{24,8},{28,12},{1,17},{... | collective-permute-start | bytes 393224 | tf_op jit(solution)/shard_map/ppermute | solution.py:106
  5.9 1.5 %collective-permute-start.1 = (bf16[256,256]{1,0:T(8,128)(2,1)S(1)}, bf16[256,256]{1,0:T(8,128)(2,1)S(1)}, u32[]{:S(2)}, u32[]{:S(2)}) collective-permute-start(bf16[256,256]{1,0:T(8,128)(2,1)S(1)} %get-tuple-element.40), channel_id=1, source_target_pairs={{0,4},{4,0},{8,12},{12,8},{16,20},{20,16},{24,28},{28,24},{1,5},{5... | collective-permute-start | bytes 393224 | tf_op jit(solution)/shard_map/ppermute | solution.py:106
  7.4 1.5 %collective-permute-start.2 = (bf16[256,256]{1,0:T(8,128)(2,1)S(1)}, bf16[256,256]{1,0:T(8,128)(2,1)S(1)}, u32[]{:S(2)}, u32[]{:S(2)}) collective-permute-start(bf16[256,256]{1,0:T(8,128)(2,1)S(1)} %get-tuple-element.41), channel_id=1, source_target_pairs={{0,12},{4,8},{8,4},{12,0},{16,28},{20,24},{24,20},{28,16},{1,13},{... | collective-permute-start | bytes 393224 | tf_op jit(solution)/shard_map/ppermute | solution.py:106
  8.9 0.4 collective-permute-start.3
  9.4 1.3 %collective-permute-start.4 = (bf16[256,256]{1,0:T(8,128)(2,1)S(1)}, bf16[256,256]{1,0:T(8,128)(2,1)S(1)}, u32[]{:S(2)}, u32[]{:S(2)}) collective-permute-start(bf16[256,256]{1,0:T(8,128)(2,1)S(1)} %get-tuple-element.43), channel_id=1, source_target_pairs={{0,20},{4,16},{8,28},{12,24},{16,4},{20,0},{24,12},{28,8},{1,21},{... | collective-permute-start | bytes 393224 | tf_op jit(solution)/shard_map/ppermute | solution.py:106
  10.7 1.6 %collective-permute-done.refs_0_.refs_1_ = bf16[256,256]{1,0:T(8,128)(2,1)S(1)} collective-permute-done((bf16[256,256]{1,0:T(8,128)(2,1)S(1)}, bf16[256,256]{1,0:T(8,128)(2,1)S(1)}, u32[]{:S(2)}, u32[]{:S(2)}) %collective-permute-start) | collective-permute-done | bytes 131104 | tf_op jit(solution)/shard_map/ppermute | solution.py:106
  12.3 3.6 %collective-permute-start.5 = (bf16[256,256]{1,0:T(8,128)(2,1)S(1)}, bf16[256,256]{1,0:T(8,128)(2,1)S(1)}, u32[]{:S(2)}, u32[]{:S(2)}) collective-permute-start(bf16[256,256]{1,0:T(8,128)(2,1)S(1)} %get-tuple-element.46), channel_id=1, source_target_pairs={{0,24},{4,28},{8,16},{12,20},{16,8},{20,12},{24,0},{28,4},{1,25},{... | collective-permute-start | bytes 393224 | tf_op jit(solution)/shard_map/ppermute | solution.py:106
  15.9 1.3 %shard_map.83 = (bf16[512,512]{1,0:T(8,128)(2,1)S(1)}, bf16[256,1536]{1,0:T(8,128)(2,1)S(1)}) custom-call(bf16[512,512]{1,0:T(8,128)(2,1)} %constant.4.clone.fwd_hbm, bf16[256,1536]{1,0:T(8,128)(2,1)} %constant.5.clone.bwd_hbm, bf16[256,256]{1,0:T(8,128)(2,1)S(1)} %collective-permute-done.refs_0_.refs_1_), custom_call_target="tpu_custom_call" | custom-call | flops 1000000 | bytes 3145728 | tf_op jit(solution)/shard_map/pallas_call | solution.py:166
  17.3 1.9 %collective-permute-start.6 = (bf16[256,256]{1,0:T(8,128)(2,1)S(1)}, bf16[256,256]{1,0:T(8,128)(2,1)S(1)}, u32[]{:S(2)}, u32[]{:S(2)}) collective-permute-start(bf16[256,256]{1,0:T(8,128)(2,1)S(1)} %get-tuple-element.49), channel_id=1, source_target_pairs={{0,28},{4,24},{8,20},{12,16},{16,12},{20,8},{24,4},{28,0},{1,29},{... | collective-permute-start | bytes 393224 | tf_op jit(solution)/shard_map/ppermute | solution.py:106
  19.5 2.2 %shard_map.84 = (f32[8,512,256]{2,1,0:T(8,128)S(1)}, f32[8,512,128]{2,1,0:T(8,128)S(1)}) custom-call(bf16[512,512]{1,0:T(8,128)(2,1)S(1)} %get-tuple-element.37.fwd_ref, bf16[256,256]{1,0:T(8,128)(2,1)S(1)} %get-tuple-element.39.refs_0_, bf16[256,256]{1,0:T(8,128)(2,1)S(1)} %collective-permute-done.refs_0_.refs_1_, ...), custom_call_target="tpu_custom_call" | custom-call | flops 805306368 | bytes 4194304 | tf_op jit(solution)/shard_map/pallas_call | solution.py:191
  21.8 0.7 %shard_map.85 = (f32[512,256]{1,0:T(8,128)S(1)}, f32[8,512,128]{2,1,0:T(8,128)S(1)}) custom-call(bf16[512,512]{1,0:T(8,128)(2,1)S(1)} %get-tuple-element.37.fwd_ref, f32[8,512,256]{2,1,0:T(8,128)S(1)} %get-tuple-element.44.spec_ref, f32[8,512,128]{2,1,0:T(8,128)S(1)} %get-tuple-element.45.part_ref, bf16[256,256]{1,0:T(8,128)(2,1)S(1)} %collective-permute-done.5.in_ref), custom_call_target="tpu_custom_call" | custom-call | flops 1000000000 | bytes 4194304 | tf_op jit(solution)/shard_map/pallas_call | solution.py:250
  22.6 3.1 %collective-permute-done.6.in_ref = bf16[256,256]{1,0:T(8,128)(2,1)S(1)} collective-permute-done((bf16[256,256]{1,0:T(8,128)(2,1)S(1)}, bf16[256,256]{1,0:T(8,128)(2,1)S(1)}, u32[]{:S(2)}, u32[]{:S(2)}) %collective-permute-start.6) | collective-permute-done | bytes 131104 | tf_op jit(solution)/shard_map/ppermute | solution.py:106
  25.7 1.9 %shard_map.86 = (bf16[256,128]{1,0:T(8,128)(2,1)S(1)}, bf16[256,128]{1,0:T(8,128)(2,1)S(1)}, bf16[256,128]{1,0:T(8,128)(2,1)S(1)}, bf16[256,128]{1,0:T(8,128)(2,...) custom-call(bf16[512,512]{1,0:T(8,128)(2,1)S(1)} %get-tuple-element., ...), custom_call_target="tpu_custom_call" | custom-call | flops 1073741824 | bytes 4194304 | tf_op jit(solution)/shard_map/pallas_call | solution.py:314
  27.6 4.6 %collective-permute-start.7 = (bf16[256,128]{1,0:T(8,128)(2,1)S(1)}, bf16[256,128]{1,0:T(8,128)(2,1)S(1)}, u32[]{:S(2)}, u32[]{:S(2)}) collective-permute-start(bf16[256,128]{1,0:T(8,128)(2,1)S(1)} %get-tuple-element.51), channel_id=1, source_target_pairs={{0,4},{4,0},{8,12},{12,8},{16,20},{20,16},{24,28},{28,24},{1,5},{5... | collective-permute-start | bytes 196616 | tf_op jit(solution)/shard_map/ppermute | solution.py:106
  32.3 1.9 %collective-permute-start.8 = (bf16[256,128]{1,0:T(8,128)(2,1)S(1)}, bf16[256,128]{1,0:T(8,128)(2,1)S(1)}, u32[]{:S(2)}, u32[]{:S(2)}) collective-permute-start(bf16[256,128]{1,0:T(8,128)(2,1)S(1)} %get-tuple-element.52), channel_id=1, source_target_pairs={{0,24},{4,28},{8,16},{12,20},{16,8},{20,12},{24,0},{28,4},{1,25},{... | collective-permute-start | bytes 196616 | tf_op jit(solution)/shard_map/ppermute | solution.py:106
  34.1 1.9 %collective-permute-start.9 = (bf16[256,128]{1,0:T(8,128)(2,1)S(1)}, bf16[256,128]{1,0:T(8,128)(2,1)S(1)}, u32[]{:S(2)}, u32[]{:S(2)}) collective-permute-start(bf16[256,128]{1,0:T(8,128)(2,1)S(1)} %get-tuple-element.53), channel_id=1, source_target_pairs={{0,16},{4,20},{8,24},{12,28},{16,0},{20,4},{24,8},{28,12},{1,17},{... | collective-permute-start | bytes 196616 | tf_op jit(solution)/shard_map/ppermute | solution.py:106
  36.0 0.8 %collective-permute-start.10 = (bf16[256,128]{1,0:T(8,128)(2,1)S(1)}, bf16[256,128]{1,0:T(8,128)(2,1)S(1)}, u32[]{:S(2)}, u32[]{:S(2)}) collective-permute-start(bf16[256,128]{1,0:T(8,128)(2,1)S(1)} %get-tuple-element.54), channel_id=1, source_target_pairs={{0,20},{4,16},{8,28},{12,24},{16,4},{20,0},{24,12},{28,8},{1,21},{... | collective-permute-start | bytes 196616 | tf_op jit(solution)/shard_map/ppermute | solution.py:106
  36.9 3.1 %collective-permute-start.11 = (bf16[256,128]{1,0:T(8,128)(2,1)S(1)}, bf16[256,128]{1,0:T(8,128)(2,1)S(1)}, u32[]{:S(2)}, u32[]{:S(2)}) collective-permute-start(bf16[256,128]{1,0:T(8,128)(2,1)S(1)} %get-tuple-element.55), channel_id=1, source_target_pairs={{0,8},{4,12},{8,0},{12,4},{16,24},{20,28},{24,16},{28,20},{1,9},{5... | collective-permute-start | bytes 196616 | tf_op jit(solution)/shard_map/ppermute | solution.py:106
  40.0 1.3 %collective-permute-start.12 = (bf16[256,128]{1,0:T(8,128)(2,1)S(1)}, bf16[256,128]{1,0:T(8,128)(2,1)S(1)}, u32[]{:S(2)}, u32[]{:S(2)}) collective-permute-start(bf16[256,128]{1,0:T(8,128)(2,1)S(1)} %get-tuple-element.58), channel_id=1, source_target_pairs={{0,28},{4,24},{8,20},{12,16},{16,12},{20,8},{24,4},{28,0},{1,29},{... | collective-permute-start | bytes 196616 | tf_op jit(solution)/shard_map/ppermute | solution.py:106
  41.3 0.8 %collective-permute-start.13 = (bf16[256,128]{1,0:T(8,128)(2,1)S(1)}, bf16[256,128]{1,0:T(8,128)(2,1)S(1)}, u32[]{:S(2)}, u32[]{:S(2)}) collective-permute-start(bf16[256,128]{1,0:T(8,128)(2,1)S(1)} %get-tuple-element.59), channel_id=1, source_target_pairs={{0,12},{4,8},{8,4},{12,0},{16,28},{20,24},{24,20},{28,16},{1,13},{... | collective-permute-start | bytes 196616 | tf_op jit(solution)/shard_map/ppermute | solution.py:106
  42.1 1.9 %collective-permute-done.9.refs_3_ = bf16[256,128]{1,0:T(8,128)(2,1)S(1)} collective-permute-done((bf16[256,128]{1,0:T(8,128)(2,1)S(1)}, bf16[256,128]{1,0:T(8,128)(2,1)S(1)}, u32[]{:S(2)}, u32[]{:S(2)}) %collective-permute-start.9) | collective-permute-done | bytes 65568 | tf_op jit(solution)/shard_map/ppermute | solution.py:106
  44.1 1.7 %collective-permute-done.10.refs_4_ = bf16[256,128]{1,0:T(8,128)(2,1)S(1)} collective-permute-done((bf16[256,128]{1,0:T(8,128)(2,1)S(1)}, bf16[256,128]{1,0:T(8,128)(2,1)S(1)}, u32[]{:S(2)}, u32[]{:S(2)}) %collective-permute-start.10) | collective-permute-done | bytes 65568 | tf_op jit(solution)/shard_map/ppermute | solution.py:106
  45.9 1.7 %shard_map.87 = (bf16[256,1024]{1,0:T(8,128)(2,1)S(1)}, f32[256,1024]{1,0:T(8,128)S(1)}, f32[256,1024]{1,0:T(8,128)S(1)}) custom-call(bf16[256,1024]{1,0:T(8,128)(2,1)S(1)} %copy-done.2, bf16[256,1024]{1,0:T(8,128)(2,1)S(1)} %copy-done, bf16[256,1024]{1,0:T(8,128)(2,1)S(1)} %copy-done.1, f32[1,1024]{1,0:T(1,128)S(1)} %bitcast.3, ...), custom_call_target="tpu_custom_call" | custom-call | flops 1073741824 | bytes 2621440 | tf_op jit(solution)/shard_map/pallas_call | solution.py:395
  48.3 0.5 collective-permute-start.15
  49.1 0.4 collective-permute-done.17.arrived_ref
  49.6 1.6 %collective-permute-start.18 = (bf16[256,512]{1,0:T(8,128)(2,1)S(1)}, bf16[256,512]{1,0:T(8,128)(2,1)S(1)}, u32[]{:S(2)}, u32[]{:S(2)}) collective-permute-start(bf16[256,512]{1,0:T(8,128)(2,1)S(1)} %shard_map.94), channel_id=1, source_target_pairs={{0,2},{2,0},{1,3},{3,1},{4,6},{6,4},{5,7},{7,5},{8,10},{10,8},{9,1... | collective-permute-start | bytes 786440 | tf_op jit(solution)/shard_map/ppermute | solution.py:622
  51.2 0.6 collective-permute-start.16
  51.9 1.3 %shard_map.90 = (bf16[256,1024]{1,0:T(8,128)(2,1)S(1)}, f32[256,1024]{1,0:T(8,128)S(1)}) custom-call(bf16[256,1024]{1,0:T(8,128)(2,1)S(1)} %shard_map.89.gated_ref, bf16[1024,4096]{1,0:T(8,128)(2,1)S(1)} %bitcast.2), custom_call_target="tpu_custom_call" | custom-call | flops 1073741824 | bytes 4194304 | tf_op jit(solution)/shard_map/pallas_call | solution.py:498
  53.3 5.6 %collective-permute-done.18.refs_1_ = bf16[256,512]{1,0:T(8,128)(2,1)S(1)} collective-permute-done((bf16[256,512]{1,0:T(8,128)(2,1)S(1)}, bf16[256,512]{1,0:T(8,128)(2,1)S(1)}, u32[]{:S(2)}, u32[]{:S(2)}) %collective-permute-start.18) | collective-permute-done | bytes 262176 | tf_op jit(solution)/shard_map/ppermute | solution.py:622
  58.8 4.8 %collective-permute-done.16.refs_0_ = bf16[256,512]{1,0:T(8,128)(2,1)S(1)} collective-permute-done((bf16[256,512]{1,0:T(8,128)(2,1)S(1)}, bf16[256,512]{1,0:T(8,128)(2,1)S(1)}, u32[]{:S(2)}, u32[]{:S(2)}) %collective-permute-start.16) | collective-permute-done | bytes 262176 | tf_op jit(solution)/shard_map/ppermute | solution.py:622
  63.7 0.9 %shard_map.96 = bf16[256,1024]{1,0:T(8,128)(2,1)} custom-call(f32[256,1024]{1,0:T(8,128)S(1)} %get-tuple-element.61.own_ref, bf16[256,1024]{1,0:T(8,128)(2,1)S(1)} %collective-permute-done.14.near_ref, bf16[256,512]{1,0:T(8,128)(2,1)S(1)} %collective-permute-done.16.refs_0_, bf16[256,512]{1,0:T(8,128)(2,1)S(1)} %collective-permute-done.18.refs_1_, ...), custom_call_target="tpu_custom_call" | custom-call | flops 262144 | bytes 2097152 | tf_op jit(solution)/shard_map/pallas_call | solution.py:565
  (34 shorter events, 1.8 us)
Async XLA Ops:
  1.8 10.5 %collective-permute-start = (bf16[256,256]{1,0:T(8,128)(2,1)S(1)}, bf16[256,256]{1,0:T(8,128)(2,1)S(1)}, u32[]{:S(2)}, u32[]{:S(2)}) collective-permute-start(bf16[256,256]{1,0:T(8,128)(2,1)S(1)} %get-tuple-element.36), channel_id=1, source_target_pairs={{0,16},{4,20},{8,24},{12,28},{16,0},{20,4},{24,8},{28,12},{1,17},{... | collective-permute-start | bytes 393224 | tf_op jit(solution)/shard_map/ppermute | solution.py:106
  5.9 11.4 %collective-permute-start.1 = (bf16[256,256]{1,0:T(8,128)(2,1)S(1)}, bf16[256,256]{1,0:T(8,128)(2,1)S(1)}, u32[]{:S(2)}, u32[]{:S(2)}) collective-permute-start(bf16[256,256]{1,0:T(8,128)(2,1)S(1)} %get-tuple-element.40), channel_id=1, source_target_pairs={{0,4},{4,0},{8,12},{12,8},{16,20},{20,16},{24,28},{28,24},{1,5},{5... | collective-permute-start | bytes 393224 | tf_op jit(solution)/shard_map/ppermute | solution.py:106
  7.4 11.7 %collective-permute-start.2 = (bf16[256,256]{1,0:T(8,128)(2,1)S(1)}, bf16[256,256]{1,0:T(8,128)(2,1)S(1)}, u32[]{:S(2)}, u32[]{:S(2)}) collective-permute-start(bf16[256,256]{1,0:T(8,128)(2,1)S(1)} %get-tuple-element.41), channel_id=1, source_target_pairs={{0,12},{4,8},{8,4},{12,0},{16,28},{20,24},{24,20},{28,16},{1,13},{... | collective-permute-start | bytes 393224 | tf_op jit(solution)/shard_map/ppermute | solution.py:106
  8.9 10.6 %collective-permute-start.3 = (bf16[256,256]{1,0:T(8,128)(2,1)S(1)}, bf16[256,256]{1,0:T(8,128)(2,1)S(1)}, u32[]{:S(2)}, u32[]{:S(2)}) collective-permute-start(bf16[256,256]{1,0:T(8,128)(2,1)S(1)} %get-tuple-element.42), channel_id=1, source_target_pairs={{0,8},{4,12},{8,0},{12,4},{16,24},{20,28},{24,16},{28,20},{1,9},{5... | collective-permute-start | bytes 393224 | tf_op jit(solution)/shard_map/ppermute | solution.py:106
  9.4 10.1 %collective-permute-start.4 = (bf16[256,256]{1,0:T(8,128)(2,1)S(1)}, bf16[256,256]{1,0:T(8,128)(2,1)S(1)}, u32[]{:S(2)}, u32[]{:S(2)}) collective-permute-start(bf16[256,256]{1,0:T(8,128)(2,1)S(1)} %get-tuple-element.43), channel_id=1, source_target_pairs={{0,20},{4,16},{8,28},{12,24},{16,4},{20,0},{24,12},{28,8},{1,21},{... | collective-permute-start | bytes 393224 | tf_op jit(solution)/shard_map/ppermute | solution.py:106
  12.3 9.5 %collective-permute-start.5 = (bf16[256,256]{1,0:T(8,128)(2,1)S(1)}, bf16[256,256]{1,0:T(8,128)(2,1)S(1)}, u32[]{:S(2)}, u32[]{:S(2)}) collective-permute-start(bf16[256,256]{1,0:T(8,128)(2,1)S(1)} %get-tuple-element.46), channel_id=1, source_target_pairs={{0,24},{4,28},{8,16},{12,20},{16,8},{20,12},{24,0},{28,4},{1,25},{... | collective-permute-start | bytes 393224 | tf_op jit(solution)/shard_map/ppermute | solution.py:106
  17.3 8.4 %collective-permute-start.6 = (bf16[256,256]{1,0:T(8,128)(2,1)S(1)}, bf16[256,256]{1,0:T(8,128)(2,1)S(1)}, u32[]{:S(2)}, u32[]{:S(2)}) collective-permute-start(bf16[256,256]{1,0:T(8,128)(2,1)S(1)} %get-tuple-element.49), channel_id=1, source_target_pairs={{0,28},{4,24},{8,20},{12,16},{16,12},{20,8},{24,4},{28,0},{1,29},{... | collective-permute-start | bytes 393224 | tf_op jit(solution)/shard_map/ppermute | solution.py:106
  21.8 24.0 %slice-start = ((s8[8388608]{0:T(1024)(128)(4,1)}), s8[4194304]{0:T(1024)(128)(4,1)S(1)}, s32[]{:S(2)}) async-start(s8[8388608]{0:T(1024)(128)(4,1)} %bitcast.1), calls=%async_computation | async-start | bytes 8388608
  22.5 23.3 %copy-start = (bf16[256,1024]{1,0:T(8,128)(2,1)S(1)}, bf16[256,1024]{1,0:T(8,128)(2,1)}, u32[]{:S(2)}) copy-start(bf16[256,1024]{1,0:T(8,128)(2,1)} %keys_ref.3) | copy-start | bytes 1572868
  22.5 23.3 %copy-start.1 = (bf16[256,1024]{1,0:T(8,128)(2,1)S(1)}, bf16[256,1024]{1,0:T(8,128)(2,1)}, u32[]{:S(2)}) copy-start(bf16[256,1024]{1,0:T(8,128)(2,1)} %values_ref.3) | copy-start | bytes 1572868
  22.5 23.3 %copy-start.2 = (bf16[256,1024]{1,0:T(8,128)(2,1)S(1)}, bf16[256,1024]{1,0:T(8,128)(2,1)}, u32[]{:S(2)}) copy-start(bf16[256,1024]{1,0:T(8,128)(2,1)} %queries_ref.3) | copy-start | bytes 1572868
  22.6 23.3 %copy-start.3 = (f32[1024]{0:T(1024)S(1)}, f32[1024]{0:T(1024)}, u32[]{:S(2)}) copy-start(f32[1024]{0:T(1024)} %param.12) | copy-start | bytes 12292
  25.7 20.2 %slice-start.1 = ((s8[8388608]{0:T(1024)(128)(4,1)}), s8[4194304]{0:T(1024)(128)(4,1)S(1)}, s32[]{:S(2)}) async-start(s8[8388608]{0:T(1024)(128)(4,1)} %bitcast.1), calls=%async_computation.1 | async-start | bytes 8388608
  27.6 12.4 %collective-permute-start.7 = (bf16[256,128]{1,0:T(8,128)(2,1)S(1)}, bf16[256,128]{1,0:T(8,128)(2,1)S(1)}, u32[]{:S(2)}, u32[]{:S(2)}) collective-permute-start(bf16[256,128]{1,0:T(8,128)(2,1)S(1)} %get-tuple-element.51), channel_id=1, source_target_pairs={{0,4},{4,0},{8,12},{12,8},{16,20},{20,16},{24,28},{28,24},{1,5},{5... | collective-permute-start | bytes 196616 | tf_op jit(solution)/shard_map/ppermute | solution.py:106
  32.3 9.1 %collective-permute-start.8 = (bf16[256,128]{1,0:T(8,128)(2,1)S(1)}, bf16[256,128]{1,0:T(8,128)(2,1)S(1)}, u32[]{:S(2)}, u32[]{:S(2)}) collective-permute-start(bf16[256,128]{1,0:T(8,128)(2,1)S(1)} %get-tuple-element.52), channel_id=1, source_target_pairs={{0,24},{4,28},{8,16},{12,20},{16,8},{20,12},{24,0},{28,4},{1,25},{... | collective-permute-start | bytes 196616 | tf_op jit(solution)/shard_map/ppermute | solution.py:106
  34.1 10.0 %collective-permute-start.9 = (bf16[256,128]{1,0:T(8,128)(2,1)S(1)}, bf16[256,128]{1,0:T(8,128)(2,1)S(1)}, u32[]{:S(2)}, u32[]{:S(2)}) collective-permute-start(bf16[256,128]{1,0:T(8,128)(2,1)S(1)} %get-tuple-element.53), channel_id=1, source_target_pairs={{0,16},{4,20},{8,24},{12,28},{16,0},{20,4},{24,8},{28,12},{1,17},{... | collective-permute-start | bytes 196616 | tf_op jit(solution)/shard_map/ppermute | solution.py:106
  36.0 9.8 %collective-permute-start.10 = (bf16[256,128]{1,0:T(8,128)(2,1)S(1)}, bf16[256,128]{1,0:T(8,128)(2,1)S(1)}, u32[]{:S(2)}, u32[]{:S(2)}) collective-permute-start(bf16[256,128]{1,0:T(8,128)(2,1)S(1)} %get-tuple-element.54), channel_id=1, source_target_pairs={{0,20},{4,16},{8,28},{12,24},{16,4},{20,0},{24,12},{28,8},{1,21},{... | collective-permute-start | bytes 196616 | tf_op jit(solution)/shard_map/ppermute | solution.py:106
  36.9 9.0 %collective-permute-start.11 = (bf16[256,128]{1,0:T(8,128)(2,1)S(1)}, bf16[256,128]{1,0:T(8,128)(2,1)S(1)}, u32[]{:S(2)}, u32[]{:S(2)}) collective-permute-start(bf16[256,128]{1,0:T(8,128)(2,1)S(1)} %get-tuple-element.55), channel_id=1, source_target_pairs={{0,8},{4,12},{8,0},{12,4},{16,24},{20,28},{24,16},{28,20},{1,9},{5... | collective-permute-start | bytes 196616 | tf_op jit(solution)/shard_map/ppermute | solution.py:106
  40.0 7.6 %collective-permute-start.12 = (bf16[256,128]{1,0:T(8,128)(2,1)S(1)}, bf16[256,128]{1,0:T(8,128)(2,1)S(1)}, u32[]{:S(2)}, u32[]{:S(2)}) collective-permute-start(bf16[256,128]{1,0:T(8,128)(2,1)S(1)} %get-tuple-element.58), channel_id=1, source_target_pairs={{0,28},{4,24},{8,20},{12,16},{16,12},{20,8},{24,4},{28,0},{1,29},{... | collective-permute-start | bytes 196616 | tf_op jit(solution)/shard_map/ppermute | solution.py:106
  41.3 6.3 %collective-permute-start.13 = (bf16[256,128]{1,0:T(8,128)(2,1)S(1)}, bf16[256,128]{1,0:T(8,128)(2,1)S(1)}, u32[]{:S(2)}, u32[]{:S(2)}) collective-permute-start(bf16[256,128]{1,0:T(8,128)(2,1)S(1)} %get-tuple-element.59), channel_id=1, source_target_pairs={{0,12},{4,8},{8,4},{12,0},{16,28},{20,24},{24,20},{28,16},{1,13},{... | collective-permute-start | bytes 196616 | tf_op jit(solution)/shard_map/ppermute | solution.py:106
  48.0 1.6 %collective-permute-start.17 = (bf16[256,512]{1,0:T(8,128)(2,1)S(1)}, bf16[256,512]{1,0:T(8,128)(2,1)S(1)}, u32[]{:S(2)}, u32[]{:S(2)}) collective-permute-start(bf16[256,512]{1,0:T(8,128)(2,1)S(1)} %get-tuple-element.66), channel_id=1, source_target_pairs={{0,1},{1,0},{2,3},{3,2},{4,5},{5,4},{6,7},{7,6},{8,9},{9,8},{10,11... | collective-permute-start | bytes 786440 | tf_op jit(solution)/shard_map/ppermute | solution.py:621
  48.3 2.9 %collective-permute-start.15 = (bf16[256,512]{1,0:T(8,128)(2,1)S(1)}, bf16[256,512]{1,0:T(8,128)(2,1)S(1)}, u32[]{:S(2)}, u32[]{:S(2)}) collective-permute-start(bf16[256,512]{1,0:T(8,128)(2,1)S(1)} %shard_map.92), channel_id=1, source_target_pairs={{0,1},{1,0},{2,3},{3,2},{4,5},{5,4},{6,7},{7,6},{8,9},{9,8},{10,11... | collective-permute-start | bytes 786440 | tf_op jit(solution)/shard_map/ppermute | solution.py:621
  49.6 9.2 %collective-permute-start.18 = (bf16[256,512]{1,0:T(8,128)(2,1)S(1)}, bf16[256,512]{1,0:T(8,128)(2,1)S(1)}, u32[]{:S(2)}, u32[]{:S(2)}) collective-permute-start(bf16[256,512]{1,0:T(8,128)(2,1)S(1)} %shard_map.94), channel_id=1, source_target_pairs={{0,2},{2,0},{1,3},{3,1},{4,6},{6,4},{5,7},{7,5},{8,10},{10,8},{9,1... | collective-permute-start | bytes 786440 | tf_op jit(solution)/shard_map/ppermute | solution.py:622
  51.2 12.4 %collective-permute-start.16 = (bf16[256,512]{1,0:T(8,128)(2,1)S(1)}, bf16[256,512]{1,0:T(8,128)(2,1)S(1)}, u32[]{:S(2)}, u32[]{:S(2)}) collective-permute-start(bf16[256,512]{1,0:T(8,128)(2,1)S(1)} %shard_map.93), channel_id=1, source_target_pairs={{0,2},{2,0},{1,3},{3,1},{4,6},{6,4},{5,7},{7,5},{8,10},{10,8},{9,1... | collective-permute-start | bytes 786440 | tf_op jit(solution)/shard_map/ppermute | solution.py:622
  53.2 10.5 %collective-permute-start.14 = (bf16[256,1024]{1,0:T(8,128)(2,1)S(1)}, bf16[256,1024]{1,0:T(8,128)(2,1)S(1)}, u32[]{:S(2)}, u32[]{:S(2)}) collective-permute-start(bf16[256,1024]{1,0:T(8,128)(2,1)S(1)} %get-tuple-element.62), channel_id=1, source_target_pairs={{0,1},{1,0},{2,3},{3,2},{4,5},{5,4},{6,7},{7,6},{8,9},{9,8},{10,11... | collective-permute-start | bytes 1572872 | tf_op jit(solution)/shard_map/ppermute | solution.py:625

commit v15 on v14

--- a/solution.py
+++ b/solution.py
@@ -97,7 +97,7 @@
     half = n_peers // 2
     near, far = list(range(1, half)), list(range(half, n_peers))
     if back:
-        return [0, near[0], far[2], far[0], far[1], near[1], far[3]] + near[2:]
+        return [0, near[0], far[2], far[0], near[1], far[1], far[3]] + near[2:]
     return [0, far[0], near[0]] + near[:0:-1] + far[1:]
 
 
@@ -593,12 +593,12 @@
         fwd, bwd = load_tables(fwd, bwd, received[1:2])
         early, part = spectra(received[:-2], fwd, n_peers)
         back = exchange(conv_fast(early, part, received[-2:], fwd, bwd), n_peers, True)
-        slots = slots_of(n_peers, True)[-2:]
+        slots = slots_of(n_peers, True)[-3:]
         gated, send_part, own_part = gate_early(
-            queries, keys, values, skip, out_weight, back[:-2], n_peers
+            queries, keys, values, skip, out_weight, back[:-3], n_peers
         )
         late, last = gate_late(
-            queries, keys, values, skip, out_weight, send_part, back[-2:], slots, sends[-1]
+            queries, keys, values, skip, out_weight, send_part, back[-3:], slots, sends[-1]
         )
         sent = [
             *(late_project(out_weight, late, send_part, slots, [s], BF16)[0] for s in sends[:-1]),

time: 64.7 us -> 64.4 us (level)
    ppermute x14, starting transfers between devices: 28.9 us -> 28.2 us  [exchange(): lax.ppermute(block, 'seq', [(i, i ^ slot) for i in range(n_peers)])]
  transfers between devices with their start and end apart: 19 -> 19, of which waited for: 9 -> 11; matrix products, arithmetic and copies ran while one was open for 0% -> 0% of each run, Pallas kernels for 12% -> 13%
where the time goes in v15:
time: 64.4 us; the launch traced here: 64.2 us
  starting transfers between devices  31.1 us (48%)
  waiting for transfers between devices  19.8 us (31%)
  Pallas kernels  13 us (20%)
    ppermute x14, starting transfers between devices, exchange(): lax.ppermute(block, 'seq', [(i, i ^ slot) for i in range(n_peers)])  28.2 us
    ppermute x2, waiting for transfers between devices, body(): lax.ppermute(add(*pair), 'fsdp', across)  10.4 us
    ppermute x14, waiting for transfers between devices, exchange(): lax.ppermute(block, 'seq', [(i, i ^ slot) for i in range(n_peers)])  9.27 us
    pallas_call x1, Pallas kernels, spectra(): pl.pallas_call(functools.partial(spectra_kernel, n_peers), in_specs=[whol...  2.16 us
    ppermute x2, starting transfers between devices, body(): lax.ppermute(add(*pair), 'fsdp', across)  2.16 us
    pallas_call x1, Pallas kernels, conv_fast(): pl.pallas_call(conv_kernel, in_specs=[whole] * 6, out_specs=[whole] * n_b...  1.93 us
    pallas_call x1, Pallas kernels, pre(): pl.pallas_call(functools.partial(pre_kernel, n_peers), in_specs=[pl.Block...  1.77 us
    pallas_call x1, Pallas kernels, gate_early(): pl.pallas_call(functools.partial(gate_early_kernel, n_peers), in_specs=[w...  1.68 us
  transfers between devices with their start and end apart: 19, of which 11 were waited for; matrix products, arithmetic and copies ran while one was open for 0% of the time, Pallas kernels for 13%

profile of v15, /device:TPU:0, one launch (start us, length us, event | category | flops | bytes accessed | tf_op | source)
XLA Modules:
  0.0 64.2 jit_solution(15272808384528753125)
XLA Ops:
  0.0 1.8 %shard_map.82 = (bf16[256,256]{1,0:T(8,128)(2,1)S(1)}, bf16[256,256]{1,0:T(8,128)(2,1)S(1)}, bf16[256,256]{1,0:T(8,128)(2,1)S(1)}, bf16[256,256]{1,0:T(8,128)(2,...) custom-call(bf16[256,1024]{1,0:T(8,128)(2,1)} %keys_ref.3, ...), custom_call_target="tpu_custom_call" | custom-call | flops 262144 | bytes 3145728 | tf_op jit(solution)/shard_map/pallas_call | solution.py:78
  1.8 4.1 %collective-permute-start = (bf16[256,256]{1,0:T(8,128)(2,1)S(1)}, bf16[256,256]{1,0:T(8,128)(2,1)S(1)}, u32[]{:S(2)}, u32[]{:S(2)}) collective-permute-start(bf16[256,256]{1,0:T(8,128)(2,1)S(1)} %get-tuple-element.36), channel_id=1, source_target_pairs={{0,16},{4,20},{8,24},{12,28},{16,0},{20,4},{24,8},{28,12},{1,17},{... | collective-permute-start | bytes 393224 | tf_op jit(solution)/shard_map/ppermute | solution.py:106
  5.9 1.5 %collective-permute-start.1 = (bf16[256,256]{1,0:T(8,128)(2,1)S(1)}, bf16[256,256]{1,0:T(8,128)(2,1)S(1)}, u32[]{:S(2)}, u32[]{:S(2)}) collective-permute-start(bf16[256,256]{1,0:T(8,128)(2,1)S(1)} %get-tuple-element.40), channel_id=1, source_target_pairs={{0,4},{4,0},{8,12},{12,8},{16,20},{20,16},{24,28},{28,24},{1,5},{5... | collective-permute-start | bytes 393224 | tf_op jit(solution)/shard_map/ppermute | solution.py:106
  7.4 1.5 %collective-permute-start.2 = (bf16[256,256]{1,0:T(8,128)(2,1)S(1)}, bf16[256,256]{1,0:T(8,128)(2,1)S(1)}, u32[]{:S(2)}, u32[]{:S(2)}) collective-permute-start(bf16[256,256]{1,0:T(8,128)(2,1)S(1)} %get-tuple-element.41), channel_id=1, source_target_pairs={{0,12},{4,8},{8,4},{12,0},{16,28},{20,24},{24,20},{28,16},{1,13},{... | collective-permute-start | bytes 393224 | tf_op jit(solution)/shard_map/ppermute | solution.py:106
  8.9 0.4 collective-permute-start.3
  9.4 1.3 %collective-permute-start.4 = (bf16[256,256]{1,0:T(8,128)(2,1)S(1)}, bf16[256,256]{1,0:T(8,128)(2,1)S(1)}, u32[]{:S(2)}, u32[]{:S(2)}) collective-permute-start(bf16[256,256]{1,0:T(8,128)(2,1)S(1)} %get-tuple-element.43), channel_id=1, source_target_pairs={{0,20},{4,16},{8,28},{12,24},{16,4},{20,0},{24,12},{28,8},{1,21},{... | collective-permute-start | bytes 393224 | tf_op jit(solution)/shard_map/ppermute | solution.py:106
  10.7 1.6 %collective-permute-done.refs_0_.refs_1_ = bf16[256,256]{1,0:T(8,128)(2,1)S(1)} collective-permute-done((bf16[256,256]{1,0:T(8,128)(2,1)S(1)}, bf16[256,256]{1,0:T(8,128)(2,1)S(1)}, u32[]{:S(2)}, u32[]{:S(2)}) %collective-permute-start) | collective-permute-done | bytes 131104 | tf_op jit(solution)/shard_map/ppermute | solution.py:106
  12.3 3.6 %collective-permute-start.5 = (bf16[256,256]{1,0:T(8,128)(2,1)S(1)}, bf16[256,256]{1,0:T(8,128)(2,1)S(1)}, u32[]{:S(2)}, u32[]{:S(2)}) collective-permute-start(bf16[256,256]{1,0:T(8,128)(2,1)S(1)} %get-tuple-element.46), channel_id=1, source_target_pairs={{0,24},{4,28},{8,16},{12,20},{16,8},{20,12},{24,0},{28,4},{1,25},{... | collective-permute-start | bytes 393224 | tf_op jit(solution)/shard_map/ppermute | solution.py:106
  15.9 1.3 %shard_map.83 = (bf16[512,512]{1,0:T(8,128)(2,1)S(1)}, bf16[256,1536]{1,0:T(8,128)(2,1)S(1)}) custom-call(bf16[512,512]{1,0:T(8,128)(2,1)} %constant.4.clone.fwd_hbm, bf16[256,1536]{1,0:T(8,128)(2,1)} %constant.5.clone.bwd_hbm, bf16[256,256]{1,0:T(8,128)(2,1)S(1)} %collective-permute-done.refs_0_.refs_1_), custom_call_target="tpu_custom_call" | custom-call | flops 1000000 | bytes 3145728 | tf_op jit(solution)/shard_map/pallas_call | solution.py:166
  17.3 1.9 %collective-permute-start.6 = (bf16[256,256]{1,0:T(8,128)(2,1)S(1)}, bf16[256,256]{1,0:T(8,128)(2,1)S(1)}, u32[]{:S(2)}, u32[]{:S(2)}) collective-permute-start(bf16[256,256]{1,0:T(8,128)(2,1)S(1)} %get-tuple-element.49), channel_id=1, source_target_pairs={{0,28},{4,24},{8,20},{12,16},{16,12},{20,8},{24,4},{28,0},{1,29},{... | collective-permute-start | bytes 393224 | tf_op jit(solution)/shard_map/ppermute | solution.py:106
  19.5 2.2 %shard_map.84 = (f32[8,512,256]{2,1,0:T(8,128)S(1)}, f32[8,512,128]{2,1,0:T(8,128)S(1)}) custom-call(bf16[512,512]{1,0:T(8,128)(2,1)S(1)} %get-tuple-element.37.fwd_ref, bf16[256,256]{1,0:T(8,128)(2,1)S(1)} %get-tuple-element.39.refs_0_, bf16[256,256]{1,0:T(8,128)(2,1)S(1)} %collective-permute-done.refs_0_.refs_1_, ...), custom_call_target="tpu_custom_call" | custom-call | flops 805306368 | bytes 4194304 | tf_op jit(solution)/shard_map/pallas_call | solution.py:191
  21.8 0.7 %shard_map.85 = (f32[512,256]{1,0:T(8,128)S(1)}, f32[8,512,128]{2,1,0:T(8,128)S(1)}) custom-call(bf16[512,512]{1,0:T(8,128)(2,1)S(1)} %get-tuple-element.37.fwd_ref, f32[8,512,256]{2,1,0:T(8,128)S(1)} %get-tuple-element.44.spec_ref, f32[8,512,128]{2,1,0:T(8,128)S(1)} %get-tuple-element.45.part_ref, bf16[256,256]{1,0:T(8,128)(2,1)S(1)} %collective-permute-done.5.in_ref), custom_call_target="tpu_custom_call" | custom-call | flops 1000000000 | bytes 4194304 | tf_op jit(solution)/shard_map/pallas_call | solution.py:250
  22.6 3.1 %collective-permute-done.6.in_ref = bf16[256,256]{1,0:T(8,128)(2,1)S(1)} collective-permute-done((bf16[256,256]{1,0:T(8,128)(2,1)S(1)}, bf16[256,256]{1,0:T(8,128)(2,1)S(1)}, u32[]{:S(2)}, u32[]{:S(2)}) %collective-permute-start.6) | collective-permute-done | bytes 131104 | tf_op jit(solution)/shard_map/ppermute | solution.py:106
  25.7 1.9 %shard_map.86 = (bf16[256,128]{1,0:T(8,128)(2,1)S(1)}, bf16[256,128]{1,0:T(8,128)(2,1)S(1)}, bf16[256,128]{1,0:T(8,128)(2,1)S(1)}, bf16[256,128]{1,0:T(8,128)(2,...) custom-call(bf16[512,512]{1,0:T(8,128)(2,1)S(1)} %get-tuple-element., ...), custom_call_target="tpu_custom_call" | custom-call | flops 1073741824 | bytes 4194304 | tf_op jit(solution)/shard_map/pallas_call | solution.py:314
  27.6 4.6 %collective-permute-start.7 = (bf16[256,128]{1,0:T(8,128)(2,1)S(1)}, bf16[256,128]{1,0:T(8,128)(2,1)S(1)}, u32[]{:S(2)}, u32[]{:S(2)}) collective-permute-start(bf16[256,128]{1,0:T(8,128)(2,1)S(1)} %get-tuple-element.51), channel_id=1, source_target_pairs={{0,4},{4,0},{8,12},{12,8},{16,20},{20,16},{24,28},{28,24},{1,5},{5... | collective-permute-start | bytes 196616 | tf_op jit(solution)/shard_map/ppermute | solution.py:106
  32.3 1.9 %collective-permute-start.8 = (bf16[256,128]{1,0:T(8,128)(2,1)S(1)}, bf16[256,128]{1,0:T(8,128)(2,1)S(1)}, u32[]{:S(2)}, u32[]{:S(2)}) collective-permute-start(bf16[256,128]{1,0:T(8,128)(2,1)S(1)} %get-tuple-element.52), channel_id=1, source_target_pairs={{0,24},{4,28},{8,16},{12,20},{16,8},{20,12},{24,0},{28,4},{1,25},{... | collective-permute-start | bytes 196616 | tf_op jit(solution)/shard_map/ppermute | solution.py:106
  34.1 1.9 %collective-permute-start.9 = (bf16[256,128]{1,0:T(8,128)(2,1)S(1)}, bf16[256,128]{1,0:T(8,128)(2,1)S(1)}, u32[]{:S(2)}, u32[]{:S(2)}) collective-permute-start(bf16[256,128]{1,0:T(8,128)(2,1)S(1)} %get-tuple-element.53), channel_id=1, source_target_pairs={{0,16},{4,20},{8,24},{12,28},{16,0},{20,4},{24,8},{28,12},{1,17},{... | collective-permute-start | bytes 196616 | tf_op jit(solution)/shard_map/ppermute | solution.py:106
  36.0 0.6 collective-permute-start.10
  36.6 3.4 %collective-permute-start.11 = (bf16[256,128]{1,0:T(8,128)(2,1)S(1)}, bf16[256,128]{1,0:T(8,128)(2,1)S(1)}, u32[]{:S(2)}, u32[]{:S(2)}) collective-permute-start(bf16[256,128]{1,0:T(8,128)(2,1)S(1)} %get-tuple-element.57), channel_id=1, source_target_pairs={{0,20},{4,16},{8,28},{12,24},{16,4},{20,0},{24,12},{28,8},{1,21},{... | collective-permute-start | bytes 196616 | tf_op jit(solution)/shard_map/ppermute | solution.py:106
  40.0 1.3 %collective-permute-start.12 = (bf16[256,128]{1,0:T(8,128)(2,1)S(1)}, bf16[256,128]{1,0:T(8,128)(2,1)S(1)}, u32[]{:S(2)}, u32[]{:S(2)}) collective-permute-start(bf16[256,128]{1,0:T(8,128)(2,1)S(1)} %get-tuple-element.58), channel_id=1, source_target_pairs={{0,28},{4,24},{8,20},{12,16},{16,12},{20,8},{24,4},{28,0},{1,29},{... | collective-permute-start | bytes 196616 | tf_op jit(solution)/shard_map/ppermute | solution.py:106
  41.5 0.9 %collective-permute-done.9.refs_3_ = bf16[256,128]{1,0:T(8,128)(2,1)S(1)} collective-permute-done((bf16[256,128]{1,0:T(8,128)(2,1)S(1)}, bf16[256,128]{1,0:T(8,128)(2,1)S(1)}, u32[]{:S(2)}, u32[]{:S(2)}) %collective-permute-start.9) | collective-permute-done | bytes 65568 | tf_op jit(solution)/shard_map/ppermute | solution.py:106
  42.4 1.7 %shard_map.87 = (bf16[256,1024]{1,0:T(8,128)(2,1)S(1)}, f32[256,1024]{1,0:T(8,128)S(1)}, f32[256,1024]{1,0:T(8,128)S(1)}) custom-call(bf16[256,1024]{1,0:T(8,128)(2,1)S(1)} %copy-done.2, bf16[256,1024]{1,0:T(8,128)(2,1)S(1)} %copy-done, bf16[256,1024]{1,0:T(8,128)(2,1)S(1)} %copy-done.1, f32[1,1024]{1,0:T(1,128)S(1)} %bitcast.3, ...), custom_call_target="tpu_custom_call" | custom-call | flops 1073741824 | bytes 2621440 | tf_op jit(solution)/shard_map/pallas_call | solution.py:395
  44.1 1.7 %collective-permute-done.11.refs_0_ = bf16[256,128]{1,0:T(8,128)(2,1)S(1)} collective-permute-done((bf16[256,128]{1,0:T(8,128)(2,1)S(1)}, bf16[256,128]{1,0:T(8,128)(2,1)S(1)}, u32[]{:S(2)}, u32[]{:S(2)}) %collective-permute-start.11) | collective-permute-done | bytes 65568 | tf_op jit(solution)/shard_map/ppermute | solution.py:106
  45.8 1.3 %collective-permute-done.12.refs_1_ = bf16[256,128]{1,0:T(8,128)(2,1)S(1)} collective-permute-done((bf16[256,128]{1,0:T(8,128)(2,1)S(1)}, bf16[256,128]{1,0:T(8,128)(2,1)S(1)}, u32[]{:S(2)}, u32[]{:S(2)}) %collective-permute-start.12) | collective-permute-done | bytes 65568 | tf_op jit(solution)/shard_map/ppermute | solution.py:106
  48.0 0.6 collective-permute-start.15
  48.6 0.4 shard_map.91
  49.3 1.6 %collective-permute-start.18 = (bf16[256,512]{1,0:T(8,128)(2,1)S(1)}, bf16[256,512]{1,0:T(8,128)(2,1)S(1)}, u32[]{:S(2)}, u32[]{:S(2)}) collective-permute-start(bf16[256,512]{1,0:T(8,128)(2,1)S(1)} %shard_map.94), channel_id=1, source_target_pairs={{0,2},{2,0},{1,3},{3,1},{4,6},{6,4},{5,7},{7,5},{8,10},{10,8},{9,1... | collective-permute-start | bytes 786440 | tf_op jit(solution)/shard_map/ppermute | solution.py:622
  50.9 0.6 collective-permute-start.16
  51.6 1.3 %shard_map.90 = (bf16[256,1024]{1,0:T(8,128)(2,1)S(1)}, f32[256,1024]{1,0:T(8,128)S(1)}) custom-call(bf16[256,1024]{1,0:T(8,128)(2,1)S(1)} %shard_map.89.gated_ref, bf16[1024,4096]{1,0:T(8,128)(2,1)S(1)} %bitcast.2), custom_call_target="tpu_custom_call" | custom-call | flops 1073741824 | bytes 4194304 | tf_op jit(solution)/shard_map/pallas_call | solution.py:498
  53.0 5.5 %collective-permute-done.18.refs_1_ = bf16[256,512]{1,0:T(8,128)(2,1)S(1)} collective-permute-done((bf16[256,512]{1,0:T(8,128)(2,1)S(1)}, bf16[256,512]{1,0:T(8,128)(2,1)S(1)}, u32[]{:S(2)}, u32[]{:S(2)}) %collective-permute-start.18) | collective-permute-done | bytes 262176 | tf_op jit(solution)/shard_map/ppermute | solution.py:622
  58.5 4.8 %collective-permute-done.16.refs_0_ = bf16[256,512]{1,0:T(8,128)(2,1)S(1)} collective-permute-done((bf16[256,512]{1,0:T(8,128)(2,1)S(1)}, bf16[256,512]{1,0:T(8,128)(2,1)S(1)}, u32[]{:S(2)}, u32[]{:S(2)}) %collective-permute-start.16) | collective-permute-done | bytes 262176 | tf_op jit(solution)/shard_map/ppermute | solution.py:622
  63.3 0.9 %shard_map.96 = bf16[256,1024]{1,0:T(8,128)(2,1)} custom-call(f32[256,1024]{1,0:T(8,128)S(1)} %get-tuple-element.61.own_ref, bf16[256,1024]{1,0:T(8,128)(2,1)S(1)} %collective-permute-done.14.near_ref, bf16[256,512]{1,0:T(8,128)(2,1)S(1)} %collective-permute-done.16.refs_0_, bf16[256,512]{1,0:T(8,128)(2,1)S(1)} %collective-permute-done.18.refs_1_, ...), custom_call_target="tpu_custom_call" | custom-call | flops 262144 | bytes 2097152 | tf_op jit(solution)/shard_map/pallas_call | solution.py:565
  (34 shorter events, 2.1 us)
Async XLA Ops:
  1.8 10.5 %collective-permute-start = (bf16[256,256]{1,0:T(8,128)(2,1)S(1)}, bf16[256,256]{1,0:T(8,128)(2,1)S(1)}, u32[]{:S(2)}, u32[]{:S(2)}) collective-permute-start(bf16[256,256]{1,0:T(8,128)(2,1)S(1)} %get-tuple-element.36), channel_id=1, source_target_pairs={{0,16},{4,20},{8,24},{12,28},{16,0},{20,4},{24,8},{28,12},{1,17},{... | collective-permute-start | bytes 393224 | tf_op jit(solution)/shard_map/ppermute | solution.py:106
  5.9 11.4 %collective-permute-start.1 = (bf16[256,256]{1,0:T(8,128)(2,1)S(1)}, bf16[256,256]{1,0:T(8,128)(2,1)S(1)}, u32[]{:S(2)}, u32[]{:S(2)}) collective-permute-start(bf16[256,256]{1,0:T(8,128)(2,1)S(1)} %get-tuple-element.40), channel_id=1, source_target_pairs={{0,4},{4,0},{8,12},{12,8},{16,20},{20,16},{24,28},{28,24},{1,5},{5... | collective-permute-start | bytes 393224 | tf_op jit(solution)/shard_map/ppermute | solution.py:106
  7.4 11.7 %collective-permute-start.2 = (bf16[256,256]{1,0:T(8,128)(2,1)S(1)}, bf16[256,256]{1,0:T(8,128)(2,1)S(1)}, u32[]{:S(2)}, u32[]{:S(2)}) collective-permute-start(bf16[256,256]{1,0:T(8,128)(2,1)S(1)} %get-tuple-element.41), channel_id=1, source_target_pairs={{0,12},{4,8},{8,4},{12,0},{16,28},{20,24},{24,20},{28,16},{1,13},{... | collective-permute-start | bytes 393224 | tf_op jit(solution)/shard_map/ppermute | solution.py:106
  8.9 10.6 %collective-permute-start.3 = (bf16[256,256]{1,0:T(8,128)(2,1)S(1)}, bf16[256,256]{1,0:T(8,128)(2,1)S(1)}, u32[]{:S(2)}, u32[]{:S(2)}) collective-permute-start(bf16[256,256]{1,0:T(8,128)(2,1)S(1)} %get-tuple-element.42), channel_id=1, source_target_pairs={{0,8},{4,12},{8,0},{12,4},{16,24},{20,28},{24,16},{28,20},{1,9},{5... | collective-permute-start | bytes 393224 | tf_op jit(solution)/shard_map/ppermute | solution.py:106
  9.4 10.1 %collective-permute-start.4 = (bf16[256,256]{1,0:T(8,128)(2,1)S(1)}, bf16[256,256]{1,0:T(8,128)(2,1)S(1)}, u32[]{:S(2)}, u32[]{:S(2)}) collective-permute-start(bf16[256,256]{1,0:T(8,128)(2,1)S(1)} %get-tuple-element.43), channel_id=1, source_target_pairs={{0,20},{4,16},{8,28},{12,24},{16,4},{20,0},{24,12},{28,8},{1,21},{... | collective-permute-start | bytes 393224 | tf_op jit(solution)/shard_map/ppermute | solution.py:106
  12.3 9.5 %collective-permute-start.5 = (bf16[256,256]{1,0:T(8,128)(2,1)S(1)}, bf16[256,256]{1,0:T(8,128)(2,1)S(1)}, u32[]{:S(2)}, u32[]{:S(2)}) collective-permute-start(bf16[256,256]{1,0:T(8,128)(2,1)S(1)} %get-tuple-element.46), channel_id=1, source_target_pairs={{0,24},{4,28},{8,16},{12,20},{16,8},{20,12},{24,0},{28,4},{1,25},{... | collective-permute-start | bytes 393224 | tf_op jit(solution)/shard_map/ppermute | solution.py:106
  17.3 8.4 %collective-permute-start.6 = (bf16[256,256]{1,0:T(8,128)(2,1)S(1)}, bf16[256,256]{1,0:T(8,128)(2,1)S(1)}, u32[]{:S(2)}, u32[]{:S(2)}) collective-permute-start(bf16[256,256]{1,0:T(8,128)(2,1)S(1)} %get-tuple-element.49), channel_id=1, source_target_pairs={{0,28},{4,24},{8,20},{12,16},{16,12},{20,8},{24,4},{28,0},{1,29},{... | collective-permute-start | bytes 393224 | tf_op jit(solution)/shard_map/ppermute | solution.py:106
  21.8 20.5 %slice-start = ((s8[8388608]{0:T(1024)(128)(4,1)}), s8[4194304]{0:T(1024)(128)(4,1)S(1)}, s32[]{:S(2)}) async-start(s8[8388608]{0:T(1024)(128)(4,1)} %bitcast.1), calls=%async_computation | async-start | bytes 8388608
  22.5 19.8 %copy-start = (bf16[256,1024]{1,0:T(8,128)(2,1)S(1)}, bf16[256,1024]{1,0:T(8,128)(2,1)}, u32[]{:S(2)}) copy-start(bf16[256,1024]{1,0:T(8,128)(2,1)} %keys_ref.3) | copy-start | bytes 1572868
  22.5 19.8 %copy-start.1 = (bf16[256,1024]{1,0:T(8,128)(2,1)S(1)}, bf16[256,1024]{1,0:T(8,128)(2,1)}, u32[]{:S(2)}) copy-start(bf16[256,1024]{1,0:T(8,128)(2,1)} %values_ref.3) | copy-start | bytes 1572868
  22.5 19.8 %copy-start.2 = (bf16[256,1024]{1,0:T(8,128)(2,1)S(1)}, bf16[256,1024]{1,0:T(8,128)(2,1)}, u32[]{:S(2)}) copy-start(bf16[256,1024]{1,0:T(8,128)(2,1)} %queries_ref.3) | copy-start | bytes 1572868
  22.6 19.8 %copy-start.3 = (f32[1024]{0:T(1024)S(1)}, f32[1024]{0:T(1024)}, u32[]{:S(2)}) copy-start(f32[1024]{0:T(1024)} %param.12) | copy-start | bytes 12292
  25.7 16.7 %slice-start.1 = ((s8[8388608]{0:T(1024)(128)(4,1)}), s8[4194304]{0:T(1024)(128)(4,1)S(1)}, s32[]{:S(2)}) async-start(s8[8388608]{0:T(1024)(128)(4,1)} %bitcast.1), calls=%async_computation.1 | async-start | bytes 8388608
  27.6 12.4 %collective-permute-start.7 = (bf16[256,128]{1,0:T(8,128)(2,1)S(1)}, bf16[256,128]{1,0:T(8,128)(2,1)S(1)}, u32[]{:S(2)}, u32[]{:S(2)}) collective-permute-start(bf16[256,128]{1,0:T(8,128)(2,1)S(1)} %get-tuple-element.51), channel_id=1, source_target_pairs={{0,4},{4,0},{8,12},{12,8},{16,20},{20,16},{24,28},{28,24},{1,5},{5... | collective-permute-start | bytes 196616 | tf_op jit(solution)/shard_map/ppermute | solution.py:106
  32.3 9.1 %collective-permute-start.8 = (bf16[256,128]{1,0:T(8,128)(2,1)S(1)}, bf16[256,128]{1,0:T(8,128)(2,1)S(1)}, u32[]{:S(2)}, u32[]{:S(2)}) collective-permute-start(bf16[256,128]{1,0:T(8,128)(2,1)S(1)} %get-tuple-element.52), channel_id=1, source_target_pairs={{0,24},{4,28},{8,16},{12,20},{16,8},{20,12},{24,0},{28,4},{1,25},{... | collective-permute-start | bytes 196616 | tf_op jit(solution)/shard_map/ppermute | solution.py:106
  34.1 8.2 %collective-permute-start.9 = (bf16[256,128]{1,0:T(8,128)(2,1)S(1)}, bf16[256,128]{1,0:T(8,128)(2,1)S(1)}, u32[]{:S(2)}, u32[]{:S(2)}) collective-permute-start(bf16[256,128]{1,0:T(8,128)(2,1)S(1)} %get-tuple-element.53), channel_id=1, source_target_pairs={{0,16},{4,20},{8,24},{12,28},{16,0},{20,4},{24,8},{28,12},{1,17},{... | collective-permute-start | bytes 196616 | tf_op jit(solution)/shard_map/ppermute | solution.py:106
  36.0 6.3 %collective-permute-start.10 = (bf16[256,128]{1,0:T(8,128)(2,1)S(1)}, bf16[256,128]{1,0:T(8,128)(2,1)S(1)}, u32[]{:S(2)}, u32[]{:S(2)}) collective-permute-start(bf16[256,128]{1,0:T(8,128)(2,1)S(1)} %get-tuple-element.54), channel_id=1, source_target_pairs={{0,8},{4,12},{8,0},{12,4},{16,24},{20,28},{24,16},{28,20},{1,9},{5... | collective-permute-start | bytes 196616 | tf_op jit(solution)/shard_map/ppermute | solution.py:106
  36.6 9.1 %collective-permute-start.11 = (bf16[256,128]{1,0:T(8,128)(2,1)S(1)}, bf16[256,128]{1,0:T(8,128)(2,1)S(1)}, u32[]{:S(2)}, u32[]{:S(2)}) collective-permute-start(bf16[256,128]{1,0:T(8,128)(2,1)S(1)} %get-tuple-element.57), channel_id=1, source_target_pairs={{0,20},{4,16},{8,28},{12,24},{16,4},{20,0},{24,12},{28,8},{1,21},{... | collective-permute-start | bytes 196616 | tf_op jit(solution)/shard_map/ppermute | solution.py:106
  40.0 7.1 %collective-permute-start.12 = (bf16[256,128]{1,0:T(8,128)(2,1)S(1)}, bf16[256,128]{1,0:T(8,128)(2,1)S(1)}, u32[]{:S(2)}, u32[]{:S(2)}) collective-permute-start(bf16[256,128]{1,0:T(8,128)(2,1)S(1)} %get-tuple-element.58), channel_id=1, source_target_pairs={{0,28},{4,24},{8,20},{12,16},{16,12},{20,8},{24,4},{28,0},{1,29},{... | collective-permute-start | bytes 196616 | tf_op jit(solution)/shard_map/ppermute | solution.py:106
  41.3 5.9 %collective-permute-start.13 = (bf16[256,128]{1,0:T(8,128)(2,1)S(1)}, bf16[256,128]{1,0:T(8,128)(2,1)S(1)}, u32[]{:S(2)}, u32[]{:S(2)}) collective-permute-start(bf16[256,128]{1,0:T(8,128)(2,1)S(1)} %get-tuple-element.59), channel_id=1, source_target_pairs={{0,12},{4,8},{8,4},{12,0},{16,28},{20,24},{24,20},{28,16},{1,13},{... | collective-permute-start | bytes 196616 | tf_op jit(solution)/shard_map/ppermute | solution.py:106
  47.6 1.6 %collective-permute-start.17 = (bf16[256,512]{1,0:T(8,128)(2,1)S(1)}, bf16[256,512]{1,0:T(8,128)(2,1)S(1)}, u32[]{:S(2)}, u32[]{:S(2)}) collective-permute-start(bf16[256,512]{1,0:T(8,128)(2,1)S(1)} %get-tuple-element.66), channel_id=1, source_target_pairs={{0,1},{1,0},{2,3},{3,2},{4,5},{5,4},{6,7},{7,6},{8,9},{9,8},{10,11... | collective-permute-start | bytes 786440 | tf_op jit(solution)/shard_map/ppermute | solution.py:621
  48.0 2.8 %collective-permute-start.15 = (bf16[256,512]{1,0:T(8,128)(2,1)S(1)}, bf16[256,512]{1,0:T(8,128)(2,1)S(1)}, u32[]{:S(2)}, u32[]{:S(2)}) collective-permute-start(bf16[256,512]{1,0:T(8,128)(2,1)S(1)} %shard_map.92), channel_id=1, source_target_pairs={{0,1},{1,0},{2,3},{3,2},{4,5},{5,4},{6,7},{7,6},{8,9},{9,8},{10,11... | collective-permute-start | bytes 786440 | tf_op jit(solution)/shard_map/ppermute | solution.py:621
  49.3 9.2 %collective-permute-start.18 = (bf16[256,512]{1,0:T(8,128)(2,1)S(1)}, bf16[256,512]{1,0:T(8,128)(2,1)S(1)}, u32[]{:S(2)}, u32[]{:S(2)}) collective-permute-start(bf16[256,512]{1,0:T(8,128)(2,1)S(1)} %shard_map.94), channel_id=1, source_target_pairs={{0,2},{2,0},{1,3},{3,1},{4,6},{6,4},{5,7},{7,5},{8,10},{10,8},{9,1... | collective-permute-start | bytes 786440 | tf_op jit(solution)/shard_map/ppermute | solution.py:622
  50.9 12.4 %collective-permute-start.16 = (bf16[256,512]{1,0:T(8,128)(2,1)S(1)}, bf16[256,512]{1,0:T(8,128)(2,1)S(1)}, u32[]{:S(2)}, u32[]{:S(2)}) collective-permute-start(bf16[256,512]{1,0:T(8,128)(2,1)S(1)} %shard_map.93), channel_id=1, source_target_pairs={{0,2},{2,0},{1,3},{3,1},{4,6},{6,4},{5,7},{7,5},{8,10},{10,8},{9,1... | collective-permute-start | bytes 786440 | tf_op jit(solution)/shard_map/ppermute | solution.py:622
  52.9 10.4 %collective-permute-start.14 = (bf16[256,1024]{1,0:T(8,128)(2,1)S(1)}, bf16[256,1024]{1,0:T(8,128)(2,1)S(1)}, u32[]{:S(2)}, u32[]{:S(2)}) collective-permute-start(bf16[256,1024]{1,0:T(8,128)(2,1)S(1)} %get-tuple-element.62), channel_id=1, source_target_pairs={{0,1},{1,0},{2,3},{3,2},{4,5},{5,4},{6,7},{7,6},{8,9},{9,8},{10,11... | collective-permute-start | bytes 1572872 | tf_op jit(solution)/shard_map/ppermute | solution.py:625

commit v16 on v15

--- a/solution.py
+++ b/solution.py
@@ -98,7 +98,7 @@
     near, far = list(range(1, half)), list(range(half, n_peers))
     if back:
         return [0, near[0], far[2], far[0], near[1], far[1], far[3]] + near[2:]
-    return [0, far[0], near[0]] + near[:0:-1] + far[1:]
+    return [0, far[0], near[0]] + near[:0:-1] + [far[1], far[3], far[2]]
 
 
 def exchange(blocks, n_peers, back):

time: 64.4 us -> 64 us (level)
  transfers between devices with their start and end apart: 19 -> 19, of which waited for: 11 -> 10; matrix products, arithmetic and copies ran while one was open for 0% -> 0% of each run, Pallas kernels for 13% -> 13%
where the time goes in v16:
time: 64 us; the launch traced here: 63.8 us
  starting transfers between devices  31.1 us (49%)
  waiting for transfers between devices  19.4 us (30%)
  Pallas kernels  13.1 us (20%)
    ppermute x14, starting transfers between devices, exchange(): lax.ppermute(block, 'seq', [(i, i ^ slot) for i in range(n_peers)])  28.2 us
    ppermute x2, waiting for transfers between devices, body(): lax.ppermute(add(*pair), 'fsdp', across)  10.4 us
    ppermute x14, waiting for transfers between devices, exchange(): lax.ppermute(block, 'seq', [(i, i ^ slot) for i in range(n_peers)])  8.84 us
    pallas_call x1, Pallas kernels, spectra(): pl.pallas_call(functools.partial(spectra_kernel, n_peers), in_specs=[whol...  2.16 us
    ppermute x2, starting transfers between devices, body(): lax.ppermute(add(*pair), 'fsdp', across)  2.16 us
    pallas_call x1, Pallas kernels, conv_fast(): pl.pallas_call(conv_kernel, in_specs=[whole] * 6, out_specs=[whole] * n_b...  2.03 us
    pallas_call x1, Pallas kernels, pre(): pl.pallas_call(functools.partial(pre_kernel, n_peers), in_specs=[pl.Block...  1.77 us
    pallas_call x1, Pallas kernels, gate_early(): pl.pallas_call(functools.partial(gate_early_kernel, n_peers), in_specs=[w...  1.68 us
  transfers between devices with their start and end apart: 19, of which 10 were waited for; matrix products, arithmetic and copies ran while one was open for 0% of the time, Pallas kernels for 13%

profile of v16, /device:TPU:0, one launch (start us, length us, event | category | flops | bytes accessed | tf_op | source)
XLA Modules:
  0.0 63.8 jit_solution(13761954112825391508)
XLA Ops:
  0.0 1.8 %shard_map.82 = (bf16[256,256]{1,0:T(8,128)(2,1)S(1)}, bf16[256,256]{1,0:T(8,128)(2,1)S(1)}, bf16[256,256]{1,0:T(8,128)(2,1)S(1)}, bf16[256,256]{1,0:T(8,128)(2,...) custom-call(bf16[256,1024]{1,0:T(8,128)(2,1)} %keys_ref.3, ...), custom_call_target="tpu_custom_call" | custom-call | flops 262144 | bytes 3145728 | tf_op jit(solution)/shard_map/pallas_call | solution.py:78
  1.8 4.1 %collective-permute-start = (bf16[256,256]{1,0:T(8,128)(2,1)S(1)}, bf16[256,256]{1,0:T(8,128)(2,1)S(1)}, u32[]{:S(2)}, u32[]{:S(2)}) collective-permute-start(bf16[256,256]{1,0:T(8,128)(2,1)S(1)} %get-tuple-element.36), channel_id=1, source_target_pairs={{0,16},{4,20},{8,24},{12,28},{16,0},{20,4},{24,8},{28,12},{1,17},{... | collective-permute-start | bytes 393224 | tf_op jit(solution)/shard_map/ppermute | solution.py:106
  5.9 1.5 %collective-permute-start.1 = (bf16[256,256]{1,0:T(8,128)(2,1)S(1)}, bf16[256,256]{1,0:T(8,128)(2,1)S(1)}, u32[]{:S(2)}, u32[]{:S(2)}) collective-permute-start(bf16[256,256]{1,0:T(8,128)(2,1)S(1)} %get-tuple-element.40), channel_id=1, source_target_pairs={{0,4},{4,0},{8,12},{12,8},{16,20},{20,16},{24,28},{28,24},{1,5},{5... | collective-permute-start | bytes 393224 | tf_op jit(solution)/shard_map/ppermute | solution.py:106
  7.4 1.5 %collective-permute-start.2 = (bf16[256,256]{1,0:T(8,128)(2,1)S(1)}, bf16[256,256]{1,0:T(8,128)(2,1)S(1)}, u32[]{:S(2)}, u32[]{:S(2)}) collective-permute-start(bf16[256,256]{1,0:T(8,128)(2,1)S(1)} %get-tuple-element.41), channel_id=1, source_target_pairs={{0,12},{4,8},{8,4},{12,0},{16,28},{20,24},{24,20},{28,16},{1,13},{... | collective-permute-start | bytes 393224 | tf_op jit(solution)/shard_map/ppermute | solution.py:106
  8.9 0.4 collective-permute-start.3
  9.4 1.3 %collective-permute-start.4 = (bf16[256,256]{1,0:T(8,128)(2,1)S(1)}, bf16[256,256]{1,0:T(8,128)(2,1)S(1)}, u32[]{:S(2)}, u32[]{:S(2)}) collective-permute-start(bf16[256,256]{1,0:T(8,128)(2,1)S(1)} %get-tuple-element.43), channel_id=1, source_target_pairs={{0,20},{4,16},{8,28},{12,24},{16,4},{20,0},{24,12},{28,8},{1,21},{... | collective-permute-start | bytes 393224 | tf_op jit(solution)/shard_map/ppermute | solution.py:106
  10.7 1.6 %collective-permute-done.refs_0_.refs_1_ = bf16[256,256]{1,0:T(8,128)(2,1)S(1)} collective-permute-done((bf16[256,256]{1,0:T(8,128)(2,1)S(1)}, bf16[256,256]{1,0:T(8,128)(2,1)S(1)}, u32[]{:S(2)}, u32[]{:S(2)}) %collective-permute-start) | collective-permute-done | bytes 131104 | tf_op jit(solution)/shard_map/ppermute | solution.py:106
  12.3 4.6 %collective-permute-start.5 = (bf16[256,256]{1,0:T(8,128)(2,1)S(1)}, bf16[256,256]{1,0:T(8,128)(2,1)S(1)}, u32[]{:S(2)}, u32[]{:S(2)}) collective-permute-start(bf16[256,256]{1,0:T(8,128)(2,1)S(1)} %get-tuple-element.46), channel_id=1, source_target_pairs={{0,28},{4,24},{8,20},{12,16},{16,12},{20,8},{24,4},{28,0},{1,29},{... | collective-permute-start | bytes 393224 | tf_op jit(solution)/shard_map/ppermute | solution.py:106
  16.9 1.3 %shard_map.83 = (bf16[512,512]{1,0:T(8,128)(2,1)S(1)}, bf16[256,1536]{1,0:T(8,128)(2,1)S(1)}) custom-call(bf16[512,512]{1,0:T(8,128)(2,1)} %constant.4.clone.fwd_hbm, bf16[256,1536]{1,0:T(8,128)(2,1)} %constant.5.clone.bwd_hbm, bf16[256,256]{1,0:T(8,128)(2,1)S(1)} %collective-permute-done.refs_0_.refs_1_), custom_call_target="tpu_custom_call" | custom-call | flops 1000000 | bytes 3145728 | tf_op jit(solution)/shard_map/pallas_call | solution.py:166
  18.2 0.9 %collective-permute-start.6 = (bf16[256,256]{1,0:T(8,128)(2,1)S(1)}, bf16[256,256]{1,0:T(8,128)(2,1)S(1)}, u32[]{:S(2)}, u32[]{:S(2)}) collective-permute-start(bf16[256,256]{1,0:T(8,128)(2,1)S(1)} %get-tuple-element.49), channel_id=1, source_target_pairs={{0,24},{4,28},{8,16},{12,20},{16,8},{20,12},{24,0},{28,4},{1,25},{... | collective-permute-start | bytes 393224 | tf_op jit(solution)/shard_map/ppermute | solution.py:106
  19.1 0.8 %collective-permute-done.3.refs_4_ = bf16[256,256]{1,0:T(8,128)(2,1)S(1)} collective-permute-done((bf16[256,256]{1,0:T(8,128)(2,1)S(1)}, bf16[256,256]{1,0:T(8,128)(2,1)S(1)}, u32[]{:S(2)}, u32[]{:S(2)}) %collective-permute-start.3) | collective-permute-done | bytes 131104 | tf_op jit(solution)/shard_map/ppermute | solution.py:106
  20.0 2.2 %shard_map.84 = (f32[8,512,256]{2,1,0:T(8,128)S(1)}, f32[8,512,128]{2,1,0:T(8,128)S(1)}) custom-call(bf16[512,512]{1,0:T(8,128)(2,1)S(1)} %get-tuple-element.37.fwd_ref, bf16[256,256]{1,0:T(8,128)(2,1)S(1)} %get-tuple-element.39.refs_0_, bf16[256,256]{1,0:T(8,128)(2,1)S(1)} %collective-permute-done.refs_0_.refs_1_, ...), custom_call_target="tpu_custom_call" | custom-call | flops 805306368 | bytes 4194304 | tf_op jit(solution)/shard_map/pallas_call | solution.py:191
  22.1 1.2 %collective-permute-done.5.in_ref = bf16[256,256]{1,0:T(8,128)(2,1)S(1)} collective-permute-done((bf16[256,256]{1,0:T(8,128)(2,1)S(1)}, bf16[256,256]{1,0:T(8,128)(2,1)S(1)}, u32[]{:S(2)}, u32[]{:S(2)}) %collective-permute-start.5) | collective-permute-done | bytes 131104 | tf_op jit(solution)/shard_map/ppermute | solution.py:106
  23.3 0.6 shard_map.85
  24.0 1.0 %collective-permute-done.6.in_ref = bf16[256,256]{1,0:T(8,128)(2,1)S(1)} collective-permute-done((bf16[256,256]{1,0:T(8,128)(2,1)S(1)}, bf16[256,256]{1,0:T(8,128)(2,1)S(1)}, u32[]{:S(2)}, u32[]{:S(2)}) %collective-permute-start.6) | collective-permute-done | bytes 131104 | tf_op jit(solution)/shard_map/ppermute | solution.py:106
  25.1 2.0 %shard_map.86 = (bf16[256,128]{1,0:T(8,128)(2,1)S(1)}, bf16[256,128]{1,0:T(8,128)(2,1)S(1)}, bf16[256,128]{1,0:T(8,128)(2,1)S(1)}, bf16[256,128]{1,0:T(8,128)(2,...) custom-call(bf16[512,512]{1,0:T(8,128)(2,1)S(1)} %get-tuple-element., ...), custom_call_target="tpu_custom_call" | custom-call | flops 1073741824 | bytes 4194304 | tf_op jit(solution)/shard_map/pallas_call | solution.py:314
  27.1 4.6 %collective-permute-start.7 = (bf16[256,128]{1,0:T(8,128)(2,1)S(1)}, bf16[256,128]{1,0:T(8,128)(2,1)S(1)}, u32[]{:S(2)}, u32[]{:S(2)}) collective-permute-start(bf16[256,128]{1,0:T(8,128)(2,1)S(1)} %get-tuple-element.51), channel_id=1, source_target_pairs={{0,4},{4,0},{8,12},{12,8},{16,20},{20,16},{24,28},{28,24},{1,5},{5... | collective-permute-start | bytes 196616 | tf_op jit(solution)/shard_map/ppermute | solution.py:106
  31.7 2.3 %collective-permute-start.8 = (bf16[256,128]{1,0:T(8,128)(2,1)S(1)}, bf16[256,128]{1,0:T(8,128)(2,1)S(1)}, u32[]{:S(2)}, u32[]{:S(2)}) collective-permute-start(bf16[256,128]{1,0:T(8,128)(2,1)S(1)} %get-tuple-element.52), channel_id=1, source_target_pairs={{0,24},{4,28},{8,16},{12,20},{16,8},{20,12},{24,0},{28,4},{1,25},{... | collective-permute-start | bytes 196616 | tf_op jit(solution)/shard_map/ppermute | solution.py:106
  34.1 1.6 %collective-permute-start.9 = (bf16[256,128]{1,0:T(8,128)(2,1)S(1)}, bf16[256,128]{1,0:T(8,128)(2,1)S(1)}, u32[]{:S(2)}, u32[]{:S(2)}) collective-permute-start(bf16[256,128]{1,0:T(8,128)(2,1)S(1)} %get-tuple-element.53), channel_id=1, source_target_pairs={{0,16},{4,20},{8,24},{12,28},{16,0},{20,4},{24,8},{28,12},{1,17},{... | collective-permute-start | bytes 196616 | tf_op jit(solution)/shard_map/ppermute | solution.py:106
  35.6 0.6 collective-permute-start.10
  36.2 3.0 %collective-permute-start.11 = (bf16[256,128]{1,0:T(8,128)(2,1)S(1)}, bf16[256,128]{1,0:T(8,128)(2,1)S(1)}, u32[]{:S(2)}, u32[]{:S(2)}) collective-permute-start(bf16[256,128]{1,0:T(8,128)(2,1)S(1)} %get-tuple-element.57), channel_id=1, source_target_pairs={{0,20},{4,16},{8,28},{12,24},{16,4},{20,0},{24,12},{28,8},{1,21},{... | collective-permute-start | bytes 196616 | tf_op jit(solution)/shard_map/ppermute | solution.py:106
  39.2 1.7 %collective-permute-start.12 = (bf16[256,128]{1,0:T(8,128)(2,1)S(1)}, bf16[256,128]{1,0:T(8,128)(2,1)S(1)}, u32[]{:S(2)}, u32[]{:S(2)}) collective-permute-start(bf16[256,128]{1,0:T(8,128)(2,1)S(1)} %get-tuple-element.58), channel_id=1, source_target_pairs={{0,28},{4,24},{8,20},{12,16},{16,12},{20,8},{24,4},{28,0},{1,29},{... | collective-permute-start | bytes 196616 | tf_op jit(solution)/shard_map/ppermute | solution.py:106
  40.9 3.2 %collective-permute-done.9.refs_3_ = bf16[256,128]{1,0:T(8,128)(2,1)S(1)} collective-permute-done((bf16[256,128]{1,0:T(8,128)(2,1)S(1)}, bf16[256,128]{1,0:T(8,128)(2,1)S(1)}, u32[]{:S(2)}, u32[]{:S(2)}) %collective-permute-start.9) | collective-permute-done | bytes 65568 | tf_op jit(solution)/shard_map/ppermute | solution.py:106
  44.2 1.7 %shard_map.87 = (bf16[256,1024]{1,0:T(8,128)(2,1)S(1)}, f32[256,1024]{1,0:T(8,128)S(1)}, f32[256,1024]{1,0:T(8,128)S(1)}) custom-call(bf16[256,1024]{1,0:T(8,128)(2,1)S(1)} %copy-done.2, bf16[256,1024]{1,0:T(8,128)(2,1)S(1)} %copy-done, bf16[256,1024]{1,0:T(8,128)(2,1)S(1)} %copy-done.1, f32[1,1024]{1,0:T(1,128)S(1)} %bitcast.3, ...), custom_call_target="tpu_custom_call" | custom-call | flops 1073741824 | bytes 2621440 | tf_op jit(solution)/shard_map/pallas_call | solution.py:395
  46.3 0.5 collective-permute-done.13.refs_2_
  47.6 0.6 collective-permute-start.15
  48.9 1.6 %collective-permute-start.18 = (bf16[256,512]{1,0:T(8,128)(2,1)S(1)}, bf16[256,512]{1,0:T(8,128)(2,1)S(1)}, u32[]{:S(2)}, u32[]{:S(2)}) collective-permute-start(bf16[256,512]{1,0:T(8,128)(2,1)S(1)} %shard_map.94), channel_id=1, source_target_pairs={{0,2},{2,0},{1,3},{3,1},{4,6},{6,4},{5,7},{7,5},{8,10},{10,8},{9,1... | collective-permute-start | bytes 786440 | tf_op jit(solution)/shard_map/ppermute | solution.py:622
  50.5 0.6 collective-permute-start.16
  51.2 1.3 %shard_map.90 = (bf16[256,1024]{1,0:T(8,128)(2,1)S(1)}, f32[256,1024]{1,0:T(8,128)S(1)}) custom-call(bf16[256,1024]{1,0:T(8,128)(2,1)S(1)} %shard_map.89.gated_ref, bf16[1024,4096]{1,0:T(8,128)(2,1)S(1)} %bitcast.2), custom_call_target="tpu_custom_call" | custom-call | flops 1073741824 | bytes 4194304 | tf_op jit(solution)/shard_map/pallas_call | solution.py:498
  52.6 5.5 %collective-permute-done.18.refs_1_ = bf16[256,512]{1,0:T(8,128)(2,1)S(1)} collective-permute-done((bf16[256,512]{1,0:T(8,128)(2,1)S(1)}, bf16[256,512]{1,0:T(8,128)(2,1)S(1)}, u32[]{:S(2)}, u32[]{:S(2)}) %collective-permute-start.18) | collective-permute-done | bytes 262176 | tf_op jit(solution)/shard_map/ppermute | solution.py:622
  58.1 4.8 %collective-permute-done.16.refs_0_ = bf16[256,512]{1,0:T(8,128)(2,1)S(1)} collective-permute-done((bf16[256,512]{1,0:T(8,128)(2,1)S(1)}, bf16[256,512]{1,0:T(8,128)(2,1)S(1)}, u32[]{:S(2)}, u32[]{:S(2)}) %collective-permute-start.16) | collective-permute-done | bytes 262176 | tf_op jit(solution)/shard_map/ppermute | solution.py:622
  62.9 0.9 %shard_map.96 = bf16[256,1024]{1,0:T(8,128)(2,1)} custom-call(f32[256,1024]{1,0:T(8,128)S(1)} %get-tuple-element.61.own_ref, bf16[256,1024]{1,0:T(8,128)(2,1)S(1)} %collective-permute-done.14.near_ref, bf16[256,512]{1,0:T(8,128)(2,1)S(1)} %collective-permute-done.16.refs_0_, bf16[256,512]{1,0:T(8,128)(2,1)S(1)} %collective-permute-done.18.refs_1_, ...), custom_call_target="tpu_custom_call" | custom-call | flops 262144 | bytes 2097152 | tf_op jit(solution)/shard_map/pallas_call | solution.py:565
  (34 shorter events, 2.1 us)
Async XLA Ops:
  1.8 10.5 %collective-permute-start = (bf16[256,256]{1,0:T(8,128)(2,1)S(1)}, bf16[256,256]{1,0:T(8,128)(2,1)S(1)}, u32[]{:S(2)}, u32[]{:S(2)}) collective-permute-start(bf16[256,256]{1,0:T(8,128)(2,1)S(1)} %get-tuple-element.36), channel_id=1, source_target_pairs={{0,16},{4,20},{8,24},{12,28},{16,0},{20,4},{24,8},{28,12},{1,17},{... | collective-permute-start | bytes 393224 | tf_op jit(solution)/shard_map/ppermute | solution.py:106
  5.9 12.3 %collective-permute-start.1 = (bf16[256,256]{1,0:T(8,128)(2,1)S(1)}, bf16[256,256]{1,0:T(8,128)(2,1)S(1)}, u32[]{:S(2)}, u32[]{:S(2)}) collective-permute-start(bf16[256,256]{1,0:T(8,128)(2,1)S(1)} %get-tuple-element.40), channel_id=1, source_target_pairs={{0,4},{4,0},{8,12},{12,8},{16,20},{20,16},{24,28},{28,24},{1,5},{5... | collective-permute-start | bytes 393224 | tf_op jit(solution)/shard_map/ppermute | solution.py:106
  7.4 11.7 %collective-permute-start.2 = (bf16[256,256]{1,0:T(8,128)(2,1)S(1)}, bf16[256,256]{1,0:T(8,128)(2,1)S(1)}, u32[]{:S(2)}, u32[]{:S(2)}) collective-permute-start(bf16[256,256]{1,0:T(8,128)(2,1)S(1)} %get-tuple-element.41), channel_id=1, source_target_pairs={{0,12},{4,8},{8,4},{12,0},{16,28},{20,24},{24,20},{28,16},{1,13},{... | collective-permute-start | bytes 393224 | tf_op jit(solution)/shard_map/ppermute | solution.py:106
  8.9 11.1 %collective-permute-start.3 = (bf16[256,256]{1,0:T(8,128)(2,1)S(1)}, bf16[256,256]{1,0:T(8,128)(2,1)S(1)}, u32[]{:S(2)}, u32[]{:S(2)}) collective-permute-start(bf16[256,256]{1,0:T(8,128)(2,1)S(1)} %get-tuple-element.42), channel_id=1, source_target_pairs={{0,8},{4,12},{8,0},{12,4},{16,24},{20,28},{24,16},{28,20},{1,9},{5... | collective-permute-start | bytes 393224 | tf_op jit(solution)/shard_map/ppermute | solution.py:106
  9.4 10.6 %collective-permute-start.4 = (bf16[256,256]{1,0:T(8,128)(2,1)S(1)}, bf16[256,256]{1,0:T(8,128)(2,1)S(1)}, u32[]{:S(2)}, u32[]{:S(2)}) collective-permute-start(bf16[256,256]{1,0:T(8,128)(2,1)S(1)} %get-tuple-element.43), channel_id=1, source_target_pairs={{0,20},{4,16},{8,28},{12,24},{16,4},{20,0},{24,12},{28,8},{1,21},{... | collective-permute-start | bytes 393224 | tf_op jit(solution)/shard_map/ppermute | solution.py:106
  12.3 11.1 %collective-permute-start.5 = (bf16[256,256]{1,0:T(8,128)(2,1)S(1)}, bf16[256,256]{1,0:T(8,128)(2,1)S(1)}, u32[]{:S(2)}, u32[]{:S(2)}) collective-permute-start(bf16[256,256]{1,0:T(8,128)(2,1)S(1)} %get-tuple-element.46), channel_id=1, source_target_pairs={{0,28},{4,24},{8,20},{12,16},{16,12},{20,8},{24,4},{28,0},{1,29},{... | collective-permute-start | bytes 393224 | tf_op jit(solution)/shard_map/ppermute | solution.py:106
  18.2 6.9 %collective-permute-start.6 = (bf16[256,256]{1,0:T(8,128)(2,1)S(1)}, bf16[256,256]{1,0:T(8,128)(2,1)S(1)}, u32[]{:S(2)}, u32[]{:S(2)}) collective-permute-start(bf16[256,256]{1,0:T(8,128)(2,1)S(1)} %get-tuple-element.49), channel_id=1, source_target_pairs={{0,24},{4,28},{8,16},{12,20},{16,8},{20,12},{24,0},{28,4},{1,25},{... | collective-permute-start | bytes 393224 | tf_op jit(solution)/shard_map/ppermute | solution.py:106
  23.3 20.8 %slice-start = ((s8[8388608]{0:T(1024)(128)(4,1)}), s8[4194304]{0:T(1024)(128)(4,1)S(1)}, s32[]{:S(2)}) async-start(s8[8388608]{0:T(1024)(128)(4,1)} %bitcast.1), calls=%async_computation | async-start | bytes 8388608
  24.0 20.2 %copy-start = (bf16[256,1024]{1,0:T(8,128)(2,1)S(1)}, bf16[256,1024]{1,0:T(8,128)(2,1)}, u32[]{:S(2)}) copy-start(bf16[256,1024]{1,0:T(8,128)(2,1)} %keys_ref.3) | copy-start | bytes 1572868
  24.0 20.2 %copy-start.1 = (bf16[256,1024]{1,0:T(8,128)(2,1)S(1)}, bf16[256,1024]{1,0:T(8,128)(2,1)}, u32[]{:S(2)}) copy-start(bf16[256,1024]{1,0:T(8,128)(2,1)} %values_ref.3) | copy-start | bytes 1572868
  24.0 20.2 %copy-start.2 = (bf16[256,1024]{1,0:T(8,128)(2,1)S(1)}, bf16[256,1024]{1,0:T(8,128)(2,1)}, u32[]{:S(2)}) copy-start(bf16[256,1024]{1,0:T(8,128)(2,1)} %queries_ref.3) | copy-start | bytes 1572868
  24.0 20.2 %copy-start.3 = (f32[1024]{0:T(1024)S(1)}, f32[1024]{0:T(1024)}, u32[]{:S(2)}) copy-start(f32[1024]{0:T(1024)} %param.12) | copy-start | bytes 12292
  25.1 19.1 %slice-start.1 = ((s8[8388608]{0:T(1024)(128)(4,1)}), s8[4194304]{0:T(1024)(128)(4,1)S(1)}, s32[]{:S(2)}) async-start(s8[8388608]{0:T(1024)(128)(4,1)} %bitcast.1), calls=%async_computation.1 | async-start | bytes 8388608
  27.1 12.1 %collective-permute-start.7 = (bf16[256,128]{1,0:T(8,128)(2,1)S(1)}, bf16[256,128]{1,0:T(8,128)(2,1)S(1)}, u32[]{:S(2)}, u32[]{:S(2)}) collective-permute-start(bf16[256,128]{1,0:T(8,128)(2,1)S(1)} %get-tuple-element.51), channel_id=1, source_target_pairs={{0,4},{4,0},{8,12},{12,8},{16,20},{20,16},{24,28},{28,24},{1,5},{5... | collective-permute-start | bytes 196616 | tf_op jit(solution)/shard_map/ppermute | solution.py:106
  31.7 9.2 %collective-permute-start.8 = (bf16[256,128]{1,0:T(8,128)(2,1)S(1)}, bf16[256,128]{1,0:T(8,128)(2,1)S(1)}, u32[]{:S(2)}, u32[]{:S(2)}) collective-permute-start(bf16[256,128]{1,0:T(8,128)(2,1)S(1)} %get-tuple-element.52), channel_id=1, source_target_pairs={{0,24},{4,28},{8,16},{12,20},{16,8},{20,12},{24,0},{28,4},{1,25},{... | collective-permute-start | bytes 196616 | tf_op jit(solution)/shard_map/ppermute | solution.py:106
  34.1 10.1 %collective-permute-start.9 = (bf16[256,128]{1,0:T(8,128)(2,1)S(1)}, bf16[256,128]{1,0:T(8,128)(2,1)S(1)}, u32[]{:S(2)}, u32[]{:S(2)}) collective-permute-start(bf16[256,128]{1,0:T(8,128)(2,1)S(1)} %get-tuple-element.53), channel_id=1, source_target_pairs={{0,16},{4,20},{8,24},{12,28},{16,0},{20,4},{24,8},{28,12},{1,17},{... | collective-permute-start | bytes 196616 | tf_op jit(solution)/shard_map/ppermute | solution.py:106
  35.6 8.5 %collective-permute-start.10 = (bf16[256,128]{1,0:T(8,128)(2,1)S(1)}, bf16[256,128]{1,0:T(8,128)(2,1)S(1)}, u32[]{:S(2)}, u32[]{:S(2)}) collective-permute-start(bf16[256,128]{1,0:T(8,128)(2,1)S(1)} %get-tuple-element.54), channel_id=1, source_target_pairs={{0,8},{4,12},{8,0},{12,4},{16,24},{20,28},{24,16},{28,20},{1,9},{5... | collective-permute-start | bytes 196616 | tf_op jit(solution)/shard_map/ppermute | solution.py:106
  36.2 9.7 %collective-permute-start.11 = (bf16[256,128]{1,0:T(8,128)(2,1)S(1)}, bf16[256,128]{1,0:T(8,128)(2,1)S(1)}, u32[]{:S(2)}, u32[]{:S(2)}) collective-permute-start(bf16[256,128]{1,0:T(8,128)(2,1)S(1)} %get-tuple-element.57), channel_id=1, source_target_pairs={{0,20},{4,16},{8,28},{12,24},{16,4},{20,0},{24,12},{28,8},{1,21},{... | collective-permute-start | bytes 196616 | tf_op jit(solution)/shard_map/ppermute | solution.py:106
  39.2 7.1 %collective-permute-start.12 = (bf16[256,128]{1,0:T(8,128)(2,1)S(1)}, bf16[256,128]{1,0:T(8,128)(2,1)S(1)}, u32[]{:S(2)}, u32[]{:S(2)}) collective-permute-start(bf16[256,128]{1,0:T(8,128)(2,1)S(1)} %get-tuple-element.58), channel_id=1, source_target_pairs={{0,28},{4,24},{8,20},{12,16},{16,12},{20,8},{24,4},{28,0},{1,29},{... | collective-permute-start | bytes 196616 | tf_op jit(solution)/shard_map/ppermute | solution.py:106
  40.9 5.9 %collective-permute-start.13 = (bf16[256,128]{1,0:T(8,128)(2,1)S(1)}, bf16[256,128]{1,0:T(8,128)(2,1)S(1)}, u32[]{:S(2)}, u32[]{:S(2)}) collective-permute-start(bf16[256,128]{1,0:T(8,128)(2,1)S(1)} %get-tuple-element.59), channel_id=1, source_target_pairs={{0,12},{4,8},{8,4},{12,0},{16,28},{20,24},{24,20},{28,16},{1,13},{... | collective-permute-start | bytes 196616 | tf_op jit(solution)/shard_map/ppermute | solution.py:106
  47.2 1.6 %collective-permute-start.17 = (bf16[256,512]{1,0:T(8,128)(2,1)S(1)}, bf16[256,512]{1,0:T(8,128)(2,1)S(1)}, u32[]{:S(2)}, u32[]{:S(2)}) collective-permute-start(bf16[256,512]{1,0:T(8,128)(2,1)S(1)} %get-tuple-element.66), channel_id=1, source_target_pairs={{0,1},{1,0},{2,3},{3,2},{4,5},{5,4},{6,7},{7,6},{8,9},{9,8},{10,11... | collective-permute-start | bytes 786440 | tf_op jit(solution)/shard_map/ppermute | solution.py:621
  47.6 2.8 %collective-permute-start.15 = (bf16[256,512]{1,0:T(8,128)(2,1)S(1)}, bf16[256,512]{1,0:T(8,128)(2,1)S(1)}, u32[]{:S(2)}, u32[]{:S(2)}) collective-permute-start(bf16[256,512]{1,0:T(8,128)(2,1)S(1)} %shard_map.92), channel_id=1, source_target_pairs={{0,1},{1,0},{2,3},{3,2},{4,5},{5,4},{6,7},{7,6},{8,9},{9,8},{10,11... | collective-permute-start | bytes 786440 | tf_op jit(solution)/shard_map/ppermute | solution.py:621
  48.9 9.2 %collective-permute-start.18 = (bf16[256,512]{1,0:T(8,128)(2,1)S(1)}, bf16[256,512]{1,0:T(8,128)(2,1)S(1)}, u32[]{:S(2)}, u32[]{:S(2)}) collective-permute-start(bf16[256,512]{1,0:T(8,128)(2,1)S(1)} %shard_map.94), channel_id=1, source_target_pairs={{0,2},{2,0},{1,3},{3,1},{4,6},{6,4},{5,7},{7,5},{8,10},{10,8},{9,1... | collective-permute-start | bytes 786440 | tf_op jit(solution)/shard_map/ppermute | solution.py:622
  50.5 12.4 %collective-permute-start.16 = (bf16[256,512]{1,0:T(8,128)(2,1)S(1)}, bf16[256,512]{1,0:T(8,128)(2,1)S(1)}, u32[]{:S(2)}, u32[]{:S(2)}) collective-permute-start(bf16[256,512]{1,0:T(8,128)(2,1)S(1)} %shard_map.93), channel_id=1, source_target_pairs={{0,2},{2,0},{1,3},{3,1},{4,6},{6,4},{5,7},{7,5},{8,10},{10,8},{9,1... | collective-permute-start | bytes 786440 | tf_op jit(solution)/shard_map/ppermute | solution.py:622
  52.5 10.4 %collective-permute-start.14 = (bf16[256,1024]{1,0:T(8,128)(2,1)S(1)}, bf16[256,1024]{1,0:T(8,128)(2,1)S(1)}, u32[]{:S(2)}, u32[]{:S(2)}) collective-permute-start(bf16[256,1024]{1,0:T(8,128)(2,1)S(1)} %get-tuple-element.62), channel_id=1, source_target_pairs={{0,1},{1,0},{2,3},{3,2},{4,5},{5,4},{6,7},{7,6},{8,9},{9,8},{10,11... | collective-permute-start | bytes 1572872 | tf_op jit(solution)/shard_map/ppermute | solution.py:625

commit v17 on v16

--- a/solution.py
+++ b/solution.py
@@ -97,7 +97,7 @@
     half = n_peers // 2
     near, far = list(range(1, half)), list(range(half, n_peers))
     if back:
-        return [0, near[0], far[2], far[0], near[1], far[1], far[3]] + near[2:]
+        return [0, near[0], far[3], far[0], near[1], far[1], far[2]] + near[2:]
     return [0, far[0], near[0]] + near[:0:-1] + [far[1], far[3], far[2]]
 
 

time: 64 us -> 63.5 us (level)
  waiting for transfers between devices: 19.4 us -> 18.7 us
    ppermute x14, waiting for transfers between devices: 8.84 us -> 8.1 us  [exchange(): lax.ppermute(block, 'seq', [(i, i ^ slot) for i in range(n_peers)])]
  transfers between devices with their start and end apart: 19 -> 19, of which waited for: 10 -> 11; matrix products, arithmetic and copies ran while one was open for 0% -> 0% of each run, Pallas kernels for 13% -> 13%
where the time goes in v17:
time: 63.5 us; the launch traced here: 63.3 us
  starting transfers between devices  31.3 us (49%)
  waiting for transfers between devices  18.7 us (29%)
  Pallas kernels  13.1 us (21%)
    ppermute x14, starting transfers between devices, exchange(): lax.ppermute(block, 'seq', [(i, i ^ slot) for i in range(n_peers)])  28.5 us
    ppermute x2, waiting for transfers between devices, body(): lax.ppermute(add(*pair), 'fsdp', across)  10.4 us
    ppermute x14, waiting for transfers between devices, exchange(): lax.ppermute(block, 'seq', [(i, i ^ slot) for i in range(n_peers)])  8.1 us
    pallas_call x1, Pallas kernels, spectra(): pl.pallas_call(functools.partial(spectra_kernel, n_peers), in_specs=[whol...  2.16 us
    ppermute x2, starting transfers between devices, body(): lax.ppermute(add(*pair), 'fsdp', across)  2.16 us
    pallas_call x1, Pallas kernels, conv_fast(): pl.pallas_call(conv_kernel, in_specs=[whole] * 6, out_specs=[whole] * n_b...  2.03 us
    pallas_call x1, Pallas kernels, pre(): pl.pallas_call(functools.partial(pre_kernel, n_peers), in_specs=[pl.Block...  1.77 us
    pallas_call x1, Pallas kernels, gate_early(): pl.pallas_call(functools.partial(gate_early_kernel, n_peers), in_specs=[w...  1.68 us
  transfers between devices with their start and end apart: 19, of which 11 were waited for; matrix products, arithmetic and copies ran while one was open for 0% of the time, Pallas kernels for 13%

profile of v17, /device:TPU:0, one launch (start us, length us, event | category | flops | bytes accessed | tf_op | source)
XLA Modules:
  0.0 63.3 jit_solution(9361890970073901595)
XLA Ops:
  0.0 1.8 %shard_map.82 = (bf16[256,256]{1,0:T(8,128)(2,1)S(1)}, bf16[256,256]{1,0:T(8,128)(2,1)S(1)}, bf16[256,256]{1,0:T(8,128)(2,1)S(1)}, bf16[256,256]{1,0:T(8,128)(2,...) custom-call(bf16[256,1024]{1,0:T(8,128)(2,1)} %keys_ref.3, ...), custom_call_target="tpu_custom_call" | custom-call | flops 262144 | bytes 3145728 | tf_op jit(solution)/shard_map/pallas_call | solution.py:78
  1.8 4.1 %collective-permute-start = (bf16[256,256]{1,0:T(8,128)(2,1)S(1)}, bf16[256,256]{1,0:T(8,128)(2,1)S(1)}, u32[]{:S(2)}, u32[]{:S(2)}) collective-permute-start(bf16[256,256]{1,0:T(8,128)(2,1)S(1)} %get-tuple-element.36), channel_id=1, source_target_pairs={{0,16},{4,20},{8,24},{12,28},{16,0},{20,4},{24,8},{28,12},{1,17},{... | collective-permute-start | bytes 393224 | tf_op jit(solution)/shard_map/ppermute | solution.py:106
  5.9 1.5 %collective-permute-start.1 = (bf16[256,256]{1,0:T(8,128)(2,1)S(1)}, bf16[256,256]{1,0:T(8,128)(2,1)S(1)}, u32[]{:S(2)}, u32[]{:S(2)}) collective-permute-start(bf16[256,256]{1,0:T(8,128)(2,1)S(1)} %get-tuple-element.40), channel_id=1, source_target_pairs={{0,4},{4,0},{8,12},{12,8},{16,20},{20,16},{24,28},{28,24},{1,5},{5... | collective-permute-start | bytes 393224 | tf_op jit(solution)/shard_map/ppermute | solution.py:106
  7.4 1.5 %collective-permute-start.2 = (bf16[256,256]{1,0:T(8,128)(2,1)S(1)}, bf16[256,256]{1,0:T(8,128)(2,1)S(1)}, u32[]{:S(2)}, u32[]{:S(2)}) collective-permute-start(bf16[256,256]{1,0:T(8,128)(2,1)S(1)} %get-tuple-element.41), channel_id=1, source_target_pairs={{0,12},{4,8},{8,4},{12,0},{16,28},{20,24},{24,20},{28,16},{1,13},{... | collective-permute-start | bytes 393224 | tf_op jit(solution)/shard_map/ppermute | solution.py:106
  8.9 0.4 collective-permute-start.3
  9.4 1.3 %collective-permute-start.4 = (bf16[256,256]{1,0:T(8,128)(2,1)S(1)}, bf16[256,256]{1,0:T(8,128)(2,1)S(1)}, u32[]{:S(2)}, u32[]{:S(2)}) collective-permute-start(bf16[256,256]{1,0:T(8,128)(2,1)S(1)} %get-tuple-element.43), channel_id=1, source_target_pairs={{0,20},{4,16},{8,28},{12,24},{16,4},{20,0},{24,12},{28,8},{1,21},{... | collective-permute-start | bytes 393224 | tf_op jit(solution)/shard_map/ppermute | solution.py:106
  10.7 1.6 %collective-permute-done.refs_0_.refs_1_ = bf16[256,256]{1,0:T(8,128)(2,1)S(1)} collective-permute-done((bf16[256,256]{1,0:T(8,128)(2,1)S(1)}, bf16[256,256]{1,0:T(8,128)(2,1)S(1)}, u32[]{:S(2)}, u32[]{:S(2)}) %collective-permute-start) | collective-permute-done | bytes 131104 | tf_op jit(solution)/shard_map/ppermute | solution.py:106
  12.3 4.6 %collective-permute-start.5 = (bf16[256,256]{1,0:T(8,128)(2,1)S(1)}, bf16[256,256]{1,0:T(8,128)(2,1)S(1)}, u32[]{:S(2)}, u32[]{:S(2)}) collective-permute-start(bf16[256,256]{1,0:T(8,128)(2,1)S(1)} %get-tuple-element.46), channel_id=1, source_target_pairs={{0,28},{4,24},{8,20},{12,16},{16,12},{20,8},{24,4},{28,0},{1,29},{... | collective-permute-start | bytes 393224 | tf_op jit(solution)/shard_map/ppermute | solution.py:106
  16.9 1.3 %shard_map.83 = (bf16[512,512]{1,0:T(8,128)(2,1)S(1)}, bf16[256,1536]{1,0:T(8,128)(2,1)S(1)}) custom-call(bf16[512,512]{1,0:T(8,128)(2,1)} %constant.4.clone.fwd_hbm, bf16[256,1536]{1,0:T(8,128)(2,1)} %constant.5.clone.bwd_hbm, bf16[256,256]{1,0:T(8,128)(2,1)S(1)} %collective-permute-done.refs_0_.refs_1_), custom_call_target="tpu_custom_call" | custom-call | flops 1000000 | bytes 3145728 | tf_op jit(solution)/shard_map/pallas_call | solution.py:166
  18.2 0.9 %collective-permute-start.6 = (bf16[256,256]{1,0:T(8,128)(2,1)S(1)}, bf16[256,256]{1,0:T(8,128)(2,1)S(1)}, u32[]{:S(2)}, u32[]{:S(2)}) collective-permute-start(bf16[256,256]{1,0:T(8,128)(2,1)S(1)} %get-tuple-element.49), channel_id=1, source_target_pairs={{0,24},{4,28},{8,16},{12,20},{16,8},{20,12},{24,0},{28,4},{1,25},{... | collective-permute-start | bytes 393224 | tf_op jit(solution)/shard_map/ppermute | solution.py:106
  19.1 0.8 %collective-permute-done.3.refs_4_ = bf16[256,256]{1,0:T(8,128)(2,1)S(1)} collective-permute-done((bf16[256,256]{1,0:T(8,128)(2,1)S(1)}, bf16[256,256]{1,0:T(8,128)(2,1)S(1)}, u32[]{:S(2)}, u32[]{:S(2)}) %collective-permute-start.3) | collective-permute-done | bytes 131104 | tf_op jit(solution)/shard_map/ppermute | solution.py:106
  20.0 2.2 %shard_map.84 = (f32[8,512,256]{2,1,0:T(8,128)S(1)}, f32[8,512,128]{2,1,0:T(8,128)S(1)}) custom-call(bf16[512,512]{1,0:T(8,128)(2,1)S(1)} %get-tuple-element.37.fwd_ref, bf16[256,256]{1,0:T(8,128)(2,1)S(1)} %get-tuple-element.39.refs_0_, bf16[256,256]{1,0:T(8,128)(2,1)S(1)} %collective-permute-done.refs_0_.refs_1_, ...), custom_call_target="tpu_custom_call" | custom-call | flops 805306368 | bytes 4194304 | tf_op jit(solution)/shard_map/pallas_call | solution.py:191
  22.1 1.2 %collective-permute-done.5.in_ref = bf16[256,256]{1,0:T(8,128)(2,1)S(1)} collective-permute-done((bf16[256,256]{1,0:T(8,128)(2,1)S(1)}, bf16[256,256]{1,0:T(8,128)(2,1)S(1)}, u32[]{:S(2)}, u32[]{:S(2)}) %collective-permute-start.5) | collective-permute-done | bytes 131104 | tf_op jit(solution)/shard_map/ppermute | solution.py:106
  23.3 0.6 shard_map.85
  24.0 1.0 %collective-permute-done.6.in_ref = bf16[256,256]{1,0:T(8,128)(2,1)S(1)} collective-permute-done((bf16[256,256]{1,0:T(8,128)(2,1)S(1)}, bf16[256,256]{1,0:T(8,128)(2,1)S(1)}, u32[]{:S(2)}, u32[]{:S(2)}) %collective-permute-start.6) | collective-permute-done | bytes 131104 | tf_op jit(solution)/shard_map/ppermute | solution.py:106
  25.1 2.0 %shard_map.86 = (bf16[256,128]{1,0:T(8,128)(2,1)S(1)}, bf16[256,128]{1,0:T(8,128)(2,1)S(1)}, bf16[256,128]{1,0:T(8,128)(2,1)S(1)}, bf16[256,128]{1,0:T(8,128)(2,...) custom-call(bf16[512,512]{1,0:T(8,128)(2,1)S(1)} %get-tuple-element., ...), custom_call_target="tpu_custom_call" | custom-call | flops 1073741824 | bytes 4194304 | tf_op jit(solution)/shard_map/pallas_call | solution.py:314
  27.1 4.6 %collective-permute-start.7 = (bf16[256,128]{1,0:T(8,128)(2,1)S(1)}, bf16[256,128]{1,0:T(8,128)(2,1)S(1)}, u32[]{:S(2)}, u32[]{:S(2)}) collective-permute-start(bf16[256,128]{1,0:T(8,128)(2,1)S(1)} %get-tuple-element.51), channel_id=1, source_target_pairs={{0,4},{4,0},{8,12},{12,8},{16,20},{20,16},{24,28},{28,24},{1,5},{5... | collective-permute-start | bytes 196616 | tf_op jit(solution)/shard_map/ppermute | solution.py:106
  31.7 2.2 %collective-permute-start.8 = (bf16[256,128]{1,0:T(8,128)(2,1)S(1)}, bf16[256,128]{1,0:T(8,128)(2,1)S(1)}, u32[]{:S(2)}, u32[]{:S(2)}) collective-permute-start(bf16[256,128]{1,0:T(8,128)(2,1)S(1)} %get-tuple-element.52), channel_id=1, source_target_pairs={{0,28},{4,24},{8,20},{12,16},{16,12},{20,8},{24,4},{28,0},{1,29},{... | collective-permute-start | bytes 196616 | tf_op jit(solution)/shard_map/ppermute | solution.py:106
  34.0 2.1 %collective-permute-start.9 = (bf16[256,128]{1,0:T(8,128)(2,1)S(1)}, bf16[256,128]{1,0:T(8,128)(2,1)S(1)}, u32[]{:S(2)}, u32[]{:S(2)}) collective-permute-start(bf16[256,128]{1,0:T(8,128)(2,1)S(1)} %get-tuple-element.53), channel_id=1, source_target_pairs={{0,16},{4,20},{8,24},{12,28},{16,0},{20,4},{24,8},{28,12},{1,17},{... | collective-permute-start | bytes 196616 | tf_op jit(solution)/shard_map/ppermute | solution.py:106
  36.3 3.7 %collective-permute-start.11 = (bf16[256,128]{1,0:T(8,128)(2,1)S(1)}, bf16[256,128]{1,0:T(8,128)(2,1)S(1)}, u32[]{:S(2)}, u32[]{:S(2)}) collective-permute-start(bf16[256,128]{1,0:T(8,128)(2,1)S(1)} %get-tuple-element.57), channel_id=1, source_target_pairs={{0,20},{4,16},{8,28},{12,24},{16,4},{20,0},{24,12},{28,8},{1,21},{... | collective-permute-start | bytes 196616 | tf_op jit(solution)/shard_map/ppermute | solution.py:106
  40.3 0.9 %collective-permute-start.13 = (bf16[256,128]{1,0:T(8,128)(2,1)S(1)}, bf16[256,128]{1,0:T(8,128)(2,1)S(1)}, u32[]{:S(2)}, u32[]{:S(2)}) collective-permute-start(bf16[256,128]{1,0:T(8,128)(2,1)S(1)} %get-tuple-element.59), channel_id=1, source_target_pairs={{0,12},{4,8},{8,4},{12,0},{16,28},{20,24},{24,20},{28,16},{1,13},{... | collective-permute-start | bytes 196616 | tf_op jit(solution)/shard_map/ppermute | solution.py:106
  41.2 2.7 %collective-permute-done.9.refs_3_ = bf16[256,128]{1,0:T(8,128)(2,1)S(1)} collective-permute-done((bf16[256,128]{1,0:T(8,128)(2,1)S(1)}, bf16[256,128]{1,0:T(8,128)(2,1)S(1)}, u32[]{:S(2)}, u32[]{:S(2)}) %collective-permute-start.9) | collective-permute-done | bytes 65568 | tf_op jit(solution)/shard_map/ppermute | solution.py:106
  44.0 1.7 %shard_map.87 = (bf16[256,1024]{1,0:T(8,128)(2,1)S(1)}, f32[256,1024]{1,0:T(8,128)S(1)}, f32[256,1024]{1,0:T(8,128)S(1)}) custom-call(bf16[256,1024]{1,0:T(8,128)(2,1)S(1)} %copy-done.2, bf16[256,1024]{1,0:T(8,128)(2,1)S(1)} %copy-done, bf16[256,1024]{1,0:T(8,128)(2,1)S(1)} %copy-done.1, f32[1,1024]{1,0:T(1,128)S(1)} %bitcast.3, ...), custom_call_target="tpu_custom_call" | custom-call | flops 1073741824 | bytes 2621440 | tf_op jit(solution)/shard_map/pallas_call | solution.py:395
  45.7 0.5 collective-permute-done.12.refs_1_
  47.1 0.5 collective-permute-start.15
  47.7 0.4 shard_map.91
  48.4 1.5 %collective-permute-start.18 = (bf16[256,512]{1,0:T(8,128)(2,1)S(1)}, bf16[256,512]{1,0:T(8,128)(2,1)S(1)}, u32[]{:S(2)}, u32[]{:S(2)}) collective-permute-start(bf16[256,512]{1,0:T(8,128)(2,1)S(1)} %shard_map.94), channel_id=1, source_target_pairs={{0,2},{2,0},{1,3},{3,1},{4,6},{6,4},{5,7},{7,5},{8,10},{10,8},{9,1... | collective-permute-start | bytes 786440 | tf_op jit(solution)/shard_map/ppermute | solution.py:622
  50.0 0.6 collective-permute-start.16
  50.7 1.3 %shard_map.90 = (bf16[256,1024]{1,0:T(8,128)(2,1)S(1)}, f32[256,1024]{1,0:T(8,128)S(1)}) custom-call(bf16[256,1024]{1,0:T(8,128)(2,1)S(1)} %shard_map.89.gated_ref, bf16[1024,4096]{1,0:T(8,128)(2,1)S(1)} %bitcast.2), custom_call_target="tpu_custom_call" | custom-call | flops 1073741824 | bytes 4194304 | tf_op jit(solution)/shard_map/pallas_call | solution.py:498
  52.1 5.5 %collective-permute-done.18.refs_1_ = bf16[256,512]{1,0:T(8,128)(2,1)S(1)} collective-permute-done((bf16[256,512]{1,0:T(8,128)(2,1)S(1)}, bf16[256,512]{1,0:T(8,128)(2,1)S(1)}, u32[]{:S(2)}, u32[]{:S(2)}) %collective-permute-start.18) | collective-permute-done | bytes 262176 | tf_op jit(solution)/shard_map/ppermute | solution.py:622
  57.6 4.8 %collective-permute-done.16.refs_0_ = bf16[256,512]{1,0:T(8,128)(2,1)S(1)} collective-permute-done((bf16[256,512]{1,0:T(8,128)(2,1)S(1)}, bf16[256,512]{1,0:T(8,128)(2,1)S(1)}, u32[]{:S(2)}, u32[]{:S(2)}) %collective-permute-start.16) | collective-permute-done | bytes 262176 | tf_op jit(solution)/shard_map/ppermute | solution.py:622
  62.4 0.9 %shard_map.96 = bf16[256,1024]{1,0:T(8,128)(2,1)} custom-call(f32[256,1024]{1,0:T(8,128)S(1)} %get-tuple-element.61.own_ref, bf16[256,1024]{1,0:T(8,128)(2,1)S(1)} %collective-permute-done.14.near_ref, bf16[256,512]{1,0:T(8,128)(2,1)S(1)} %collective-permute-done.16.refs_0_, bf16[256,512]{1,0:T(8,128)(2,1)S(1)} %collective-permute-done.18.refs_1_, ...), custom_call_target="tpu_custom_call" | custom-call | flops 262144 | bytes 2097152 | tf_op jit(solution)/shard_map/pallas_call | solution.py:565
  (34 shorter events, 2.0 us)
Async XLA Ops:
  1.8 10.5 %collective-permute-start = (bf16[256,256]{1,0:T(8,128)(2,1)S(1)}, bf16[256,256]{1,0:T(8,128)(2,1)S(1)}, u32[]{:S(2)}, u32[]{:S(2)}) collective-permute-start(bf16[256,256]{1,0:T(8,128)(2,1)S(1)} %get-tuple-element.36), channel_id=1, source_target_pairs={{0,16},{4,20},{8,24},{12,28},{16,0},{20,4},{24,8},{28,12},{1,17},{... | collective-permute-start | bytes 393224 | tf_op jit(solution)/shard_map/ppermute | solution.py:106
  5.9 12.3 %collective-permute-start.1 = (bf16[256,256]{1,0:T(8,128)(2,1)S(1)}, bf16[256,256]{1,0:T(8,128)(2,1)S(1)}, u32[]{:S(2)}, u32[]{:S(2)}) collective-permute-start(bf16[256,256]{1,0:T(8,128)(2,1)S(1)} %get-tuple-element.40), channel_id=1, source_target_pairs={{0,4},{4,0},{8,12},{12,8},{16,20},{20,16},{24,28},{28,24},{1,5},{5... | collective-permute-start | bytes 393224 | tf_op jit(solution)/shard_map/ppermute | solution.py:106
  7.4 11.7 %collective-permute-start.2 = (bf16[256,256]{1,0:T(8,128)(2,1)S(1)}, bf16[256,256]{1,0:T(8,128)(2,1)S(1)}, u32[]{:S(2)}, u32[]{:S(2)}) collective-permute-start(bf16[256,256]{1,0:T(8,128)(2,1)S(1)} %get-tuple-element.41), channel_id=1, source_target_pairs={{0,12},{4,8},{8,4},{12,0},{16,28},{20,24},{24,20},{28,16},{1,13},{... | collective-permute-start | bytes 393224 | tf_op jit(solution)/shard_map/ppermute | solution.py:106
  8.9 11.1 %collective-permute-start.3 = (bf16[256,256]{1,0:T(8,128)(2,1)S(1)}, bf16[256,256]{1,0:T(8,128)(2,1)S(1)}, u32[]{:S(2)}, u32[]{:S(2)}) collective-permute-start(bf16[256,256]{1,0:T(8,128)(2,1)S(1)} %get-tuple-element.42), channel_id=1, source_target_pairs={{0,8},{4,12},{8,0},{12,4},{16,24},{20,28},{24,16},{28,20},{1,9},{5... | collective-permute-start | bytes 393224 | tf_op jit(solution)/shard_map/ppermute | solution.py:106
  9.4 10.6 %collective-permute-start.4 = (bf16[256,256]{1,0:T(8,128)(2,1)S(1)}, bf16[256,256]{1,0:T(8,128)(2,1)S(1)}, u32[]{:S(2)}, u32[]{:S(2)}) collective-permute-start(bf16[256,256]{1,0:T(8,128)(2,1)S(1)} %get-tuple-element.43), channel_id=1, source_target_pairs={{0,20},{4,16},{8,28},{12,24},{16,4},{20,0},{24,12},{28,8},{1,21},{... | collective-permute-start | bytes 393224 | tf_op jit(solution)/shard_map/ppermute | solution.py:106
  12.3 11.1 %collective-permute-start.5 = (bf16[256,256]{1,0:T(8,128)(2,1)S(1)}, bf16[256,256]{1,0:T(8,128)(2,1)S(1)}, u32[]{:S(2)}, u32[]{:S(2)}) collective-permute-start(bf16[256,256]{1,0:T(8,128)(2,1)S(1)} %get-tuple-element.46), channel_id=1, source_target_pairs={{0,28},{4,24},{8,20},{12,16},{16,12},{20,8},{24,4},{28,0},{1,29},{... | collective-permute-start | bytes 393224 | tf_op jit(solution)/shard_map/ppermute | solution.py:106
  18.2 6.9 %collective-permute-start.6 = (bf16[256,256]{1,0:T(8,128)(2,1)S(1)}, bf16[256,256]{1,0:T(8,128)(2,1)S(1)}, u32[]{:S(2)}, u32[]{:S(2)}) collective-permute-start(bf16[256,256]{1,0:T(8,128)(2,1)S(1)} %get-tuple-element.49), channel_id=1, source_target_pairs={{0,24},{4,28},{8,16},{12,20},{16,8},{20,12},{24,0},{28,4},{1,25},{... | collective-permute-start | bytes 393224 | tf_op jit(solution)/shard_map/ppermute | solution.py:106
  23.3 20.6 %slice-start = ((s8[8388608]{0:T(1024)(128)(4,1)}), s8[4194304]{0:T(1024)(128)(4,1)S(1)}, s32[]{:S(2)}) async-start(s8[8388608]{0:T(1024)(128)(4,1)} %bitcast.1), calls=%async_computation | async-start | bytes 8388608
  24.0 20.0 %copy-start = (bf16[256,1024]{1,0:T(8,128)(2,1)S(1)}, bf16[256,1024]{1,0:T(8,128)(2,1)}, u32[]{:S(2)}) copy-start(bf16[256,1024]{1,0:T(8,128)(2,1)} %keys_ref.3) | copy-start | bytes 1572868
  24.0 20.0 %copy-start.1 = (bf16[256,1024]{1,0:T(8,128)(2,1)S(1)}, bf16[256,1024]{1,0:T(8,128)(2,1)}, u32[]{:S(2)}) copy-start(bf16[256,1024]{1,0:T(8,128)(2,1)} %values_ref.3) | copy-start | bytes 1572868
  24.0 19.9 %copy-start.2 = (bf16[256,1024]{1,0:T(8,128)(2,1)S(1)}, bf16[256,1024]{1,0:T(8,128)(2,1)}, u32[]{:S(2)}) copy-start(bf16[256,1024]{1,0:T(8,128)(2,1)} %queries_ref.3) | copy-start | bytes 1572868
  24.0 19.9 %copy-start.3 = (f32[1024]{0:T(1024)S(1)}, f32[1024]{0:T(1024)}, u32[]{:S(2)}) copy-start(f32[1024]{0:T(1024)} %param.12) | copy-start | bytes 12292
  25.1 18.9 %slice-start.1 = ((s8[8388608]{0:T(1024)(128)(4,1)}), s8[4194304]{0:T(1024)(128)(4,1)S(1)}, s32[]{:S(2)}) async-start(s8[8388608]{0:T(1024)(128)(4,1)} %bitcast.1), calls=%async_computation.1 | async-start | bytes 8388608
  27.1 12.9 %collective-permute-start.7 = (bf16[256,128]{1,0:T(8,128)(2,1)S(1)}, bf16[256,128]{1,0:T(8,128)(2,1)S(1)}, u32[]{:S(2)}, u32[]{:S(2)}) collective-permute-start(bf16[256,128]{1,0:T(8,128)(2,1)S(1)} %get-tuple-element.51), channel_id=1, source_target_pairs={{0,4},{4,0},{8,12},{12,8},{16,20},{20,16},{24,28},{28,24},{1,5},{5... | collective-permute-start | bytes 196616 | tf_op jit(solution)/shard_map/ppermute | solution.py:106
  31.7 8.6 %collective-permute-start.8 = (bf16[256,128]{1,0:T(8,128)(2,1)S(1)}, bf16[256,128]{1,0:T(8,128)(2,1)S(1)}, u32[]{:S(2)}, u32[]{:S(2)}) collective-permute-start(bf16[256,128]{1,0:T(8,128)(2,1)S(1)} %get-tuple-element.52), channel_id=1, source_target_pairs={{0,28},{4,24},{8,20},{12,16},{16,12},{20,8},{24,4},{28,0},{1,29},{... | collective-permute-start | bytes 196616 | tf_op jit(solution)/shard_map/ppermute | solution.py:106
  34.0 10.0 %collective-permute-start.9 = (bf16[256,128]{1,0:T(8,128)(2,1)S(1)}, bf16[256,128]{1,0:T(8,128)(2,1)S(1)}, u32[]{:S(2)}, u32[]{:S(2)}) collective-permute-start(bf16[256,128]{1,0:T(8,128)(2,1)S(1)} %get-tuple-element.53), channel_id=1, source_target_pairs={{0,16},{4,20},{8,24},{12,28},{16,0},{20,4},{24,8},{28,12},{1,17},{... | collective-permute-start | bytes 196616 | tf_op jit(solution)/shard_map/ppermute | solution.py:106
  36.0 7.9 %collective-permute-start.10 = (bf16[256,128]{1,0:T(8,128)(2,1)S(1)}, bf16[256,128]{1,0:T(8,128)(2,1)S(1)}, u32[]{:S(2)}, u32[]{:S(2)}) collective-permute-start(bf16[256,128]{1,0:T(8,128)(2,1)S(1)} %get-tuple-element.54), channel_id=1, source_target_pairs={{0,8},{4,12},{8,0},{12,4},{16,24},{20,28},{24,16},{28,20},{1,9},{5... | collective-permute-start | bytes 196616 | tf_op jit(solution)/shard_map/ppermute | solution.py:106
  36.3 9.4 %collective-permute-start.11 = (bf16[256,128]{1,0:T(8,128)(2,1)S(1)}, bf16[256,128]{1,0:T(8,128)(2,1)S(1)}, u32[]{:S(2)}, u32[]{:S(2)}) collective-permute-start(bf16[256,128]{1,0:T(8,128)(2,1)S(1)} %get-tuple-element.57), channel_id=1, source_target_pairs={{0,20},{4,16},{8,28},{12,24},{16,4},{20,0},{24,12},{28,8},{1,21},{... | collective-permute-start | bytes 196616 | tf_op jit(solution)/shard_map/ppermute | solution.py:106
  40.0 6.2 %collective-permute-start.12 = (bf16[256,128]{1,0:T(8,128)(2,1)S(1)}, bf16[256,128]{1,0:T(8,128)(2,1)S(1)}, u32[]{:S(2)}, u32[]{:S(2)}) collective-permute-start(bf16[256,128]{1,0:T(8,128)(2,1)S(1)} %get-tuple-element.58), channel_id=1, source_target_pairs={{0,24},{4,28},{8,16},{12,20},{16,8},{20,12},{24,0},{28,4},{1,25},{... | collective-permute-start | bytes 196616 | tf_op jit(solution)/shard_map/ppermute | solution.py:106
  40.3 6.0 %collective-permute-start.13 = (bf16[256,128]{1,0:T(8,128)(2,1)S(1)}, bf16[256,128]{1,0:T(8,128)(2,1)S(1)}, u32[]{:S(2)}, u32[]{:S(2)}) collective-permute-start(bf16[256,128]{1,0:T(8,128)(2,1)S(1)} %get-tuple-element.59), channel_id=1, source_target_pairs={{0,12},{4,8},{8,4},{12,0},{16,28},{20,24},{24,20},{28,16},{1,13},{... | collective-permute-start | bytes 196616 | tf_op jit(solution)/shard_map/ppermute | solution.py:106
  46.7 1.6 %collective-permute-start.17 = (bf16[256,512]{1,0:T(8,128)(2,1)S(1)}, bf16[256,512]{1,0:T(8,128)(2,1)S(1)}, u32[]{:S(2)}, u32[]{:S(2)}) collective-permute-start(bf16[256,512]{1,0:T(8,128)(2,1)S(1)} %get-tuple-element.66), channel_id=1, source_target_pairs={{0,1},{1,0},{2,3},{3,2},{4,5},{5,4},{6,7},{7,6},{8,9},{9,8},{10,11... | collective-permute-start | bytes 786440 | tf_op jit(solution)/shard_map/ppermute | solution.py:621
  47.1 2.8 %collective-permute-start.15 = (bf16[256,512]{1,0:T(8,128)(2,1)S(1)}, bf16[256,512]{1,0:T(8,128)(2,1)S(1)}, u32[]{:S(2)}, u32[]{:S(2)}) collective-permute-start(bf16[256,512]{1,0:T(8,128)(2,1)S(1)} %shard_map.92), channel_id=1, source_target_pairs={{0,1},{1,0},{2,3},{3,2},{4,5},{5,4},{6,7},{7,6},{8,9},{9,8},{10,11... | collective-permute-start | bytes 786440 | tf_op jit(solution)/shard_map/ppermute | solution.py:621
  48.4 9.2 %collective-permute-start.18 = (bf16[256,512]{1,0:T(8,128)(2,1)S(1)}, bf16[256,512]{1,0:T(8,128)(2,1)S(1)}, u32[]{:S(2)}, u32[]{:S(2)}) collective-permute-start(bf16[256,512]{1,0:T(8,128)(2,1)S(1)} %shard_map.94), channel_id=1, source_target_pairs={{0,2},{2,0},{1,3},{3,1},{4,6},{6,4},{5,7},{7,5},{8,10},{10,8},{9,1... | collective-permute-start | bytes 786440 | tf_op jit(solution)/shard_map/ppermute | solution.py:622
  50.0 12.4 %collective-permute-start.16 = (bf16[256,512]{1,0:T(8,128)(2,1)S(1)}, bf16[256,512]{1,0:T(8,128)(2,1)S(1)}, u32[]{:S(2)}, u32[]{:S(2)}) collective-permute-start(bf16[256,512]{1,0:T(8,128)(2,1)S(1)} %shard_map.93), channel_id=1, source_target_pairs={{0,2},{2,0},{1,3},{3,1},{4,6},{6,4},{5,7},{7,5},{8,10},{10,8},{9,1... | collective-permute-start | bytes 786440 | tf_op jit(solution)/shard_map/ppermute | solution.py:622
  52.0 10.4 %collective-permute-start.14 = (bf16[256,1024]{1,0:T(8,128)(2,1)S(1)}, bf16[256,1024]{1,0:T(8,128)(2,1)S(1)}, u32[]{:S(2)}, u32[]{:S(2)}) collective-permute-start(bf16[256,1024]{1,0:T(8,128)(2,1)S(1)} %get-tuple-element.62), channel_id=1, source_target_pairs={{0,1},{1,0},{2,3},{3,2},{4,5},{5,4},{6,7},{7,6},{8,9},{9,8},{10,11... | collective-permute-start | bytes 1572872 | tf_op jit(solution)/shard_map/ppermute | solution.py:625
